TPU v7x, 32 devices: a whole 2x2x4 slice. The times are simulated.
32 devices in a mesh: fsdp: 4 (over y, x), seq: 8 (over z, core).
Axes of the slice: x: 2, y: 2, z: 4, core: 2. Of those that a mesh axis runs over, the one named last changes fastest.
Arguments:
- tokens: bfloat16 [16384, 1024], P(('fsdp', 'seq')), may hold values from -6 to 6
- cotangent: bfloat16 [16384, 1024], P(('fsdp', 'seq')), may hold values from -6 to 6
- segment_ids: int32 [16384], P(('fsdp', 'seq')), may hold values from 0 to 1, as said below
- valid: int32 [16384], P(('fsdp', 'seq')), may hold values from 0 to 1, as said below
- project_in: float32 [1024, 3072], P(('fsdp', 'seq')), may hold values from -0.1875 to 0.1875
- project_out: float32 [1024, 1024], P(('fsdp', 'seq')), may hold values from -4 to 4
- hidden_up: float32 [1024, 4096], P(('fsdp', 'seq')), may hold values from -0.1875 to 0.1875
- hidden_down: float32 [4096, 1024], P(('fsdp', 'seq')), may hold values from -0.09375 to 0.09375
- gains_biases: float32 [14, 1024], P(None, ('fsdp', 'seq')), may hold values from -0.9 to 1.45
- moment_in: float32 [1024, 3072], P(('fsdp', 'seq')), may hold values from -56 to 56
- moment_out: float32 [1024, 1024], P(('fsdp', 'seq')), may hold values from -6 to 6
- moment_up: float32 [1024, 4096], P(('fsdp', 'seq')), may hold values from -20 to 20
- moment_down: float32 [4096, 1024], P(('fsdp', 'seq')), may hold values from -40 to 40
- moment_gains: float32 [14, 1024], P(None, ('fsdp', 'seq')), may hold values from -64 to 64
- square_in: float32 [1024, 3072], P(('fsdp', 'seq')), may hold values from 7.0144 to 28.0576
- square_out: float32 [1024, 1024], P(('fsdp', 'seq')), may hold values from 0.04704 to 0.18816
- square_up: float32 [1024, 4096], P(('fsdp', 'seq')), may hold values from 0.9864 to 3.9456
- square_down: float32 [4096, 1024], P(('fsdp', 'seq')), may hold values from 3.9456 to 15.7824
- square_gains: float32 [14, 1024], P(None, ('fsdp', 'seq')), may hold values from 10.96 to 43.84
Outputs:
- block_output: bfloat16 [16384, 1024], P(('fsdp', 'seq'))
- input_grad: float32 [16384, 1024], P(('fsdp', 'seq'))
- new_project_in: float32 [1024, 3072], P(('fsdp', 'seq'))
- new_project_out: float32 [1024, 1024], P(('fsdp', 'seq'))
- new_hidden_up: float32 [1024, 4096], P(('fsdp', 'seq'))
- new_hidden_down: float32 [4096, 1024], P(('fsdp', 'seq'))
- new_gains: float32 [14, 1024], P(None, ('fsdp', 'seq'))
- new_moment_in: float32 [1024, 3072], P(('fsdp', 'seq'))
- new_moment_out: float32 [1024, 1024], P(('fsdp', 'seq'))
- new_moment_up: float32 [1024, 4096], P(('fsdp', 'seq'))
- new_moment_down: float32 [4096, 1024], P(('fsdp', 'seq'))
- new_moment_gains: float32 [14, 1024], P(None, ('fsdp', 'seq'))
- new_square_in: float32 [1024, 3072], P(('fsdp', 'seq'))
- new_square_out: float32 [1024, 1024], P(('fsdp', 'seq'))
- new_square_up: float32 [1024, 4096], P(('fsdp', 'seq'))
- new_square_down: float32 [4096, 1024], P(('fsdp', 'seq'))
- new_square_gains: float32 [14, 1024], P(None, ('fsdp', 'seq'))
- down_bias_gradient: float32 [1024], P(('fsdp', 'seq'))
Inputs may be any that keep to these rules, and one draw needn't show every extreme that they name: `segment_ids`: each stream of 4096 consecutive tokens holds 2 images in order, each 1370 consecutive tokens, with padding between and around them; ids never fall within a stream and start again at 0 in the next; padding carries the id of the image before it, 0 before the first. `valid`: 1 exactly on the tokens of the images.
All inputs are finite; a program needn't handle non-finite values.
Results may differ from a plain program's by a relative error of at most 0.012.
The roundings to bfloat16 on the way count: a program that leaves them out, or rounds other values in their place, can miss the bound.
Values may be sent and summed in bfloat16 or wider, within the bound.
No kernel may reach another device: no remote copies, remote signals or barrier semaphores. Data moves between devices by JAX's collectives and lax.ppermute only.
A program may use at most 192 MiB of HBM per device.

v0:
```python
import jax
import jax.numpy as jnp
from jax import lax
from jax.sharding import PartitionSpec as P

D = 1024
FF = 4096
HEADS = 16
HEAD_DIM = 64
IMG_LEN = 1370
QBLOCK = 512
STEP = 10


masked_score = -1e30


def layer_norm(values, gain, shift):
    average = jnp.mean(values, axis=-1, keepdims=True)
    centered = values - average
    variance = jnp.mean(centered * centered, axis=-1, keepdims=True)
    return centered * lax.rsqrt(variance + 1e-06) * gain + shift


def exact_gelu(values):
    return jax.nn.gelu(values, approximate=False)


def plain_product(left, right):
    return jnp.dot(left, right, preferred_element_type=jnp.float32)


def inner_rows(left, right):
    return lax.dot_general(
        left, right, (((0,), (0,)), ((), ())), preferred_element_type=jnp.float32
    )


def inner_cols(left, right):
    return lax.dot_general(
        left, right, (((1,), (1,)), ((), ())), preferred_element_type=jnp.float32
    )


def adamw(param, moment, square, grad, rate, decay):
    new_moment = 0.9 * moment + 0.1 * grad
    new_square = 0.999 * square + 0.001 * grad * grad
    corrected = new_moment / (1.0 - 0.9**STEP)
    scaled = jnp.sqrt(new_square / (1.0 - 0.999**STEP)) + 1e-08
    return (param - rate * (corrected / scaled + decay * param), new_moment, new_square)


def window_setup(stream, labels):
    margin = IMG_LEN
    widths = ((margin, margin), (0, 0), (0, 0))
    key_pad = jnp.pad(stream[:, 1], widths)
    value_pad = jnp.pad(stream[:, 2], widths)
    seg_pad = jnp.pad(labels[0], (margin, margin), constant_values=-1)
    valid_pad = jnp.pad(labels[1], (margin, margin))
    return (key_pad, value_pad, seg_pad, valid_pad)


def block_scores(query_block, key_window, seg_query, valid_query, seg_key, valid_key):
    allowed = (
        (seg_query[:, None] == seg_key[None, :])
        & (valid_query[:, None] == 1)
        & (valid_key[None, :] == 1)
    )
    scores = jnp.einsum(
        "qhd,khd->hqk", query_block, key_window, preferred_element_type=jnp.float32
    ) * HEAD_DIM ** (-0.5)
    return (jnp.where(allowed[None], scores, masked_score), allowed.astype(jnp.float32)[None])


def attend(stream, labels):
    length = stream.shape[0]
    span = QBLOCK + 2 * IMG_LEN
    key_pad, value_pad, seg_pad, valid_pad = window_setup(stream, labels)

    def one_block(number):
        begin = number * QBLOCK
        query_block = lax.dynamic_slice_in_dim(stream[:, 0], begin, QBLOCK, 0)
        seg_query = lax.dynamic_slice_in_dim(labels[0], begin, QBLOCK, 0)
        valid_query = lax.dynamic_slice_in_dim(labels[1], begin, QBLOCK, 0)
        key_window = lax.dynamic_slice_in_dim(key_pad, begin, span, 0)
        value_window = lax.dynamic_slice_in_dim(value_pad, begin, span, 0)
        seg_key = lax.dynamic_slice_in_dim(seg_pad, begin, span, 0)
        valid_key = lax.dynamic_slice_in_dim(valid_pad, begin, span, 0)
        masked, allowed = block_scores(
            query_block, key_window, seg_query, valid_query, seg_key, valid_key
        )
        top = jnp.max(masked, axis=-1, keepdims=True)
        weights = jnp.exp(masked - top) * allowed
        total = (
            jnp.sum(weights, axis=-1, keepdims=True)
            + (1 - valid_query).astype(jnp.float32)[None, :, None]
        )
        probs = (weights / total).astype(jnp.bfloat16)
        output = jnp.einsum("hqk,khd->qhd", probs, value_window, preferred_element_type=jnp.float32)
        return (output.astype(jnp.bfloat16), (top + jnp.log(total))[..., 0])

    outputs, log_totals = lax.map(one_block, jnp.arange(length // QBLOCK))
    return (outputs.reshape(length, stream.shape[2], stream.shape[3]), log_totals)


def attend_back(stream, labels, log_totals, grad_out):
    length = stream.shape[0]
    span = QBLOCK + 2 * IMG_LEN
    key_pad, value_pad, seg_pad, valid_pad = window_setup(stream, labels)
    zero = jnp.zeros((length + 2 * IMG_LEN, stream.shape[2], stream.shape[3]), jnp.float32)

    def one_block(carry, number):
        key_grad, value_grad = carry
        begin = number * QBLOCK
        query_block = lax.dynamic_slice_in_dim(stream[:, 0], begin, QBLOCK, 0)
        seg_query = lax.dynamic_slice_in_dim(labels[0], begin, QBLOCK, 0)
        valid_query = lax.dynamic_slice_in_dim(labels[1], begin, QBLOCK, 0)
        key_window = lax.dynamic_slice_in_dim(key_pad, begin, span, 0)
        value_window = lax.dynamic_slice_in_dim(value_pad, begin, span, 0)
        seg_key = lax.dynamic_slice_in_dim(seg_pad, begin, span, 0)
        valid_key = lax.dynamic_slice_in_dim(valid_pad, begin, span, 0)
        masked, allowed = block_scores(
            query_block, key_window, seg_query, valid_query, seg_key, valid_key
        )
        probs = jnp.exp(masked - log_totals[number][..., None]) * allowed
        grad_block = lax.dynamic_slice_in_dim(grad_out, begin, QBLOCK, 0)
        value_part = jnp.einsum(
            "hqk,qhd->khd",
            probs.astype(jnp.bfloat16),
            grad_block,
            preferred_element_type=jnp.float32,
        )
        grad_probs = jnp.einsum(
            "qhd,khd->hqk", grad_block, value_window, preferred_element_type=jnp.float32
        )
        centre = jnp.sum(grad_probs * probs, axis=-1, keepdims=True)
        grad_scores = (probs * (grad_probs - centre)).astype(jnp.bfloat16)
        query_part = jnp.einsum(
            "hqk,khd->qhd", grad_scores, key_window, preferred_element_type=jnp.float32
        ) * HEAD_DIM ** (-0.5)
        key_part = jnp.einsum(
            "hqk,qhd->khd", grad_scores, query_block, preferred_element_type=jnp.float32
        ) * HEAD_DIM ** (-0.5)
        key_grad = lax.dynamic_update_slice_in_dim(
            key_grad, lax.dynamic_slice_in_dim(key_grad, begin, span, 0) + key_part, begin, 0
        )
        value_grad = lax.dynamic_update_slice_in_dim(
            value_grad, lax.dynamic_slice_in_dim(value_grad, begin, span, 0) + value_part, begin, 0
        )
        return ((key_grad, value_grad), query_part)

    (key_grad, value_grad), query_parts = lax.scan(
        one_block, (zero, zero), jnp.arange(length // QBLOCK)
    )
    query_grad = query_parts.reshape(length, stream.shape[2], stream.shape[3])
    inner_keys = key_grad[IMG_LEN : IMG_LEN + length]
    inner_values = value_grad[IMG_LEN : IMG_LEN + length]
    return jnp.stack([query_grad, inner_keys, inner_values], axis=1).astype(jnp.bfloat16)


def on_device(
    tokens,
    cotangent,
    segment_ids,
    valid,
    project_in,
    project_out,
    hidden_up,
    hidden_down,
    gains_biases,
    moment_in,
    moment_out,
    moment_up,
    moment_down,
    moment_gains,
    square_in,
    square_out,
    square_up,
    square_down,
    square_gains,
):
    rows = tokens.shape[0]
    width = tokens.shape[1]
    whole_in, whole_out, whole_up, whole_down, whole_gains = (
        lax.all_gather(project_in.astype(jnp.bfloat16), ("fsdp", "seq"), axis=0, tiled=True),
        lax.all_gather(project_out.astype(jnp.bfloat16), ("fsdp", "seq"), axis=0, tiled=True),
        lax.all_gather(hidden_up.astype(jnp.bfloat16), ("fsdp", "seq"), axis=0, tiled=True),
        lax.all_gather(hidden_down.astype(jnp.bfloat16), ("fsdp", "seq"), axis=0, tiled=True),
        lax.all_gather(gains_biases.astype(jnp.bfloat16), ("fsdp", "seq"), axis=1, tiled=True),
    )
    vectors = whole_gains.astype(jnp.float32)
    gain_one, shift_one, bias_query, bias_value, bias_out = (
        vectors[0],
        vectors[1],
        vectors[2],
        vectors[3],
        vectors[4],
    )
    scale_one, gain_two, shift_two, bias_down, scale_two = (
        vectors[5],
        vectors[6],
        vectors[7],
        vectors[8],
        vectors[9],
    )
    bias_up = vectors[10:].reshape(-1)
    bias_in = jnp.concatenate([bias_query, jnp.zeros_like(bias_query), bias_value])
    labels = (
        lax.all_gather(segment_ids, "seq", axis=0, tiled=True),
        lax.all_gather(valid, "seq", axis=0, tiled=True),
    )
    inputs = tokens.astype(jnp.float32)
    norm_one, norm_one_back = jax.vjp(layer_norm, inputs, gain_one, shift_one)
    normed_one = norm_one.astype(jnp.bfloat16)
    mixed = (plain_product(normed_one, whole_in) + bias_in).astype(jnp.bfloat16)
    stream = lax.all_to_all(
        mixed.reshape(rows, 3, HEADS, HEAD_DIM), "seq", split_axis=2, concat_axis=0, tiled=True
    )
    attended, log_totals = attend(stream, labels)
    returned = lax.all_to_all(attended, "seq", split_axis=0, concat_axis=1, tiled=True)
    attended_rows = returned.reshape(rows, width)
    projected = plain_product(attended_rows, whole_out) + bias_out
    second = inputs + scale_one * projected
    norm_two, norm_two_back = jax.vjp(layer_norm, second, gain_two, shift_two)
    normed_two = norm_two.astype(jnp.bfloat16)
    upward = plain_product(normed_two, whole_up) + bias_up
    activated, gelu_back = jax.vjp(exact_gelu, upward)
    active = activated.astype(jnp.bfloat16)
    branch = plain_product(active, whole_down) + bias_down
    block_output = (second + scale_two * branch).astype(jnp.bfloat16)
    back_in, back_out, back_up, back_down = (whole_in, whole_out, whole_up, whole_down)
    grad_rows = cotangent.astype(jnp.float32) * valid.astype(jnp.float32)[:, None]
    grad_scale_two = jnp.sum(grad_rows * branch, axis=0)
    grad_branch = (scale_two * grad_rows).astype(jnp.bfloat16)
    grad_bias_down = jnp.sum(grad_branch.astype(jnp.float32), axis=0)
    grad_down = inner_rows(active, grad_branch)
    grad_active = inner_cols(grad_branch, back_down)
    grad_upward = gelu_back(grad_active)[0].astype(jnp.bfloat16)
    grad_bias_up = jnp.sum(grad_upward.astype(jnp.float32), axis=0)
    grad_up = inner_rows(normed_two, grad_upward)
    grad_norm_two = inner_cols(grad_upward, back_up)
    second_part, grad_gain_two, grad_shift_two = norm_two_back(grad_norm_two)
    grad_second = grad_rows + second_part
    grad_scale_one = jnp.sum(grad_second * projected, axis=0)
    grad_projected = (scale_one * grad_second).astype(jnp.bfloat16)
    grad_bias_out = jnp.sum(grad_projected.astype(jnp.float32), axis=0)
    grad_out = inner_rows(attended_rows, grad_projected)
    grad_attended = inner_cols(grad_projected, back_out).astype(jnp.bfloat16)
    grad_stream = lax.all_to_all(
        grad_attended.reshape(rows, HEADS, HEAD_DIM), "seq", split_axis=1, concat_axis=0, tiled=True
    )
    grad_mixed_stream = attend_back(stream, labels, log_totals, grad_stream)
    grad_mixed = lax.all_to_all(
        grad_mixed_stream, "seq", split_axis=0, concat_axis=2, tiled=True
    ).reshape(rows, 3 * width)
    grad_mixed_wide = grad_mixed.astype(jnp.float32)
    grad_bias_query = jnp.sum(grad_mixed_wide[:, :width], axis=0)
    grad_bias_value = jnp.sum(grad_mixed_wide[:, 2 * width :], axis=0)
    grad_in = inner_rows(normed_one, grad_mixed)
    grad_norm_one = inner_cols(grad_mixed, back_in)
    first_part, grad_gain_one, grad_shift_one = norm_one_back(grad_norm_one)
    input_grad = grad_second + first_part
    grad_small = jnp.concatenate(
        [
            jnp.stack(
                [
                    grad_gain_one,
                    grad_shift_one,
                    grad_bias_query,
                    grad_bias_value,
                    grad_bias_out,
                    grad_scale_one,
                    grad_gain_two,
                    grad_shift_two,
                    grad_bias_down,
                    grad_scale_two,
                ]
            ),
            grad_bias_up.reshape(-1, width),
        ],
        axis=0,
    )
    summed_in, summed_out, summed_up, summed_down, summed_gains = (
        lax.psum_scatter(grad_in, ("fsdp", "seq"), scatter_dimension=0, tiled=True),
        lax.psum_scatter(grad_out, ("fsdp", "seq"), scatter_dimension=0, tiled=True),
        lax.psum_scatter(grad_up, ("fsdp", "seq"), scatter_dimension=0, tiled=True),
        lax.psum_scatter(grad_down, ("fsdp", "seq"), scatter_dimension=0, tiled=True),
        lax.psum_scatter(grad_small, ("fsdp", "seq"), scatter_dimension=1, tiled=True),
    )
    rate_out = max(1, 4 * D // IMG_LEN) ** (-0.5)
    new_in, new_moment_in, new_square_in = adamw(
        project_in, moment_in, square_in, summed_in, D ** (-0.5), 0.04
    )
    new_out, new_moment_out, new_square_out = adamw(
        project_out, moment_out, square_out, summed_out, rate_out, 0.04
    )
    new_up, new_moment_up, new_square_up = adamw(
        hidden_up, moment_up, square_up, summed_up, D ** (-0.5), 0.04
    )
    new_down, new_moment_down, new_square_down = adamw(
        hidden_down, moment_down, square_down, summed_down, FF ** (-0.5), 0.04
    )
    new_gains, new_moment_gains, new_square_gains = adamw(
        gains_biases, moment_gains, square_gains, summed_gains, 0.2, 0.0
    )
    return (
        block_output,
        input_grad,
        new_in,
        new_out,
        new_up,
        new_down,
        new_gains,
        new_moment_in,
        new_moment_out,
        new_moment_up,
        new_moment_down,
        new_moment_gains,
        new_square_in,
        new_square_out,
        new_square_up,
        new_square_down,
        new_square_gains,
        summed_gains[8],
    )


def solution(mesh):
    return jax.shard_map(
        on_device,
        mesh=mesh,
        in_specs=(
            P(("fsdp", "seq"), None),
            P(("fsdp", "seq"), None),
            P(("fsdp", "seq")),
            P(("fsdp", "seq")),
            P(("fsdp", "seq"), None),
            P(("fsdp", "seq"), None),
            P(("fsdp", "seq"), None),
            P(("fsdp", "seq"), None),
            P(None, ("fsdp", "seq")),
            P(("fsdp", "seq"), None),
            P(("fsdp", "seq"), None),
            P(("fsdp", "seq"), None),
            P(("fsdp", "seq"), None),
            P(None, ("fsdp", "seq")),
            P(("fsdp", "seq"), None),
            P(("fsdp", "seq"), None),
            P(("fsdp", "seq"), None),
            P(("fsdp", "seq"), None),
            P(None, ("fsdp", "seq")),
        ),
        out_specs=(
            P(("fsdp", "seq"), None),
            P(("fsdp", "seq"), None),
            P(("fsdp", "seq"), None),
            P(("fsdp", "seq"), None),
            P(("fsdp", "seq"), None),
            P(("fsdp", "seq"), None),
            P(None, ("fsdp", "seq")),
            P(("fsdp", "seq"), None),
            P(("fsdp", "seq"), None),
            P(("fsdp", "seq"), None),
            P(("fsdp", "seq"), None),
            P(None, ("fsdp", "seq")),
            P(("fsdp", "seq"), None),
            P(("fsdp", "seq"), None),
            P(("fsdp", "seq"), None),
            P(("fsdp", "seq"), None),
            P(None, ("fsdp", "seq")),
            P(("fsdp", "seq")),
        ),
        check_vma=False,
    )
```

profile of v0, /device:TPU:0, one launch (start us, length us, event | category | flops | bytes accessed | tf_op | source)
XLA Modules:
  0.0 2137.9 jit_solution(355387276926485944)
XLA Ops:
  9.7 44.1 %all-gather = bf16[32,32,14]{1,2,0:T(8,128)(2,1)S(1)} all-gather(bf16[1,32,14]{1,2,0:T(8,128)(2,1)S(1)} %convert_bitcast_fusion), channel_id=1, replica_groups=mesh['fsdp'=4,'seq'=8] {'fsdp','seq'}, dimensions={0}, use_global_device_ids=true | all-gather | bytes 29568 | tf_op jit(solution)/shard_map/all_gather | solution.py:189
  57.8 26.2 %all-gather.8.cloned.1.call-done = bf16[1024,3072]{1,0:T(8,128)(2,1)} async-done(((bf16[32,3072]{1,0:T(8,128)(2,1)}), bf16[1024,3072]{1,0:T(8,128)(2,1)}) %all-gather.8.cloned.1.call-update) | async-done | bytes 6291472 | tf_op jit(solution)/shard_map/all_gather | solution.py:185
  84.1 7.8 add_convert_fusion.1
  103.4 84.7 %all-gather.2 = s32[8,1,512]{2,1,0:T(1,128)S(1)} all-gather(s32[1,1,512]{2,1,0:T(1,128)S(1)} %bitcast.206), channel_id=1, replica_groups=mesh['fsdp'=4,'seq'=8] {'seq'}, dimensions={0}, use_global_device_ids=true | all-gather | bytes 18432 | tf_op jit(solution)/shard_map/all_gather | solution.py:210
  188.2 13.3 all-gather.1
  216.7 179.9 %while.26 = (s32[]{:T(128)}, bf16[8,512,2,64]{1,3,2,0:T(8,128)(2,1)}, f32[8,2,512]{2,1,0:T(2,128)}, s32[8]{0:T(128)S(1)}, bf16[6836,2,64]{0,2,1:T(8,128)(2,1)}, ...) while((s32[]{:T(128)}, ...), condition=%wide.region_5.6_spmd, body=%wide.region_2.5_spmd.sunk | while | flops 905844416 | bytes 70784432 | solution.py:102
  409.2 25.5 %all-to-all-done.1 = bf16[8,2,32768]{2,1,0:T(2,128)(2,1)} async-done(((bf16[8,2,32768]{2,1,0:T(2,128)(2,1)}), bf16[8,2,32768]{2,1,0:T(2,128)(2,1)}, u32[]{:S(2)}, u32[]{:S(2)}) %all-to-all-start.1) | async-done | bytes 1048608 | tf_op jit(solution)/shard_map/all_to_all | solution.py:220
  446.3 27.5 %multiply_convert_fusion.1 = (bf16[512,4096]{1,0:T(8,128)(2,1)S(1)}, f32[512,4096]{1,0:T(8,128)}, f32[512,4096]{1,0:T(8,128)}) fusion(f32[4096]{0:T(1024)S(1)} %bitcast.196, bf16[1024,4096]{1,0:T(8,128)(2,1)} %all-gather.12.cloned.1.call-done, f32[512,1024]{1,0:T(8,128)S(1)} %get-tuple-element.239, f32[1024]{0:T(1024)S(1)} %bitcast.207, ...), kind=kOutput, calls=%fused_computation.65 | convolution fusion | flops 4436000768 | bytes 31485952 | tf_op jit(solution)/shard_map/dot_general | solution.py:30
  475.8 8.4 fusion.76
  484.7 184.2 %reduce-scatter.14.cloned.1.call-done = f32[128,1024]{1,0:T(8,128)} async-done(((f32[4096,1024]{1,0:T(8,128)}), f32[128,1024]{1,0:T(8,128)}) %reduce-scatter.14.cloned.1.call-update) | async-done | bytes 524304 | tf_op jit(solution)/shard_map/reduce_scatter | solution.py:287
  672.2 75.3 %all-gather.14.cloned.1.call-done = bf16[4096,1024]{1,0:T(8,128)(2,1)} async-done(((bf16[128,1024]{1,0:T(8,128)(2,1)}), bf16[4096,1024]{1,0:T(8,128)(2,1)}) %all-gather.14.cloned.1.call-update) | async-done | bytes 8388624 | tf_op jit(solution)/shard_map/all_gather | solution.py:188
  747.5 14.1 convert_reduce_fusion
  761.7 9.6 multiply_reduce_fusion.2
  780.7 26.5 %all-to-all-done.2 = bf16[512,16,64]{0,2,1:T(8,128)(2,1)S(1)} async-done(((bf16[512,16,64]{0,2,1:T(8,128)(2,1)}), bf16[512,16,64]{0,2,1:T(8,128)(2,1)S(1)}, u32[]{:S(2)}, u32[]{:S(2)}) %all-to-all-start.2) | async-done | bytes 1048608 | tf_op jit(solution)/shard_map/all_to_all | solution.py:249
  812.2 554.1 %while.27 = (s32[]{:T(128)}, f32[6836,2,64]{0,2,1:T(8,128)}, f32[6836,2,64]{0,2,1:T(8,128)}, bf16[8,512,2,64]{1,3,2,0:T(8,128)(2,1)}, s32[8]{0:T(128)S(1)}, /*in...) while((s32[]{:T(128)}, f32[6836,2,64]{0,2,1:T(8,128)}, ...), condition=%wide.region_12.13_spmd, body=%wide.region_10.12_spmd.sunk | while | flops 2172508416 | bytes 268659808 | solution.py:152
  823.6 7.9 exponential_multiply_fusion.3
  831.5 10.6 multiply_reduce_fusion.7
  842.2 7.0 multiply_convert_fusion.10
  855.4 8.2 dynamic_update_slice.29
  873.9 8.2 dynamic_update_slice.30
  893.3 7.9 exponential_multiply_fusion.3
  901.2 10.6 multiply_reduce_fusion.7
  911.8 7.0 multiply_convert_fusion.10
  925.0 8.2 dynamic_update_slice.29
  943.6 8.1 dynamic_update_slice.30
  962.9 7.9 exponential_multiply_fusion.3
  970.8 10.6 multiply_reduce_fusion.7
  981.5 7.0 multiply_convert_fusion.10
  994.7 8.1 dynamic_update_slice.29
  1013.1 8.1 dynamic_update_slice.30
  1032.5 7.9 exponential_multiply_fusion.3
  1040.4 10.6 multiply_reduce_fusion.7
  1051.0 7.0 multiply_convert_fusion.10
  1064.2 8.0 dynamic_update_slice.29
  1082.6 8.0 dynamic_update_slice.30
  1101.9 7.9 exponential_multiply_fusion.3
  1109.8 10.6 multiply_reduce_fusion.7
  1120.4 7.0 multiply_convert_fusion.10
  1133.6 8.0 dynamic_update_slice.29
  1152.0 8.0 dynamic_update_slice.30
  1171.2 7.9 exponential_multiply_fusion.3
  1179.1 10.6 multiply_reduce_fusion.7
  1203.0 7.9 dynamic_update_slice.29
  1221.3 7.9 dynamic_update_slice.30
  1240.4 7.9 exponential_multiply_fusion.3
  1248.3 10.6 multiply_reduce_fusion.7
  1258.9 7.0 multiply_convert_fusion.10
  1272.1 7.8 dynamic_update_slice.29
  1290.3 7.8 dynamic_update_slice.30
  1309.3 7.9 exponential_multiply_fusion.3
  1317.2 10.6 multiply_reduce_fusion.7
  1341.0 7.4 dynamic_update_slice.29
  1358.8 7.4 dynamic_update_slice.30
  1372.9 11.0 copy.83
  1383.8 8.9 reshape.418
  1396.6 71.4 %all-to-all-done.3 = bf16[8,2,98304]{2,1,0:T(2,128)(2,1)S(1)} async-done(((bf16[8,2,98304]{2,1,0:T(2,128)(2,1)}), bf16[8,2,98304]{2,1,0:T(2,128)(2,1)S(1)}, u32[]{:S(2)}, u32[]{:S(2)}) %all-to-all-start.3) | async-done | bytes 3145760 | tf_op jit(solution)/shard_map/all_to_all | solution.py:253
  1474.2 13.6 copy.90
  1497.5 9.2 multiply_reduce_fusion.1
  1513.6 8.2 fusion.73
  1523.3 10.5 fusion.79
  1534.0 105.8 %reduce-scatter.16.cloned.1.call-done = f32[32,14]{1,0:T(8,128)} async-done(((f32[1024,14]{1,0:T(8,128)}), f32[32,14]{1,0:T(8,128)}) %reduce-scatter.16.cloned.1.call-update) | async-done | bytes 1808
  1641.7 139.5 %reduce-scatter.10.cloned.1.call-done = f32[32,1024]{1,0:T(8,128)} async-done(((f32[1024,1024]{1,0:T(8,128)}), f32[32,1024]{1,0:T(8,128)}) %reduce-scatter.10.cloned.1.call-update) | async-done | bytes 131088 | tf_op jit(solution)/shard_map/reduce_scatter | solution.py:285
  1782.9 157.5 %reduce-scatter.8.cloned.1.call-done = f32[32,3072]{1,0:T(8,128)} async-done(((f32[1024,3072]{1,0:T(8,128)}), f32[32,3072]{1,0:T(8,128)}) %reduce-scatter.8.cloned.1.call-update) | async-done | bytes 393232 | tf_op jit(solution)/shard_map/reduce_scatter | solution.py:284
  1942.6 185.9 %reduce-scatter.12.cloned.1.call-done = f32[32,4096]{1,0:T(8,128)} async-done(((f32[1024,4096]{1,0:T(8,128)}), f32[32,4096]{1,0:T(8,128)}) %reduce-scatter.12.cloned.1.call-update) | async-done | bytes 524304 | tf_op jit(solution)/shard_map/reduce_scatter | solution.py:286
  (473 shorter events, 508.4 us)
Async XLA Ops:
  7.2 76.9 %copy-start.4 = (bf16[512,1024]{1,0:T(8,128)(2,1)S(1)}, bf16[512,1024]{1,0:T(8,128)(2,1)}, u32[]{:S(2)}) copy-start(bf16[512,1024]{1,0:T(8,128)(2,1)} %param.23) | copy-start | bytes 3145732
  7.2 76.9 %all-gather.8.cloned.1.call-start = ((), (), s32[]{:S(2)}) async-start(), calls=%async_computation.9 | async-start | bytes 6488064 | tf_op jit(solution)/shard_map/all_gather | solution.py:185
  54.0 30.0 %copy-start.24 = (f32[1024,14]{0,1:T(8,128)}, f32[1024,14]{0,1:T(8,128)S(1)}, u32[]{:S(2)}) copy-start(f32[1024,14]{0,1:T(8,128)S(1)} %reshape.413) | copy-start | bytes 172036
  54.7 29.4 %copy-start.34 = (f32[1,1024]{1,0:T(1,128)}, f32[1,1024]{1,0:T(1,128)S(1)}, u32[]{:S(2)}) copy-start(f32[1,1024]{1,0:T(1,128)S(1)} %get-tuple-element.261) | copy-start | bytes 12292
  54.7 29.4 %copy-start.55 = (f32[1,1024]{1,0:T(1,128)}, f32[1,1024]{1,0:T(1,128)S(1)}, u32[]{:S(2)}) copy-start(f32[1,1024]{1,0:T(1,128)S(1)} %get-tuple-element.260) | copy-start | bytes 12292
  56.1 27.9 %copy-start.28 = (f32[512]{0:T(512)}, f32[512]{0:T(512)S(1)}, u32[]{:S(2)}) copy-start(f32[512]{0:T(512)S(1)} %broadcast_multiply_fusion.1) | copy-start | bytes 6148
  57.8 26.3 %copy-start.30 = (f32[512]{0:T(512)}, f32[512]{0:T(512)S(1)}, u32[]{:S(2)}) copy-start(f32[512]{0:T(512)S(1)} %fusion.62) | copy-start | bytes 6148
  57.8 26.3 %copy-start.45 = (f32[512]{0:T(512)}, f32[512]{0:T(512)S(1)}, u32[]{:S(2)}) copy-start(f32[512]{0:T(512)S(1)} %fusion.71) | copy-start | bytes 6148
  97.0 91.2 %copy-start.64 = (s32[512]{0:T(512)S(1)}, s32[512]{0:T(512)}, u32[]{:S(2)}) copy-start(s32[512]{0:T(512)} %param.25) | copy-start | bytes 6148
  97.0 105.3 %all-to-all-start = ((bf16[512,3,16,64]{0,3,1,2:T(8,128)(2,1)}), bf16[512,3,16,64]{0,3,1,2:T(8,128)(2,1)S(1)}, u32[]{:S(2)}, u32[]{:S(2)}) async-start(bf16[512,3,16,64]{0,3,1,2:T(8,128)(2,1)} %copy.74), calls=%async_computation | async-start | bytes 6291456 | tf_op jit(solution)/shard_map/all_to_all | solution.py:216
  100.8 340.4 %all-gather.10.cloned.1.call-start = ((), (), s32[]{:S(2)}) async-start(), calls=%async_computation.10 | async-start | bytes 2162688 | tf_op jit(solution)/shard_map/all_gather | solution.py:186
  101.5 344.7 %all-gather.12.cloned.1.call-start = ((), (), s32[]{:S(2)}) async-start(), calls=%async_computation.11 | async-start | bytes 8650752 | tf_op jit(solution)/shard_map/all_gather | solution.py:187
  396.6 11.8 copy-start.52
  403.8 30.8 %all-to-all-start.1 = ((bf16[8,2,32768]{2,1,0:T(2,128)(2,1)}), bf16[8,2,32768]{2,1,0:T(2,128)(2,1)}, u32[]{:S(2)}, u32[]{:S(2)}) async-start(bf16[8,2,32768]{2,1,0:T(2,128)(2,1)} %reshape.416), calls=%async_computation.1 | async-start | bytes 2097152 | tf_op jit(solution)/shard_map/all_to_all | solution.py:220
  408.1 33.2 %copy-start.5 = (bf16[512,1024]{1,0:T(8,128)(2,1)S(1)}, bf16[512,1024]{1,0:T(8,128)(2,1)}, u32[]{:S(2)}) copy-start(bf16[512,1024]{1,0:T(8,128)(2,1)} %param.23) | copy-start | bytes 3145732
  408.1 33.2 %copy-start.36 = (f32[1,1024]{1,0:T(1,128)S(1)}, f32[1,1024]{1,0:T(1,128)}, u32[]{:S(2)}) copy-start(f32[1,1024]{1,0:T(1,128)} %get-tuple-element.262) | copy-start | bytes 12292
  408.1 33.1 %copy-start.60 = (f32[1,1024]{1,0:T(1,128)S(1)}, f32[1,1024]{1,0:T(1,128)}, u32[]{:S(2)}) copy-start(f32[1,1024]{1,0:T(1,128)} %get-tuple-element.257) | copy-start | bytes 12292
  408.1 260.8 %reduce-scatter.14.cloned.1.call-start = ((), (), s32[]{:S(2)}) async-start(), calls=%async_computation.16 | async-start | bytes 17301504 | tf_op jit(solution)/shard_map/reduce_scatter | solution.py:287
  408.4 363.6 %copy-start.41 = (f32[512]{0:T(512)}, f32[512]{0:T(512)S(1)}, u32[]{:S(2)}) copy-start(f32[512]{0:T(512)S(1)} %convert_element_type.117) | copy-start | bytes 6148
  445.9 325.4 %copy-start.9 = (f32[512,1024]{1,0:T(8,128)}, f32[512,1024]{1,0:T(8,128)S(1)}, u32[]{:S(2)}) copy-start(f32[512,1024]{1,0:T(8,128)S(1)} %get-tuple-element.239) | copy-start | bytes 6291460
  445.9 325.4 %copy-start.32 = (f32[512]{0:T(512)}, f32[512]{0:T(512)S(1)}, u32[]{:S(2)}) copy-start(f32[512]{0:T(512)S(1)} %broadcast_multiply_fusion) | copy-start | bytes 6148
  446.2 325.1 %copy-start.47 = (f32[512]{0:T(512)}, f32[512]{0:T(512)S(1)}, u32[]{:S(2)}) copy-start(f32[512]{0:T(512)S(1)} %fusion.72) | copy-start | bytes 6148
  446.3 29.5 %copy-start.15 = (bf16[512,1024]{1,0:T(8,128)(2,1)S(1)}, bf16[512,1024]{1,0:T(8,128)(2,1)}, u32[]{:S(2)}) copy-start(bf16[512,1024]{1,0:T(8,128)(2,1)} %param.24) | copy-start | bytes 3145732
  446.3 29.5 %copy-start.57 = (f32[1,1024]{1,0:T(1,128)S(1)}, f32[1,1024]{1,0:T(1,128)}, u32[]{:S(2)}) copy-start(f32[1,1024]{1,0:T(1,128)} %get-tuple-element.253) | copy-start | bytes 12292
  484.1 263.4 %all-gather.14.cloned.1.call-start = ((), (), s32[]{:S(2)}) async-start(), calls=%async_computation.12 | async-start | bytes 8650752 | tf_op jit(solution)/shard_map/all_gather | solution.py:188
  761.7 9.6 copy-start.67
  777.1 30.1 %all-to-all-start.2 = ((bf16[512,16,64]{0,2,1:T(8,128)(2,1)}), bf16[512,16,64]{0,2,1:T(8,128)(2,1)S(1)}, u32[]{:S(2)}, u32[]{:S(2)}) async-start(bf16[512,16,64]{0,2,1:T(8,128)(2,1)} %bitcast.40), calls=%async_computation.2 | async-start | bytes 2097152 | tf_op jit(solution)/shard_map/all_to_all | solution.py:249
  831.5 10.7 copy-start
  901.2 10.7 copy-start
  970.8 10.7 copy-start
  1040.4 10.7 copy-start
  1109.8 10.7 copy-start
  1179.1 10.7 copy-start
  1248.3 10.7 copy-start
  1317.2 10.6 copy-start
  1392.7 75.2 %all-to-all-start.3 = ((bf16[8,2,98304]{2,1,0:T(2,128)(2,1)}), bf16[8,2,98304]{2,1,0:T(2,128)(2,1)S(1)}, u32[]{:S(2)}, u32[]{:S(2)}) async-start(bf16[8,2,98304]{2,1,0:T(2,128)(2,1)} %reshape.418), calls=%async_computation.3 | async-start | bytes 6291456 | tf_op jit(solution)/shard_map/all_to_all | solution.py:253
  1396.5 243.2 %reduce-scatter.16.cloned.1.call-start = ((), (), s32[]{:S(2)}) async-start(), calls=%async_computation.17 | async-start | bytes 540672
  1488.7 8.7 slice-start
  1489.9 7.5 copy-start.8
  1489.9 7.5 copy-start.10
  1489.9 7.5 copy-start.16
  1489.9 7.5 copy-start.42
  1489.9 7.5 copy-start.44
  1489.9 7.5 copy-start.58
  1490.0 7.5 copy-start.59
  1490.0 7.5 copy-start.61
  1497.5 9.2 copy-start.37
  1497.5 9.2 copy-start.62
  1497.5 9.2 copy-start.63
  1507.8 273.3 %reduce-scatter.10.cloned.1.call-start = ((), (), s32[]{:S(2)}) async-start(), calls=%async_computation.14 | async-start | bytes 4325376 | tf_op jit(solution)/shard_map/reduce_scatter | solution.py:285
  1512.9 427.5 %reduce-scatter.8.cloned.1.call-start = ((), (), s32[]{:S(2)}) async-start(), calls=%async_computation.13 | async-start | bytes 12976128 | tf_op jit(solution)/shard_map/reduce_scatter | solution.py:284
  1521.8 606.7 %reduce-scatter.12.cloned.1.call-start = ((), (), s32[]{:S(2)}) async-start(), calls=%async_computation.15 | async-start | bytes 17301504 | tf_op jit(solution)/shard_map/reduce_scatter | solution.py:286
  1533.8 107.2 %copy-start.27 = (f32[14,32]{1,0:T(8,128)S(1)}, f32[14,32]{1,0:T(8,128)}, u32[]{:S(2)}) copy-start(f32[14,32]{1,0:T(8,128)} %param.31) | copy-start | bytes 5380
  1533.8 107.2 %copy-start.49 = (f32[14,32]{1,0:T(8,128)S(1)}, f32[14,32]{1,0:T(8,128)}, u32[]{:S(2)}) copy-start(f32[14,32]{1,0:T(8,128)} %param.36) | copy-start | bytes 5380
  1533.8 107.2 %copy-start.50 = (f32[14,32]{1,0:T(8,128)S(1)}, f32[14,32]{1,0:T(8,128)}, u32[]{:S(2)}) copy-start(f32[14,32]{1,0:T(8,128)} %param.41) | copy-start | bytes 5380
  1533.8 247.3 %copy-start.21 = (f32[32,1024]{1,0:T(8,128)S(1)}, f32[32,1024]{1,0:T(8,128)}, u32[]{:S(2)}) copy-start(f32[32,1024]{1,0:T(8,128)} %param.28) | copy-start | bytes 393220
  1533.8 247.3 %copy-start.25 = (f32[32,1024]{1,0:T(8,128)S(1)}, f32[32,1024]{1,0:T(8,128)}, u32[]{:S(2)}) copy-start(f32[32,1024]{1,0:T(8,128)} %param.33) | copy-start | bytes 393220
  1533.8 247.3 %copy-start.26 = (f32[32,1024]{1,0:T(8,128)S(1)}, f32[32,1024]{1,0:T(8,128)}, u32[]{:S(2)}) copy-start(f32[32,1024]{1,0:T(8,128)} %param.38) | copy-start | bytes 393220
  1533.9 406.5 %copy-start.14 = (f32[32,3072]{1,0:T(8,128)S(1)}, f32[32,3072]{1,0:T(8,128)}, u32[]{:S(2)}) copy-start(f32[32,3072]{1,0:T(8,128)} %param.27) | copy-start | bytes 1179652
  1533.9 406.5 %copy-start.22 = (f32[32,3072]{1,0:T(8,128)S(1)}, f32[32,3072]{1,0:T(8,128)}, u32[]{:S(2)}) copy-start(f32[32,3072]{1,0:T(8,128)} %param.32) | copy-start | bytes 1179652
  1533.9 406.5 %copy-start.23 = (f32[32,3072]{1,0:T(8,128)S(1)}, f32[32,3072]{1,0:T(8,128)}, u32[]{:S(2)}) copy-start(f32[32,3072]{1,0:T(8,128)} %param.37) | copy-start | bytes 1179652
  1533.9 594.6 %copy-start.13 = (f32[32,4096]{1,0:T(8,128)S(1)}, f32[32,4096]{1,0:T(8,128)}, u32[]{:S(2)}) copy-start(f32[32,4096]{1,0:T(8,128)} %param.29) | copy-start | bytes 1572868
  1533.9 594.6 %copy-start.18 = (f32[32,4096]{1,0:T(8,128)S(1)}, f32[32,4096]{1,0:T(8,128)}, u32[]{:S(2)}) copy-start(f32[32,4096]{1,0:T(8,128)} %param.34) | copy-start | bytes 1572868
  1533.9 594.6 %copy-start.19 = (f32[32,4096]{1,0:T(8,128)S(1)}, f32[32,4096]{1,0:T(8,128)}, u32[]{:S(2)}) copy-start(f32[32,4096]{1,0:T(8,128)} %param.39) | copy-start | bytes 1572868
  (41 other events, 157.4 us)
Sparse Core Ops, SparseCore 0:
  11.6 72.4 all-gather.7
  105.2 74.6 all-gather.9
  183.4 77.2 all-gather.11
  484.3 184.5 reduce-scatter.13
  672.4 75.1 all-gather.13
  1507.9 131.7 reduce-scatter.15
  1642.1 138.9 reduce-scatter.9
  1788.2 152.1 reduce-scatter.7
  1942.7 185.7 reduce-scatter.11
where the time goes:
time: 2150 us; the launch traced here: 2140 us
  waiting for transfers between devices  998 us (46%)
  matrix products  453 us (21%)
  local copies, waits for them, and re-layouts  309 us (14%)
  other arithmetic  176 us (8%)
  blocking collectives  142 us (7%)
  loops' own time  28.4 us (1%)
    reduce_scatter x1, waiting for transfers between devices, on_device(): lax.psum_scatter(grad_up, ('fsdp', 'seq'), scatter_dimension=0, tiled=True)  186 us
    reduce_scatter x1, waiting for transfers between devices, on_device(): lax.psum_scatter(grad_down, ('fsdp', 'seq'), scatter_dimension=0, tiled=T...  184 us
    reduce_scatter x1, waiting for transfers between devices, on_device(): lax.psum_scatter(grad_in, ('fsdp', 'seq'), scatter_dimension=0, tiled=True)  158 us
    reduce_scatter x1, waiting for transfers between devices, on_device(): lax.psum_scatter(grad_out, ('fsdp', 'seq'), scatter_dimension=0, tiled=True)  139 us
    dot_general x16, matrix products, block_scores(): jnp.einsum('qhd,khd->hqk', query_block, key_window, preferred_element_typ...  108 us
    unnamed x10, waiting for transfers between devices  106 us
    dot_general x8, matrix products, one_block(): jnp.einsum('qhd,khd->hqk', grad_block, value_window, preferred_element_ty...  85.1 us
    all_gather x1, blocking collectives, on_device(): lax.all_gather(valid, 'seq', axis=0, tiled=True)  84.7 us
  transfers between devices with their start and end apart: 13, of which 10 were waited for; matrix products, arithmetic and copies ran while one was open for 11% of the time, Pallas kernels for 0%

commit v1 on v0

v1 whole, which is shorter than its diff:
```python
import jax
import jax.numpy as jnp
from jax import lax
from jax.experimental import pallas as pl
from jax.experimental.pallas import tpu as pltpu
from jax.sharding import PartitionSpec as P

D = 1024
FF = 4096
HEADS = 16
HEAD_DIM = 64
IMG_LEN = 1370
WINDOW = 1408
TILE = 352
VMEM_BYTES = 56 * 1024 * 1024
STEP = 10


masked_score = -1e30


def layer_norm(values, gain, shift):
    average = jnp.mean(values, axis=-1, keepdims=True)
    centered = values - average
    variance = jnp.mean(centered * centered, axis=-1, keepdims=True)
    return centered * lax.rsqrt(variance + 1e-06) * gain + shift


def exact_gelu(values):
    return jax.nn.gelu(values, approximate=False)


def plain_product(left, right):
    return jnp.dot(left, right, preferred_element_type=jnp.float32)


def inner_rows(left, right):
    return lax.dot_general(
        left, right, (((0,), (0,)), ((), ())), preferred_element_type=jnp.float32
    )


def inner_cols(left, right):
    return lax.dot_general(
        left, right, (((1,), (1,)), ((), ())), preferred_element_type=jnp.float32
    )


def adamw(param, moment, square, grad, rate, decay):
    new_moment = 0.9 * moment + 0.1 * grad
    new_square = 0.999 * square + 0.001 * grad * grad
    corrected = new_moment / (1.0 - 0.9**STEP)
    scaled = jnp.sqrt(new_square / (1.0 - 0.999**STEP)) + 1e-08
    return (param - rate * (corrected / scaled + decay * param), new_moment, new_square)


def head_lanes(shape):
    return lax.broadcasted_iota(jnp.int32, shape, 1) // HEAD_DIM


def window_of(starts_ref, image, length):
    start = starts_ref[image]
    base = jnp.clip(start // 16 * 16, 0, length - WINDOW)
    return (pl.multiple_of(base, 16), start - base)


def image_mask(position, offset):
    return (position >= offset) & (position < offset + IMG_LEN)


def attend_kernel(starts_ref, q_ref, k_ref, v_ref, wide_ref, out_ref, log_ref):
    image, tile = pl.program_id(0), pl.program_id(1)
    length, lanes = q_ref.shape
    base, offset = window_of(starts_ref, image, length)
    rows = pl.ds(pl.multiple_of(base + tile * TILE, 16), TILE)

    @pl.when((image == 0) & (tile == 0))
    def clear():
        wide_ref[...] = jnp.zeros_like(wide_ref)
        out_ref[...] = jnp.zeros_like(out_ref)
        log_ref[...] = jnp.zeros_like(log_ref)

    query = q_ref[rows, :].astype(jnp.float32) * HEAD_DIM ** (-0.5)
    keys = k_ref[pl.ds(base, WINDOW), :]
    values = v_ref[pl.ds(base, WINDOW), :]
    key_ok = image_mask(lax.broadcasted_iota(jnp.int32, (1, WINDOW), 1), offset)
    bias = jnp.where(key_ok, 0.0, masked_score)
    row_ok = image_mask(lax.broadcasted_iota(jnp.int32, (TILE, 1), 0) + tile * TILE, offset)
    head_of = head_lanes((TILE, lanes))
    total_out = jnp.zeros((TILE, lanes), jnp.float32)
    total_log = jnp.zeros((TILE, lanes), jnp.float32)
    for head in range(lanes // HEAD_DIM):
        mine = head_of == head
        part = jnp.where(mine, query, 0.0).astype(jnp.bfloat16)
        scores = inner_cols(part, keys) + bias
        top = jnp.max(scores, axis=1, keepdims=True)
        weights = jnp.exp(scores - top)
        total = jnp.sum(weights, axis=1, keepdims=True)
        probs = (weights * (1.0 / total)).astype(jnp.bfloat16)
        total_out = jnp.where(mine, plain_product(probs, values), total_out)
        total_log = jnp.where(mine, top + jnp.log(total), total_log)
    merged = jnp.where(row_ok, total_out, wide_ref[rows, :])
    wide_ref[rows, :] = merged
    out_ref[rows, :] = merged.astype(jnp.bfloat16)
    log_ref[rows, :] = jnp.where(row_ok, total_log, log_ref[rows, :])


def attend(starts, query, keys, values):
    length, lanes = query.shape
    whole = pl.BlockSpec((length, lanes), lambda image, tile, starts: (0, 0))
    wide = jax.ShapeDtypeStruct((length, lanes), jnp.float32)
    images = length // IMG_LEN
    return pl.pallas_call(
        attend_kernel,
        grid_spec=pltpu.PrefetchScalarGridSpec(
            num_scalar_prefetch=1,
            grid=(images, WINDOW // TILE),
            in_specs=[whole] * 3,
            out_specs=[whole] * 3,
        ),
        out_shape=(wide, jax.ShapeDtypeStruct((length, lanes), jnp.bfloat16), wide),
        compiler_params=pltpu.CompilerParams(
            vmem_limit_bytes=VMEM_BYTES, dimension_semantics=("arbitrary", "arbitrary")
        ),
        cost_estimate=pl.CostEstimate(
            flops=images * WINDOW * WINDOW * lanes * 8,
            bytes_accessed=length * lanes * 16,
            transcendentals=images * WINDOW * WINDOW * lanes // HEAD_DIM,
        ),
        name="attend_forward",
    )(starts, query, keys, values)


def attend_back_kernel(
    starts_ref, q_ref, k_ref, v_ref, wide_ref, log_ref, go_ref, grad_ref, key_acc, value_acc
):
    image, tile = pl.program_id(0), pl.program_id(1)
    length, lanes = q_ref.shape
    base, offset = window_of(starts_ref, image, length)
    rows = pl.ds(pl.multiple_of(base + tile * TILE, 16), TILE)
    window = pl.ds(base, WINDOW)

    @pl.when((image == 0) & (tile == 0))
    def clear():
        grad_ref[...] = jnp.zeros_like(grad_ref)

    @pl.when(tile == 0)
    def clear_sums():
        key_acc[...] = jnp.zeros_like(key_acc)
        value_acc[...] = jnp.zeros_like(value_acc)

    query = q_ref[rows, :].astype(jnp.float32) * HEAD_DIM ** (-0.5)
    keys = k_ref[window, :]
    values = v_ref[window, :]
    key_ok = image_mask(lax.broadcasted_iota(jnp.int32, (1, WINDOW), 1), offset)
    bias = jnp.where(key_ok, 0.0, masked_score)
    row_ok = image_mask(lax.broadcasted_iota(jnp.int32, (TILE, 1), 0) + tile * TILE, offset)
    head_of = head_lanes((TILE, lanes))
    grad_out = jnp.where(row_ok, go_ref[rows, :].astype(jnp.float32), 0.0)
    centre_parts = grad_out * wide_ref[rows, :]
    logs = jnp.where(row_ok, log_ref[rows, :], -masked_score)
    query_grad = jnp.zeros((TILE, lanes), jnp.float32)
    for head in range(lanes // HEAD_DIM):
        mine = head_of == head
        part = jnp.where(mine, query, 0.0).astype(jnp.bfloat16)
        grad_part = jnp.where(mine, grad_out, 0.0).astype(jnp.bfloat16)
        centre = jnp.sum(jnp.where(mine, centre_parts, 0.0), axis=1, keepdims=True)
        log_total = jnp.max(jnp.where(mine, logs, masked_score), axis=1, keepdims=True)
        probs = jnp.exp(inner_cols(part, keys) + bias - log_total)
        grad_probs = inner_cols(grad_part, values)
        grad_scores = (probs * (grad_probs - centre)).astype(jnp.bfloat16)
        query_grad = jnp.where(mine, plain_product(grad_scores, keys), query_grad)
        key_acc[...] += inner_rows(part, grad_scores)
        value_acc[...] += inner_rows(grad_part, probs.astype(jnp.bfloat16))
    old = grad_ref[rows, 0:lanes].astype(jnp.float32)
    merged = jnp.where(row_ok, query_grad * HEAD_DIM ** (-0.5), old)
    grad_ref[rows, 0:lanes] = merged.astype(jnp.bfloat16)

    @pl.when(tile == pl.num_programs(1) - 1)
    def flush():
        inside = image_mask(lax.broadcasted_iota(jnp.int32, (WINDOW, 1), 0), offset)
        for slot, sums in ((1, key_acc), (2, value_acc)):
            columns = slice(slot * lanes, (slot + 1) * lanes)
            old = grad_ref[window, columns].astype(jnp.float32)
            merged = jnp.where(inside, sums[...].T, old)
            grad_ref[window, columns] = merged.astype(jnp.bfloat16)


def attend_back(starts, query, keys, values, wide, logs, grad_out):
    length, lanes = query.shape
    whole = pl.BlockSpec((length, lanes), lambda image, tile, starts: (0, 0))
    images = length // IMG_LEN
    return pl.pallas_call(
        attend_back_kernel,
        grid_spec=pltpu.PrefetchScalarGridSpec(
            num_scalar_prefetch=1,
            grid=(images, WINDOW // TILE),
            in_specs=[whole] * 6,
            out_specs=pl.BlockSpec((length, 3 * lanes), lambda image, tile, starts: (0, 0)),
            scratch_shapes=[pltpu.VMEM((lanes, WINDOW), jnp.float32)] * 2,
        ),
        out_shape=jax.ShapeDtypeStruct((length, 3 * lanes), jnp.bfloat16),
        compiler_params=pltpu.CompilerParams(
            vmem_limit_bytes=VMEM_BYTES, dimension_semantics=("arbitrary", "arbitrary")
        ),
        cost_estimate=pl.CostEstimate(
            flops=images * WINDOW * WINDOW * lanes * 20,
            bytes_accessed=length * lanes * 22,
            transcendentals=images * WINDOW * WINDOW * lanes // HEAD_DIM,
        ),
        name="attend_backward",
    )(starts, query, keys, values, wide, logs, grad_out)


def norm_mix_kernel(x_ref, gain_ref, shift_ref, weight_ref, bias_ref, a_ref, q_ref, k_ref, v_ref):
    lanes = q_ref.shape[1]
    normed = layer_norm(x_ref[...].astype(jnp.float32), gain_ref[...], shift_ref[...])
    normed = normed.astype(jnp.bfloat16)
    a_ref[...] = normed
    mixed = (plain_product(normed, weight_ref[...]) + bias_ref[...]).astype(jnp.bfloat16)
    q_ref[...] = mixed[:, :lanes]
    k_ref[...] = mixed[:, lanes : 2 * lanes]
    v_ref[...] = mixed[:, 2 * lanes :]


def norm_mix(stream, gain, shift, weight, bias):
    length, width = stream.shape
    lanes = weight.shape[1] // 3
    block = 512
    row = lambda size: pl.BlockSpec((block, size), lambda i: (i, 0))
    fixed = lambda *shape: pl.BlockSpec(shape, lambda i: (0, 0))
    part = jax.ShapeDtypeStruct((length, lanes), jnp.bfloat16)
    return pl.pallas_call(
        norm_mix_kernel,
        grid=(length // block,),
        in_specs=[
            row(width), fixed(1, width), fixed(1, width), fixed(width, 3 * lanes), fixed(1, 3 * lanes)
        ],
        out_specs=[row(width), row(lanes), row(lanes), row(lanes)],
        out_shape=(jax.ShapeDtypeStruct((length, width), jnp.bfloat16), part, part, part),
        compiler_params=pltpu.CompilerParams(vmem_limit_bytes=VMEM_BYTES),
        cost_estimate=pl.CostEstimate(
            flops=length * width * lanes * 6, bytes_accessed=length * width * 4, transcendentals=0
        ),
        name="norm_mix",
    )(stream, gain[None], shift[None], weight, bias[None])


def on_device(
    tokens,
    cotangent,
    segment_ids,
    valid,
    project_in,
    project_out,
    hidden_up,
    hidden_down,
    gains_biases,
    moment_in,
    moment_out,
    moment_up,
    moment_down,
    moment_gains,
    square_in,
    square_out,
    square_up,
    square_down,
    square_gains,
):
    rows = tokens.shape[0]
    width = tokens.shape[1]
    both = ("fsdp", "seq")
    streams, group = lax.axis_size("fsdp"), lax.axis_size("seq")
    count = streams * group
    share = width // count
    lanes = width // group
    length = rows * group
    images = length // IMG_LEN

    owned = project_in.astype(jnp.bfloat16).reshape(share, 3, group, lanes)
    owned = owned.transpose(2, 0, 1, 3).reshape(group, share, 3 * lanes)
    position = lax.broadcasted_iota(jnp.int32, (images, rows), 1)
    found = (segment_ids[None, :] == lax.broadcasted_iota(jnp.int32, (images, rows), 0)) & (
        valid[None, :] == 1
    )
    first = jnp.min(jnp.where(found, position, rows), axis=1)
    small = jnp.concatenate(
        [
            gains_biases.astype(jnp.bfloat16).reshape(-1),
            (first // 32).astype(jnp.bfloat16),
            (first % 32).astype(jnp.bfloat16),
        ]
    )
    vector_size = gains_biases.size
    extra = -(-small.shape[0] // (3 * lanes))
    small = jnp.pad(small, (0, extra * 3 * lanes - small.shape[0])).reshape(1, extra, 3 * lanes)
    blocks = jnp.concatenate([owned, jnp.broadcast_to(small, (group, extra, 3 * lanes))], axis=1)
    blocks = jnp.broadcast_to(blocks[None], (streams, *blocks.shape))
    blocks = blocks.reshape(count, share + extra, 3 * lanes)
    blocks = lax.all_to_all(blocks, both, split_axis=0, concat_axis=0, tiled=True)
    mine_in = blocks[:, :share].reshape(width, 3 * lanes)
    small = blocks[:, share:].reshape(count, -1)
    vectors = small[:, :vector_size].reshape(count, -1, share).transpose(1, 0, 2)
    vectors = vectors.reshape(-1, width).astype(jnp.float32)
    first = small[:, vector_size : vector_size + 2 * images].astype(jnp.int32)
    first = first[:, :images] * 32 + first[:, images:]
    first = lax.dynamic_slice_in_dim(first, lax.axis_index("fsdp") * group, group, 0)
    offsets = lax.broadcasted_iota(jnp.int32, (group, images), 0) * rows
    starts = jnp.min(jnp.where(first < rows, first + offsets, length), axis=0)

    stream = lax.all_gather(tokens, "seq", axis=0, tiled=True)

    packed = jnp.concatenate(
        [
            project_in.astype(jnp.bfloat16).reshape(share, 3, width).transpose(1, 0, 2),
            project_out.astype(jnp.bfloat16)[None],
            hidden_up.astype(jnp.bfloat16).reshape(share, -1, width).transpose(1, 0, 2),
            hidden_down.astype(jnp.bfloat16).reshape(-1, share, width),
        ],
        axis=0,
    )
    gathered = lax.all_gather(packed, both, axis=0, tiled=False)
    fold = FF // width
    whole_in = gathered[:, 0:3].transpose(0, 2, 1, 3).reshape(width, 3 * width)
    whole_out = gathered[:, 3].reshape(width, width)
    whole_up = gathered[:, 4 : 4 + fold].transpose(0, 2, 1, 3).reshape(width, FF)
    whole_down = gathered[:, 4 + fold :].reshape(FF, width)

    gain_one, shift_one, bias_query, bias_value, bias_out = (
        vectors[0],
        vectors[1],
        vectors[2],
        vectors[3],
        vectors[4],
    )
    scale_one, gain_two, shift_two, bias_down, scale_two = (
        vectors[5],
        vectors[6],
        vectors[7],
        vectors[8],
        vectors[9],
    )
    bias_up = vectors[10:].reshape(-1)
    column = lax.axis_index("seq") * lanes
    bias_in = jnp.concatenate(
        [
            lax.dynamic_slice_in_dim(bias_query, column, lanes, 0),
            jnp.zeros((lanes,), jnp.float32),
            lax.dynamic_slice_in_dim(bias_value, column, lanes, 0),
        ]
    )
    normed_one, query, keys, values = norm_mix(stream, gain_one, shift_one, mine_in, bias_in)
    wide, attended, logs = attend(starts, query, keys, values)
    returned = lax.all_to_all(
        attended.reshape(group, rows, lanes), "seq", split_axis=0, concat_axis=0, tiled=True
    )
    attended_rows = returned.transpose(1, 0, 2).reshape(rows, width)
    inputs = tokens.astype(jnp.float32)
    projected = plain_product(attended_rows, whole_out) + bias_out
    second = inputs + scale_one * projected
    norm_two, norm_two_back = jax.vjp(layer_norm, second, gain_two, shift_two)
    normed_two = norm_two.astype(jnp.bfloat16)
    upward = plain_product(normed_two, whole_up) + bias_up
    activated, gelu_back = jax.vjp(exact_gelu, upward)
    active = activated.astype(jnp.bfloat16)
    branch = plain_product(active, whole_down) + bias_down
    block_output = (second + scale_two * branch).astype(jnp.bfloat16)
    grad_rows = cotangent.astype(jnp.float32) * valid.astype(jnp.float32)[:, None]
    grad_scale_two = jnp.sum(grad_rows * branch, axis=0)
    grad_branch = (scale_two * grad_rows).astype(jnp.bfloat16)
    grad_bias_down = jnp.sum(grad_branch.astype(jnp.float32), axis=0)
    grad_down = inner_rows(active, grad_branch)
    grad_active = inner_cols(grad_branch, whole_down)
    grad_upward = gelu_back(grad_active)[0].astype(jnp.bfloat16)
    grad_bias_up = jnp.sum(grad_upward.astype(jnp.float32), axis=0)
    grad_up = inner_rows(normed_two, grad_upward)
    grad_norm_two = inner_cols(grad_upward, whole_up)
    second_part, grad_gain_two, grad_shift_two = norm_two_back(grad_norm_two)
    grad_second = grad_rows + second_part
    grad_scale_one = jnp.sum(grad_second * projected, axis=0)
    grad_projected = (scale_one * grad_second).astype(jnp.bfloat16)
    grad_bias_out = jnp.sum(grad_projected.astype(jnp.float32), axis=0)
    grad_out = inner_rows(attended_rows, grad_projected)
    grad_attended = inner_cols(grad_projected, whole_out).astype(jnp.bfloat16)
    grad_stream = lax.all_to_all(
        grad_attended.reshape(rows, group, lanes).transpose(1, 0, 2),
        "seq",
        split_axis=0,
        concat_axis=0,
        tiled=True,
    ).reshape(length, lanes)

    grad_packed = jnp.concatenate(
        [
            grad_out.astype(jnp.bfloat16).reshape(count, 1, share, width),
            grad_up.astype(jnp.bfloat16).reshape(count, share, fold, width).transpose(0, 2, 1, 3),
            grad_down.astype(jnp.bfloat16).reshape(count, fold, share, width),
        ],
        axis=1,
    )
    summed = lax.psum_scatter(grad_packed, both, scatter_dimension=0, tiled=True)[0]
    summed = summed.astype(jnp.float32)
    summed_out = summed[0]
    summed_up = summed[1 : 1 + fold].transpose(1, 0, 2).reshape(share, FF)
    summed_down = summed[1 + fold :].reshape(fold * share, width)

    grad_mixed_stream = attend_back(starts, query, keys, values, wide, logs, grad_stream)
    grad_mixed = lax.all_to_all(
        grad_mixed_stream.reshape(group, rows, 3 * lanes),
        "seq",
        split_axis=0,
        concat_axis=0,
        tiled=True,
    )
    grad_mixed = grad_mixed.reshape(group, rows, 3, lanes).transpose(1, 2, 0, 3)
    grad_mixed = grad_mixed.reshape(rows, 3 * width)
    grad_in = inner_rows(normed_one, grad_mixed_stream).astype(jnp.bfloat16)
    parts = lax.all_to_all(
        grad_in.reshape(count, share, 3 * lanes), both, split_axis=0, concat_axis=0, tiled=True
    )
    parts = parts.reshape(streams, group, share, 3, lanes).astype(jnp.float32)
    summed_in = jnp.sum(parts, axis=0).transpose(1, 2, 0, 3).reshape(share, 3 * width)

    grad_mixed_wide = grad_mixed.astype(jnp.float32)
    grad_bias_query = jnp.sum(grad_mixed_wide[:, :width], axis=0)
    grad_bias_value = jnp.sum(grad_mixed_wide[:, 2 * width :], axis=0)
    grad_norm_one = inner_cols(grad_mixed, whole_in)
    norm_one_back = jax.vjp(layer_norm, inputs, gain_one, shift_one)[1]
    first_part, grad_gain_one, grad_shift_one = norm_one_back(grad_norm_one)
    input_grad = grad_second + first_part
    grad_small = jnp.concatenate(
        [
            jnp.stack(
                [
                    grad_gain_one,
                    grad_shift_one,
                    grad_bias_query,
                    grad_bias_value,
                    grad_bias_out,
                    grad_scale_one,
                    grad_gain_two,
                    grad_shift_two,
                    grad_bias_down,
                    grad_scale_two,
                ]
            ),
            grad_bias_up.reshape(-1, width),
        ],
        axis=0,
    )
    small_rows = grad_small.shape[0]
    parts = grad_small.reshape(small_rows, count, share).transpose(1, 0, 2)
    parts = lax.all_to_all(
        parts.reshape(count, small_rows * share), both, split_axis=0, concat_axis=0, tiled=True
    )
    summed_gains = jnp.sum(parts, axis=0).reshape(small_rows, share)
    rate_out = max(1, 4 * D // IMG_LEN) ** (-0.5)
    new_in, new_moment_in, new_square_in = adamw(
        project_in, moment_in, square_in, summed_in, D ** (-0.5), 0.04
    )
    new_out, new_moment_out, new_square_out = adamw(
        project_out, moment_out, square_out, summed_out, rate_out, 0.04
    )
    new_up, new_moment_up, new_square_up = adamw(
        hidden_up, moment_up, square_up, summed_up, D ** (-0.5), 0.04
    )
    new_down, new_moment_down, new_square_down = adamw(
        hidden_down, moment_down, square_down, summed_down, FF ** (-0.5), 0.04
    )
    new_gains, new_moment_gains, new_square_gains = adamw(
        gains_biases, moment_gains, square_gains, summed_gains, 0.2, 0.0
    )
    return (
        block_output,
        input_grad,
        new_in,
        new_out,
        new_up,
        new_down,
        new_gains,
        new_moment_in,
        new_moment_out,
        new_moment_up,
        new_moment_down,
        new_moment_gains,
        new_square_in,
        new_square_out,
        new_square_up,
        new_square_down,
        new_square_gains,
        summed_gains[8],
    )


def solution(mesh):
    return jax.shard_map(
        on_device,
        mesh=mesh,
        in_specs=(
            P(("fsdp", "seq"), None),
            P(("fsdp", "seq"), None),
            P(("fsdp", "seq")),
            P(("fsdp", "seq")),
            P(("fsdp", "seq"), None),
            P(("fsdp", "seq"), None),
            P(("fsdp", "seq"), None),
            P(("fsdp", "seq"), None),
            P(None, ("fsdp", "seq")),
            P(("fsdp", "seq"), None),
            P(("fsdp", "seq"), None),
            P(("fsdp", "seq"), None),
            P(("fsdp", "seq"), None),
            P(None, ("fsdp", "seq")),
            P(("fsdp", "seq"), None),
            P(("fsdp", "seq"), None),
            P(("fsdp", "seq"), None),
            P(("fsdp", "seq"), None),
            P(None, ("fsdp", "seq")),
        ),
        out_specs=(
            P(("fsdp", "seq"), None),
            P(("fsdp", "seq"), None),
            P(("fsdp", "seq"), None),
            P(("fsdp", "seq"), None),
            P(("fsdp", "seq"), None),
            P(("fsdp", "seq"), None),
            P(None, ("fsdp", "seq")),
            P(("fsdp", "seq"), None),
            P(("fsdp", "seq"), None),
            P(("fsdp", "seq"), None),
            P(("fsdp", "seq"), None),
            P(None, ("fsdp", "seq")),
            P(("fsdp", "seq"), None),
            P(("fsdp", "seq"), None),
            P(("fsdp", "seq"), None),
            P(("fsdp", "seq"), None),
            P(None, ("fsdp", "seq")),
            P(("fsdp", "seq")),
        ),
        check_vma=False,
    )
```

time: 2150 us -> 721 us (0.34)
  waiting for transfers between devices: 998 us -> 318 us
  matrix products: 453 us -> 96.5 us
  local copies, waits for them, and re-layouts: 309 us -> 118 us
  other arithmetic: 176 us -> 39.6 us
  blocking collectives: 142 us -> 29.7 us
  Pallas kernels: 0 us -> 74.3 us
  loops' own time: 28.4 us -> 0 us
    reduce_scatter x4 -> x1, waiting for transfers between devices: 667 us -> 0.01 us  [on_device(): lax.psum_scatter(grad_packed, both, scatter_dimension=0, tiled=True)[0]]
    dot_general x56 -> x0, matrix products: 341 us -> none  [the longest x16 108 us: block_scores(): jnp.einsum('qhd,khd->hqk', query_block, key_window, preferred_element_typ...]
    all_gather x3 -> x0, blocking collectives: 142 us -> none  [the longest x1 84.7 us: on_device(): lax.all_gather(valid, 'seq', axis=0, tiled=True)]
    dynamic_update_slice x16 -> x0, local copies, waits for them, and re-layouts: 127 us -> none  [the longest x8 63.6 us: one_block(): lax.dynamic_update_slice_in_dim(key_grad, lax.dynamic_slice_in_dim(key_gr...]
    unnamed x10 -> x3, waiting for transfers between devices: 106 us -> 0.71 us
    pallas_call x0 -> x3, Pallas kernels: none -> 74.3 us  [the longest x1 35.4 us: attend_back(): pl.pallas_call(attend_back_kernel, grid_spec=pltpu.PrefetchScalarGridSpec...]
    all_gather x4 -> x2, waiting for transfers between devices: 102 us -> 166 us  [the longest x1 131 us: on_device(): gathered = lax.all_gather(packed, both, axis=0, tiled=False)]
    convert_element_type x20 -> x8, other arithmetic: 60.8 us -> 4.59 us  [the longest x1 1.26 us: on_device(): summed = summed.astype(jnp.float32)]
  transfers between devices with their start and end apart: 13 -> 8, of which waited for: 10 -> 6; matrix products, arithmetic and copies ran while one was open for 11% -> 16% of each run, Pallas kernels for 0% -> 10%
where the time goes in v1:
time: 721 us; the launch traced here: 713 us
  waiting for transfers between devices  318 us (44%)
  local copies, waits for them, and re-layouts  118 us (16%)
  matrix products  96.5 us (13%)
  Pallas kernels  74.3 us (10%)
  other arithmetic  39.6 us (5%)
  blocking collectives  29.7 us (4%)
  starting transfers between devices  21.1 us (3%)
  between operations  15.2 us (2%)
    all_gather x1, waiting for transfers between devices, on_device(): gathered = lax.all_gather(packed, both, axis=0, tiled=False)  131 us
    all_to_all x1, waiting for transfers between devices, on_device(): lax.all_to_all(grad_mixed_stream.reshape(group, rows, 3 * lanes), 'seq',...  55.5 us
    all_to_all x1, waiting for transfers between devices, on_device(): lax.all_to_all(blocks, both, split_axis=0, concat_axis=0, tiled=True)  51.1 us
    dot_general x3, matrix products, plain_product(): return jnp.dot(left, right, preferred_element_type=jnp.float32)  40.5 us
    all_to_all x1, waiting for transfers between devices, on_device(): lax.all_to_all(grad_in.reshape(count, share, 3 * lanes), both, split_axis...  39.3 us
    pallas_call x1, Pallas kernels, attend_back(): pl.pallas_call(attend_back_kernel, grid_spec=pltpu.PrefetchScalarGridSpec...  35.4 us
    all_gather x1, waiting for transfers between devices, on_device(): stream = lax.all_gather(tokens, 'seq', axis=0, tiled=True)  34.4 us
    dot_general x4, matrix products, inner_cols(): lax.dot_general(left, right, (((1,), (1,)), ((), ())), preferred_element_...  29.9 us
  transfers between devices with their start and end apart: 8, of which 6 were waited for; matrix products, arithmetic and copies ran while one was open for 16% of the time, Pallas kernels for 10%

profile of v1, /device:TPU:0, one launch (start us, length us, event | category | flops | bytes accessed | tf_op | source)
XLA Modules:
  0.0 713.2 jit_solution(6966908447176406074)
XLA Ops:
  8.0 0.9 convert_bitcast_fusion
  9.0 1.1 convert_element_type.102
  10.4 1.1 convert_element_type.111
  11.7 1.1 convert_element_type.112
  13.0 0.7 pad_maximum_fusion.1
  13.7 1.4 copy.131
  15.9 1.0 broadcast_in_dim.52
  16.9 7.3 %all-to-all-start = ((bf16[32,34,384]{2,1,0:T(8,128)(2,1)}), bf16[32,34,384]{2,1,0:T(8,128)(2,1)S(1)}, u32[]{:S(2)}, u32[]{:S(2)}) async-start(bf16[32,34,384]{2,1,0:T(8,128)(2,1)} %bitcast.1), calls=%async_computation | async-start | bytes 1966080 | tf_op jit(solution)/shard_map/all_to_all | solution.py:300
  24.2 51.1 %all-to-all-done = bf16[32,34,384]{2,1,0:T(8,128)(2,1)S(1)} async-done(((bf16[32,34,384]{2,1,0:T(8,128)(2,1)}), bf16[32,34,384]{2,1,0:T(8,128)(2,1)S(1)}, u32[]{:S(2)}, u32[]{:S(2)}) %all-to-all-start) | async-done | bytes 835616 | tf_op jit(solution)/shard_map/all_to_all | solution.py:300
  75.5 1.5 slice_reduce_fusion.5
  79.1 1.0 slice.146
  80.8 34.4 %all-gather.4.cloned.1.call-done.x_ref = bf16[4096,1024]{1,0:T(8,128)(2,1)} async-done(((bf16[512,1024]{1,0:T(8,128)(2,1)}), bf16[4096,1024]{1,0:T(8,128)(2,1)}) %all-gather.4.cloned.1.call-update) | async-done | bytes 8388624 | tf_op jit(solution)/shard_map/all_gather | solution.py:311
  115.2 12.8 %norm_mix.1 = (bf16[4096,1024]{1,0:T(8,128)(2,1)}, bf16[4096,128]{1,0:T(8,128)(2,1)}, bf16[4096,128]{1,0:T(8,128)(2,1)}, bf16[4096,128]{1,0:T(8,128)(2,1)}) custom-call(bf16[4096,1024]{1,0:T(8,128)(2,1)} %all-gather.4.cloned.1.call-done.x_ref, f32[1,1024]{1,0:T(1,128)} %slice.113.gain_ref, f32[1,1024]{1,0:T(1,128)} %slice.115.shift_ref, ...), custom_call_target="tpu_custom_call" | custom-call | flops 3221225472 | bytes 16777216 | tf_op jit(solution)/shard_map/norm_mix/pallas_call | solution.py:233
  127.9 26.2 %attend_forward.1 = (f32[4096,128]{1,0:T(8,128)}, bf16[4096,128]{1,0:T(8,128)(2,1)}, f32[4096,128]{1,0:T(8,128)}) custom-call(s32[2]{0:T(128)} %select_reduce_fusion.starts_ref, bf16[4096,128]{1,0:T(8,128)(2,1)} %get-tuple-element.25.q_ref, bf16[4096,128]{1,0:T(8,128)(2,1)} %get-tuple-element.26.k_ref, bf16[4096,128]{1,0:T(8,128)(2,1)} %get-tuple-element.27.v_ref), custom_call_target="tpu_custom_call" | custom-call | flops 4060086272 | bytes 8388608 | tf_op jit(solution)/shard_map/attend_forward/pallas_call | solution.py:113
  154.1 2.3 copy.128
  156.4 3.6 all-to-all-start.1
  160.7 131.4 %all-gather.6.cloned.1.call-done = bf16[384,32,1024]{2,1,0:T(8,128)(2,1)} async-done(((bf16[12,32,1024]{2,1,0:T(8,128)(2,1)}), bf16[384,32,1024]{2,1,0:T(8,128)(2,1)}) %all-gather.6.cloned.1.call-update) | async-done | bytes 25165840 | tf_op jit(solution)/shard_map/all_gather | solution.py:322
  292.1 3.2 slice.149
  295.2 12.3 %fusion.48 = (bf16[32,4,32,1024]{3,2,1,0:T(8,128)(2,1)}, bf16[32,32,4,1024]{3,1,2,0:T(8,128)(2,1)}) fusion(bf16[32,12,32,1024]{3,2,1,0:T(8,128)(2,1)} %bitcast.119), kind=kLoop, calls=%fused_computation.150 | loop fusion | bytes 33554432 | tf_op jit(solution)/shard_map/slice | solution.py:327
  307.6 1.0 copy-done.16
  308.6 5.7 fusion.47
  314.6 7.6 %copy.132 = bf16[32,32,4,1024]{3,2,1,0:T(4,128)(2,1)} copy(bf16[32,32,4,1024]{3,1,2,0:T(8,128)(2,1)S(1)} %bitcast.114) | data formatting | bytes 16777216 | tf_op jit(solution)/shard_map/transpose | solution.py:326
  322.2 12.1 %copy.148 = bf16[128,8,4,1024]{3,1,2,0:T(8,128)(2,1)} copy(bf16[128,8,4,1024]{3,2,1,0:T(4,128)(2,1)} %bitcast.112) | data formatting | bytes 16777216
  334.3 27.8 %multiply_convert_fusion = (bf16[512,4096]{1,0:T(8,128)(2,1)}, f32[512,4096]{1,0:T(8,128)}, f32[512,4096]{1,0:T(8,128)}) fusion(f32[4096]{0:T(1024)S(1)} %add.184, bf16[1024,4096]{1,0:T(8,128)(2,1)} %bitcast.124, f32[512,1024]{1,0:T(8,128)S(1)} %get-tuple-element.77, f32[1024]{0:T(1024)S(1)} %add.181, f32[1024]{0:T(1024)S(1)} %mul.404, f32[512]{0:T(512)S(1)} %fusion.28, ...), kind=kOutput, calls=%fused_computation.7 | convolution fusion | flops 4436000768 | bytes 31485952 | tf_op jit(solution)/shard_map/dot_general | solution.py:34
  362.0 15.0 %convert_reduce_fusion = (f32[4096]{0:T(1024)S(1)}, bf16[512,4096]{1,0:T(8,128)(2,1)}) fusion(f32[512,4096]{1,0:T(8,128)} %get-tuple-element.75, bf16[4096,1024]{1,0:T(8,128)(2,1)} %bitcast.126, bf16[512,1024]{1,0:T(8,128)(2,1)} %param.20, f32[512]{0:T(512)S(1)} %convert_element_type.117, f32[1024]{0:T(1024)S(1)} %mul.399, ...), kind=kOutput, calls=%fused_computation.5 | convolution fusion | flops 4332711936 | bytes 30447616 | tf_op jit(solution)/shard_map/dot_general | solution.py:44
  377.0 7.2 %multiply_reduce_fusion.1 = (f32[1024]{0:T(1024)S(1)}, f32[512]{0:T(512)S(1)}, f32[1024]{0:T(1024)S(1)}, f32[512,1024]{1,0:T(8,128)S(1)}) fusion(f32[512,1024]{1,0:T(8,128)S(1)} %get-tuple-element.77, f32[512]{0:T(512)S(1)} %fusion.28, f32[512]{0:T(512)S(1)} %broadcast_multiply_fusion.1, f32[1024]{0:T(1024)S(1)} %mul.404, ...), kind=kOutput, calls=%fused_computation.41 | convolution fusion | flops 4299159040 | bytes 16795648 | tf_op jit(solution)/shard_map/dot_general | solution.py:44
  384.2 7.7 %convolution_convert_fusion.1 = bf16[1024,4096]{1,0:T(8,128)(2,1)} fusion(bf16[512,4096]{1,0:T(8,128)(2,1)S(1)} %copy-done.48, f32[512,1024]{1,0:T(8,128)S(1)} %get-tuple-element.77, f32[1024]{0:T(1024)S(1)} %add.181, f32[1024]{0:T(1024)S(1)} %mul.404, f32[512]{0:T(512)S(1)} %fusion.28, f32[512]{0:T(512)S(1)} %broadcast_multiply_fusion.1), kind=kOutput, calls=%fused_computation.22 | convolution fusion | flops 4301783040 | bytes 14692352 | tf_op jit(solution)/shard_map/dot_general | solution.py:38
  391.9 0.7 fusion.45
  392.7 1.3 copy-done
  394.5 1.3 convolution_convert_fusion.2
  395.8 14.5 %reshape.272 = bf16[32,32,4,1024]{3,2,1,0:T(4,128)(2,1)} reshape(bf16[1024,4096]{1,0:T(8,128)(2,1)} %convolution_convert_fusion.1) | data formatting | bytes 16777216 | tf_op jit(solution)/shard_map/reshape | solution.py:396
  410.3 10.4 %copy.158 = bf16[32,32,4,1024]{3,1,2,0:T(8,128)(2,1)} copy(bf16[32,32,4,1024]{3,2,1,0:T(4,128)(2,1)} %reshape.272) | data formatting | bytes 16777216 | tf_op jit(solution)/shard_map/reshape | solution.py:396
  420.7 7.3 %convolution_convert_fusion = bf16[4096,1024]{1,0:T(8,128)(2,1)S(1)} fusion(bf16[512,4096]{1,0:T(8,128)(2,1)} %get-tuple-element.74, bf16[512,1024]{1,0:T(8,128)(2,1)S(1)} %copy-done.14, f32[512]{0:T(512)S(1)} %convert_element_type.117, f32[1024]{0:T(1024)S(1)} %mul.399), kind=kOutput, calls=%fused_computation.21 | convolution fusion | flops 4301258752 | bytes 13637632 | tf_op jit(solution)/shard_map/dot_general | solution.py:38
  428.0 12.6 %pad_maximum_fusion = bf16[32,9,32,1024]{3,2,1,0:T(8,128)(2,1)} fusion(bf16[32,4,32,1024]{3,2,1,0:T(8,128)(2,1)S(1)} %bitcast.130, bf16[32,4,32,1024]{3,2,1,0:T(8,128)(2,1)S(1)} %bitcast.117, bf16[32,1,32,1024]{3,2,1,0:T(8,128)(2,1)S(1)} %bitcast.134), kind=kLoop, calls=%fused_computation | loop fusion | flops 18874368 | bytes 37748736 | tf_op jit(solution)/shard_map/concatenate | solution.py:393
  440.7 1.6 copy-done.12
  442.2 1.3 fusion.14
  443.7 29.7 %all_to_all.35 = bf16[8,512,128]{2,1,0:T(8,128)(2,1)} all-to-all(bf16[8,512,128]{2,1,0:T(8,128)(2,1)S(1)} %bitcast.132), channel_id=1, replica_groups=mesh['fsdp'=4,'seq'=8] {'seq'}, dimensions={0} | all-to-all | bytes 2097152 | tf_op jit(solution)/shard_map/all_to_all | solution.py:385
  473.4 35.4 %attend_backward.1 = bf16[4096,384]{1,0:T(8,128)(2,1)} custom-call(s32[2]{0:T(128)} %select_reduce_fusion.starts_ref, bf16[4096,128]{1,0:T(8,128)(2,1)} %get-tuple-element.25.q_ref, bf16[4096,128]{1,0:T(8,128)(2,1)} %get-tuple-element.26.k_ref, bf16[4096,128]{1,0:T(8,128)(2,1)} %get-tuple-element.27.v_ref, f32[4096,128]{1,0:T(8,128)} %get-tuple-element.29.wide_ref, ...), custom_call_target="tpu_custom_call" | custom-call | flops 10150215680 | bytes 11534336 | tf_op jit(solution)/shard_map/attend_backward/pallas_call | solution.py:193
  508.8 9.9 %convolution_convert_fusion.4 = bf16[1024,384]{1,0:T(8,128)(2,1)} fusion(bf16[4096,1024]{1,0:T(8,128)(2,1)} %get-tuple-element.31, bf16[4096,384]{1,0:T(8,128)(2,1)} %attend_backward.1), kind=kOutput, calls=%fused_computation.55 | convolution fusion | flops 3221618688 | bytes 12320768 | tf_op jit(solution)/shard_map/dot_general | solution.py:38
  518.7 3.3 all-to-all-start.4
  522.1 2.9 copy.135
  525.0 39.3 %all-to-all-done.4 = bf16[32,32,384]{2,1,0:T(8,128)(2,1)} async-done(((bf16[32,32,384]{2,1,0:T(8,128)(2,1)}), bf16[32,32,384]{2,1,0:T(8,128)(2,1)}, u32[]{:S(2)}, u32[]{:S(2)}) %all-to-all-start.4) | async-done | bytes 786464 | tf_op jit(solution)/shard_map/all_to_all | solution.py:418
  564.2 3.9 all-to-all-start.3
  569.4 7.0 slice_bitcast_fusion.1
  576.5 12.0 %copy.137 = bf16[32,32,3,1024]{3,2,1,0:T(4,128)(2,1)} copy(bf16[32,32,3,1024]{3,1,2,0:T(8,128)(2,1)} %slice_bitcast_fusion.1) | data formatting | bytes 12582912 | tf_op jit(solution)/shard_map/transpose | solution.py:324
  588.5 10.2 %copy.149 = bf16[128,8,3,1024]{3,1,2,0:T(8,128)(2,1)} copy(bf16[128,8,3,1024]{3,2,1,0:T(4,128)(2,1)} %bitcast.111) | data formatting | bytes 12582912
  601.4 3.7 reshape.277
  605.1 3.0 reduce_sum.197
  608.1 1.3 copy.138
  609.4 55.5 %all-to-all-done.3 = bf16[8,512,384]{1,2,0:T(8,128)(2,1)S(1)} async-done(((bf16[8,512,384]{1,2,0:T(8,128)(2,1)}), bf16[8,512,384]{1,2,0:T(8,128)(2,1)S(1)}, u32[]{:S(2)}, u32[]{:S(2)}) %all-to-all-start.3) | async-done | bytes 3145760 | tf_op jit(solution)/shard_map/all_to_all | solution.py:408
  665.1 3.8 convert_element_type.129
  669.0 6.5 fusion.37
  675.5 1.0 fusion.13
  676.6 7.1 multiply_reduce_fusion
  684.0 2.6 slice_reduce_fusion
  687.2 0.8 all_to_all.28
  688.0 2.7 all-to-all-start.5
  690.7 1.3 multiply_subtract_fusion.2
  692.0 6.1 all-to-all-done.5
  698.7 1.4 multiply_subtract_fusion.4
  700.1 1.3 convert_element_type.128
  701.5 1.8 multiply_subtract_fusion.3
  703.3 1.4 multiply_subtract_fusion.1
  704.8 1.4 multiply_subtract_fusion
  (202 shorter events, 13.0 us)
Async XLA Ops:
  7.2 108.0 %all-gather.4.cloned.1.call-start = ((), (), s32[]{:S(2)}) async-start(), calls=%async_computation.7 | async-start | bytes 9437184 | tf_op jit(solution)/shard_map/all_gather | solution.py:311
  7.9 284.1 %all-gather.6.cloned.1.call-start = ((), (), s32[]{:S(2)}) async-start(), calls=%async_computation.9 | async-start | bytes 25952256 | tf_op jit(solution)/shard_map/all_gather | solution.py:322
  8.9 6.2 copy-start.31
  8.9 6.3 copy-start.38
  8.9 6.3 copy-start.44
  9.0 6.4 copy-start.6
  16.9 58.4 %all-to-all-start = ((bf16[32,34,384]{2,1,0:T(8,128)(2,1)}), bf16[32,34,384]{2,1,0:T(8,128)(2,1)S(1)}, u32[]{:S(2)}, u32[]{:S(2)}) async-start(bf16[32,34,384]{2,1,0:T(8,128)(2,1)} %bitcast.1), calls=%async_computation | async-start | bytes 1966080 | tf_op jit(solution)/shard_map/all_to_all | solution.py:300
  156.4 151.2 %all-to-all-start.1 = ((bf16[8,512,128]{1,2,0:T(8,128)(2,1)}), bf16[8,512,128]{1,2,0:T(8,128)(2,1)S(1)}, u32[]{:S(2)}, u32[]{:S(2)}) async-start(bf16[8,512,128]{1,2,0:T(8,128)(2,1)} %copy.128), calls=%async_computation.1 | async-start | bytes 2097152 | tf_op jit(solution)/shard_map/all_to_all | solution.py:354
  159.9 540.1 %reduce-scatter.2.cloned.1.call-start = ((), (), s32[]{:S(2)}) async-start(), calls=%async_computation.8 | async-start | bytes 19464192 | tf_op jit(solution)/shard_map/reduce_scatter | solution.py:401
  160.2 260.5 %copy-start.33 = (f32[512]{0:T(512)}, f32[512]{0:T(512)S(1)}, u32[]{:S(2)}) copy-start(f32[512]{0:T(512)S(1)} %convert_element_type.117) | copy-start | bytes 6148
  160.3 260.4 %copy-start.39 = (f32[1024]{0:T(1024)}, f32[1024]{0:T(1024)S(1)}, u32[]{:S(2)}) copy-start(f32[1024]{0:T(1024)S(1)} %mul.399) | copy-start | bytes 12292
  160.6 148.0 %copy-start.41 = (f32[1024]{0:T(1024)}, f32[1024]{0:T(1024)S(1)}, u32[]{:S(2)}) copy-start(f32[1024]{0:T(1024)S(1)} %add.176) | copy-start | bytes 12292
  307.6 1.0 copy-start.16
  308.6 6.0 slice-start
  308.6 6.0 slice-start.1
  314.2 77.7 %copy-start.3 = (f32[512,1024]{1,0:T(8,128)}, f32[512,1024]{1,0:T(8,128)S(1)}, u32[]{:S(2)}) copy-start(f32[512,1024]{1,0:T(8,128)S(1)} %get-tuple-element.77) | copy-start | bytes 6291460
  362.0 15.0 %copy-start.2 = (bf16[128,8,4,1024]{3,1,2,0:T(8,128)(2,1)S(1)}, bf16[128,8,4,1024]{3,1,2,0:T(8,128)(2,1)}, u32[]{:S(2)}) copy-start(bf16[128,8,4,1024]{3,1,2,0:T(8,128)(2,1)} %copy.148) | copy-start | bytes 25165828
  377.0 7.2 %copy-start.48 = (bf16[512,4096]{1,0:T(8,128)(2,1)S(1)}, bf16[512,4096]{1,0:T(8,128)(2,1)}, u32[]{:S(2)}) copy-start(bf16[512,4096]{1,0:T(8,128)(2,1)} %get-tuple-element.95) | copy-start | bytes 12582916
  391.9 2.1 copy-start.13
  391.9 2.6 copy-start.17
  392.7 1.3 copy-start
  392.7 3.1 copy-start.35
  410.3 10.4 %copy-start.14 = (bf16[512,1024]{1,0:T(8,128)(2,1)S(1)}, bf16[512,1024]{1,0:T(8,128)(2,1)}, u32[]{:S(2)}) copy-start(bf16[512,1024]{1,0:T(8,128)(2,1)} %param.20) | copy-start | bytes 3145732
  420.7 7.3 %slice-start.2 = ((s8[8388608]{0:T(1024)(128)(4,1)}), s8[4194304]{0:T(1024)(128)(4,1)S(1)}, s32[]{:S(2)}) async-start(s8[8388608]{0:T(1024)(128)(4,1)} %bitcast.115), calls=%async_computation.12 | async-start | bytes 8388608
  420.7 7.3 %slice-start.3 = ((s8[8388608]{0:T(1024)(128)(4,1)}), s8[4194304]{0:T(1024)(128)(4,1)S(1)}, s32[]{:S(2)}) async-start(s8[8388608]{0:T(1024)(128)(4,1)} %bitcast.115), calls=%async_computation.13 | async-start | bytes 8388608
  440.6 1.6 copy-start.12
  508.8 13.2 %copy-start.8 = (bf16[4096,384]{1,0:T(8,128)(2,1)S(1)}, bf16[4096,384]{1,0:T(8,128)(2,1)}, u32[]{:S(2)}) copy-start(bf16[4096,384]{1,0:T(8,128)(2,1)} %attend_backward.1) | copy-start | bytes 9437188
  518.7 45.5 %all-to-all-start.4 = ((bf16[32,32,384]{2,1,0:T(8,128)(2,1)}), bf16[32,32,384]{2,1,0:T(8,128)(2,1)}, u32[]{:S(2)}, u32[]{:S(2)}) async-start(bf16[32,32,384]{2,1,0:T(8,128)(2,1)} %bitcast.152), calls=%async_computation.4 | async-start | bytes 1572864 | tf_op jit(solution)/shard_map/all_to_all | solution.py:418
  525.0 43.1 %copy-start.30 = (f32[1,32,32]{2,0,1:T(1,128)S(1)}, f32[1,32,32]{2,0,1:T(1,128)}, u32[]{:S(2)}) copy-start(f32[1,32,32]{2,0,1:T(1,128)} %get-tuple-element.83) | copy-start | bytes 12292
  525.0 43.8 %copy-start.29 = (f32[32,32]{1,0:T(8,128)S(1)}, f32[32,32]{1,0:T(8,128)}, u32[]{:S(2)}) copy-start(f32[32,32]{1,0:T(8,128)} %get-tuple-element.47) | copy-start | bytes 12292
  564.2 100.6 %all-to-all-start.3 = ((bf16[8,512,384]{1,2,0:T(8,128)(2,1)}), bf16[8,512,384]{1,2,0:T(8,128)(2,1)S(1)}, u32[]{:S(2)}, u32[]{:S(2)}) async-start(bf16[8,512,384]{1,2,0:T(8,128)(2,1)} %copy.135), calls=%async_computation.3 | async-start | bytes 6291456 | tf_op jit(solution)/shard_map/all_to_all | solution.py:408
  588.5 12.3 %copy-start.45 = (f32[512]{0:T(512)S(1)}, f32[512]{0:T(512)}, u32[]{:S(2)}) copy-start(f32[512]{0:T(512)} %get-tuple-element.82) | copy-start | bytes 6148
  665.0 3.8 copy-start.5
  665.0 3.8 copy-start.32
  665.1 3.8 copy-start.37
  665.1 11.4 %slice-start.4 = ((s8[8388608]{0:T(1024)(128)(4,1)}), s8[4194304]{0:T(1024)(128)(4,1)S(1)}, s32[]{:S(2)}) async-start(s8[8388608]{0:T(1024)(128)(4,1)} %bitcast.127), calls=%async_computation.14 | async-start | bytes 8388608
  668.9 7.6 %copy-start.1 = (f32[512,1024]{1,0:T(8,128)S(1)}, f32[512,1024]{1,0:T(8,128)}, u32[]{:S(2)}) copy-start(f32[512,1024]{1,0:T(8,128)} %copy-done) | copy-start | bytes 6291460
  668.9 7.6 %copy-start.4 = (f32[512,1024]{1,0:T(8,128)S(1)}, f32[512,1024]{1,0:T(8,128)}, u32[]{:S(2)}) copy-start(f32[512,1024]{1,0:T(8,128)} %copy-done.3) | copy-start | bytes 6291460
  668.9 7.6 %slice-start.5 = ((s8[8388608]{0:T(1024)(128)(4,1)}), s8[4194304]{0:T(1024)(128)(4,1)S(1)}, s32[]{:S(2)}) async-start(s8[8388608]{0:T(1024)(128)(4,1)} %bitcast.127), calls=%async_computation.15 | async-start | bytes 8388608
  668.9 7.6 %copy-start.15 = (bf16[512,1024]{1,0:T(8,128)(2,1)S(1)}, bf16[512,1024]{1,0:T(8,128)(2,1)}, u32[]{:S(2)}) copy-start(bf16[512,1024]{1,0:T(8,128)(2,1)} %param.20) | copy-start | bytes 3145732
  668.9 7.6 %copy-start.34 = (f32[512]{0:T(512)S(1)}, f32[512]{0:T(512)}, u32[]{:S(2)}) copy-start(f32[512]{0:T(512)} %copy-done.33) | copy-start | bytes 6148
  668.9 7.6 %copy-start.36 = (f32[512]{0:T(512)S(1)}, f32[512]{0:T(512)}, u32[]{:S(2)}) copy-start(f32[512]{0:T(512)} %copy-done.35) | copy-start | bytes 6148
  668.9 7.6 %copy-start.40 = (f32[1024]{0:T(1024)S(1)}, f32[1024]{0:T(1024)}, u32[]{:S(2)}) copy-start(f32[1024]{0:T(1024)} %copy-done.39) | copy-start | bytes 12292
  668.9 7.6 %copy-start.42 = (f32[1024]{0:T(1024)S(1)}, f32[1024]{0:T(1024)}, u32[]{:S(2)}) copy-start(f32[1024]{0:T(1024)} %copy-done.41) | copy-start | bytes 12292
  668.9 7.6 %copy-start.43 = (f32[1024]{0:T(1024)S(1)}, f32[1024]{0:T(1024)}, u32[]{:S(2)}) copy-start(f32[1024]{0:T(1024)} %add.187) | copy-start | bytes 12292
  669.0 7.6 %copy-start.46 = (f32[512,1024]{1,0:T(8,128)S(1)}, f32[512,1024]{1,0:T(8,128)}, u32[]{:S(2)}) copy-start(f32[512,1024]{1,0:T(8,128)} %get-tuple-element.90) | copy-start | bytes 6291460
  669.0 7.6 %copy-start.47 = (bf16[512,4096]{1,0:T(8,128)(2,1)S(1)}, bf16[512,4096]{1,0:T(8,128)(2,1)}, u32[]{:S(2)}) copy-start(bf16[512,4096]{1,0:T(8,128)(2,1)} %get-tuple-element.74) | copy-start | bytes 12582916
  683.6 3.2 copy-start.28
  683.6 3.3 copy-start.27
  683.6 3.3 copy-start.25
  683.7 7.0 copy-start.7
  683.7 7.0 copy-start.23
  683.7 7.0 copy-start.24
  686.7 14.8 %copy-start.22 = (f32[32,1024]{1,0:T(8,128)S(1)}, f32[32,1024]{1,0:T(8,128)}, u32[]{:S(2)}) copy-start(f32[32,1024]{1,0:T(8,128)} %param.24) | copy-start | bytes 393220
  687.0 16.3 %copy-start.10 = (f32[32,4096]{1,0:T(8,128)S(1)}, f32[32,4096]{1,0:T(8,128)}, u32[]{:S(2)}) copy-start(f32[32,4096]{1,0:T(8,128)} %param.25) | copy-start | bytes 1572868
  687.0 16.3 %copy-start.18 = (f32[32,4096]{1,0:T(8,128)S(1)}, f32[32,4096]{1,0:T(8,128)}, u32[]{:S(2)}) copy-start(f32[32,4096]{1,0:T(8,128)} %param.30) | copy-start | bytes 1572868
  687.0 16.3 %copy-start.19 = (f32[32,4096]{1,0:T(8,128)S(1)}, f32[32,4096]{1,0:T(8,128)}, u32[]{:S(2)}) copy-start(f32[32,4096]{1,0:T(8,128)} %param.35) | copy-start | bytes 1572868
  688.0 13.5 %copy-start.26 = (f32[32,1024]{1,0:T(8,128)S(1)}, f32[32,1024]{1,0:T(8,128)}, u32[]{:S(2)}) copy-start(f32[32,1024]{1,0:T(8,128)} %param.29) | copy-start | bytes 393220
  688.0 10.1 %all-to-all-start.5 = ((f32[32,1,448]{2,1,0:T(1,128)}), f32[32,1,448]{2,1,0:T(1,128)S(1)}, u32[]{:S(2)}, u32[]{:S(2)}) async-start(f32[32,1,448]{2,1,0:T(1,128)} %all_to_all.28), calls=%async_computation.6 | async-start | bytes 131072 | tf_op jit(solution)/shard_map/all_to_all | solution.py:453
  700.1 4.6 copy-start.9
  701.4 3.4 copy-start.11
  701.4 3.4 copy-start.20
  701.4 3.4 copy-start.21
Sparse Core Ops, SparseCore 0:
  9.6 105.5 all-gather.3
  118.2 173.8 all-gather.5
  440.8 254.5 reduce-scatter.1

commit v2 on v1

--- a/solution.py
+++ b/solution.py
@@ -212,9 +212,13 @@
     )(starts, query, keys, values, wide, logs, grad_out)
 
 
-def norm_mix_kernel(x_ref, gain_ref, shift_ref, weight_ref, bias_ref, a_ref, q_ref, k_ref, v_ref):
+def norm_mix_kernel(
+    core_ref, own_ref, other_ref, gain_ref, shift_ref, weight_ref, bias_ref, a_ref, q_ref, k_ref, v_ref
+):
     lanes = q_ref.shape[1]
-    normed = layer_norm(x_ref[...].astype(jnp.float32), gain_ref[...], shift_ref[...])
+    mine = lax.rem(pl.program_id(0), 2) == core_ref[0]
+    own, other = own_ref[...].astype(jnp.float32), other_ref[...].astype(jnp.float32)
+    normed = layer_norm(jnp.where(mine, own, other), gain_ref[...], shift_ref[...])
     normed = normed.astype(jnp.bfloat16)
     a_ref[...] = normed
     mixed = (plain_product(normed, weight_ref[...]) + bias_ref[...]).astype(jnp.bfloat16)
@@ -223,27 +227,204 @@
     v_ref[...] = mixed[:, 2 * lanes :]
 
 
-def norm_mix(stream, gain, shift, weight, bias):
-    length, width = stream.shape
+def norm_mix(core, own, other, block, gain, shift, weight, bias):
+    length, width = own.shape[0] * 2, own.shape[1]
     lanes = weight.shape[1] // 3
-    block = 512
-    row = lambda size: pl.BlockSpec((block, size), lambda i: (i, 0))
-    fixed = lambda *shape: pl.BlockSpec(shape, lambda i: (0, 0))
+    row = lambda size: pl.BlockSpec((block, size), lambda i, core: (i, 0))
+    half = pl.BlockSpec((block, width), lambda i, core: (i // 2, 0))
+    fixed = lambda *shape: pl.BlockSpec(shape, lambda i, core: (0, 0))
     part = jax.ShapeDtypeStruct((length, lanes), jnp.bfloat16)
     return pl.pallas_call(
         norm_mix_kernel,
-        grid=(length // block,),
-        in_specs=[
-            row(width), fixed(1, width), fixed(1, width), fixed(width, 3 * lanes), fixed(1, 3 * lanes)
-        ],
-        out_specs=[row(width), row(lanes), row(lanes), row(lanes)],
+        grid_spec=pltpu.PrefetchScalarGridSpec(
+            num_scalar_prefetch=1,
+            grid=(length // block,),
+            in_specs=[
+                half,
+                half,
+                fixed(1, width),
+                fixed(1, width),
+                fixed(width, 3 * lanes),
+                fixed(1, 3 * lanes),
+            ],
+            out_specs=[row(width), row(lanes), row(lanes), row(lanes)],
+        ),
         out_shape=(jax.ShapeDtypeStruct((length, width), jnp.bfloat16), part, part, part),
         compiler_params=pltpu.CompilerParams(vmem_limit_bytes=VMEM_BYTES),
         cost_estimate=pl.CostEstimate(
             flops=length * width * lanes * 6, bytes_accessed=length * width * 4, transcendentals=0
         ),
         name="norm_mix",
-    )(stream, gain[None], shift[None], weight, bias[None])
+    )(core, own, other, gain[None], shift[None], weight, bias[None])
+
+
+def mlp_kernel(
+    h_ref, gm_ref, up_ref, down_ref, bias_ref, grad_ref, m_ref, gh_ref, bias_grad_ref, turned_ref
+):
+    tile = pl.program_id(0)
+    width = h_ref.shape[1]
+    chips, up_rows, units = up_ref.shape
+    part, down_rows = down_ref.shape[0], down_ref.shape[1]
+    folds = width // units
+
+    @pl.when(tile == 0)
+    def clear():
+        m_ref[...] = jnp.zeros_like(m_ref)
+        gh_ref[...] = jnp.zeros_like(gh_ref)
+        turned_ref[...] = h_ref[...].T
+
+    weight_up = up_ref[...].reshape(width, units)
+    weight_down = down_ref[...].reshape(units, width)
+    gm = gm_ref[...]
+    upward = plain_product(h_ref[...], weight_up) + bias_ref[...]
+    normal = 0.5 * (1.0 + lax.erf(upward * 0.5**0.5))
+    slope = normal + upward * jnp.exp(upward * upward * -0.5) * (0.5 / jnp.pi) ** 0.5
+    active = (upward * normal).astype(jnp.bfloat16)
+    grad_up = (inner_cols(gm, weight_down) * slope).astype(jnp.bfloat16)
+    bias_grad_ref[...] = jnp.sum(grad_up.astype(jnp.float32), axis=0, keepdims=True)
+    m_ref[...] += plain_product(active, weight_down)
+    gh_ref[...] += inner_cols(grad_up, weight_up)
+    up_grad = plain_product(turned_ref[...], grad_up).astype(jnp.bfloat16)
+    row = pl.multiple_of(tile // folds * up_rows, up_rows)
+    column = pl.multiple_of(lax.rem(tile, folds) * units, units)
+    grad_ref[:, pl.ds(row, up_rows), pl.ds(column, units)] = up_grad.reshape(chips, up_rows, units)
+    down_grad = inner_rows(active, gm).astype(jnp.bfloat16).reshape(part, down_rows, width)
+    base = 2 * up_rows
+    if chips > 1:
+        grad_ref[pl.ds(tile * part, part), base : base + down_rows, :] = down_grad
+    else:
+        start = pl.multiple_of(base + tile * down_rows, down_rows)
+        grad_ref[:, pl.ds(start, down_rows), :] = down_grad
+
+
+def mlp(normed, gm, packed, up_rows, bias):
+    rows, width = normed.shape
+    chips = packed.shape[0]
+    hidden = bias.shape[0]
+    units = 256
+    folds = width // units
+    once = dict(pipeline_mode=pl.Buffered(1))
+    fixed = pl.BlockSpec((rows, width), lambda j: (0, 0), **once)
+    if chips > 1:
+        part = units * chips // hidden
+        down = pl.BlockSpec((part, units // part, width), lambda j: (j, 2 * up_rows * part // units, 0))
+    else:
+        down = pl.BlockSpec((1, units, width), lambda j: (0, 2 * up_rows // units + j, 0))
+    total = jax.ShapeDtypeStruct((rows, width), jnp.float32)
+    return pl.pallas_call(
+        mlp_kernel,
+        grid=(hidden // units,),
+        in_specs=[
+            fixed,
+            fixed,
+            pl.BlockSpec((chips, up_rows, units), lambda j: (0, j // folds, lax.rem(j, folds))),
+            down,
+            pl.BlockSpec((1, units), lambda j: (0, j)),
+        ],
+        out_specs=[
+            pl.BlockSpec(packed.shape, lambda j: (0, 0, 0), **once),
+            fixed,
+            fixed,
+            pl.BlockSpec((1, units), lambda j: (0, j)),
+        ],
+        out_shape=(
+            jax.ShapeDtypeStruct(packed.shape, jnp.bfloat16),
+            total,
+            total,
+            jax.ShapeDtypeStruct((1, hidden), jnp.float32),
+        ),
+        scratch_shapes=[pltpu.VMEM((width, rows), jnp.bfloat16)],
+        compiler_params=pltpu.CompilerParams(vmem_limit_bytes=VMEM_BYTES),
+        cost_estimate=pl.CostEstimate(
+            flops=rows * width * hidden * 12,
+            bytes_accessed=packed.size * 4 + rows * width * 12,
+            transcendentals=rows * hidden * 2,
+        ),
+        name="mlp_both_ways",
+    )(normed, gm, packed, packed, bias[None])
+
+
+def finish_kernel(
+    grad_ref, weight_ref, x_ref, gx_ref, gain_ref, out_ref, gain_grad_ref, shift_grad_ref, sums_ref, acc_ref
+):
+    step = pl.program_id(0)
+    parts = [grad_ref[slot] for slot in range(grad_ref.shape[0])]
+    grad = jnp.concatenate(parts, axis=1)
+    width = x_ref.shape[1]
+    product = inner_cols(grad, weight_ref[...].reshape(width, width))
+    sums_ref[...] = jnp.sum(grad.astype(jnp.float32), axis=0, keepdims=True)[None]
+
+    @pl.when(step == 0)
+    def begin():
+        acc_ref[...] = product
+
+    @pl.when(step > 0)
+    def further():
+        acc_ref[...] += product
+
+    @pl.when(step == pl.num_programs(0) - 1)
+    def end():
+        values = x_ref[...].astype(jnp.float32)
+        centered = values - jnp.mean(values, axis=1, keepdims=True)
+        scale = lax.rsqrt(jnp.mean(centered * centered, axis=1, keepdims=True) + 1e-06)
+        unit = centered * scale
+        grad_norm = acc_ref[...]
+        gain_grad_ref[...] = jnp.sum(grad_norm * unit, axis=0, keepdims=True)
+        shift_grad_ref[...] = jnp.sum(grad_norm, axis=0, keepdims=True)
+        grad_unit = grad_norm * gain_ref[...]
+        mean = jnp.mean(grad_unit, axis=1, keepdims=True)
+        slant = jnp.mean(grad_unit * unit, axis=1, keepdims=True)
+        out_ref[...] = gx_ref[...] + scale * (grad_unit - mean - unit * slant)
+
+
+def finish(grads, weights, inputs, gx, gain):
+    rows, width = inputs.shape
+    group, lanes = grads.shape[0], grads.shape[2] // 3
+    if lanes % 128:
+        grads = grads.reshape(group, rows, 3, lanes).transpose(2, 0, 1, 3)
+        grads = grads.reshape(3 * group, rows, lanes)
+        grad_spec = pl.BlockSpec((group, rows, lanes), lambda k: (k, 0, 0))
+    else:
+        grad_spec = pl.BlockSpec((group, rows, lanes), lambda k: (0, 0, k))
+    share = weights.shape[1] // 3
+    if share % 16:
+        weights = weights.reshape(-1, 3, share, width).transpose(1, 0, 2, 3).reshape(1, -1, width)
+        share = width
+    fixed = lambda *shape: pl.BlockSpec(shape, lambda k: (0, 0))
+    vector = jax.ShapeDtypeStruct((1, width), jnp.float32)
+    return pl.pallas_call(
+        finish_kernel,
+        grid=(3,),
+        in_specs=[
+            grad_spec,
+            pl.BlockSpec((weights.shape[0], share, width), lambda k: (0, k, 0)),
+            fixed(rows, width),
+            fixed(rows, width),
+            fixed(1, width),
+        ],
+        out_specs=[
+            fixed(rows, width),
+            fixed(1, width),
+            fixed(1, width),
+            pl.BlockSpec((1, 1, width), lambda k: (k, 0, 0)),
+        ],
+        out_shape=(
+            jax.ShapeDtypeStruct((rows, width), jnp.float32),
+            vector,
+            vector,
+            jax.ShapeDtypeStruct((3, 1, width), jnp.float32),
+        ),
+        scratch_shapes=[pltpu.VMEM((rows, width), jnp.float32)],
+        compiler_params=pltpu.CompilerParams(vmem_limit_bytes=VMEM_BYTES),
+        cost_estimate=pl.CostEstimate(
+            flops=rows * width * width * 6, bytes_accessed=width * width * 16, transcendentals=0
+        ),
+        name="finish_input",
+    )(grads, weights, inputs, gx, gain[None])
+
+
+def swap_cores(value):
+    return lax.ppermute(value, "core", [(0, 1), (1, 0)])
 
 
 def on_device(
@@ -269,13 +450,26 @@
 ):
     rows = tokens.shape[0]
     width = tokens.shape[1]
-    both = ("fsdp", "seq")
-    streams, group = lax.axis_size("fsdp"), lax.axis_size("seq")
+    everyone = ("fsdp", "line", "core")
+    chip_axes = ("fsdp", "line")
+    seq = ("line", "core")
+    streams, line = lax.axis_size("fsdp"), lax.axis_size("line")
+    group = 2 * line
     count = streams * group
+    chips = streams * line
     share = width // count
     lanes = width // group
     length = rows * group
     images = length // IMG_LEN
+    core = lax.axis_index("core")
+    first_core = core == 0
+
+    def in_order(own, other, axis):
+        return jnp.concatenate(
+            [jnp.where(first_core, own, other), jnp.where(first_core, other, own)], axis=axis
+        )
+
+    line_tokens = lax.all_gather(tokens, "line", axis=0, tiled=True)
 
     owned = project_in.astype(jnp.bfloat16).reshape(share, 3, group, lanes)
     owned = owned.transpose(2, 0, 1, 3).reshape(group, share, 3 * lanes)
@@ -295,9 +489,10 @@
     extra = -(-small.shape[0] // (3 * lanes))
     small = jnp.pad(small, (0, extra * 3 * lanes - small.shape[0])).reshape(1, extra, 3 * lanes)
     blocks = jnp.concatenate([owned, jnp.broadcast_to(small, (group, extra, 3 * lanes))], axis=1)
+    blocks = lax.all_to_all(blocks, seq, split_axis=0, concat_axis=0, tiled=True)
     blocks = jnp.broadcast_to(blocks[None], (streams, *blocks.shape))
+    blocks = lax.all_to_all(blocks, "fsdp", split_axis=0, concat_axis=0, tiled=True)
     blocks = blocks.reshape(count, share + extra, 3 * lanes)
-    blocks = lax.all_to_all(blocks, both, split_axis=0, concat_axis=0, tiled=True)
     mine_in = blocks[:, :share].reshape(width, 3 * lanes)
     small = blocks[:, share:].reshape(count, -1)
     vectors = small[:, :vector_size].reshape(count, -1, share).transpose(1, 0, 2)
@@ -308,23 +503,49 @@
     offsets = lax.broadcasted_iota(jnp.int32, (group, images), 0) * rows
     starts = jnp.min(jnp.where(first < rows, first + offsets, length), axis=0)
 
-    stream = lax.all_gather(tokens, "seq", axis=0, tiled=True)
-
+    half = FF // 2
+    unit_block = FF // count
+    up_blocks = hidden_up.astype(jnp.bfloat16).reshape(share, chips, 2, unit_block)
+    up_first = up_blocks[:, :, 0].reshape(share, half)
+    up_second = up_blocks[:, :, 1].reshape(share, half)
+    out_rows = project_out.astype(jnp.bfloat16)
+    received = swap_cores(
+        jnp.concatenate(
+            [jnp.where(first_core, up_second, up_first).reshape(-1, width), out_rows], axis=0
+        )
+    )
+    folds = half // width
+    up_rows = in_order(
+        jnp.where(first_core, up_first, up_second),
+        received[: share * folds].reshape(share, half),
+        0,
+    )
     packed = jnp.concatenate(
         [
-            project_in.astype(jnp.bfloat16).reshape(share, 3, width).transpose(1, 0, 2),
-            project_out.astype(jnp.bfloat16)[None],
-            hidden_up.astype(jnp.bfloat16).reshape(share, -1, width).transpose(1, 0, 2),
-            hidden_down.astype(jnp.bfloat16).reshape(-1, share, width),
+            up_rows.reshape(2 * share, folds, width).transpose(1, 0, 2).reshape(-1, width),
+            hidden_down.astype(jnp.bfloat16),
+            in_order(out_rows, received[share * folds :], 0),
         ],
         axis=0,
     )
-    gathered = lax.all_gather(packed, both, axis=0, tiled=False)
-    fold = FF // width
-    whole_in = gathered[:, 0:3].transpose(0, 2, 1, 3).reshape(width, 3 * width)
-    whole_out = gathered[:, 3].reshape(width, width)
-    whole_up = gathered[:, 4 : 4 + fold].transpose(0, 2, 1, 3).reshape(width, FF)
-    whole_down = gathered[:, 4 + fold :].reshape(FF, width)
+    packed, line_tokens = lax.optimization_barrier((packed, line_tokens))
+    gathered = lax.all_gather(packed, chip_axes, axis=0, tiled=False)
+    in_rows = project_in.astype(jnp.bfloat16).reshape(share, 3, width).transpose(1, 0, 2)
+    in_rows, gathered = lax.optimization_barrier((in_rows.reshape(-1, width), gathered))
+    gathered_in = lax.all_gather(in_rows, everyone, axis=0, tiled=False)
+    up_end = 2 * share * folds
+    down_end = up_end + half // chips
+    whole_out = gathered[:, down_end:].reshape(width, width)
+    direct = (2 * share) % 16 == 0
+    if direct:
+        mlp_weights, mlp_up_rows = gathered, 2 * share
+    else:
+        mlp_weights = jnp.concatenate(
+            [gathered[:, n * 2 * share : (n + 1) * 2 * share].reshape(width, width) for n in range(folds)]
+            + [gathered[:, up_end:down_end].reshape(half, width)],
+            axis=0,
+        )[None]
+        mlp_up_rows = width
 
     gain_one, shift_one, bias_query, bias_value, bias_out = (
         vectors[0],
@@ -340,8 +561,10 @@
         vectors[8],
         vectors[9],
     )
-    bias_up = vectors[10:].reshape(-1)
-    column = lax.axis_index("seq") * lanes
+    bias_up = lax.dynamic_index_in_dim(
+        vectors[10:].reshape(chips, 2, unit_block), core, axis=1, keepdims=False
+    ).reshape(half)
+    column = lax.axis_index(seq) * lanes
     bias_in = jnp.concatenate(
         [
             lax.dynamic_slice_in_dim(bias_query, column, lanes, 0),
@@ -349,10 +572,23 @@
             lax.dynamic_slice_in_dim(bias_value, column, lanes, 0),
         ]
     )
-    normed_one, query, keys, values = norm_mix(stream, gain_one, shift_one, mine_in, bias_in)
+    grad_rows = cotangent.astype(jnp.float32) * valid.astype(jnp.float32)[:, None]
+    grad_branch = (scale_two * grad_rows).astype(jnp.bfloat16)
+    grad_branch_chip = jnp.concatenate([grad_branch, swap_cores(grad_branch)], axis=0)
+
+    normed_one, query, keys, values = norm_mix(
+        core.reshape(1),
+        line_tokens,
+        swap_cores(line_tokens),
+        rows,
+        gain_one,
+        shift_one,
+        mine_in,
+        bias_in,
+    )
     wide, attended, logs = attend(starts, query, keys, values)
     returned = lax.all_to_all(
-        attended.reshape(group, rows, lanes), "seq", split_axis=0, concat_axis=0, tiled=True
+        attended.reshape(group, rows, lanes), seq, split_axis=0, concat_axis=0, tiled=True
     )
     attended_rows = returned.transpose(1, 0, 2).reshape(rows, width)
     inputs = tokens.astype(jnp.float32)
@@ -360,82 +596,74 @@
     second = inputs + scale_one * projected
     norm_two, norm_two_back = jax.vjp(layer_norm, second, gain_two, shift_two)
     normed_two = norm_two.astype(jnp.bfloat16)
-    upward = plain_product(normed_two, whole_up) + bias_up
-    activated, gelu_back = jax.vjp(exact_gelu, upward)
-    active = activated.astype(jnp.bfloat16)
-    branch = plain_product(active, whole_down) + bias_down
+    normed_chip = jnp.concatenate([normed_two, swap_cores(normed_two)], axis=0)
+    grad_packed, branch_part, grad_norm_part, grad_bias_up = mlp(
+        normed_chip, grad_branch_chip, mlp_weights, mlp_up_rows, bias_up
+    )
+    grad_norm_two = grad_norm_part[:rows] + swap_cores(grad_norm_part[rows:])
+    branch = branch_part[:rows] + swap_cores(branch_part[rows:]) + bias_down
     block_output = (second + scale_two * branch).astype(jnp.bfloat16)
-    grad_rows = cotangent.astype(jnp.float32) * valid.astype(jnp.float32)[:, None]
     grad_scale_two = jnp.sum(grad_rows * branch, axis=0)
-    grad_branch = (scale_two * grad_rows).astype(jnp.bfloat16)
     grad_bias_down = jnp.sum(grad_branch.astype(jnp.float32), axis=0)
-    grad_down = inner_rows(active, grad_branch)
-    grad_active = inner_cols(grad_branch, whole_down)
-    grad_upward = gelu_back(grad_active)[0].astype(jnp.bfloat16)
-    grad_bias_up = jnp.sum(grad_upward.astype(jnp.float32), axis=0)
-    grad_up = inner_rows(normed_two, grad_upward)
-    grad_norm_two = inner_cols(grad_upward, whole_up)
     second_part, grad_gain_two, grad_shift_two = norm_two_back(grad_norm_two)
     grad_second = grad_rows + second_part
     grad_scale_one = jnp.sum(grad_second * projected, axis=0)
     grad_projected = (scale_one * grad_second).astype(jnp.bfloat16)
     grad_bias_out = jnp.sum(grad_projected.astype(jnp.float32), axis=0)
-    grad_out = inner_rows(attended_rows, grad_projected)
     grad_attended = inner_cols(grad_projected, whole_out).astype(jnp.bfloat16)
     grad_stream = lax.all_to_all(
         grad_attended.reshape(rows, group, lanes).transpose(1, 0, 2),
-        "seq",
+        seq,
         split_axis=0,
         concat_axis=0,
         tiled=True,
     ).reshape(length, lanes)
-
-    grad_packed = jnp.concatenate(
-        [
-            grad_out.astype(jnp.bfloat16).reshape(count, 1, share, width),
-            grad_up.astype(jnp.bfloat16).reshape(count, share, fold, width).transpose(0, 2, 1, 3),
-            grad_down.astype(jnp.bfloat16).reshape(count, fold, share, width),
-        ],
-        axis=1,
-    )
-    summed = lax.psum_scatter(grad_packed, both, scatter_dimension=0, tiled=True)[0]
-    summed = summed.astype(jnp.float32)
-    summed_out = summed[0]
-    summed_up = summed[1 : 1 + fold].transpose(1, 0, 2).reshape(share, FF)
-    summed_down = summed[1 + fold :].reshape(fold * share, width)
+    grad_out = inner_rows(attended_rows, grad_projected).astype(jnp.bfloat16)
+    grad_out = grad_out.reshape(chips, 2 * share, width)
+    if direct:
+        grad_packed = lax.dynamic_update_slice_in_dim(grad_packed, grad_out, down_end, 1)
+    else:
+        grad_packed = jnp.concatenate(
+            [
+                grad_packed[0, n * width : (n + 1) * width].reshape(chips, 2 * share, width)
+                for n in range(folds)
+            ]
+            + [grad_packed[0, folds * width :].reshape(chips, -1, width), grad_out],
+            axis=1,
+        )
+    summed = lax.psum_scatter(grad_packed, chip_axes, scatter_dimension=0, tiled=True)[0]
 
     grad_mixed_stream = attend_back(starts, query, keys, values, wide, logs, grad_stream)
     grad_mixed = lax.all_to_all(
-        grad_mixed_stream.reshape(group, rows, 3 * lanes),
-        "seq",
+        grad_mixed_stream.reshape(group, rows, 3 * lanes), seq, split_axis=0, concat_axis=0, tiled=True
+    )
+    grad_in = inner_rows(normed_one, grad_mixed_stream).astype(jnp.bfloat16)
+    parts = lax.all_to_all(
+        grad_in.reshape(streams, group * share, 3 * lanes),
+        "fsdp",
         split_axis=0,
         concat_axis=0,
         tiled=True,
     )
-    grad_mixed = grad_mixed.reshape(group, rows, 3, lanes).transpose(1, 2, 0, 3)
-    grad_mixed = grad_mixed.reshape(rows, 3 * width)
-    grad_in = inner_rows(normed_one, grad_mixed_stream).astype(jnp.bfloat16)
-    parts = lax.all_to_all(
-        grad_in.reshape(count, share, 3 * lanes), both, split_axis=0, concat_axis=0, tiled=True
-    )
-    parts = parts.reshape(streams, group, share, 3, lanes).astype(jnp.float32)
-    summed_in = jnp.sum(parts, axis=0).transpose(1, 2, 0, 3).reshape(share, 3 * width)
-
-    grad_mixed_wide = grad_mixed.astype(jnp.float32)
-    grad_bias_query = jnp.sum(grad_mixed_wide[:, :width], axis=0)
-    grad_bias_value = jnp.sum(grad_mixed_wide[:, 2 * width :], axis=0)
-    grad_norm_one = inner_cols(grad_mixed, whole_in)
-    norm_one_back = jax.vjp(layer_norm, inputs, gain_one, shift_one)[1]
-    first_part, grad_gain_one, grad_shift_one = norm_one_back(grad_norm_one)
-    input_grad = grad_second + first_part
+    parts = jnp.sum(parts.astype(jnp.float32), axis=0).reshape(group, share, 3 * lanes)
+    parts = lax.all_to_all(parts, seq, split_axis=0, concat_axis=0, tiled=True)
+    summed_in = parts.reshape(group, share, 3, lanes).transpose(1, 2, 0, 3).reshape(share, 3 * width)
+
+    input_grad, grad_gain_one, grad_shift_one, mixed_sums = finish(
+        grad_mixed, gathered_in, tokens, grad_second, gain_one
+    )
+    up_sums = grad_bias_up.reshape(chips, unit_block)
+    up_sums = jnp.where(
+        (lax.broadcasted_iota(jnp.int32, (1, 2, 1), 1) == core), up_sums[:, None, :], 0.0
+    )
     grad_small = jnp.concatenate(
         [
             jnp.stack(
                 [
-                    grad_gain_one,
-                    grad_shift_one,
-                    grad_bias_query,
-                    grad_bias_value,
+                    grad_gain_one[0],
+                    grad_shift_one[0],
+                    mixed_sums[0, 0],
+                    mixed_sums[2, 0],
                     grad_bias_out,
                     grad_scale_one,
                     grad_gain_two,
@@ -444,16 +672,27 @@
                     grad_scale_two,
                 ]
             ),
-            grad_bias_up.reshape(-1, width),
+            up_sums.reshape(-1, width),
         ],
         axis=0,
     )
     small_rows = grad_small.shape[0]
     parts = grad_small.reshape(small_rows, count, share).transpose(1, 0, 2)
     parts = lax.all_to_all(
-        parts.reshape(count, small_rows * share), both, split_axis=0, concat_axis=0, tiled=True
+        parts.reshape(count, small_rows * share), everyone, split_axis=0, concat_axis=0, tiled=True
     )
     summed_gains = jnp.sum(parts, axis=0).reshape(small_rows, share)
+
+    up_sum = summed[:up_end].reshape(folds, 2, share, width)
+    out_sum = summed[down_end:].reshape(1, 2, share, width)
+    both_sums = jnp.concatenate([up_sum, out_sum], axis=0)
+    own_sums = jnp.where(first_core, both_sums[:, 0], both_sums[:, 1])
+    other_sums = swap_cores(jnp.where(first_core, both_sums[:, 1], both_sums[:, 0]))
+    summed_down = summed[up_end:down_end].astype(jnp.float32)
+    summed_out = own_sums[folds].astype(jnp.float32) + other_sums[folds].astype(jnp.float32)
+    own_up = own_sums[:folds].transpose(1, 0, 2).reshape(share, chips, 1, unit_block)
+    other_up = other_sums[:folds].transpose(1, 0, 2).reshape(share, chips, 1, unit_block)
+    summed_up = in_order(own_up, other_up, 2).reshape(share, FF).astype(jnp.float32)
     rate_out = max(1, 4 * D // IMG_LEN) ** (-0.5)
     new_in, new_moment_in, new_square_in = adamw(
         project_in, moment_in, square_in, summed_in, D ** (-0.5), 0.04
@@ -493,49 +732,53 @@
 
 
 def solution(mesh):
+    streams, group = mesh.shape["fsdp"], mesh.shape["seq"]
+    fine = jax.sharding.Mesh(
+        mesh.devices.reshape(streams, group // 2, 2), ("fsdp", "line", "core")
+    )
     return jax.shard_map(
         on_device,
-        mesh=mesh,
+        mesh=fine,
         in_specs=(
-            P(("fsdp", "seq"), None),
-            P(("fsdp", "seq"), None),
-            P(("fsdp", "seq")),
-            P(("fsdp", "seq")),
-            P(("fsdp", "seq"), None),
-            P(("fsdp", "seq"), None),
-            P(("fsdp", "seq"), None),
-            P(("fsdp", "seq"), None),
-            P(None, ("fsdp", "seq")),
-            P(("fsdp", "seq"), None),
-            P(("fsdp", "seq"), None),
-            P(("fsdp", "seq"), None),
-            P(("fsdp", "seq"), None),
-            P(None, ("fsdp", "seq")),
-            P(("fsdp", "seq"), None),
-            P(("fsdp", "seq"), None),
-            P(("fsdp", "seq"), None),
-            P(("fsdp", "seq"), None),
-            P(None, ("fsdp", "seq")),
+            P(("fsdp", "line", "core"), None),
+            P(("fsdp", "line", "core"), None),
+            P(("fsdp", "line", "core")),
+            P(("fsdp", "line", "core")),
+            P(("fsdp", "line", "core"), None),
+            P(("fsdp", "line", "core"), None),
+            P(("fsdp", "line", "core"), None),
+            P(("fsdp", "line", "core"), None),
+            P(None, ("fsdp", "line", "core")),
+            P(("fsdp", "line", "core"), None),
+            P(("fsdp", "line", "core"), None),
+            P(("fsdp", "line", "core"), None),
+            P(("fsdp", "line", "core"), None),
+            P(None, ("fsdp", "line", "core")),
+            P(("fsdp", "line", "core"), None),
+            P(("fsdp", "line", "core"), None),
+            P(("fsdp", "line", "core"), None),
+            P(("fsdp", "line", "core"), None),
+            P(None, ("fsdp", "line", "core")),
         ),
         out_specs=(
-            P(("fsdp", "seq"), None),
-            P(("fsdp", "seq"), None),
-            P(("fsdp", "seq"), None),
-            P(("fsdp", "seq"), None),
-            P(("fsdp", "seq"), None),
-            P(("fsdp", "seq"), None),
-            P(None, ("fsdp", "seq")),
-            P(("fsdp", "seq"), None),
-            P(("fsdp", "seq"), None),
-            P(("fsdp", "seq"), None),
-            P(("fsdp", "seq"), None),
-            P(None, ("fsdp", "seq")),
-            P(("fsdp", "seq"), None),
-            P(("fsdp", "seq"), None),
-            P(("fsdp", "seq"), None),
-            P(("fsdp", "seq"), None),
-            P(None, ("fsdp", "seq")),
-            P(("fsdp", "seq")),
+            P(("fsdp", "line", "core"), None),
+            P(("fsdp", "line", "core"), None),
+            P(("fsdp", "line", "core"), None),
+            P(("fsdp", "line", "core"), None),
+            P(("fsdp", "line", "core"), None),
+            P(("fsdp", "line", "core"), None),
+            P(None, ("fsdp", "line", "core")),
+            P(("fsdp", "line", "core"), None),
+            P(("fsdp", "line", "core"), None),
+            P(("fsdp", "line", "core"), None),
+            P(("fsdp", "line", "core"), None),
+            P(None, ("fsdp", "line", "core")),
+            P(("fsdp", "line", "core"), None),
+            P(("fsdp", "line", "core"), None),
+            P(("fsdp", "line", "core"), None),
+            P(("fsdp", "line", "core"), None),
+            P(None, ("fsdp", "line", "core")),
+            P(("fsdp", "line", "core")),
         ),
         check_vma=False,
     )

time: 721 us -> 755 us (1.047)
  blocking collectives: 29.7 us -> 117 us
  matrix products: 96.5 us -> 16.2 us
  local copies, waits for them, and re-layouts: 118 us -> 55.9 us
  Pallas kernels: 74.3 us -> 125 us
  waiting for transfers between devices: 318 us -> 364 us
    all_to_all x0 -> x3, blocking collectives: none -> 59.6 us  [the longest x1 25.7 us: on_device(): parts = lax.all_to_all(parts, seq, split_axis=0, concat_axis=0, tiled=True)]
    pallas_call x1 -> x3, Pallas kernels: 12.8 us -> 64 us  [the longest x1 39.3 us: mlp(): pl.pallas_call(mlp_kernel, grid=(hidden // units,), in_specs=[fixed, fixe...]
    dot_general x3 -> x1, matrix products: 40.5 us -> 4.85 us  [plain_product(): return jnp.dot(left, right, preferred_element_type=jnp.float32)]
    dot_general x4 -> x1, matrix products: 29.9 us -> 1.29 us  [inner_cols(): lax.dot_general(left, right, (((1,), (1,)), ((), ())), preferred_element_...]
    all_to_all x5 -> x4, waiting for transfers between devices: 152 us -> 180 us  [the longest x1 129 us: on_device(): lax.all_to_all(grad_mixed_stream.reshape(group, rows, 3 * lanes), seq, sp...]
    all_to_all x1, blocking collectives: 29.7 us -> 57.3 us  [on_device(): lax.all_to_all(grad_attended.reshape(rows, group, lanes).transpose(1, 0,...]
    transpose x5 -> x3, local copies, waits for them, and re-layouts: 28.1 us -> 2.83 us  [the longest x1 2.03 us: on_device(): parts.reshape(group, share, 3, lanes).transpose(1, 2, 0, 3)]
    reshape x6 -> x5, local copies, waits for them, and re-layouts: 28.2 us -> 3.7 us  [the longest x1 1.94 us: on_device(): parts.reshape(group, share, 3, lanes).transpose(1, 2, 0, 3)]
  transfers between devices with their start and end apart: 8 -> 15, of which waited for: 6 -> 8; matrix products, arithmetic and copies ran while one was open for 16% -> 13% of each run, Pallas kernels for 10% -> 17%
where the time goes in v2:
time: 755 us; the launch traced here: 746 us
  waiting for transfers between devices  364 us (48%)
  Pallas kernels  125 us (17%)
  blocking collectives  117 us (15%)
  local copies, waits for them, and re-layouts  55.9 us (7%)
  other arithmetic  36.2 us (5%)
  starting transfers between devices  16.9 us (2%)
  matrix products  16.2 us (2%)
  between operations  15 us (2%)
    all_to_all x1, waiting for transfers between devices, on_device(): lax.all_to_all(grad_mixed_stream.reshape(group, rows, 3 * lanes), seq, sp...  129 us
    all_gather x1, waiting for transfers between devices, on_device(): gathered = lax.all_gather(packed, chip_axes, axis=0, tiled=False)  102 us
    all_gather x1, waiting for transfers between devices, on_device(): line_tokens = lax.all_gather(tokens, 'line', axis=0, tiled=True)  79.3 us
    all_to_all x1, blocking collectives, on_device(): lax.all_to_all(grad_attended.reshape(rows, group, lanes).transpose(1, 0,...  57.3 us
    pallas_call x1, Pallas kernels, mlp(): pl.pallas_call(mlp_kernel, grid=(hidden // units,), in_specs=[fixed, fixe...  39.3 us
    all_to_all x1, waiting for transfers between devices, on_device(): lax.all_to_all(attended.reshape(group, rows, lanes), seq, split_axis=0, c...  35.8 us
    pallas_call x1, Pallas kernels, attend_back(): pl.pallas_call(attend_back_kernel, grid_spec=pltpu.PrefetchScalarGridSpec...  34.6 us
    pallas_call x1, Pallas kernels, attend(): pl.pallas_call(attend_kernel, grid_spec=pltpu.PrefetchScalarGridSpec(num_...  26.1 us
  transfers between devices with their start and end apart: 15, of which 8 were waited for; matrix products, arithmetic and copies ran while one was open for 13% of the time, Pallas kernels for 17%

profile of v2, /device:TPU:0, one launch (start us, length us, event | category | flops | bytes accessed | tf_op | source)
XLA Modules:
  0.0 746.3 jit_solution(13604388594530254576)
XLA Ops:
  8.0 1.0 convert_element_type.109
  8.9 1.1 convert_element_type.108
  11.3 1.0 collective-permute-done
  13.8 79.3 %all-gather.6.cloned.1.call-done.own_ref = bf16[2048,1024]{1,0:T(8,128)(2,1)} async-done(((bf16[512,1024]{1,0:T(8,128)(2,1)}), bf16[2048,1024]{1,0:T(8,128)(2,1)}) %all-gather.6.cloned.1.call-update) | async-done | bytes 4194320 | tf_op jit(solution)/shard_map/all_gather | solution.py:472
  94.0 11.8 %all_to_all.45 = bf16[8,34,384]{2,1,0:T(8,128)(2,1)S(1)} all-to-all(bf16[8,34,384]{2,1,0:T(8,128)(2,1)S(1)} %pad_maximum_fusion.3), channel_id=1, replica_groups=mesh['fsdp'=4,'line'=4,'core'=2] {'line','core'}, dimensions={0} | all-to-all | bytes 417792 | tf_op jit(solution)/shard_map/all_to_all | solution.py:492
  105.8 1.0 broadcast_in_dim.63
  106.8 3.7 all-to-all-start.1
  111.5 10.0 %all-to-all-done.1 = bf16[4,8,34,384]{3,1,2,0:T(8,128)(2,1)S(1)} async-done(((bf16[4,8,34,384]{3,1,2,0:T(8,128)(2,1)}), bf16[4,8,34,384]{3,1,2,0:T(8,128)(2,1)S(1)}, u32[]{:S(2)}, u32[]{:S(2)}) %all-to-all-start.1) | async-done | bytes 835616 | tf_op jit(solution)/shard_map/all_to_all | solution.py:494
  121.9 1.0 slice_reduce_fusion.2
  124.2 1.1 copy.137
  126.8 102.5 %all-gather.8.cloned.1.call-done = bf16[5120,1024]{1,0:T(8,128)(2,1)} async-done(((bf16[320,1024]{1,0:T(8,128)(2,1)}), bf16[5120,1024]{1,0:T(8,128)(2,1)}) %all-gather.8.cloned.1.call-update) | async-done | bytes 10485776 | tf_op jit(solution)/shard_map/all_gather | solution.py:532
  229.4 14.3 %norm_mix.1 = (bf16[4096,1024]{1,0:T(8,128)(2,1)}, bf16[4096,128]{1,0:T(8,128)(2,1)}, bf16[4096,128]{1,0:T(8,128)(2,1)}, bf16[4096,128]{1,0:T(8,128)(2,1)}) custom-call(s32[1]{0:T(128)} %bitcast.3.core_ref, bf16[2048,1024]{1,0:T(8,128)(2,1)} %all-gather.6.cloned.1.call-done.own_ref, bf16[2048,1024]{1,0:T(8,128)(2,1)} %collective-permute-done.1.other_ref, ...), custom_call_target="tpu_custom_call" | custom-call | flops 3221225472 | bytes 16777216 | tf_op jit(solution)/shard_map/norm_mix/pallas_call | solution.py:237
  243.6 26.1 %attend_forward.1 = (f32[4096,128]{1,0:T(8,128)}, bf16[4096,128]{1,0:T(8,128)(2,1)}, f32[4096,128]{1,0:T(8,128)}) custom-call(s32[2]{0:T(128)} %select_reduce_fusion.starts_ref, bf16[4096,128]{1,0:T(8,128)(2,1)} %get-tuple-element.38.q_ref, bf16[4096,128]{1,0:T(8,128)(2,1)} %get-tuple-element.39.k_ref, bf16[4096,128]{1,0:T(8,128)(2,1)} %get-tuple-element.40.v_ref), custom_call_target="tpu_custom_call" | custom-call | flops 4060086272 | bytes 8388608 | tf_op jit(solution)/shard_map/attend_forward/pallas_call | solution.py:113
  269.7 2.4 copy.138
  272.1 3.6 all-to-all-start.2
  277.5 1.9 convert_reduce_fusion
  279.8 3.2 slice.162
  282.9 35.8 %all-to-all-done.2 = bf16[8,512,128]{1,2,0:T(8,128)(2,1)S(1)} async-done(((bf16[8,512,128]{1,2,0:T(8,128)(2,1)}), bf16[8,512,128]{1,2,0:T(8,128)(2,1)S(1)}, u32[]{:S(2)}, u32[]{:S(2)}) %all-to-all-start.2) | async-done | bytes 1048608 | tf_op jit(solution)/shard_map/all_to_all | solution.py:590
  318.7 1.0 copy-done.13
  319.7 4.9 fusion.29
  325.5 1.4 add_convert_fusion.1
  326.9 0.9 slice.205
  328.5 1.5 reshape.317
  330.0 1.3 dynamic-slice_bitcast_fusion.bias_ref
  331.4 3.0 pad_maximum_fusion.1.gm_ref
  334.4 3.1 pad_maximum_fusion.h_ref
  337.5 39.3 %mlp_both_ways.1 = (bf16[16,320,1024]{2,1,0:T(8,128)(2,1)}, f32[1024,1024]{1,0:T(8,128)}, f32[1024,1024]{1,0:T(8,128)}, f32[1,2048]{1,0:T(1,128)}) custom-call(bf16[1024,1024]{1,0:T(8,128)(2,1)} %pad_maximum_fusion.h_ref, bf16[1024,1024]{1,0:T(8,128)(2,1)} %pad_maximum_fusion.1.gm_ref, bf16[16,320,1024]{2,1,0:T(8,128)(2,1)} %bitcast.152, ...), custom_call_target="tpu_custom_call" | custom-call | flops 25769803776 | bytes 33554432 | tf_op jit(solution)/shard_map/mlp_both_ways/pallas_call | solution.py:314
  376.7 3.3 slice.172
  380.6 1.4 slice.169
  382.0 1.4 add.187
  383.4 1.2 collective-permute-done.5
  384.7 3.7 multiply_reduce_fusion.1
  388.4 4.2 multiply_reduce_fusion
  392.6 1.2 multiply_reduce_fusion.2
  393.8 0.9 convert_reduce_fusion.1
  394.7 1.0 copy-done.14
  395.8 1.3 convolution_convert_fusion
  397.0 1.5 constant_dynamic-update-slice_fusion.11
  398.6 1.6 copy-done.7
  400.1 1.3 fusion
  401.6 57.3 %all_to_all.46 = bf16[8,512,128]{2,1,0:T(8,128)(2,1)} all-to-all(bf16[8,512,128]{2,1,0:T(8,128)(2,1)S(1)} %bitcast.122), channel_id=1, replica_groups=mesh['fsdp'=4,'line'=4,'core'=2] {'line','core'}, dimensions={0} | all-to-all | bytes 2097152 | tf_op jit(solution)/shard_map/all_to_all | solution.py:614
  458.9 34.6 %attend_backward.1 = bf16[4096,384]{1,0:T(8,128)(2,1)} custom-call(s32[2]{0:T(128)} %select_reduce_fusion.starts_ref, bf16[4096,128]{1,0:T(8,128)(2,1)} %get-tuple-element.38.q_ref, bf16[4096,128]{1,0:T(8,128)(2,1)} %get-tuple-element.39.k_ref, bf16[4096,128]{1,0:T(8,128)(2,1)} %get-tuple-element.40.v_ref, f32[4096,128]{1,0:T(8,128)} %get-tuple-element.45.wide_ref, ...), custom_call_target="tpu_custom_call" | custom-call | flops 10150215680 | bytes 11534336 | tf_op jit(solution)/shard_map/attend_backward/pallas_call | solution.py:193
  493.5 8.8 %convolution_convert_fusion.2 = bf16[1024,384]{1,0:T(8,128)(2,1)S(1)} fusion(bf16[4096,1024]{1,0:T(8,128)(2,1)} %get-tuple-element.50, bf16[4096,384]{1,0:T(8,128)(2,1)} %attend_backward.1), kind=kOutput, calls=%fused_computation.22 | convolution fusion | flops 3221618688 | bytes 12320768 | tf_op jit(solution)/shard_map/dot_general | solution.py:38
  502.3 22.1 %all_to_all.47 = bf16[4,256,384]{2,1,0:T(8,128)(2,1)S(1)} all-to-all(bf16[4,256,384]{2,1,0:T(8,128)(2,1)S(1)} %bitcast.145), channel_id=1, replica_groups=mesh['fsdp'=4,'line'=4,'core'=2] {'fsdp'}, dimensions={0} | all-to-all | bytes 1572864 | tf_op jit(solution)/shard_map/all_to_all | solution.py:641
  524.6 25.7 %all_to_all.48 = f32[8,32,384]{2,1,0:T(8,128)} all-to-all(f32[8,32,384]{2,1,0:T(8,128)S(1)} %bitcast.130), channel_id=1, replica_groups=mesh['fsdp'=4,'line'=4,'core'=2] {'line','core'}, dimensions={0} | all-to-all | bytes 786432 | tf_op jit(solution)/shard_map/all_to_all | solution.py:649
  550.2 4.0 all-to-all-start.4
  557.0 1.4 concatenate.69
  558.3 1.4 concatenate.70
  559.7 1.4 concatenate.71
  561.1 1.4 concatenate.72
  562.4 1.4 concatenate.74
  563.8 1.9 reshape.323
  565.7 2.0 copy.142
  567.7 129.1 %all-to-all-done.4.grad_ref = bf16[8,512,384]{2,1,0:T(8,128)(2,1)S(1)} async-done(((bf16[8,512,384]{2,1,0:T(8,128)(2,1)}), bf16[8,512,384]{2,1,0:T(8,128)(2,1)S(1)}, u32[]{:S(2)}, u32[]{:S(2)}) %all-to-all-start.4) | async-done | bytes 3145760 | tf_op jit(solution)/shard_map/all_to_all | solution.py:637
  696.9 1.7 copy-done.1
  698.5 10.5 %finish_input.1 = (f32[512,1024]{1,0:T(8,128)}, f32[1,1024]{1,0:T(1,128)}, f32[1,1024]{1,0:T(1,128)}, f32[3,1,1024]{2,1,0:T(1,128)}) custom-call(bf16[8,512,384]{2,1,0:T(8,128)(2,1)} %copy-done.1, bf16[32,96,1024]{2,1,0:T(8,128)(2,1)} %bitcast.121, bf16[512,1024]{1,0:T(8,128)(2,1)} %x_ref.1, f32[512,1024]{1,0:T(8,128)} %copy-done, f32[1,1024]{1,0:T(1,128)} %slice.154.gain_ref), custom_call_target="tpu_custom_call" | custom-call | flops 3221225472 | bytes 16777216 | tf_op jit(solution)/shard_map/finish_input/pallas_call | solution.py:395
  709.6 1.3 reduce.55
  711.0 1.3 reduce.56
  718.8 3.6 all-to-all-start.7
  722.4 2.6 multiply_subtract_fusion.2
  725.0 4.8 all-to-all-done.7
  732.0 1.0 slice.207
  733.2 2.3 multiply_subtract_fusion
  737.1 1.4 multiply_subtract_fusion.1
  (197 shorter events, 27.4 us)
Async XLA Ops:
  7.2 85.9 %all-gather.6.cloned.1.call-start = ((), (), s32[]{:S(2)}) async-start(), calls=%async_computation.9 | async-start | bytes 5242880 | tf_op jit(solution)/shard_map/all_gather | solution.py:472
  7.9 3.3 copy-start.8
  7.9 221.4 %all-gather.8.cloned.1.call-start = ((), (), s32[]{:S(2)}) async-start(), calls=%async_computation.11 | async-start | bytes 11141120 | tf_op jit(solution)/shard_map/all_gather | solution.py:532
  10.6 2.3 copy-start.11
  10.7 1.6 collective-permute-start
  12.3 80.9 %copy-start.23 = (f32[14,32]{1,0:T(8,128)S(1)}, f32[14,32]{1,0:T(8,128)}, u32[]{:S(2)}) copy-start(f32[14,32]{1,0:T(8,128)} %param.27) | copy-start | bytes 5380
  12.3 81.0 %copy-start.37 = (s32[512]{0:T(512)S(1)}, s32[512]{0:T(512)}, u32[]{:S(2)}) copy-start(s32[512]{0:T(512)} %param.22) | copy-start | bytes 6148
  12.3 81.0 %copy-start.38 = (s32[512]{0:T(512)S(1)}, s32[512]{0:T(512)}, u32[]{:S(2)}) copy-start(s32[512]{0:T(512)} %param.21) | copy-start | bytes 6148
  12.4 81.2 %copy-start.5 = (f32[32,3072]{1,0:T(8,128)S(1)}, f32[32,3072]{1,0:T(8,128)}, u32[]{:S(2)}) copy-start(f32[32,3072]{1,0:T(8,128)} %param.23) | copy-start | bytes 1179652
  93.1 136.3 %collective-permute-start.1 = (bf16[2048,1024]{1,0:T(8,128)(2,1)}, bf16[2048,1024]{1,0:T(8,128)(2,1)}, u32[]{:S(2)}, u32[]{:S(2)}) collective-permute-start(bf16[2048,1024]{1,0:T(8,128)(2,1)} %all-gather.6.cloned.1.call-done.own_ref), channel_id=1, source_target_pairs={{0,1},{1,0},{2,3},{3,2},{4,5},{5,4},{6,7},{7,6},{8,9},{9,8},{10,11... | collective-permute-start | bytes 12582920 | tf_op jit(solution)/shard_map/ppermute | solution.py:427
  106.8 14.8 %all-to-all-start.1 = ((bf16[4,8,34,384]{3,1,2,0:T(8,128)(2,1)}), bf16[4,8,34,384]{3,1,2,0:T(8,128)(2,1)S(1)}, u32[]{:S(2)}, u32[]{:S(2)}) async-start(bf16[4,8,34,384]{3,1,2,0:T(8,128)(2,1)} %broadcast_in_dim.63), calls=%async_computation.1 | async-start | bytes 1671168 | tf_op jit(solution)/shard_map/all_to_all | solution.py:494
  110.5 586.4 %all-gather.10.cloned.1.call-start = ((), (), s32[]{:S(2)}) async-start(), calls=%async_computation.12 | async-start | bytes 6488064 | tf_op jit(solution)/shard_map/all_gather | solution.py:535
  121.9 121.8 %copy-start.15 = (f32[32,14,32]{2,1,0:T(8,128)}, f32[32,14,32]{2,1,0:T(8,128)S(1)}, u32[]{:S(2)}) copy-start(f32[32,14,32]{2,1,0:T(8,128)S(1)} %reshape.332) | copy-start | bytes 172036
  269.7 7.7 %copy-start.2 = (bf16[512,1024]{1,0:T(8,128)(2,1)S(1)}, bf16[512,1024]{1,0:T(8,128)(2,1)}, u32[]{:S(2)}) copy-start(bf16[512,1024]{1,0:T(8,128)(2,1)} %param.20) | copy-start | bytes 3145732
  272.1 46.6 %all-to-all-start.2 = ((bf16[8,512,128]{1,2,0:T(8,128)(2,1)}), bf16[8,512,128]{1,2,0:T(8,128)(2,1)S(1)}, u32[]{:S(2)}, u32[]{:S(2)}) async-start(bf16[8,512,128]{1,2,0:T(8,128)(2,1)} %copy.138), calls=%async_computation.2 | async-start | bytes 2097152 | tf_op jit(solution)/shard_map/all_to_all | solution.py:590
  275.7 455.4 %reduce-scatter.2.cloned.1.call-start = ((), (), s32[]{:S(2)}) async-start(), calls=%async_computation.10 | async-start | bytes 11141120 | tf_op jit(solution)/shard_map/reduce_scatter | solution.py:634
  275.9 7.0 copy-start.25
  276.7 43.1 %copy-start.30 = (f32[1024]{0:T(1024)}, f32[1024]{0:T(1024)S(1)}, u32[]{:S(2)}) copy-start(f32[1024]{0:T(1024)S(1)} %mul.318) | copy-start | bytes 12292
  279.4 51.9 %collective-permute-start.3 = (bf16[512,1024]{1,0:T(8,128)(2,1)}, bf16[512,1024]{1,0:T(8,128)(2,1)}, u32[]{:S(2)}, u32[]{:S(2)}) collective-permute-start(bf16[512,1024]{1,0:T(8,128)(2,1)} %get-tuple-element.75), channel_id=1, source_target_pairs={{0,1},{1,0},{2,3},{3,2},{4,5},{5,4},{6,7},{7,6},{8,9},{9,8},{10,11... | collective-permute-start | bytes 3145736 | tf_op jit(solution)/shard_map/ppermute | solution.py:427
  318.7 1.0 copy-start.13
  324.6 0.9 copy-start.34
  324.9 0.6 copy-start.27
  326.9 7.5 %collective-permute-start.2 = (bf16[512,1024]{1,0:T(8,128)(2,1)}, bf16[512,1024]{1,0:T(8,128)(2,1)}, u32[]{:S(2)}, u32[]{:S(2)}) collective-permute-start(bf16[512,1024]{1,0:T(8,128)(2,1)} %add_convert_fusion.1), channel_id=1, source_target_pairs={{0,1},{1,0},{2,3},{3,2},{4,5},{5,4},{6,7},{7,6},{8,9},{9,8},{10,11... | collective-permute-start | bytes 3145736 | tf_op jit(solution)/shard_map/ppermute | solution.py:427
  376.7 3.8 copy-start.3
  380.1 4.6 collective-permute-start.5
  382.0 6.4 collective-permute-start.4
  383.4 4.9 copy-start.28
  383.4 5.0 copy-start.4
  383.4 5.0 copy-start.26
  383.4 5.0 copy-start.33
  388.4 4.2 copy-start.10
  388.4 4.2 copy-start.32
  392.6 1.2 copy-start.31
  393.8 3.2 copy-start
  393.8 2.0 copy-start.14
  398.5 1.6 copy-start.7
  550.2 4.6 copy-start.29
  550.2 146.6 %all-to-all-start.4 = ((bf16[8,512,384]{2,1,0:T(8,128)(2,1)}), bf16[8,512,384]{2,1,0:T(8,128)(2,1)S(1)}, u32[]{:S(2)}, u32[]{:S(2)}) async-start(bf16[8,512,384]{2,1,0:T(8,128)(2,1)} %bitcast.125), calls=%async_computation.4 | async-start | bytes 6291456 | tf_op jit(solution)/shard_map/all_to_all | solution.py:637
  696.9 1.7 copy-start.1
  698.5 17.7 %copy-start.22 = (f32[1,32,32]{2,1,0:T(8,128)S(1)}, f32[1,32,32]{2,1,0:T(8,128)}, u32[]{:S(2)}) copy-start(f32[1,32,32]{2,1,0:T(8,128)} %concatenate.73) | copy-start | bytes 12292
  713.3 17.1 %copy-start.24 = (f32[14,32]{1,0:T(8,128)S(1)}, f32[14,32]{1,0:T(8,128)}, u32[]{:S(2)}) copy-start(f32[14,32]{1,0:T(8,128)} %param.27) | copy-start | bytes 5380
  713.3 17.1 %copy-start.35 = (f32[14,32]{1,0:T(8,128)S(1)}, f32[14,32]{1,0:T(8,128)}, u32[]{:S(2)}) copy-start(f32[14,32]{1,0:T(8,128)} %param.32) | copy-start | bytes 5380
  713.3 17.1 %copy-start.36 = (f32[14,32]{1,0:T(8,128)S(1)}, f32[14,32]{1,0:T(8,128)}, u32[]{:S(2)}) copy-start(f32[14,32]{1,0:T(8,128)} %param.37) | copy-start | bytes 5380
  718.8 11.0 %all-to-all-start.7 = ((f32[32,1,448]{2,1,0:T(1,128)}), f32[32,1,448]{2,1,0:T(1,128)S(1)}, u32[]{:S(2)}, u32[]{:S(2)}) async-start(f32[32,1,448]{2,1,0:T(1,128)} %all_to_all.36), calls=%async_computation.8 | async-start | bytes 131072 | tf_op jit(solution)/shard_map/all_to_all | solution.py:681
  722.4 10.8 %copy-start.9 = (f32[128,1024]{1,0:T(8,128)S(1)}, f32[128,1024]{1,0:T(8,128)}, u32[]{:S(2)}) copy-start(f32[128,1024]{1,0:T(8,128)} %param.26) | copy-start | bytes 1572868
  722.4 10.8 %copy-start.18 = (f32[128,1024]{1,0:T(8,128)S(1)}, f32[128,1024]{1,0:T(8,128)}, u32[]{:S(2)}) copy-start(f32[128,1024]{1,0:T(8,128)} %param.31) | copy-start | bytes 1572868
  722.4 10.8 %copy-start.19 = (f32[128,1024]{1,0:T(8,128)S(1)}, f32[128,1024]{1,0:T(8,128)}, u32[]{:S(2)}) copy-start(f32[128,1024]{1,0:T(8,128)} %param.36) | copy-start | bytes 1572868
  733.1 2.5 collective-permute-start.6
  735.6 1.4 copy-start.6
  735.6 1.4 copy-start.16
  735.6 1.4 copy-start.17
  737.1 1.4 copy-start.12
  737.1 1.4 copy-start.20
  737.1 1.4 copy-start.21
Sparse Core Ops, SparseCore 0:
  9.6 83.4 all-gather.5
  96.4 132.8 all-gather.7
  232.9 84.8 all-gather.9
  398.7 313.8 reduce-scatter.1

commit v3 on v2

--- a/solution.py
+++ b/solution.py
@@ -1,3 +1,5 @@
+import math
+
 import jax
 import jax.numpy as jnp
 from jax import lax
@@ -259,12 +261,21 @@
 
 
 def mlp_kernel(
-    h_ref, gm_ref, up_ref, down_ref, bias_ref, grad_ref, m_ref, gh_ref, bias_grad_ref, turned_ref
+    h_ref,
+    gm_ref,
+    up_ref,
+    down_ref,
+    bias_ref,
+    up_grad_ref,
+    down_grad_ref,
+    m_ref,
+    gh_ref,
+    bias_grad_ref,
+    turned_ref,
 ):
     tile = pl.program_id(0)
     width = h_ref.shape[1]
     chips, up_rows, units = up_ref.shape
-    part, down_rows = down_ref.shape[0], down_ref.shape[1]
     folds = width // units
 
     @pl.when(tile == 0)
@@ -287,19 +298,15 @@
     up_grad = plain_product(turned_ref[...], grad_up).astype(jnp.bfloat16)
     row = pl.multiple_of(tile // folds * up_rows, up_rows)
     column = pl.multiple_of(lax.rem(tile, folds) * units, units)
-    grad_ref[:, pl.ds(row, up_rows), pl.ds(column, units)] = up_grad.reshape(chips, up_rows, units)
-    down_grad = inner_rows(active, gm).astype(jnp.bfloat16).reshape(part, down_rows, width)
-    base = 2 * up_rows
-    if chips > 1:
-        grad_ref[pl.ds(tile * part, part), base : base + down_rows, :] = down_grad
-    else:
-        start = pl.multiple_of(base + tile * down_rows, down_rows)
-        grad_ref[:, pl.ds(start, down_rows), :] = down_grad
-
-
-def mlp(normed, gm, packed, up_rows, bias):
+    up_grad = up_grad.reshape(chips, up_rows, units)
+    up_grad_ref[:, pl.ds(row, up_rows), pl.ds(column, units)] = up_grad
+    down_grad = inner_rows(active, gm).astype(jnp.bfloat16)
+    down_grad_ref[...] = down_grad.reshape(down_grad_ref.shape)
+
+
+def mlp(normed, gm, up, down, up_rows, bias):
     rows, width = normed.shape
-    chips = packed.shape[0]
+    chips = up.shape[0]
     hidden = bias.shape[0]
     units = 256
     folds = width // units
@@ -307,9 +314,9 @@
     fixed = pl.BlockSpec((rows, width), lambda j: (0, 0), **once)
     if chips > 1:
         part = units * chips // hidden
-        down = pl.BlockSpec((part, units // part, width), lambda j: (j, 2 * up_rows * part // units, 0))
+        down_spec = pl.BlockSpec((part, units // part, width), lambda j: (j, 0, 0))
     else:
-        down = pl.BlockSpec((1, units, width), lambda j: (0, 2 * up_rows // units + j, 0))
+        down_spec = pl.BlockSpec((1, units, width), lambda j: (0, j, 0))
     total = jax.ShapeDtypeStruct((rows, width), jnp.float32)
     return pl.pallas_call(
         mlp_kernel,
@@ -318,17 +325,19 @@
             fixed,
             fixed,
             pl.BlockSpec((chips, up_rows, units), lambda j: (0, j // folds, lax.rem(j, folds))),
-            down,
+            down_spec,
             pl.BlockSpec((1, units), lambda j: (0, j)),
         ],
         out_specs=[
-            pl.BlockSpec(packed.shape, lambda j: (0, 0, 0), **once),
+            pl.BlockSpec(up.shape, lambda j: (0, 0, 0), **once),
+            down_spec,
             fixed,
             fixed,
             pl.BlockSpec((1, units), lambda j: (0, j)),
         ],
         out_shape=(
-            jax.ShapeDtypeStruct(packed.shape, jnp.bfloat16),
+            jax.ShapeDtypeStruct(up.shape, jnp.bfloat16),
+            jax.ShapeDtypeStruct(down.shape, jnp.bfloat16),
             total,
             total,
             jax.ShapeDtypeStruct((1, hidden), jnp.float32),
@@ -337,11 +346,11 @@
         compiler_params=pltpu.CompilerParams(vmem_limit_bytes=VMEM_BYTES),
         cost_estimate=pl.CostEstimate(
             flops=rows * width * hidden * 12,
-            bytes_accessed=packed.size * 4 + rows * width * 12,
+            bytes_accessed=(up.size + down.size) * 4 + rows * width * 12,
             transcendentals=rows * hidden * 2,
         ),
         name="mlp_both_ways",
-    )(normed, gm, packed, packed, bias[None])
+    )(normed, gm, up, down, bias[None])
 
 
 def finish_kernel(
@@ -427,6 +436,65 @@
     return lax.ppermute(value, "core", [(0, 1), (1, 0)])
 
 
+def line_pieces(value, axis):
+    size = lax.axis_size(axis)
+    if size == 2:
+        other = lax.ppermute(value, axis, [(0, 1), (1, 0)])
+        return [(None, other)]
+    pieces = []
+    for sign in (-1, 1):
+        moving = value
+        for step in range(1, size):
+            pairs = [(i, i - sign) for i in range(size) if 0 <= i - sign < size]
+            pairs = [(i, j) for i, j in pairs if 0 <= i + sign * (step - 1) < size]
+            moving = lax.ppermute(moving, axis, pairs)
+            pieces.append((sign * step, moving))
+    return pieces
+
+
+def line_order(value, pieces, axis):
+    place = lax.axis_index(axis)
+    size = lax.axis_size(axis)
+    if size == 2:
+        other = pieces[0][1]
+        return jnp.where(place == 0, jnp.stack([value, other]), jnp.stack([other, value]))
+    whole = jnp.zeros((size, *value.shape), value.dtype)
+    for distance, piece in sorted(pieces, key=lambda item: -abs(item[0])) + [(0, value)]:
+        slot = jnp.clip(place + distance, 0, size - 1)
+        whole = lax.dynamic_update_index_in_dim(whole, piece, slot, 0)
+    return whole
+
+
+def gather_line(value, axis):
+    return line_order(value, line_pieces(value, axis), axis)
+
+
+def rounded_sum(*terms):
+    return sum(term.astype(jnp.float32) for term in terms).astype(jnp.bfloat16)
+
+
+def scatter_line(value, axis, dim):
+    place = lax.axis_index(axis)
+    size = lax.axis_size(axis)
+    pick = lambda slot: lax.dynamic_index_in_dim(
+        value, jnp.clip(slot, 0, size - 1), dim, keepdims=False
+    )
+    if size == 2:
+        return rounded_sum(pick(place), lax.ppermute(pick(1 - place), axis, [(0, 1), (1, 0)]))
+    sums = []
+    for sign in (-1, 1):
+        moving = None
+        for step in range(1, size):
+            start = 0 if sign < 0 else size - 1
+            pairs = [(i, i - sign) for i in range(size) if 0 <= i - sign < size]
+            pairs = [(i, j) for i, j in pairs if abs(i - start) <= step - 1]
+            own = pick(place - sign * (size - step))
+            payload = own if moving is None else rounded_sum(own, moving)
+            moving = lax.ppermute(payload, axis, pairs)
+        sums.append(moving)
+    return rounded_sum(pick(place), *sums)
+
+
 def on_device(
     tokens,
     cotangent,
@@ -450,10 +518,10 @@
 ):
     rows = tokens.shape[0]
     width = tokens.shape[1]
-    everyone = ("fsdp", "line", "core")
-    chip_axes = ("fsdp", "line")
+    everyone = ("outer", "inner", "line", "core")
+    planes = ("outer", "inner")
     seq = ("line", "core")
-    streams, line = lax.axis_size("fsdp"), lax.axis_size("line")
+    streams, line = lax.axis_size(planes), lax.axis_size("line")
     group = 2 * line
     count = streams * group
     chips = streams * line
@@ -469,7 +537,10 @@
             [jnp.where(first_core, own, other), jnp.where(first_core, other, own)], axis=axis
         )
 
-    line_tokens = lax.all_gather(tokens, "line", axis=0, tiled=True)
+    pieces = line_pieces(tokens, "line")
+    own_tokens = line_order(tokens, pieces, "line").reshape(-1, width)
+    swapped = [(distance, swap_cores(piece)) for distance, piece in pieces]
+    other_tokens = line_order(swap_cores(tokens), swapped, "line").reshape(-1, width)
 
     owned = project_in.astype(jnp.bfloat16).reshape(share, 3, group, lanes)
     owned = owned.transpose(2, 0, 1, 3).reshape(group, share, 3 * lanes)
@@ -490,8 +561,7 @@
     small = jnp.pad(small, (0, extra * 3 * lanes - small.shape[0])).reshape(1, extra, 3 * lanes)
     blocks = jnp.concatenate([owned, jnp.broadcast_to(small, (group, extra, 3 * lanes))], axis=1)
     blocks = lax.all_to_all(blocks, seq, split_axis=0, concat_axis=0, tiled=True)
-    blocks = jnp.broadcast_to(blocks[None], (streams, *blocks.shape))
-    blocks = lax.all_to_all(blocks, "fsdp", split_axis=0, concat_axis=0, tiled=True)
+    blocks = gather_line(gather_line(blocks, "inner"), "outer")
     blocks = blocks.reshape(count, share + extra, 3 * lanes)
     mine_in = blocks[:, :share].reshape(width, 3 * lanes)
     small = blocks[:, share:].reshape(count, -1)
@@ -499,7 +569,7 @@
     vectors = vectors.reshape(-1, width).astype(jnp.float32)
     first = small[:, vector_size : vector_size + 2 * images].astype(jnp.int32)
     first = first[:, :images] * 32 + first[:, images:]
-    first = lax.dynamic_slice_in_dim(first, lax.axis_index("fsdp") * group, group, 0)
+    first = lax.dynamic_slice_in_dim(first, lax.axis_index(planes) * group, group, 0)
     offsets = lax.broadcasted_iota(jnp.int32, (group, images), 0) * rows
     starts = jnp.min(jnp.where(first < rows, first + offsets, length), axis=0)
 
@@ -520,6 +590,8 @@
         received[: share * folds].reshape(share, half),
         0,
     )
+    up_end = 2 * share * folds
+    down_end = up_end + half // chips
     packed = jnp.concatenate(
         [
             up_rows.reshape(2 * share, folds, width).transpose(1, 0, 2).reshape(-1, width),
@@ -528,24 +600,21 @@
         ],
         axis=0,
     )
-    packed, line_tokens = lax.optimization_barrier((packed, line_tokens))
-    gathered = lax.all_gather(packed, chip_axes, axis=0, tiled=False)
-    in_rows = project_in.astype(jnp.bfloat16).reshape(share, 3, width).transpose(1, 0, 2)
-    in_rows, gathered = lax.optimization_barrier((in_rows.reshape(-1, width), gathered))
-    gathered_in = lax.all_gather(in_rows, everyone, axis=0, tiled=False)
-    up_end = 2 * share * folds
-    down_end = up_end + half // chips
-    whole_out = gathered[:, down_end:].reshape(width, width)
+    line_packed = gather_line(packed, "line")
+    up_out = jnp.concatenate([line_packed[:, :up_end], line_packed[:, down_end:]], axis=1)
+    up_out = gather_line(gather_line(up_out, "inner"), "outer").reshape(chips, -1, width)
+    down = gather_line(line_packed[:, up_end:down_end], "outer")
+    down = gather_line(down, "inner").swapaxes(0, 1).reshape(chips, -1, width)
+    whole_out = up_out[:, up_end:].reshape(width, width)
     direct = (2 * share) % 16 == 0
     if direct:
-        mlp_weights, mlp_up_rows = gathered, 2 * share
+        mlp_up, mlp_down, mlp_up_rows = up_out, down, 2 * share
     else:
-        mlp_weights = jnp.concatenate(
-            [gathered[:, n * 2 * share : (n + 1) * 2 * share].reshape(width, width) for n in range(folds)]
-            + [gathered[:, up_end:down_end].reshape(half, width)],
+        mlp_up = jnp.concatenate(
+            [up_out[:, n * 2 * share : (n + 1) * 2 * share].reshape(width, width) for n in range(folds)],
             axis=0,
         )[None]
-        mlp_up_rows = width
+        mlp_down, mlp_up_rows = down.reshape(1, half, width), width
 
     gain_one, shift_one, bias_query, bias_value, bias_out = (
         vectors[0],
@@ -578,8 +647,8 @@
 
     normed_one, query, keys, values = norm_mix(
         core.reshape(1),
-        line_tokens,
-        swap_cores(line_tokens),
+        own_tokens,
+        other_tokens,
         rows,
         gain_one,
         shift_one,
@@ -590,6 +659,9 @@
     returned = lax.all_to_all(
         attended.reshape(group, rows, lanes), seq, split_axis=0, concat_axis=0, tiled=True
     )
+    in_rows = project_in.astype(jnp.bfloat16).reshape(share, 3, width).transpose(1, 0, 2)
+    in_rows, returned = lax.optimization_barrier((in_rows.reshape(-1, width), returned))
+    gathered_in = lax.all_gather(in_rows, everyone, axis=0, tiled=False)
     attended_rows = returned.transpose(1, 0, 2).reshape(rows, width)
     inputs = tokens.astype(jnp.float32)
     projected = plain_product(attended_rows, whole_out) + bias_out
@@ -597,8 +669,8 @@
     norm_two, norm_two_back = jax.vjp(layer_norm, second, gain_two, shift_two)
     normed_two = norm_two.astype(jnp.bfloat16)
     normed_chip = jnp.concatenate([normed_two, swap_cores(normed_two)], axis=0)
-    grad_packed, branch_part, grad_norm_part, grad_bias_up = mlp(
-        normed_chip, grad_branch_chip, mlp_weights, mlp_up_rows, bias_up
+    grad_up, grad_down, branch_part, grad_norm_part, grad_bias_up = mlp(
+        normed_chip, grad_branch_chip, mlp_up, mlp_down, mlp_up_rows, bias_up
     )
     grad_norm_two = grad_norm_part[:rows] + swap_cores(grad_norm_part[rows:])
     branch = branch_part[:rows] + swap_cores(branch_part[rows:]) + bias_down
@@ -621,32 +693,33 @@
     grad_out = inner_rows(attended_rows, grad_projected).astype(jnp.bfloat16)
     grad_out = grad_out.reshape(chips, 2 * share, width)
     if direct:
-        grad_packed = lax.dynamic_update_slice_in_dim(grad_packed, grad_out, down_end, 1)
+        grad_up = lax.dynamic_update_slice_in_dim(grad_up, grad_out, up_end, 1)
     else:
-        grad_packed = jnp.concatenate(
+        grad_up = jnp.concatenate(
             [
-                grad_packed[0, n * width : (n + 1) * width].reshape(chips, 2 * share, width)
+                grad_up[0, n * width : (n + 1) * width].reshape(chips, 2 * share, width)
                 for n in range(folds)
             ]
-            + [grad_packed[0, folds * width :].reshape(chips, -1, width), grad_out],
+            + [grad_out],
             axis=1,
         )
-    summed = lax.psum_scatter(grad_packed, chip_axes, scatter_dimension=0, tiled=True)[0]
+    outer, inner = lax.axis_size("outer"), lax.axis_size("inner")
+    grad_up = grad_up.reshape(outer, inner, line, -1, width)
+    grad_down = grad_down.reshape(outer, inner, line, -1, width)
+    grad_down = scatter_line(scatter_line(grad_down, "outer", 0), "inner", 0)
+    grad_up = scatter_line(scatter_line(grad_up, "inner", 1), "outer", 0)
+    summed = scatter_line(jnp.concatenate([grad_up, grad_down], axis=1), "line", 0)
 
     grad_mixed_stream = attend_back(starts, query, keys, values, wide, logs, grad_stream)
     grad_mixed = lax.all_to_all(
         grad_mixed_stream.reshape(group, rows, 3 * lanes), seq, split_axis=0, concat_axis=0, tiled=True
     )
     grad_in = inner_rows(normed_one, grad_mixed_stream).astype(jnp.bfloat16)
-    parts = lax.all_to_all(
-        grad_in.reshape(streams, group * share, 3 * lanes),
-        "fsdp",
-        split_axis=0,
-        concat_axis=0,
-        tiled=True,
-    )
-    parts = jnp.sum(parts.astype(jnp.float32), axis=0).reshape(group, share, 3 * lanes)
+    parts = grad_in.reshape(outer, inner, group * share, 3 * lanes)
+    parts = scatter_line(scatter_line(parts, "inner", 1), "outer", 0)
+    parts = parts.reshape(group, share, 3 * lanes)
     parts = lax.all_to_all(parts, seq, split_axis=0, concat_axis=0, tiled=True)
+    parts = parts.astype(jnp.float32)
     summed_in = parts.reshape(group, share, 3, lanes).transpose(1, 2, 0, 3).reshape(share, 3 * width)
 
     input_grad, grad_gain_one, grad_shift_one, mixed_sums = finish(
@@ -684,11 +757,11 @@
     summed_gains = jnp.sum(parts, axis=0).reshape(small_rows, share)
 
     up_sum = summed[:up_end].reshape(folds, 2, share, width)
-    out_sum = summed[down_end:].reshape(1, 2, share, width)
+    out_sum = summed[up_end : up_end + 2 * share].reshape(1, 2, share, width)
     both_sums = jnp.concatenate([up_sum, out_sum], axis=0)
     own_sums = jnp.where(first_core, both_sums[:, 0], both_sums[:, 1])
     other_sums = swap_cores(jnp.where(first_core, both_sums[:, 1], both_sums[:, 0]))
-    summed_down = summed[up_end:down_end].astype(jnp.float32)
+    summed_down = summed[up_end + 2 * share :].astype(jnp.float32)
     summed_out = own_sums[folds].astype(jnp.float32) + other_sums[folds].astype(jnp.float32)
     own_up = own_sums[:folds].transpose(1, 0, 2).reshape(share, chips, 1, unit_block)
     other_up = other_sums[:folds].transpose(1, 0, 2).reshape(share, chips, 1, unit_block)
@@ -733,52 +806,54 @@
 
 def solution(mesh):
     streams, group = mesh.shape["fsdp"], mesh.shape["seq"]
+    outer = math.isqrt(streams)
     fine = jax.sharding.Mesh(
-        mesh.devices.reshape(streams, group // 2, 2), ("fsdp", "line", "core")
+        mesh.devices.reshape(outer, streams // outer, group // 2, 2),
+        ("outer", "inner", "line", "core"),
     )
     return jax.shard_map(
         on_device,
         mesh=fine,
         in_specs=(
-            P(("fsdp", "line", "core"), None),
-            P(("fsdp", "line", "core"), None),
-            P(("fsdp", "line", "core")),
-            P(("fsdp", "line", "core")),
-            P(("fsdp", "line", "core"), None),
-            P(("fsdp", "line", "core"), None),
-            P(("fsdp", "line", "core"), None),
-            P(("fsdp", "line", "core"), None),
-            P(None, ("fsdp", "line", "core")),
-            P(("fsdp", "line", "core"), None),
-            P(("fsdp", "line", "core"), None),
-            P(("fsdp", "line", "core"), None),
-            P(("fsdp", "line", "core"), None),
-            P(None, ("fsdp", "line", "core")),
-            P(("fsdp", "line", "core"), None),
-            P(("fsdp", "line", "core"), None),
-            P(("fsdp", "line", "core"), None),
-            P(("fsdp", "line", "core"), None),
-            P(None, ("fsdp", "line", "core")),
+            P(("outer", "inner", "line", "core"), None),
+            P(("outer", "inner", "line", "core"), None),
+            P(("outer", "inner", "line", "core")),
+            P(("outer", "inner", "line", "core")),
+            P(("outer", "inner", "line", "core"), None),
+            P(("outer", "inner", "line", "core"), None),
+            P(("outer", "inner", "line", "core"), None),
+            P(("outer", "inner", "line", "core"), None),
+            P(None, ("outer", "inner", "line", "core")),
+            P(("outer", "inner", "line", "core"), None),
+            P(("outer", "inner", "line", "core"), None),
+            P(("outer", "inner", "line", "core"), None),
+            P(("outer", "inner", "line", "core"), None),
+            P(None, ("outer", "inner", "line", "core")),
+            P(("outer", "inner", "line", "core"), None),
+            P(("outer", "inner", "line", "core"), None),
+            P(("outer", "inner", "line", "core"), None),
+            P(("outer", "inner", "line", "core"), None),
+            P(None, ("outer", "inner", "line", "core")),
         ),
         out_specs=(
-            P(("fsdp", "line", "core"), None),
-            P(("fsdp", "line", "core"), None),
-            P(("fsdp", "line", "core"), None),
-            P(("fsdp", "line", "core"), None),
-            P(("fsdp", "line", "core"), None),
-            P(("fsdp", "line", "core"), None),
-            P(None, ("fsdp", "line", "core")),
-            P(("fsdp", "line", "core"), None),
-            P(("fsdp", "line", "core"), None),
-            P(("fsdp", "line", "core"), None),
-            P(("fsdp", "line", "core"), None),
-            P(None, ("fsdp", "line", "core")),
-            P(("fsdp", "line", "core"), None),
-            P(("fsdp", "line", "core"), None),
-            P(("fsdp", "line", "core"), None),
-            P(("fsdp", "line", "core"), None),
-            P(None, ("fsdp", "line", "core")),
-            P(("fsdp", "line", "core")),
+            P(("outer", "inner", "line", "core"), None),
+            P(("outer", "inner", "line", "core"), None),
+            P(("outer", "inner", "line", "core"), None),
+            P(("outer", "inner", "line", "core"), None),
+            P(("outer", "inner", "line", "core"), None),
+            P(("outer", "inner", "line", "core"), None),
+            P(None, ("outer", "inner", "line", "core")),
+            P(("outer", "inner", "line", "core"), None),
+            P(("outer", "inner", "line", "core"), None),
+            P(("outer", "inner", "line", "core"), None),
+            P(("outer", "inner", "line", "core"), None),
+            P(None, ("outer", "inner", "line", "core")),
+            P(("outer", "inner", "line", "core"), None),
+            P(("outer", "inner", "line", "core"), None),
+            P(("outer", "inner", "line", "core"), None),
+            P(("outer", "inner", "line", "core"), None),
+            P(None, ("outer", "inner", "line", "core")),
+            P(("outer", "inner", "line", "core")),
         ),
         check_vma=False,
     )

time: 755 us -> 692 us (0.917)
  blocking collectives: 117 us -> 12.5 us
  starting transfers between devices: 16.9 us -> 82.5 us
  waiting for transfers between devices: 364 us -> 299 us
  other arithmetic: 36.2 us -> 68 us
  local copies, waits for them, and re-layouts: 55.9 us -> 66 us
    ppermute x0 -> x30, waiting for transfers between devices: none -> 243 us  [the longest x6 73.9 us: scatter_line(): moving = lax.ppermute(payload, axis, pairs)]
    all_gather x2 -> x0, waiting for transfers between devices: 182 us -> none  [the longest x1 102 us: on_device(): gathered = lax.all_gather(packed, chip_axes, axis=0, tiled=False)]
    all_to_all x1, waiting for transfers between devices: 129 us -> 0.01 us  [on_device(): lax.all_to_all(grad_mixed_stream.reshape(group, rows, 3 * lanes), seq, sp...]
    all_to_all x3 -> x0, blocking collectives: 91.2 us -> none  [the longest x1 57.3 us: on_device(): lax.all_to_all(grad_attended.reshape(rows, group, lanes).transpose(1, 0,...]
    ppermute x0 -> x30, starting transfers between devices: none -> 57.8 us  [the longest x12 23.4 us: line_pieces(): moving = lax.ppermute(moving, axis, pairs)]
    all_to_all x1 -> x2, waiting for transfers between devices: 9.99 us -> 46.3 us  [the longest x1 32.5 us: on_device(): lax.all_to_all(grad_attended.reshape(rows, group, lanes).transpose(1, 0,...]
    all_to_all x1, waiting for transfers between devices: 35.8 us -> 0.01 us  [on_device(): lax.all_to_all(attended.reshape(group, rows, lanes), seq, split_axis=0, c...]
    select_n x0 -> x9, other arithmetic: none -> 15.9 us  [line_order(): jnp.where(place == 0, jnp.stack([value, other]), jnp.stack([other, value]))]
  transfers between devices with their start and end apart: 15 -> 49, of which waited for: 8 -> 20; matrix products, arithmetic and copies ran while one was open for 13% -> 19% of each run, Pallas kernels for 17% -> 11%
where the time goes in v3:
time: 692 us; the launch traced here: 686 us
  waiting for transfers between devices  299 us (43%)
  Pallas kernels  124 us (18%)
  starting transfers between devices  82.5 us (12%)
  other arithmetic  68 us (10%)
  local copies, waits for them, and re-layouts  66 us (10%)
  matrix products  17.5 us (3%)
  between operations  16.1 us (2%)
  blocking collectives  12.5 us (2%)
    ppermute x6, waiting for transfers between devices, scatter_line(): moving = lax.ppermute(payload, axis, pairs)  73.9 us
    ppermute x6, waiting for transfers between devices, line_pieces(): other = lax.ppermute(value, axis, [(0, 1), (1, 0)])  71.6 us
    ppermute x12, waiting for transfers between devices, line_pieces(): moving = lax.ppermute(moving, axis, pairs)  60.1 us
    pallas_call x1, Pallas kernels, mlp(): pl.pallas_call(mlp_kernel, grid=(hidden // units,), in_specs=[fixed, fixe...  38 us
    ppermute x6, waiting for transfers between devices, scatter_line(): lax.ppermute(pick(1 - place), axis, [(0, 1), (1, 0)])  37.3 us
    pallas_call x1, Pallas kernels, attend_back(): pl.pallas_call(attend_back_kernel, grid_spec=pltpu.PrefetchScalarGridSpec...  34.9 us
    all_to_all x1, waiting for transfers between devices, on_device(): lax.all_to_all(grad_attended.reshape(rows, group, lanes).transpose(1, 0,...  32.5 us
    pallas_call x1, Pallas kernels, attend(): pl.pallas_call(attend_kernel, grid_spec=pltpu.PrefetchScalarGridSpec(num_...  26.1 us
  transfers between devices with their start and end apart: 49, of which 20 were waited for; matrix products, arithmetic and copies ran while one was open for 19% of the time, Pallas kernels for 11%

profile of v3, /device:TPU:0, one launch (start us, length us, event | category | flops | bytes accessed | tf_op | source)
XLA Modules:
  0.0 685.6 jit_solution(18350292563070884099)
XLA Ops:
  7.2 6.1 collective-permute-start.2
  20.1 5.1 all-to-all-start
  26.8 4.8 collective-permute-start.16
  31.6 13.7 %all-to-all-done = bf16[8,34,384]{2,1,0:T(8,128)(2,1)S(1)} async-done(((bf16[8,34,384]{2,1,0:T(8,128)(2,1)}), bf16[8,34,384]{2,1,0:T(8,128)(2,1)S(1)}, u32[]{:S(2)}, u32[]{:S(2)}) %all-to-all-start) | async-done | bytes 208928 | tf_op jit(solution)/shard_map/all_to_all | solution.py:563
  48.1 3.9 collective-permute-done
  56.0 8.2 %collective-permute-done.19 = bf16[320,1024]{1,0:T(8,128)(2,1)} collective-permute-done((bf16[320,1024]{1,0:T(8,128)(2,1)}, bf16[320,1024]{1,0:T(8,128)(2,1)}, u32[]{:S(2)}, u32[]{:S(2)}) %collective-permute-start.19) | collective-permute-done | bytes 655392 | tf_op jit(solution)/shard_map/ppermute | solution.py:450
  67.0 1.6 collective-permute-start.3
  74.4 9.5 %collective-permute-done.20 = bf16[320,1024]{1,0:T(8,128)(2,1)} collective-permute-done((bf16[320,1024]{1,0:T(8,128)(2,1)}, bf16[320,1024]{1,0:T(8,128)(2,1)}, u32[]{:S(2)}, u32[]{:S(2)}) %collective-permute-start.20) | collective-permute-done | bytes 655392 | tf_op jit(solution)/shard_map/ppermute | solution.py:450
  87.2 19.2 %collective-permute-done.6 = bf16[512,1024]{1,0:T(8,128)(2,1)} collective-permute-done((bf16[512,1024]{1,0:T(8,128)(2,1)S(1)}, bf16[512,1024]{1,0:T(8,128)(2,1)}, u32[]{:S(2)}, u32[]{:S(2)}) %collective-permute-start.6) | collective-permute-done | bytes 1048608 | tf_op jit(solution)/shard_map/ppermute | solution.py:450
  108.4 12.0 %collective-permute-done.21 = bf16[320,1024]{1,0:T(8,128)(2,1)S(1)} collective-permute-done((bf16[320,1024]{1,0:T(8,128)(2,1)}, bf16[320,1024]{1,0:T(8,128)(2,1)S(1)}, u32[]{:S(2)}, u32[]{:S(2)}) %collective-permute-start.21) | collective-permute-done | bytes 655392 | tf_op jit(solution)/shard_map/ppermute | solution.py:450
  125.1 1.9 slice_bitcast_fusion.3
  127.1 1.8 fusion.52
  128.8 1.6 collective-permute-start.22
  131.1 11.3 %collective-permute-done.7 = bf16[512,1024]{1,0:T(8,128)(2,1)S(1)} collective-permute-done((bf16[512,1024]{1,0:T(8,128)(2,1)}, bf16[512,1024]{1,0:T(8,128)(2,1)S(1)}, u32[]{:S(2)}, u32[]{:S(2)}) %collective-permute-start.7) | collective-permute-done | bytes 1048608 | tf_op jit(solution)/shard_map/ppermute | solution.py:450
  146.8 17.7 %collective-permute-done.22 = bf16[4,192,1024]{2,1,0:T(8,128)(2,1)S(1)} collective-permute-done((bf16[4,192,1024]{2,1,0:T(8,128)(2,1)S(1)}, bf16[4,192,1024]{2,1,0:T(8,128)(2,1)S(1)}, u32[]{:S(2)}, u32[]{:S(2)}) %collective-permute-start.22) | collective-permute-done | bytes 1572896 | tf_op jit(solution)/shard_map/ppermute | solution.py:442
  164.5 2.1 maximum_select_fusion.3
  172.3 1.9 copy-done.15
  174.2 14.2 %norm_mix.1 = (bf16[4096,1024]{1,0:T(8,128)(2,1)}, bf16[4096,128]{1,0:T(8,128)(2,1)}, bf16[4096,128]{1,0:T(8,128)(2,1)}, bf16[4096,128]{1,0:T(8,128)(2,1)}) custom-call(s32[1]{0:T(128)} %bitcast.10.core_ref, bf16[2048,1024]{1,0:T(8,128)(2,1)} %bitcast.263, bf16[2048,1024]{1,0:T(8,128)(2,1)} %bitcast.262, f32[1,1024]{1,0:T(1,128)} %slice.156.gain_ref, ...), custom_call_target="tpu_custom_call" | custom-call | flops 3221225472 | bytes 16777216 | tf_op jit(solution)/shard_map/norm_mix/pallas_call | solution.py:239
  188.4 26.1 %attend_forward.1 = (f32[4096,128]{1,0:T(8,128)}, bf16[4096,128]{1,0:T(8,128)(2,1)}, f32[4096,128]{1,0:T(8,128)}) custom-call(s32[2]{0:T(128)} %select_reduce_fusion.starts_ref, bf16[4096,128]{1,0:T(8,128)(2,1)} %get-tuple-element.36.q_ref, bf16[4096,128]{1,0:T(8,128)(2,1)} %get-tuple-element.37.k_ref, bf16[4096,128]{1,0:T(8,128)(2,1)} %get-tuple-element.38.v_ref), custom_call_target="tpu_custom_call" | custom-call | flops 4060086272 | bytes 8388608 | tf_op jit(solution)/shard_map/attend_forward/pallas_call | solution.py:115
  214.5 2.3 copy.104
  216.8 4.4 all-to-all-start.1
  224.7 1.9 reshape.523
  226.6 1.7 copy.103
  233.3 2.6 convert_reduce_fusion
  235.9 25.1 %collective-permute-done.26 = bf16[4,128,1024]{2,1,0:T(8,128)(2,1)S(1)} collective-permute-done((bf16[4,128,1024]{2,1,0:T(8,128)(2,1)}, bf16[4,128,1024]{2,1,0:T(8,128)(2,1)S(1)}, u32[]{:S(2)}, u32[]{:S(2)}) %collective-permute-start.26) | collective-permute-done | bytes 1048608 | tf_op jit(solution)/shard_map/ppermute | solution.py:442
  261.0 1.7 maximum_select_fusion.4
  265.1 3.8 maximum_select_fusion
  269.2 1.8 copy-done.13
  271.0 4.7 fusion.61
  281.5 3.2 pad_maximum_fusion.1.gm_ref
  285.1 25.0 %collective-permute-done.27 = bf16[2,4,128,1024]{3,2,1,0:T(8,128)(2,1)} collective-permute-done((bf16[2,4,128,1024]{3,2,1,0:T(8,128)(2,1)}, bf16[2,4,128,1024]{3,2,1,0:T(8,128)(2,1)}, u32[]{:S(2)}, u32[]{:S(2)}) %collective-permute-start.27) | collective-permute-done | bytes 2097184 | tf_op jit(solution)/shard_map/ppermute | solution.py:442
  310.1 4.4 maximum_select_fusion.1
  314.5 2.7 pad_maximum_fusion.h_ref
  317.2 38.0 %mlp_both_ways.1 = (bf16[16,192,1024]{2,1,0:T(8,128)(2,1)}, bf16[16,128,1024]{2,1,0:T(8,128)(2,1)}, f32[1024,1024]{1,0:T(8,128)}, f32[1024,1024]{1,0:T(8,128)}, f32[1,2048]{1,0:T(1,128)}) custom-call(bf16[1024,1024]{1,0:T(8,128)(2,1)} %pad_maximum_fusion.h_ref, bf16[1024,1024]{1,0:T(8,128)(2,1)} %pad_maximum_fusion.1.gm_ref, ...), custom_call_target="tpu_custom_call" | custom-call | flops 25769803776 | bytes 33554432 | tf_op jit(solution)/shard_map/mlp_both_ways/pallas_call | solution.py:321
  355.2 3.3 slice.181
  360.7 2.4 collective-permute-done.29
  363.0 3.6 multiply_reduce_fusion.1
  366.8 4.3 multiply_reduce_fusion
  377.1 4.2 all-to-all-start.2
  381.4 2.6 convolution_convert_fusion
  384.2 2.5 dynamic-slice_bitcast_fusion
  388.2 1.9 dynamic-slice_bitcast_fusion.1
  391.6 32.5 %all-to-all-done.2 = bf16[8,512,128]{2,1,0:T(8,128)(2,1)} async-done(((bf16[8,512,128]{2,1,0:T(8,128)(2,1)}), bf16[8,512,128]{2,1,0:T(8,128)(2,1)}, u32[]{:S(2)}, u32[]{:S(2)}) %all-to-all-start.2) | async-done | bytes 1048608 | tf_op jit(solution)/shard_map/all_to_all | solution.py:686
  424.1 34.9 %attend_backward.1 = bf16[4096,384]{1,0:T(8,128)(2,1)} custom-call(s32[2]{0:T(128)} %select_reduce_fusion.starts_ref, bf16[4096,128]{1,0:T(8,128)(2,1)} %get-tuple-element.36.q_ref, bf16[4096,128]{1,0:T(8,128)(2,1)} %get-tuple-element.37.k_ref, bf16[4096,128]{1,0:T(8,128)(2,1)} %get-tuple-element.38.v_ref, f32[4096,128]{1,0:T(8,128)} %get-tuple-element.42.wide_ref, ...), custom_call_target="tpu_custom_call" | custom-call | flops 10150215680 | bytes 11534336 | tf_op jit(solution)/shard_map/attend_backward/pallas_call | solution.py:195
  459.1 8.9 %convolution_convert_fusion.2 = bf16[1024,384]{1,0:T(8,128)(2,1)S(1)} fusion(bf16[4096,1024]{1,0:T(8,128)(2,1)} %get-tuple-element.47, bf16[4096,384]{1,0:T(8,128)(2,1)} %attend_backward.1), kind=kOutput, calls=%fused_computation.55 | convolution fusion | flops 3221618688 | bytes 12320768 | tf_op jit(solution)/shard_map/dot_general | solution.py:40
  468.1 2.3 collective-permute-done.32
  470.4 3.6 fusion
  476.9 2.6 fusion.1
  480.7 35.1 %collective-permute-done.31 = bf16[256,384]{1,0:T(8,128)(2,1)S(1)} collective-permute-done((bf16[256,384]{1,0:T(8,128)(2,1)S(1)}, bf16[256,384]{1,0:T(8,128)(2,1)S(1)}, u32[]{:S(2)}, u32[]{:S(2)}) %collective-permute-start.31) | collective-permute-done | bytes 196640 | tf_op jit(solution)/shard_map/ppermute | solution.py:483
  515.8 12.5 %all_to_all.35 = bf16[8,32,384]{2,1,0:T(8,128)(2,1)} all-to-all(bf16[8,32,384]{2,1,0:T(8,128)(2,1)S(1)} %bitcast.287), channel_id=1, replica_groups=mesh['outer'=2,'inner'=2,'line'=4,'core'=2] {'line','core'}, dimensions={0} | all-to-all | bytes 393216 | tf_op jit(solution)/shard_map/all_to_all | solution.py:721
  528.3 4.5 all-to-all-start.3
  532.8 1.8 fusion.4
  535.0 2.1 fusion.2
  537.2 3.8 collective-permute-start.36
  542.0 56.5 %collective-permute-done.36 = bf16[320,1024]{1,0:T(8,128)(2,1)S(1)} collective-permute-done((bf16[320,1024]{1,0:T(8,128)(2,1)S(1)}, bf16[320,1024]{1,0:T(8,128)(2,1)S(1)}, u32[]{:S(2)}, u32[]{:S(2)}) %collective-permute-start.36) | collective-permute-done | bytes 655392 | tf_op jit(solution)/shard_map/ppermute | solution.py:493
  598.5 1.6 fusion.8
  600.1 5.2 collective-permute-start.37
  612.4 6.4 collective-permute-done.37
  618.8 1.8 fusion.9
  622.0 9.3 %collective-permute-start.38 = (bf16[320,1024]{1,0:T(8,128)(2,1)S(1)}, bf16[320,1024]{1,0:T(8,128)(2,1)S(1)}, u32[]{:S(2)}, u32[]{:S(2)}) collective-permute-start(bf16[320,1024]{1,0:T(8,128)(2,1)S(1)} %get-tuple-element.97), channel_id=1, source_target_pairs={{0,2},{2,4},{4,6},{1,3},{3,5},{5,7},{8,10},{10,12},{12,14},{9,11},... | collective-permute-start | bytes 1966088 | tf_op jit(solution)/shard_map/ppermute | solution.py:493
  632.6 9.8 %collective-permute-done.41 = bf16[320,1024]{1,0:T(8,128)(2,1)S(1)} collective-permute-done((bf16[320,1024]{1,0:T(8,128)(2,1)S(1)}, bf16[320,1024]{1,0:T(8,128)(2,1)S(1)}, u32[]{:S(2)}, u32[]{:S(2)}) %collective-permute-start.41) | collective-permute-done | bytes 655392 | tf_op jit(solution)/shard_map/ppermute | solution.py:493
  648.5 10.7 %finish_input.1 = (f32[512,1024]{1,0:T(8,128)}, f32[1,1024]{1,0:T(1,128)}, f32[1,1024]{1,0:T(1,128)}, f32[3,1,1024]{2,1,0:T(1,128)}) custom-call(bf16[8,512,384]{2,1,0:T(8,128)(2,1)} %all-to-all-done.3.grad_ref, bf16[32,96,1024]{2,1,0:T(8,128)(2,1)} %bitcast.248, bf16[512,1024]{1,0:T(8,128)(2,1)} %x_ref.1, f32[512,1024]{1,0:T(8,128)} %copy-done, ...), custom_call_target="tpu_custom_call" | custom-call | flops 3221225472 | bytes 16777216 | tf_op jit(solution)/shard_map/finish_input/pallas_call | solution.py:404
  664.5 5.2 all-to-all-start.5
  670.6 6.5 all-to-all-done.5
  (380 shorter events, 100.9 us)
Async XLA Ops:
  7.2 59.7 %collective-permute-start.2 = (bf16[512,1024]{1,0:T(8,128)(2,1)}, bf16[512,1024]{1,0:T(8,128)(2,1)}, u32[]{:S(2)}, u32[]{:S(2)}) collective-permute-start(bf16[512,1024]{1,0:T(8,128)(2,1)} %x_ref.1), channel_id=1, source_target_pairs={{0,2},{2,4},{4,6},{1,3},{3,5},{5,7},{8,10},{10,12},{12,14},{9,11},... | collective-permute-start | bytes 3145736 | tf_op jit(solution)/shard_map/ppermute | solution.py:450
  13.4 55.3 %collective-permute-start.5 = (bf16[512,1024]{1,0:T(8,128)(2,1)}, bf16[512,1024]{1,0:T(8,128)(2,1)S(1)}, u32[]{:S(2)}, u32[]{:S(2)}) collective-permute-start(bf16[512,1024]{1,0:T(8,128)(2,1)} %x_ref.1), channel_id=1, source_target_pairs={{2,0},{4,2},{6,4},{3,1},{5,3},{7,5},{10,8},{12,10},{14,12},{11,9},... | collective-permute-start | bytes 3145736 | tf_op jit(solution)/shard_map/ppermute | solution.py:450
  18.7 6.6 collective-permute-start.15
  20.1 25.2 %all-to-all-start = ((bf16[8,34,384]{2,1,0:T(8,128)(2,1)}), bf16[8,34,384]{2,1,0:T(8,128)(2,1)S(1)}, u32[]{:S(2)}, u32[]{:S(2)}) async-start(bf16[8,34,384]{2,1,0:T(8,128)(2,1)} %pad_maximum_fusion.4), calls=%async_computation | async-start | bytes 491520 | tf_op jit(solution)/shard_map/all_to_all | solution.py:563
  25.5 38.7 %copy-start.12 = (bf16[512,1024]{1,0:T(8,128)(2,1)S(1)}, bf16[512,1024]{1,0:T(8,128)(2,1)}, u32[]{:S(2)}) copy-start(bf16[512,1024]{1,0:T(8,128)(2,1)} %x_ref.1) | copy-start | bytes 3145732
  26.8 27.6 %collective-permute-start.16 = (bf16[320,1024]{1,0:T(8,128)(2,1)}, bf16[320,1024]{1,0:T(8,128)(2,1)}, u32[]{:S(2)}, u32[]{:S(2)}) collective-permute-start(bf16[320,1024]{1,0:T(8,128)(2,1)} %pad_maximum_fusion.3), channel_id=1, source_target_pairs={{0,2},{2,4},{4,6},{1,3},{3,5},{5,7},{8,10},{10,12},{12,14},{9,11},... | collective-permute-start | bytes 1966088 | tf_op jit(solution)/shard_map/ppermute | solution.py:450
  45.3 6.7 collective-permute-start
  46.8 17.4 %collective-permute-start.19 = (bf16[320,1024]{1,0:T(8,128)(2,1)}, bf16[320,1024]{1,0:T(8,128)(2,1)}, u32[]{:S(2)}, u32[]{:S(2)}) collective-permute-start(bf16[320,1024]{1,0:T(8,128)(2,1)} %pad_maximum_fusion.3), channel_id=1, source_target_pairs={{2,0},{4,2},{6,4},{3,1},{5,3},{7,5},{10,8},{12,10},{14,12},{11,9},... | collective-permute-start | bytes 1966088 | tf_op jit(solution)/shard_map/ppermute | solution.py:450
  52.9 11.3 %collective-permute-start.1 = (bf16[2,8,34,384]{3,2,1,0:T(8,128)(2,1)}, bf16[2,8,34,384]{3,2,1,0:T(8,128)(2,1)}, u32[]{:S(2)}, u32[]{:S(2)}) collective-permute-start(bf16[2,8,34,384]{3,2,1,0:T(8,128)(2,1)} %maximum_select_fusion.7), channel_id=1, source_target_pairs={{0,16},{16,0},{1,17},{17,1},{2,18},{18,2},{3,19},{19,3},{4,20},{20... | collective-permute-start | bytes 1253384 | tf_op jit(solution)/shard_map/ppermute | solution.py:442
  54.4 19.2 %collective-permute-start.17 = (bf16[320,1024]{1,0:T(8,128)(2,1)}, bf16[320,1024]{1,0:T(8,128)(2,1)}, u32[]{:S(2)}, u32[]{:S(2)}) collective-permute-start(bf16[320,1024]{1,0:T(8,128)(2,1)} %collective-permute-done.16), channel_id=1, source_target_pairs={{2,4},{4,6},{3,5},{5,7},{10,12},{12,14},{11,13},{13,15},{18,20},{2... | collective-permute-start | bytes 1966088 | tf_op jit(solution)/shard_map/ppermute | solution.py:450
  64.2 106.7 %collective-permute-start.14 = (bf16[512,1024]{1,0:T(8,128)(2,1)S(1)}, bf16[512,1024]{1,0:T(8,128)(2,1)}, u32[]{:S(2)}, u32[]{:S(2)}) collective-permute-start(bf16[512,1024]{1,0:T(8,128)(2,1)S(1)} %copy-done.12), channel_id=1, source_target_pairs={{0,1},{1,0},{2,3},{3,2},{4,5},{5,4},{6,7},{7,6},{8,9},{9,8},{10,11... | collective-permute-start | bytes 3145736 | tf_op jit(solution)/shard_map/ppermute | solution.py:436
  64.2 19.7 %collective-permute-start.20 = (bf16[320,1024]{1,0:T(8,128)(2,1)}, bf16[320,1024]{1,0:T(8,128)(2,1)}, u32[]{:S(2)}, u32[]{:S(2)}) collective-permute-start(bf16[320,1024]{1,0:T(8,128)(2,1)} %collective-permute-done.19), channel_id=1, source_target_pairs={{2,0},{4,2},{3,1},{5,3},{10,8},{12,10},{11,9},{13,11},{18,16},{20,... | collective-permute-start | bytes 1966088 | tf_op jit(solution)/shard_map/ppermute | solution.py:450
  67.0 19.5 %collective-permute-start.3 = (bf16[512,1024]{1,0:T(8,128)(2,1)}, bf16[512,1024]{1,0:T(8,128)(2,1)}, u32[]{:S(2)}, u32[]{:S(2)}) collective-permute-start(bf16[512,1024]{1,0:T(8,128)(2,1)} %collective-permute-done.2), channel_id=1, source_target_pairs={{2,4},{4,6},{3,5},{5,7},{10,12},{12,14},{11,13},{13,15},{18,20},{2... | collective-permute-start | bytes 3145736 | tf_op jit(solution)/shard_map/ppermute | solution.py:450
  68.6 37.8 %collective-permute-start.6 = (bf16[512,1024]{1,0:T(8,128)(2,1)S(1)}, bf16[512,1024]{1,0:T(8,128)(2,1)}, u32[]{:S(2)}, u32[]{:S(2)}) collective-permute-start(bf16[512,1024]{1,0:T(8,128)(2,1)S(1)} %collective-permute-done.5), channel_id=1, source_target_pairs={{2,0},{4,2},{3,1},{5,3},{10,8},{12,10},{11,9},{13,11},{18,16},{20,... | collective-permute-start | bytes 3145736 | tf_op jit(solution)/shard_map/ppermute | solution.py:450
  71.0 37.4 %copy-start.29 = (f32[32,14,32]{2,1,0:T(8,128)}, f32[32,14,32]{2,1,0:T(8,128)S(1)}, u32[]{:S(2)}) copy-start(f32[32,14,32]{2,1,0:T(8,128)S(1)} %reshape.566) | copy-start | bytes 172036
  73.6 32.8 %collective-permute-start.18 = (bf16[320,1024]{1,0:T(8,128)(2,1)}, bf16[320,1024]{1,0:T(8,128)(2,1)S(1)}, u32[]{:S(2)}, u32[]{:S(2)}) collective-permute-start(bf16[320,1024]{1,0:T(8,128)(2,1)} %collective-permute-done.17), channel_id=1, source_target_pairs={{4,6},{5,7},{12,14},{13,15},{20,22},{21,23},{28,30},{29,31}} | collective-permute-start | bytes 1966088 | tf_op jit(solution)/shard_map/ppermute | solution.py:450
  83.9 36.4 %collective-permute-start.21 = (bf16[320,1024]{1,0:T(8,128)(2,1)}, bf16[320,1024]{1,0:T(8,128)(2,1)S(1)}, u32[]{:S(2)}, u32[]{:S(2)}) collective-permute-start(bf16[320,1024]{1,0:T(8,128)(2,1)} %collective-permute-done.20), channel_id=1, source_target_pairs={{2,0},{3,1},{10,8},{11,9},{18,16},{19,17},{26,24},{27,25}} | collective-permute-start | bytes 1966088 | tf_op jit(solution)/shard_map/ppermute | solution.py:450
  86.5 44.0 %collective-permute-start.4 = (bf16[512,1024]{1,0:T(8,128)(2,1)}, bf16[512,1024]{1,0:T(8,128)(2,1)S(1)}, u32[]{:S(2)}, u32[]{:S(2)}) collective-permute-start(bf16[512,1024]{1,0:T(8,128)(2,1)} %collective-permute-done.3), channel_id=1, source_target_pairs={{4,6},{5,7},{12,14},{13,15},{20,22},{21,23},{28,30},{29,31}} | collective-permute-start | bytes 3145736 | tf_op jit(solution)/shard_map/ppermute | solution.py:450
  106.4 61.6 %collective-permute-start.10 = (bf16[512,1024]{1,0:T(8,128)(2,1)}, bf16[512,1024]{1,0:T(8,128)(2,1)S(1)}, u32[]{:S(2)}, u32[]{:S(2)}) collective-permute-start(bf16[512,1024]{1,0:T(8,128)(2,1)} %collective-permute-done.3), channel_id=1, source_target_pairs={{0,1},{1,0},{2,3},{3,2},{4,5},{5,4},{6,7},{7,6},{8,9},{9,8},{10,11... | collective-permute-start | bytes 3145736 | tf_op jit(solution)/shard_map/ppermute | solution.py:436
  106.4 36.0 %collective-permute-start.7 = (bf16[512,1024]{1,0:T(8,128)(2,1)}, bf16[512,1024]{1,0:T(8,128)(2,1)S(1)}, u32[]{:S(2)}, u32[]{:S(2)}) collective-permute-start(bf16[512,1024]{1,0:T(8,128)(2,1)} %collective-permute-done.6), channel_id=1, source_target_pairs={{2,0},{3,1},{10,8},{11,9},{18,16},{19,17},{26,24},{27,25}} | collective-permute-start | bytes 3145736 | tf_op jit(solution)/shard_map/ppermute | solution.py:450
  128.8 35.6 %collective-permute-start.22 = (bf16[4,192,1024]{2,1,0:T(8,128)(2,1)S(1)}, bf16[4,192,1024]{2,1,0:T(8,128)(2,1)S(1)}, u32[]{:S(2)}, u32[]{:S(2)}) collective-permute-start(bf16[4,192,1024]{2,1,0:T(8,128)(2,1)S(1)} %get-tuple-element.111), channel_id=1, source_target_pairs={{0,8},{8,0},{1,9},{9,1},{2,10},{10,2},{3,11},{11,3},{4,12},{12,4},... | collective-permute-start | bytes 4718600 | tf_op jit(solution)/shard_map/ppermute | solution.py:442
  130.5 36.2 %collective-permute-start.8 = (bf16[512,1024]{1,0:T(8,128)(2,1)S(1)}, bf16[512,1024]{1,0:T(8,128)(2,1)S(1)}, u32[]{:S(2)}, u32[]{:S(2)}) collective-permute-start(bf16[512,1024]{1,0:T(8,128)(2,1)S(1)} %collective-permute-done.4), channel_id=1, source_target_pairs={{0,1},{1,0},{2,3},{3,2},{4,5},{5,4},{6,7},{7,6},{8,9},{9,8},{10,11... | collective-permute-start | bytes 3145736 | tf_op jit(solution)/shard_map/ppermute | solution.py:436
  142.4 25.2 %collective-permute-start.9 = (bf16[512,1024]{1,0:T(8,128)(2,1)S(1)}, bf16[512,1024]{1,0:T(8,128)(2,1)S(1)}, u32[]{:S(2)}, u32[]{:S(2)}) collective-permute-start(bf16[512,1024]{1,0:T(8,128)(2,1)S(1)} %collective-permute-done.7), channel_id=1, source_target_pairs={{0,1},{1,0},{2,3},{3,2},{4,5},{5,4},{6,7},{7,6},{8,9},{9,8},{10,11... | collective-permute-start | bytes 3145736 | tf_op jit(solution)/shard_map/ppermute | solution.py:436
  146.8 19.8 %copy-start.16 = (bf16[4,512,1024]{2,1,0:T(8,128)(2,1)}, bf16[4,512,1024]{2,1,0:T(8,128)(2,1)S(1)}, u32[]{:S(2)}) copy-start(bf16[4,512,1024]{2,1,0:T(8,128)(2,1)S(1)} %bitcast_dynamic-update-slice_fusion.7) | copy-start | bytes 12582916
  164.5 5.2 collective-permute-start.11
  166.6 3.2 collective-permute-start.12
  167.6 3.2 collective-permute-start.13
  168.0 97.1 %collective-permute-start.23 = (bf16[2,4,192,1024]{3,2,1,0:T(8,128)(2,1)}, bf16[2,4,192,1024]{3,2,1,0:T(8,128)(2,1)}, u32[]{:S(2)}, u32[]{:S(2)}) collective-permute-start(bf16[2,4,192,1024]{3,2,1,0:T(8,128)(2,1)} %maximum_select_fusion.3), channel_id=1, source_target_pairs={{0,16},{16,0},{1,17},{17,1},{2,18},{18,2},{3,19},{19,3},{4,20},{20... | collective-permute-start | bytes 9437192 | tf_op jit(solution)/shard_map/ppermute | solution.py:442
  216.8 48.3 %all-to-all-start.1 = ((bf16[8,512,128]{1,2,0:T(8,128)(2,1)}), bf16[8,512,128]{1,2,0:T(8,128)(2,1)}, u32[]{:S(2)}, u32[]{:S(2)}) async-start(bf16[8,512,128]{1,2,0:T(8,128)(2,1)} %copy.104), calls=%async_computation.1 | async-start | bytes 2097152 | tf_op jit(solution)/shard_map/all_to_all | solution.py:659
  221.2 427.2 %all-gather.3.cloned.1.call-start = ((), (), s32[]{:S(2)}) async-start(), calls=%async_computation.6 | async-start | bytes 6488064 | tf_op jit(solution)/shard_map/all_gather | solution.py:664
  221.2 39.8 %collective-permute-start.26 = (bf16[4,128,1024]{2,1,0:T(8,128)(2,1)}, bf16[4,128,1024]{2,1,0:T(8,128)(2,1)S(1)}, u32[]{:S(2)}, u32[]{:S(2)}) collective-permute-start(bf16[4,128,1024]{2,1,0:T(8,128)(2,1)} %get-tuple-element.105), channel_id=1, source_target_pairs={{0,16},{16,0},{1,17},{17,1},{2,18},{18,2},{3,19},{19,3},{4,20},{20... | collective-permute-start | bytes 3145736 | tf_op jit(solution)/shard_map/ppermute | solution.py:442
  235.9 45.6 %collective-permute-start.25 = (bf16[512,1024]{1,0:T(8,128)(2,1)}, bf16[512,1024]{1,0:T(8,128)(2,1)}, u32[]{:S(2)}, u32[]{:S(2)}) collective-permute-start(bf16[512,1024]{1,0:T(8,128)(2,1)} %get-tuple-element.73), channel_id=1, source_target_pairs={{0,1},{1,0},{2,3},{3,2},{4,5},{5,4},{6,7},{7,6},{8,9},{9,8},{10,11... | collective-permute-start | bytes 3145736 | tf_op jit(solution)/shard_map/ppermute | solution.py:436
  262.8 47.3 %collective-permute-start.27 = (bf16[2,4,128,1024]{3,2,1,0:T(8,128)(2,1)}, bf16[2,4,128,1024]{3,2,1,0:T(8,128)(2,1)}, u32[]{:S(2)}, u32[]{:S(2)}) collective-permute-start(bf16[2,4,128,1024]{3,2,1,0:T(8,128)(2,1)} %maximum_select_fusion.4), channel_id=1, source_target_pairs={{0,8},{8,0},{1,9},{9,1},{2,10},{10,2},{3,11},{11,3},{4,12},{12,4},... | collective-permute-start | bytes 6291464 | tf_op jit(solution)/shard_map/ppermute | solution.py:442
  277.0 37.5 %collective-permute-start.24 = (bf16[512,1024]{1,0:T(8,128)(2,1)S(1)}, bf16[512,1024]{1,0:T(8,128)(2,1)}, u32[]{:S(2)}, u32[]{:S(2)}) collective-permute-start(bf16[512,1024]{1,0:T(8,128)(2,1)S(1)} %add_convert_fusion.1), channel_id=1, source_target_pairs={{0,1},{1,0},{2,3},{3,2},{4,5},{5,4},{6,7},{7,6},{8,9},{9,8},{10,11... | collective-permute-start | bytes 3145736 | tf_op jit(solution)/shard_map/ppermute | solution.py:436
  358.5 4.5 collective-permute-start.29
  360.0 6.7 collective-permute-start.28
  377.1 47.0 %all-to-all-start.2 = ((bf16[8,512,128]{2,1,0:T(8,128)(2,1)}), bf16[8,512,128]{2,1,0:T(8,128)(2,1)}, u32[]{:S(2)}, u32[]{:S(2)}) async-start(bf16[8,512,128]{2,1,0:T(8,128)(2,1)} %bitcast.240), calls=%async_computation.2 | async-start | bytes 2097152 | tf_op jit(solution)/shard_map/all_to_all | solution.py:686
  387.9 82.6 %collective-permute-start.32 = (bf16[2,4,192,1024]{3,2,1,0:T(8,128)(2,1)}, bf16[2,4,192,1024]{3,2,1,0:T(8,128)(2,1)}, u32[]{:S(2)}, u32[]{:S(2)}) collective-permute-start(bf16[2,4,192,1024]{3,2,1,0:T(8,128)(2,1)} %dynamic-slice_bitcast_fusion), channel_id=1, source_target_pairs={{0,8},{8,0},{1,9},{9,1},{2,10},{10,2},{3,11},{11,3},{4,12},{12,4},... | collective-permute-start | bytes 9437192 | tf_op jit(solution)/shard_map/ppermute | solution.py:483
  390.0 86.9 %collective-permute-start.34 = (bf16[2,4,128,1024]{3,2,1,0:T(8,128)(2,1)S(1)}, bf16[2,4,128,1024]{3,2,1,0:T(8,128)(2,1)}, u32[]{:S(2)}, u32[]{:S(2)}) collective-permute-start(bf16[2,4,128,1024]{3,2,1,0:T(8,128)(2,1)S(1)} %dynamic-slice_bitcast_fusion.1), channel_id=1, source_target_pairs={{0,16},{16,0},{1,17},{17,1},{2,18},{18,2},{3,19},{19,3},{4,20},{20... | collective-permute-start | bytes 6291464 | tf_op jit(solution)/shard_map/ppermute | solution.py:483
  468.1 12.1 %collective-permute-start.30 = (bf16[2,256,384]{2,1,0:T(8,128)(2,1)S(1)}, bf16[2,256,384]{2,1,0:T(8,128)(2,1)S(1)}, u32[]{:S(2)}, u32[]{:S(2)}) collective-permute-start(bf16[2,256,384]{2,1,0:T(8,128)(2,1)S(1)} %dynamic-slice_bitcast_fusion.4), channel_id=1, source_target_pairs={{0,8},{8,0},{1,9},{9,1},{2,10},{10,2},{3,11},{11,3},{4,12},{12,4},... | collective-permute-start | bytes 1179656 | tf_op jit(solution)/shard_map/ppermute | solution.py:483
  475.4 59.2 %collective-permute-start.33 = (bf16[4,192,1024]{2,1,0:T(8,128)(2,1)}, bf16[4,192,1024]{2,1,0:T(8,128)(2,1)}, u32[]{:S(2)}, u32[]{:S(2)}) collective-permute-start(bf16[4,192,1024]{2,1,0:T(8,128)(2,1)} %dynamic-slice_bitcast_fusion.2), channel_id=1, source_target_pairs={{0,16},{16,0},{1,17},{17,1},{2,18},{18,2},{3,19},{19,3},{4,20},{20... | collective-permute-start | bytes 4718600 | tf_op jit(solution)/shard_map/ppermute | solution.py:483
  479.6 53.2 %collective-permute-start.35 = (bf16[4,128,1024]{2,1,0:T(8,128)(2,1)S(1)}, bf16[4,128,1024]{2,1,0:T(8,128)(2,1)}, u32[]{:S(2)}, u32[]{:S(2)}) collective-permute-start(bf16[4,128,1024]{2,1,0:T(8,128)(2,1)S(1)} %dynamic-slice_bitcast_fusion.3), channel_id=1, source_target_pairs={{0,8},{8,0},{1,9},{9,1},{2,10},{10,2},{3,11},{11,3},{4,12},{12,4},... | collective-permute-start | bytes 3145736 | tf_op jit(solution)/shard_map/ppermute | solution.py:483
  480.3 35.4 %collective-permute-start.31 = (bf16[256,384]{1,0:T(8,128)(2,1)S(1)}, bf16[256,384]{1,0:T(8,128)(2,1)S(1)}, u32[]{:S(2)}, u32[]{:S(2)}) collective-permute-start(bf16[256,384]{1,0:T(8,128)(2,1)S(1)} %dynamic-slice_bitcast_fusion.5), channel_id=1, source_target_pairs={{0,16},{16,0},{1,17},{17,1},{2,18},{18,2},{3,19},{19,3},{4,20},{20... | collective-permute-start | bytes 589832 | tf_op jit(solution)/shard_map/ppermute | solution.py:483
  528.3 120.1 %all-to-all-start.3 = ((bf16[8,512,384]{2,1,0:T(8,128)(2,1)}), bf16[8,512,384]{2,1,0:T(8,128)(2,1)}, u32[]{:S(2)}, u32[]{:S(2)}) async-start(bf16[8,512,384]{2,1,0:T(8,128)(2,1)} %bitcast.266), calls=%async_computation.3 | async-start | bytes 6291456 | tf_op jit(solution)/shard_map/all_to_all | solution.py:714
  537.2 61.3 %collective-permute-start.36 = (bf16[320,1024]{1,0:T(8,128)(2,1)S(1)}, bf16[320,1024]{1,0:T(8,128)(2,1)S(1)}, u32[]{:S(2)}, u32[]{:S(2)}) collective-permute-start(bf16[320,1024]{1,0:T(8,128)(2,1)S(1)} %get-tuple-element.101), channel_id=1, source_target_pairs={{0,2},{1,3},{8,10},{9,11},{16,18},{17,19},{24,26},{25,27}} | collective-permute-start | bytes 1966088 | tf_op jit(solution)/shard_map/ppermute | solution.py:493
  541.1 65.8 %copy-start.55 = (f32[1024]{0:T(1024)S(1)}, f32[1024]{0:T(1024)}, u32[]{:S(2)}) copy-start(f32[1024]{0:T(1024)} %get-tuple-element.72) | copy-start | bytes 12292
  541.1 65.8 %copy-start.68 = (f32[1,2048]{1,0:T(1,128)S(1)}, f32[1,2048]{1,0:T(1,128)}, u32[]{:S(2)}) copy-start(f32[1,2048]{1,0:T(1,128)} %get-tuple-element.53) | copy-start | bytes 24580
  541.1 66.6 %copy-start.60 = (f32[1024]{0:T(1024)S(1)}, f32[1024]{0:T(1024)}, u32[]{:S(2)}) copy-start(f32[1024]{0:T(1024)} %get-tuple-element.76) | copy-start | bytes 12292
  541.1 67.3 %copy-start.59 = (f32[1024]{0:T(1024)S(1)}, f32[1024]{0:T(1024)}, u32[]{:S(2)}) copy-start(f32[1024]{0:T(1024)} %get-tuple-element.74) | copy-start | bytes 12292
  541.1 68.0 %copy-start.57 = (f32[1024]{0:T(1024)S(1)}, f32[1024]{0:T(1024)}, u32[]{:S(2)}) copy-start(f32[1024]{0:T(1024)} %get-tuple-element.54) | copy-start | bytes 12292
  541.1 68.6 %copy-start.56 = (f32[1024]{0:T(1024)S(1)}, f32[1024]{0:T(1024)}, u32[]{:S(2)}) copy-start(f32[1024]{0:T(1024)} %get-tuple-element.56) | copy-start | bytes 12292
  541.1 69.3 %copy-start.58 = (f32[1024]{0:T(1024)S(1)}, f32[1024]{0:T(1024)}, u32[]{:S(2)}) copy-start(f32[1024]{0:T(1024)} %get-tuple-element.95) | copy-start | bytes 12292
  541.2 57.3 %collective-permute-start.39 = (bf16[320,1024]{1,0:T(8,128)(2,1)S(1)}, bf16[320,1024]{1,0:T(8,128)(2,1)S(1)}, u32[]{:S(2)}, u32[]{:S(2)}) collective-permute-start(bf16[320,1024]{1,0:T(8,128)(2,1)S(1)} %get-tuple-element.102), channel_id=1, source_target_pairs={{6,4},{7,5},{14,12},{15,13},{22,20},{23,21},{30,28},{31,29}} | collective-permute-start | bytes 1966088 | tf_op jit(solution)/shard_map/ppermute | solution.py:493
  600.1 18.7 %collective-permute-start.37 = (bf16[320,1024]{1,0:T(8,128)(2,1)}, bf16[320,1024]{1,0:T(8,128)(2,1)}, u32[]{:S(2)}, u32[]{:S(2)}) collective-permute-start(bf16[320,1024]{1,0:T(8,128)(2,1)} %get-tuple-element.99), channel_id=1, source_target_pairs={{0,2},{2,4},{1,3},{3,5},{8,10},{10,12},{9,11},{11,13},{16,18},{18,... | collective-permute-start | bytes 1966088 | tf_op jit(solution)/shard_map/ppermute | solution.py:493
  605.4 13.5 %collective-permute-start.40 = (bf16[320,1024]{1,0:T(8,128)(2,1)}, bf16[320,1024]{1,0:T(8,128)(2,1)}, u32[]{:S(2)}, u32[]{:S(2)}) collective-permute-start(bf16[320,1024]{1,0:T(8,128)(2,1)} %get-tuple-element.100), channel_id=1, source_target_pairs={{4,2},{6,4},{5,3},{7,5},{12,10},{14,12},{13,11},{15,13},{20,18},{2... | collective-permute-start | bytes 1966088 | tf_op jit(solution)/shard_map/ppermute | solution.py:493
  612.4 18.9 %copy-start.39 = (f32[32,3072]{1,0:T(8,128)S(1)}, f32[32,3072]{1,0:T(8,128)}, u32[]{:S(2)}) copy-start(f32[32,3072]{1,0:T(8,128)} %param.28) | copy-start | bytes 1179652
  612.4 18.9 %copy-start.40 = (f32[32,3072]{1,0:T(8,128)S(1)}, f32[32,3072]{1,0:T(8,128)}, u32[]{:S(2)}) copy-start(f32[32,3072]{1,0:T(8,128)} %param.33) | copy-start | bytes 1179652
  620.7 21.7 %collective-permute-start.41 = (bf16[320,1024]{1,0:T(8,128)(2,1)S(1)}, bf16[320,1024]{1,0:T(8,128)(2,1)S(1)}, u32[]{:S(2)}, u32[]{:S(2)}) collective-permute-start(bf16[320,1024]{1,0:T(8,128)(2,1)S(1)} %get-tuple-element.98), channel_id=1, source_target_pairs={{2,0},{4,2},{6,4},{3,1},{5,3},{7,5},{10,8},{12,10},{14,12},{11,9},... | collective-permute-start | bytes 1966088 | tf_op jit(solution)/shard_map/ppermute | solution.py:493
  622.0 21.6 %collective-permute-start.38 = (bf16[320,1024]{1,0:T(8,128)(2,1)S(1)}, bf16[320,1024]{1,0:T(8,128)(2,1)S(1)}, u32[]{:S(2)}, u32[]{:S(2)}) collective-permute-start(bf16[320,1024]{1,0:T(8,128)(2,1)S(1)} %get-tuple-element.97), channel_id=1, source_target_pairs={{0,2},{2,4},{4,6},{1,3},{3,5},{5,7},{8,10},{10,12},{12,14},{9,11},... | collective-permute-start | bytes 1966088 | tf_op jit(solution)/shard_map/ppermute | solution.py:493
  644.0 1.5 collective-permute-start.42
  648.5 21.3 %copy-start.28 = (f32[32,1024]{1,0:T(8,128)S(1)}, f32[32,1024]{1,0:T(8,128)}, u32[]{:S(2)}) copy-start(f32[32,1024]{1,0:T(8,128)} %param.24) | copy-start | bytes 393220
  648.5 21.3 %copy-start.42 = (f32[32,1024]{1,0:T(8,128)S(1)}, f32[32,1024]{1,0:T(8,128)}, u32[]{:S(2)}) copy-start(f32[32,1024]{1,0:T(8,128)} %param.29) | copy-start | bytes 393220
  648.5 21.3 %copy-start.43 = (f32[32,1024]{1,0:T(8,128)S(1)}, f32[32,1024]{1,0:T(8,128)}, u32[]{:S(2)}) copy-start(f32[32,1024]{1,0:T(8,128)} %param.34) | copy-start | bytes 393220
  664.5 12.6 %all-to-all-start.5 = ((f32[32,1,448]{2,1,0:T(1,128)}), f32[32,1,448]{2,1,0:T(1,128)S(1)}, u32[]{:S(2)}, u32[]{:S(2)}) async-start(f32[32,1,448]{2,1,0:T(1,128)} %all_to_all.28), calls=%async_computation.5 | async-start | bytes 131072 | tf_op jit(solution)/shard_map/all_to_all | solution.py:754
  (60 other events, 414.8 us)
Sparse Core Ops, SparseCore 0:
  360.7 84.9 all-gather.2

commit v4 on v3

--- a/solution.py
+++ b/solution.py
@@ -1,3 +1,4 @@
+import functools
 import math
 
 import jax
@@ -261,21 +262,20 @@
 
 
 def mlp_kernel(
+    pieces,
+    core_ref,
     h_ref,
     gm_ref,
-    up_ref,
-    down_ref,
     bias_ref,
-    up_grad_ref,
-    down_grad_ref,
-    m_ref,
-    gh_ref,
-    bias_grad_ref,
-    turned_ref,
+    *refs,
 ):
+    up_refs, down_refs = refs[:pieces], refs[pieces : 2 * pieces]
+    up_grad_ref, down_grad_ref, m_ref, gh_ref, bias_grad_ref, turned_ref = refs[2 * pieces :]
     tile = pl.program_id(0)
     width = h_ref.shape[1]
-    chips, up_rows, units = up_ref.shape
+    chips = up_grad_ref.shape[0]
+    up_rows = width // chips
+    units = bias_ref.shape[1]
     folds = width // units
 
     @pl.when(tile == 0)
@@ -284,8 +284,8 @@
         gh_ref[...] = jnp.zeros_like(gh_ref)
         turned_ref[...] = h_ref[...].T
 
-    weight_up = up_ref[...].reshape(width, units)
-    weight_down = down_ref[...].reshape(units, width)
+    weight_up = jnp.concatenate([ref[...].reshape(width, -1) for ref in up_refs], axis=1)
+    weight_down = jnp.concatenate([ref[...].reshape(-1, width) for ref in down_refs], axis=0)
     gm = gm_ref[...]
     upward = plain_product(h_ref[...], weight_up) + bias_ref[...]
     normal = 0.5 * (1.0 + lax.erf(upward * 0.5**0.5))
@@ -304,53 +304,87 @@
     down_grad_ref[...] = down_grad.reshape(down_grad_ref.shape)
 
 
-def mlp(normed, gm, up, down, up_rows, bias):
+def mlp(core, normed, gm, weights, bias, chips):
     rows, width = normed.shape
-    chips = up.shape[0]
-    hidden = bias.shape[0]
+    count = 2 * chips
+    share = width // count
+    half = bias.shape[0]
+    unit_block = half // chips
     units = 256
     folds = width // units
     once = dict(pipeline_mode=pl.Buffered(1))
-    fixed = pl.BlockSpec((rows, width), lambda j: (0, 0), **once)
-    if chips > 1:
-        part = units * chips // hidden
-        down_spec = pl.BlockSpec((part, units // part, width), lambda j: (j, 0, 0))
+    fixed = pl.BlockSpec((rows, width), lambda j, core: (0, 0), **once)
+    if len(weights) == 1:
+        pieces = units // unit_block
+        lane_blocks = width // unit_block
+
+        def up_spec(piece):
+            def place(j, core):
+                block = 2 * (j * pieces + piece) + core[0]
+                return (0, block // lane_blocks, lax.rem(block, lane_blocks))
+
+            return pl.BlockSpec((count, share, unit_block), place)
+
+        def down_spec(piece):
+            return pl.BlockSpec(
+                (1, unit_block, width), lambda j, core: (2 * (j * pieces + piece) + core[0], 1, 0)
+            )
+
+        weights = list(weights) * (2 * pieces)
+        weight_specs = [up_spec(n) for n in range(pieces)] + [down_spec(n) for n in range(pieces)]
+        up_grad_shape = (chips, 2 * share * (half // width) + 2 * share, width)
+        down_grad_shape = (chips, unit_block, width)
+        down_grad_spec = pl.BlockSpec((pieces, unit_block, width), lambda j, core: (j, 0, 0))
     else:
-        down_spec = pl.BlockSpec((1, units, width), lambda j: (0, j, 0))
+        pieces = 1
+        block = jnp.arange(half) // unit_block * 2 + core[0]
+        index = block * unit_block + lax.rem(jnp.arange(half), unit_block)
+        weights = [jnp.take(weights[0], index, axis=1), jnp.take(weights[1], index, axis=0)]
+        weight_specs = [
+            pl.BlockSpec((width, units), lambda j, core: (0, j)),
+            pl.BlockSpec((units, width), lambda j, core: (j, 0)),
+        ]
+        up_grad_shape = (1, half // width * width, width)
+        down_grad_shape = (1, half, width)
+        down_grad_spec = pl.BlockSpec((1, units, width), lambda j, core: (0, j, 0))
     total = jax.ShapeDtypeStruct((rows, width), jnp.float32)
-    return pl.pallas_call(
-        mlp_kernel,
-        grid=(hidden // units,),
-        in_specs=[
-            fixed,
-            fixed,
-            pl.BlockSpec((chips, up_rows, units), lambda j: (0, j // folds, lax.rem(j, folds))),
-            down_spec,
-            pl.BlockSpec((1, units), lambda j: (0, j)),
-        ],
-        out_specs=[
-            pl.BlockSpec(up.shape, lambda j: (0, 0, 0), **once),
-            down_spec,
-            fixed,
-            fixed,
-            pl.BlockSpec((1, units), lambda j: (0, j)),
-        ],
+    outs = pl.pallas_call(
+        functools.partial(mlp_kernel, pieces),
+        grid_spec=pltpu.PrefetchScalarGridSpec(
+            num_scalar_prefetch=1,
+            grid=(half // units,),
+            in_specs=[fixed, fixed, pl.BlockSpec((1, units), lambda j, core: (0, j)), *weight_specs],
+            out_specs=[
+                pl.BlockSpec(up_grad_shape, lambda j, core: (0, 0, 0), **once),
+                down_grad_spec,
+                fixed,
+                fixed,
+                pl.BlockSpec((1, units), lambda j, core: (0, j)),
+            ],
+            scratch_shapes=[pltpu.VMEM((width, rows), jnp.bfloat16)],
+        ),
         out_shape=(
-            jax.ShapeDtypeStruct(up.shape, jnp.bfloat16),
-            jax.ShapeDtypeStruct(down.shape, jnp.bfloat16),
+            jax.ShapeDtypeStruct(up_grad_shape, jnp.bfloat16),
+            jax.ShapeDtypeStruct(down_grad_shape, jnp.bfloat16),
             total,
             total,
-            jax.ShapeDtypeStruct((1, hidden), jnp.float32),
-        ),
-        scratch_shapes=[pltpu.VMEM((width, rows), jnp.bfloat16)],
+            jax.ShapeDtypeStruct((1, half), jnp.float32),
+        ),
         compiler_params=pltpu.CompilerParams(vmem_limit_bytes=VMEM_BYTES),
         cost_estimate=pl.CostEstimate(
-            flops=rows * width * hidden * 12,
-            bytes_accessed=(up.size + down.size) * 4 + rows * width * 12,
-            transcendentals=rows * hidden * 2,
+            flops=rows * width * half * 12,
+            bytes_accessed=half * width * 8 + rows * width * 12,
+            transcendentals=rows * half * 2,
         ),
         name="mlp_both_ways",
-    )(normed, gm, up, down, bias[None])
+    )(core, normed, gm, bias[None], *weights)
+    up_grad, down_grad = outs[0], outs[1]
+    if pieces == 1:
+        up_grad = up_grad.reshape(half // width, chips, 2 * share, width).swapaxes(0, 1)
+        up_grad = up_grad.reshape(chips, -1, width)
+        up_grad = jnp.pad(up_grad, ((0, 0), (0, 2 * share), (0, 0)))
+        down_grad = down_grad.reshape(chips, unit_block, width)
+    return (up_grad, down_grad, *outs[2:])
 
 
 def finish_kernel(
@@ -395,10 +429,12 @@
         grad_spec = pl.BlockSpec((group, rows, lanes), lambda k: (k, 0, 0))
     else:
         grad_spec = pl.BlockSpec((group, rows, lanes), lambda k: (0, 0, k))
-    share = weights.shape[1] // 3
-    if share % 16:
-        weights = weights.reshape(-1, 3, share, width).transpose(1, 0, 2, 3).reshape(1, -1, width)
-        share = width
+    if weights.ndim == 3:
+        share = width // weights.shape[0]
+        first = weights.shape[1] // share - 3
+        weight_spec = pl.BlockSpec((weights.shape[0], share, width), lambda k: (0, first + k, 0))
+    else:
+        weight_spec = pl.BlockSpec((width, width), lambda k: (0, k))
     fixed = lambda *shape: pl.BlockSpec(shape, lambda k: (0, 0))
     vector = jax.ShapeDtypeStruct((1, width), jnp.float32)
     return pl.pallas_call(
@@ -406,7 +442,7 @@
         grid=(3,),
         in_specs=[
             grad_spec,
-            pl.BlockSpec((weights.shape[0], share, width), lambda k: (0, k, 0)),
+            weight_spec,
             fixed(rows, width),
             fixed(rows, width),
             fixed(1, width),
@@ -537,6 +573,24 @@
             [jnp.where(first_core, own, other), jnp.where(first_core, other, own)], axis=axis
         )
 
+    unit_block = FF // count
+    low = lambda value: value.astype(jnp.bfloat16)
+    if share % 16 == 0 and unit_block == 128:
+        fold = lambda value: low(value).reshape(share, -1, width).swapaxes(0, 1).reshape(-1, width)
+        packed = jnp.concatenate(
+            [fold(hidden_up), low(hidden_down), low(project_out), fold(project_in)], axis=0
+        )
+        gathered = lax.all_gather(packed, everyone, axis=0, tiled=False)
+        out_at = FF // width * share + unit_block
+        whole_out = gathered[:, out_at : out_at + share].reshape(width, width)
+        mlp_weights, whole_in = (gathered,), gathered
+    else:
+        whole_in, whole_out, whole_up, whole_down = (
+            lax.all_gather(low(value), everyone, axis=0, tiled=True)
+            for value in (project_in, project_out, hidden_up, hidden_down)
+        )
+        mlp_weights = (whole_up, whole_down)
+
     pieces = line_pieces(tokens, "line")
     own_tokens = line_order(tokens, pieces, "line").reshape(-1, width)
     swapped = [(distance, swap_cores(piece)) for distance, piece in pieces]
@@ -574,47 +628,8 @@
     starts = jnp.min(jnp.where(first < rows, first + offsets, length), axis=0)
 
     half = FF // 2
-    unit_block = FF // count
-    up_blocks = hidden_up.astype(jnp.bfloat16).reshape(share, chips, 2, unit_block)
-    up_first = up_blocks[:, :, 0].reshape(share, half)
-    up_second = up_blocks[:, :, 1].reshape(share, half)
-    out_rows = project_out.astype(jnp.bfloat16)
-    received = swap_cores(
-        jnp.concatenate(
-            [jnp.where(first_core, up_second, up_first).reshape(-1, width), out_rows], axis=0
-        )
-    )
     folds = half // width
-    up_rows = in_order(
-        jnp.where(first_core, up_first, up_second),
-        received[: share * folds].reshape(share, half),
-        0,
-    )
     up_end = 2 * share * folds
-    down_end = up_end + half // chips
-    packed = jnp.concatenate(
-        [
-            up_rows.reshape(2 * share, folds, width).transpose(1, 0, 2).reshape(-1, width),
-            hidden_down.astype(jnp.bfloat16),
-            in_order(out_rows, received[share * folds :], 0),
-        ],
-        axis=0,
-    )
-    line_packed = gather_line(packed, "line")
-    up_out = jnp.concatenate([line_packed[:, :up_end], line_packed[:, down_end:]], axis=1)
-    up_out = gather_line(gather_line(up_out, "inner"), "outer").reshape(chips, -1, width)
-    down = gather_line(line_packed[:, up_end:down_end], "outer")
-    down = gather_line(down, "inner").swapaxes(0, 1).reshape(chips, -1, width)
-    whole_out = up_out[:, up_end:].reshape(width, width)
-    direct = (2 * share) % 16 == 0
-    if direct:
-        mlp_up, mlp_down, mlp_up_rows = up_out, down, 2 * share
-    else:
-        mlp_up = jnp.concatenate(
-            [up_out[:, n * 2 * share : (n + 1) * 2 * share].reshape(width, width) for n in range(folds)],
-            axis=0,
-        )[None]
-        mlp_down, mlp_up_rows = down.reshape(1, half, width), width
 
     gain_one, shift_one, bias_query, bias_value, bias_out = (
         vectors[0],
@@ -659,9 +674,6 @@
     returned = lax.all_to_all(
         attended.reshape(group, rows, lanes), seq, split_axis=0, concat_axis=0, tiled=True
     )
-    in_rows = project_in.astype(jnp.bfloat16).reshape(share, 3, width).transpose(1, 0, 2)
-    in_rows, returned = lax.optimization_barrier((in_rows.reshape(-1, width), returned))
-    gathered_in = lax.all_gather(in_rows, everyone, axis=0, tiled=False)
     attended_rows = returned.transpose(1, 0, 2).reshape(rows, width)
     inputs = tokens.astype(jnp.float32)
     projected = plain_product(attended_rows, whole_out) + bias_out
@@ -670,7 +682,7 @@
     normed_two = norm_two.astype(jnp.bfloat16)
     normed_chip = jnp.concatenate([normed_two, swap_cores(normed_two)], axis=0)
     grad_up, grad_down, branch_part, grad_norm_part, grad_bias_up = mlp(
-        normed_chip, grad_branch_chip, mlp_up, mlp_down, mlp_up_rows, bias_up
+        core.reshape(1), normed_chip, grad_branch_chip, mlp_weights, bias_up, chips
     )
     grad_norm_two = grad_norm_part[:rows] + swap_cores(grad_norm_part[rows:])
     branch = branch_part[:rows] + swap_cores(branch_part[rows:]) + bias_down
@@ -692,38 +704,29 @@
     ).reshape(length, lanes)
     grad_out = inner_rows(attended_rows, grad_projected).astype(jnp.bfloat16)
     grad_out = grad_out.reshape(chips, 2 * share, width)
-    if direct:
-        grad_up = lax.dynamic_update_slice_in_dim(grad_up, grad_out, up_end, 1)
-    else:
-        grad_up = jnp.concatenate(
-            [
-                grad_up[0, n * width : (n + 1) * width].reshape(chips, 2 * share, width)
-                for n in range(folds)
-            ]
-            + [grad_out],
-            axis=1,
-        )
+    grad_up = lax.dynamic_update_slice_in_dim(grad_up, grad_out, up_end, 1)
     outer, inner = lax.axis_size("outer"), lax.axis_size("inner")
     grad_up = grad_up.reshape(outer, inner, line, -1, width)
     grad_down = grad_down.reshape(outer, inner, line, -1, width)
     grad_down = scatter_line(scatter_line(grad_down, "outer", 0), "inner", 0)
     grad_up = scatter_line(scatter_line(grad_up, "inner", 1), "outer", 0)
-    summed = scatter_line(jnp.concatenate([grad_up, grad_down], axis=1), "line", 0)
-
     grad_mixed_stream = attend_back(starts, query, keys, values, wide, logs, grad_stream)
     grad_mixed = lax.all_to_all(
         grad_mixed_stream.reshape(group, rows, 3 * lanes), seq, split_axis=0, concat_axis=0, tiled=True
     )
+    plane_sums = jnp.concatenate([grad_up, grad_down], axis=1)
     grad_in = inner_rows(normed_one, grad_mixed_stream).astype(jnp.bfloat16)
     parts = grad_in.reshape(outer, inner, group * share, 3 * lanes)
     parts = scatter_line(scatter_line(parts, "inner", 1), "outer", 0)
+    parts, plane_sums, grad_mixed = lax.optimization_barrier((parts, plane_sums, grad_mixed))
+    summed = scatter_line(plane_sums, "line", 0)
     parts = parts.reshape(group, share, 3 * lanes)
     parts = lax.all_to_all(parts, seq, split_axis=0, concat_axis=0, tiled=True)
     parts = parts.astype(jnp.float32)
     summed_in = parts.reshape(group, share, 3, lanes).transpose(1, 2, 0, 3).reshape(share, 3 * width)
 
     input_grad, grad_gain_one, grad_shift_one, mixed_sums = finish(
-        grad_mixed, gathered_in, tokens, grad_second, gain_one
+        grad_mixed, whole_in, tokens, grad_second, gain_one
     )
     up_sums = grad_bias_up.reshape(chips, unit_block)
     up_sums = jnp.where(

time: 692 us -> 632 us (0.913)
  waiting for transfers between devices: 299 us -> 265 us
  starting transfers between devices: 82.5 us -> 61.9 us
  other arithmetic: 68 us -> 56.4 us
  blocking collectives: 12.5 us -> 20.1 us
    ppermute x12 -> x6, waiting for transfers between devices: 60.1 us -> 135 us  [line_pieces(): moving = lax.ppermute(moving, axis, pairs)]
    ppermute x6 -> x2, waiting for transfers between devices: 71.6 us -> 19.9 us  [line_pieces(): other = lax.ppermute(value, axis, [(0, 1), (1, 0)])]
    ppermute x6, waiting for transfers between devices: 73.9 us -> 28.3 us  [scatter_line(): moving = lax.ppermute(payload, axis, pairs)]
    all_to_all x1, waiting for transfers between devices: 32.5 us -> 13.7 us  [on_device(): lax.all_to_all(grad_attended.reshape(rows, group, lanes).transpose(1, 0,...]
    all_to_all x1, waiting for transfers between devices: 0.01 us -> 18.6 us  [on_device(): lax.all_to_all(attended.reshape(group, rows, lanes), seq, split_axis=0, c...]
    ppermute x6, waiting for transfers between devices: 37.3 us -> 22.8 us  [scatter_line(): lax.ppermute(pick(1 - place), axis, [(0, 1), (1, 0)])]
    select_n x9 -> x3, other arithmetic: 15.9 us -> 1.65 us  [line_order(): jnp.where(place == 0, jnp.stack([value, other]), jnp.stack([other, value]))]
    ppermute x6, starting transfers between devices: 22 us -> 10.5 us  [scatter_line(): moving = lax.ppermute(payload, axis, pairs)]
  transfers between devices with their start and end apart: 49 -> 38, of which waited for: 20 -> 19; matrix products, arithmetic and copies ran while one was open for 19% -> 16% of each run, Pallas kernels for 11% -> 14%
where the time goes in v4:
time: 632 us; the launch traced here: 622 us
  waiting for transfers between devices  265 us (42%)
  Pallas kernels  124 us (20%)
  local copies, waits for them, and re-layouts  65.9 us (10%)
  starting transfers between devices  61.9 us (10%)
  other arithmetic  56.4 us (9%)
  blocking collectives  20.1 us (3%)
  between operations  15.7 us (2%)
  matrix products  13.3 us (2%)
    ppermute x6, waiting for transfers between devices, line_pieces(): moving = lax.ppermute(moving, axis, pairs)  135 us
    pallas_call x1, Pallas kernels, mlp(): pl.pallas_call(functools.partial(mlp_kernel, pieces), grid_spec=pltpu.Pre...  38.6 us
    pallas_call x1, Pallas kernels, attend_back(): pl.pallas_call(attend_back_kernel, grid_spec=pltpu.PrefetchScalarGridSpec...  34.7 us
    ppermute x6, waiting for transfers between devices, scatter_line(): moving = lax.ppermute(payload, axis, pairs)  28.3 us
    pallas_call x1, Pallas kernels, attend(): pl.pallas_call(attend_kernel, grid_spec=pltpu.PrefetchScalarGridSpec(num_...  26.2 us
    ppermute x6, waiting for transfers between devices, scatter_line(): lax.ppermute(pick(1 - place), axis, [(0, 1), (1, 0)])  22.8 us
    all_to_all x1, blocking collectives, on_device(): lax.all_to_all(parts.reshape(count, small_rows * share), everyone, split_...  20.1 us
    ppermute x2, waiting for transfers between devices, line_pieces(): other = lax.ppermute(value, axis, [(0, 1), (1, 0)])  19.9 us
  transfers between devices with their start and end apart: 38, of which 19 were waited for; matrix products, arithmetic and copies ran while one was open for 16% of the time, Pallas kernels for 14%

profile of v4, /device:TPU:0, one launch (start us, length us, event | category | flops | bytes accessed | tf_op | source)
XLA Modules:
  0.0 622.2 jit_solution(2388027936832406041)
XLA Ops:
  11.2 5.9 collective-permute-start.2
  19.9 5.9 all-to-all-start
  25.8 29.9 %collective-permute-done.2 = bf16[512,1024]{1,0:T(8,128)(2,1)} collective-permute-done((bf16[512,1024]{1,0:T(8,128)(2,1)S(1)}, bf16[512,1024]{1,0:T(8,128)(2,1)}, u32[]{:S(2)}, u32[]{:S(2)}) %collective-permute-start.2) | collective-permute-done | bytes 1048608 | tf_op jit(solution)/shard_map/ppermute | solution.py:486
  55.7 1.7 collective-permute-start.3
  57.4 4.2 collective-permute-done.5
  62.9 3.2 all-to-all-done
  67.5 11.6 %collective-permute-done = bf16[8,34,384]{2,1,0:T(8,128)(2,1)S(1)} collective-permute-done((bf16[8,34,384]{2,1,0:T(8,128)(2,1)S(1)}, bf16[8,34,384]{2,1,0:T(8,128)(2,1)S(1)}, u32[]{:S(2)}, u32[]{:S(2)}) %collective-permute-start) | collective-permute-done | bytes 208928 | tf_op jit(solution)/shard_map/ppermute | solution.py:478
  79.2 1.6 collective-permute-start.1
  81.4 8.3 %collective-permute-done.1 = bf16[2,8,34,384]{3,2,1,0:T(8,128)(2,1)} collective-permute-done((bf16[2,8,34,384]{3,2,1,0:T(8,128)(2,1)S(1)}, bf16[2,8,34,384]{3,2,1,0:T(8,128)(2,1)}, u32[]{:S(2)}, u32[]{:S(2)}) %collective-permute-start.1) | collective-permute-done | bytes 417824 | tf_op jit(solution)/shard_map/ppermute | solution.py:478
  91.3 1.6 collective-permute-start.4
  92.9 28.5 %collective-permute-done.6 = bf16[512,1024]{1,0:T(8,128)(2,1)} collective-permute-done((bf16[512,1024]{1,0:T(8,128)(2,1)}, bf16[512,1024]{1,0:T(8,128)(2,1)}, u32[]{:S(2)}, u32[]{:S(2)}) %collective-permute-start.6) | collective-permute-done | bytes 1048608 | tf_op jit(solution)/shard_map/ppermute | solution.py:486
  129.5 72.8 %collective-permute-done.7 = bf16[512,1024]{1,0:T(8,128)(2,1)S(1)} collective-permute-done((bf16[512,1024]{1,0:T(8,128)(2,1)}, bf16[512,1024]{1,0:T(8,128)(2,1)S(1)}, u32[]{:S(2)}, u32[]{:S(2)}) %collective-permute-start.7) | collective-permute-done | bytes 1048608 | tf_op jit(solution)/shard_map/ppermute | solution.py:486
  213.0 3.5 collective-permute-done.13
  218.0 2.0 copy-done.5
  220.0 14.2 %norm_mix.1 = (bf16[4096,1024]{1,0:T(8,128)(2,1)}, bf16[4096,128]{1,0:T(8,128)(2,1)}, bf16[4096,128]{1,0:T(8,128)(2,1)}, bf16[4096,128]{1,0:T(8,128)(2,1)}) custom-call(s32[1]{0:T(128)} %bitcast.8.core_ref, bf16[2048,1024]{1,0:T(8,128)(2,1)} %bitcast.201, bf16[2048,1024]{1,0:T(8,128)(2,1)} %bitcast.200, f32[1,1024]{1,0:T(1,128)} %slice.135.gain_ref, ...), custom_call_target="tpu_custom_call" | custom-call | flops 3221225472 | bytes 16777216 | tf_op jit(solution)/shard_map/norm_mix/pallas_call | solution.py:240
  234.1 26.2 %attend_forward.1 = (f32[4096,128]{1,0:T(8,128)}, bf16[4096,128]{1,0:T(8,128)(2,1)}, f32[4096,128]{1,0:T(8,128)}) custom-call(s32[2]{0:T(128)} %select_reduce_fusion.starts_ref, bf16[4096,128]{1,0:T(8,128)(2,1)} %get-tuple-element.37.q_ref, bf16[4096,128]{1,0:T(8,128)(2,1)} %get-tuple-element.38.k_ref, bf16[4096,128]{1,0:T(8,128)(2,1)} %get-tuple-element.39.v_ref), custom_call_target="tpu_custom_call" | custom-call | flops 4060086272 | bytes 8388608 | tf_op jit(solution)/shard_map/attend_forward/pallas_call | solution.py:116
  260.4 2.3 copy.87
  262.7 3.8 all-to-all-start.1
  268.8 2.0 convert_reduce_fusion
  271.2 3.3 slice.178
  274.4 18.6 %all-to-all-done.1 = bf16[8,512,128]{1,2,0:T(8,128)(2,1)S(1)} async-done(((bf16[8,512,128]{1,2,0:T(8,128)(2,1)}), bf16[8,512,128]{1,2,0:T(8,128)(2,1)S(1)}, u32[]{:S(2)}, u32[]{:S(2)}) %all-to-all-start.1) | async-done | bytes 1048608 | tf_op jit(solution)/shard_map/all_to_all | solution.py:674
  294.1 4.9 fusion.44
  302.8 1.5 reshape.390
  305.7 3.1 pad_maximum_fusion.2.gm_ref
  308.7 3.1 pad_maximum_fusion.1.h_ref
  311.8 38.6 %mlp_both_ways.1 = (bf16[16,192,1024]{2,1,0:T(8,128)(2,1)}, bf16[16,128,1024]{2,1,0:T(8,128)(2,1)}, f32[1024,1024]{1,0:T(8,128)}, f32[1024,1024]{1,0:T(8,128)}, f32[1,2048]{1,0:T(1,128)}) custom-call(s32[1]{0:T(128)} %bitcast.8.core_ref, bf16[1024,1024]{1,0:T(8,128)(2,1)} %pad_maximum_fusion.1.h_ref, bf16[1024,1024]{1,0:T(8,128)(2,1)} %pad_maximum_fusion.2.gm_ref, ...), custom_call_target="tpu_custom_call" | custom-call | flops 25769803776 | bytes 29360128 | tf_op jit(solution)/shard_map/mlp_both_ways/pallas_call | solution.py:351
  350.4 3.3 slice.153
  354.3 1.5 slice.150
  358.4 3.7 multiply_reduce_fusion.1
  362.2 4.7 multiply_reduce_fusion
  372.9 4.3 all-to-all-start.2
  377.2 2.6 convolution_convert_fusion
  380.0 2.5 dynamic-slice_bitcast_fusion
  383.7 1.6 collective-permute-start.21
  385.4 3.1 dynamic-slice_bitcast_fusion.1
  388.5 1.6 collective-permute-start.23
  390.1 13.7 %all-to-all-done.2 = bf16[8,512,128]{2,1,0:T(8,128)(2,1)} async-done(((bf16[8,512,128]{2,1,0:T(8,128)(2,1)}), bf16[8,512,128]{2,1,0:T(8,128)(2,1)}, u32[]{:S(2)}, u32[]{:S(2)}) %all-to-all-start.2) | async-done | bytes 1048608 | tf_op jit(solution)/shard_map/all_to_all | solution.py:698
  403.8 34.7 %attend_backward.1 = bf16[4096,384]{1,0:T(8,128)(2,1)} custom-call(s32[2]{0:T(128)} %select_reduce_fusion.starts_ref, bf16[4096,128]{1,0:T(8,128)(2,1)} %get-tuple-element.37.q_ref, bf16[4096,128]{1,0:T(8,128)(2,1)} %get-tuple-element.38.k_ref, bf16[4096,128]{1,0:T(8,128)(2,1)} %get-tuple-element.39.v_ref, f32[4096,128]{1,0:T(8,128)} %get-tuple-element.43.wide_ref, ...), custom_call_target="tpu_custom_call" | custom-call | flops 10150215680 | bytes 11534336 | tf_op jit(solution)/shard_map/attend_backward/pallas_call | solution.py:196
  438.4 4.6 all-to-all-start.3
  443.1 2.7 fusion.1
  447.0 1.8 collective-permute-start.24
  448.8 6.2 collective-permute-done.21
  455.0 4.5 fusion
  460.7 1.6 collective-permute-start.22
  462.4 4.5 convolution_convert_fusion.2
  468.6 1.6 collective-permute-start.19
  479.1 6.3 %collective-permute-done.19 = bf16[2,256,384]{2,1,0:T(8,128)(2,1)} collective-permute-done((bf16[2,256,384]{2,1,0:T(8,128)(2,1)}, bf16[2,256,384]{2,1,0:T(8,128)(2,1)}, u32[]{:S(2)}, u32[]{:S(2)}) %collective-permute-start.19) | collective-permute-done | bytes 393248 | tf_op jit(solution)/shard_map/ppermute | solution.py:519
  486.6 1.7 collective-permute-start.20
  488.3 2.0 fusion.3
  490.3 10.4 %collective-permute-done.20 = bf16[256,384]{1,0:T(8,128)(2,1)S(1)} collective-permute-done((bf16[256,384]{1,0:T(8,128)(2,1)S(1)}, bf16[256,384]{1,0:T(8,128)(2,1)S(1)}, u32[]{:S(2)}, u32[]{:S(2)}) %collective-permute-start.20) | collective-permute-done | bytes 196640 | tf_op jit(solution)/shard_map/ppermute | solution.py:519
  501.4 2.1 fusion.2
  503.7 10.9 %all-to-all-done.3.grad_ref = bf16[8,512,384]{2,1,0:T(8,128)(2,1)} async-done(((bf16[8,512,384]{2,1,0:T(8,128)(2,1)}), bf16[8,512,384]{2,1,0:T(8,128)(2,1)}, u32[]{:S(2)}, u32[]{:S(2)}) %all-to-all-start.3) | async-done | bytes 3145760 | tf_op jit(solution)/shard_map/all_to_all | solution.py:714
  515.7 2.2 collective-permute-start.25
  517.9 10.5 %finish_input.1 = (f32[512,1024]{1,0:T(8,128)}, f32[1,1024]{1,0:T(1,128)}, f32[1,1024]{1,0:T(1,128)}, f32[3,1,1024]{2,1,0:T(1,128)}) custom-call(bf16[8,512,384]{2,1,0:T(8,128)(2,1)} %all-to-all-done.3.grad_ref, bf16[32,384,1024]{2,1,0:T(8,128)(2,1)} %bitcast.193, bf16[512,1024]{1,0:T(8,128)(2,1)} %x_ref.1, f32[512,1024]{1,0:T(8,128)} %copy-done, ...), custom_call_target="tpu_custom_call" | custom-call | flops 3221225472 | bytes 16777216 | tf_op jit(solution)/shard_map/finish_input/pallas_call | solution.py:440
  535.0 2.3 collective-permute-start.26
  537.5 13.0 %collective-permute-done.26 = bf16[320,1024]{1,0:T(8,128)(2,1)S(1)} collective-permute-done((bf16[320,1024]{1,0:T(8,128)(2,1)S(1)}, bf16[320,1024]{1,0:T(8,128)(2,1)S(1)}, u32[]{:S(2)}, u32[]{:S(2)}) %collective-permute-start.26) | collective-permute-done | bytes 655392 | tf_op jit(solution)/shard_map/ppermute | solution.py:529
  550.5 1.6 fusion.8
  552.2 1.5 collective-permute-start.29
  554.0 20.1 %all_to_all.35 = f32[32,1,448]{2,1,0:T(1,128)S(1)} all-to-all(f32[32,1,448]{2,1,0:T(1,128)S(1)} %all_to_all.28), channel_id=1, replica_groups=mesh['outer'=2,'inner'=2,'line'=4,'core'=2] {'outer','inner','line','core'}, dimensions={0} | all-to-all | bytes 114688 | tf_op jit(solution)/shard_map/all_to_all | solution.py:757
  574.1 4.0 all-to-all-start.4
  579.5 7.0 %all-to-all-done.4 = bf16[8,32,384]{2,1,0:T(8,128)(2,1)} async-done(((bf16[8,32,384]{2,1,0:T(8,128)(2,1)}), bf16[8,32,384]{2,1,0:T(8,128)(2,1)}, u32[]{:S(2)}, u32[]{:S(2)}) %all-to-all-start.4) | async-done | bytes 196640 | tf_op jit(solution)/shard_map/all_to_all | solution.py:724
  587.8 2.4 collective-permute-start.27
  594.1 10.0 %collective-permute-done.27 = bf16[320,1024]{1,0:T(8,128)(2,1)S(1)} collective-permute-done((bf16[320,1024]{1,0:T(8,128)(2,1)}, bf16[320,1024]{1,0:T(8,128)(2,1)S(1)}, u32[]{:S(2)}, u32[]{:S(2)}) %collective-permute-start.27) | collective-permute-done | bytes 655392 | tf_op jit(solution)/shard_map/ppermute | solution.py:529
  604.2 5.2 collective-permute-done.30
  (300 shorter events, 86.3 us)
Async XLA Ops:
  7.2 264.0 %all-gather.3.cloned.1.call-start = ((), (), s32[]{:S(2)}) async-start(), calls=%async_computation.6 | async-start | bytes 25952256 | tf_op jit(solution)/shard_map/all_gather | solution.py:583
  9.8 8.6 %copy-start.52 = (s32[512]{0:T(512)S(1)}, s32[512]{0:T(512)}, u32[]{:S(2)}) copy-start(s32[512]{0:T(512)} %param.22) | copy-start | bytes 6148
  9.8 8.6 %copy-start.37 = (f32[14,32]{1,0:T(8,128)S(1)}, f32[14,32]{1,0:T(8,128)}, u32[]{:S(2)}) copy-start(f32[14,32]{1,0:T(8,128)} %param.27) | copy-start | bytes 5380
  9.8 8.7 %copy-start.54 = (s32[512]{0:T(512)S(1)}, s32[512]{0:T(512)}, u32[]{:S(2)}) copy-start(s32[512]{0:T(512)} %param.21) | copy-start | bytes 6148
  9.8 8.9 %copy-start.9 = (f32[32,3072]{1,0:T(8,128)S(1)}, f32[32,3072]{1,0:T(8,128)}, u32[]{:S(2)}) copy-start(f32[32,3072]{1,0:T(8,128)} %param.23) | copy-start | bytes 1179652
  11.2 44.5 %collective-permute-start.2 = (bf16[512,1024]{1,0:T(8,128)(2,1)S(1)}, bf16[512,1024]{1,0:T(8,128)(2,1)}, u32[]{:S(2)}, u32[]{:S(2)}) collective-permute-start(bf16[512,1024]{1,0:T(8,128)(2,1)S(1)} %copy-done.4), channel_id=1, source_target_pairs={{0,2},{2,4},{4,6},{1,3},{3,5},{5,7},{8,10},{10,12},{12,14},{9,11},... | collective-permute-start | bytes 3145736 | tf_op jit(solution)/shard_map/ppermute | solution.py:486
  17.1 44.5 %collective-permute-start.5 = (bf16[512,1024]{1,0:T(8,128)(2,1)S(1)}, bf16[512,1024]{1,0:T(8,128)(2,1)}, u32[]{:S(2)}, u32[]{:S(2)}) collective-permute-start(bf16[512,1024]{1,0:T(8,128)(2,1)S(1)} %copy-done.4), channel_id=1, source_target_pairs={{2,0},{4,2},{6,4},{3,1},{5,3},{7,5},{10,8},{12,10},{14,12},{11,9},... | collective-permute-start | bytes 3145736 | tf_op jit(solution)/shard_map/ppermute | solution.py:486
  19.9 46.2 %all-to-all-start = ((bf16[8,34,384]{2,1,0:T(8,128)(2,1)}), bf16[8,34,384]{2,1,0:T(8,128)(2,1)S(1)}, u32[]{:S(2)}, u32[]{:S(2)}) async-start(bf16[8,34,384]{2,1,0:T(8,128)(2,1)} %pad_maximum_fusion.4), calls=%async_computation | async-start | bytes 491520 | tf_op jit(solution)/shard_map/all_to_all | solution.py:617
  55.7 35.5 %collective-permute-start.3 = (bf16[512,1024]{1,0:T(8,128)(2,1)}, bf16[512,1024]{1,0:T(8,128)(2,1)}, u32[]{:S(2)}, u32[]{:S(2)}) collective-permute-start(bf16[512,1024]{1,0:T(8,128)(2,1)} %collective-permute-done.2), channel_id=1, source_target_pairs={{2,4},{4,6},{3,5},{5,7},{10,12},{12,14},{11,13},{13,15},{18,20},{2... | collective-permute-start | bytes 3145736 | tf_op jit(solution)/shard_map/ppermute | solution.py:486
  61.6 59.8 %collective-permute-start.6 = (bf16[512,1024]{1,0:T(8,128)(2,1)}, bf16[512,1024]{1,0:T(8,128)(2,1)}, u32[]{:S(2)}, u32[]{:S(2)}) collective-permute-start(bf16[512,1024]{1,0:T(8,128)(2,1)} %collective-permute-done.5), channel_id=1, source_target_pairs={{2,0},{4,2},{3,1},{5,3},{10,8},{12,10},{11,9},{13,11},{18,16},{20,... | collective-permute-start | bytes 3145736 | tf_op jit(solution)/shard_map/ppermute | solution.py:486
  66.0 13.1 %collective-permute-start = (bf16[8,34,384]{2,1,0:T(8,128)(2,1)S(1)}, bf16[8,34,384]{2,1,0:T(8,128)(2,1)S(1)}, u32[]{:S(2)}, u32[]{:S(2)}) collective-permute-start(bf16[8,34,384]{2,1,0:T(8,128)(2,1)S(1)} %all-to-all-done), channel_id=1, source_target_pairs={{0,8},{8,0},{1,9},{9,1},{2,10},{10,2},{3,11},{11,3},{4,12},{12,4},... | collective-permute-start | bytes 626696 | tf_op jit(solution)/shard_map/ppermute | solution.py:478
  79.2 10.5 %collective-permute-start.1 = (bf16[2,8,34,384]{3,2,1,0:T(8,128)(2,1)S(1)}, bf16[2,8,34,384]{3,2,1,0:T(8,128)(2,1)}, u32[]{:S(2)}, u32[]{:S(2)}) collective-permute-start(bf16[2,8,34,384]{3,2,1,0:T(8,128)(2,1)S(1)} %maximum_select_fusion.2), channel_id=1, source_target_pairs={{0,16},{16,0},{1,17},{17,1},{2,18},{18,2},{3,19},{19,3},{4,20},{20... | collective-permute-start | bytes 1253384 | tf_op jit(solution)/shard_map/ppermute | solution.py:478
  80.8 135.8 %collective-permute-start.14 = (bf16[512,1024]{1,0:T(8,128)(2,1)S(1)}, bf16[512,1024]{1,0:T(8,128)(2,1)}, u32[]{:S(2)}, u32[]{:S(2)}) collective-permute-start(bf16[512,1024]{1,0:T(8,128)(2,1)S(1)} %copy-done.4), channel_id=1, source_target_pairs={{0,1},{1,0},{2,3},{3,2},{4,5},{5,4},{6,7},{7,6},{8,9},{9,8},{10,11... | collective-permute-start | bytes 3145736 | tf_op jit(solution)/shard_map/ppermute | solution.py:472
  91.2 31.5 %copy-start.28 = (bf16[4,8,2,384]{3,1,2,0:T(8,128)(2,1)}, bf16[4,8,2,384]{3,1,2,0:T(8,128)(2,1)S(1)}, u32[]{:S(2)}) copy-start(bf16[4,8,2,384]{3,1,2,0:T(8,128)(2,1)S(1)} %copy.105) | copy-start | bytes 147460
  91.3 38.2 %collective-permute-start.4 = (bf16[512,1024]{1,0:T(8,128)(2,1)}, bf16[512,1024]{1,0:T(8,128)(2,1)}, u32[]{:S(2)}, u32[]{:S(2)}) collective-permute-start(bf16[512,1024]{1,0:T(8,128)(2,1)} %collective-permute-done.3), channel_id=1, source_target_pairs={{4,6},{5,7},{12,14},{13,15},{20,22},{21,23},{28,30},{29,31}} | collective-permute-start | bytes 3145736 | tf_op jit(solution)/shard_map/ppermute | solution.py:486
  121.4 80.8 %collective-permute-start.7 = (bf16[512,1024]{1,0:T(8,128)(2,1)}, bf16[512,1024]{1,0:T(8,128)(2,1)S(1)}, u32[]{:S(2)}, u32[]{:S(2)}) collective-permute-start(bf16[512,1024]{1,0:T(8,128)(2,1)} %collective-permute-done.6), channel_id=1, source_target_pairs={{2,0},{3,1},{10,8},{11,9},{18,16},{19,17},{26,24},{27,25}} | collective-permute-start | bytes 3145736 | tf_op jit(solution)/shard_map/ppermute | solution.py:486
  123.8 78.9 %copy-start.17 = (f32[32,14,32]{2,1,0:T(8,128)}, f32[32,14,32]{2,1,0:T(8,128)S(1)}, u32[]{:S(2)}) copy-start(f32[32,14,32]{2,1,0:T(8,128)S(1)} %reshape.420) | copy-start | bytes 172036
  128.9 83.7 %collective-permute-start.10 = (bf16[512,1024]{1,0:T(8,128)(2,1)}, bf16[512,1024]{1,0:T(8,128)(2,1)S(1)}, u32[]{:S(2)}, u32[]{:S(2)}) collective-permute-start(bf16[512,1024]{1,0:T(8,128)(2,1)} %collective-permute-done.3), channel_id=1, source_target_pairs={{0,1},{1,0},{2,3},{3,2},{4,5},{5,4},{6,7},{7,6},{8,9},{9,8},{10,11... | collective-permute-start | bytes 3145736 | tf_op jit(solution)/shard_map/ppermute | solution.py:472
  128.9 83.8 %collective-permute-start.11 = (bf16[512,1024]{1,0:T(8,128)(2,1)}, bf16[512,1024]{1,0:T(8,128)(2,1)S(1)}, u32[]{:S(2)}, u32[]{:S(2)}) collective-permute-start(bf16[512,1024]{1,0:T(8,128)(2,1)} %collective-permute-done.6), channel_id=1, source_target_pairs={{0,1},{1,0},{2,3},{3,2},{4,5},{5,4},{6,7},{7,6},{8,9},{9,8},{10,11... | collective-permute-start | bytes 3145736 | tf_op jit(solution)/shard_map/ppermute | solution.py:472
  129.4 80.3 %collective-permute-start.8 = (bf16[512,1024]{1,0:T(8,128)(2,1)}, bf16[512,1024]{1,0:T(8,128)(2,1)S(1)}, u32[]{:S(2)}, u32[]{:S(2)}) collective-permute-start(bf16[512,1024]{1,0:T(8,128)(2,1)} %collective-permute-done.4), channel_id=1, source_target_pairs={{0,1},{1,0},{2,3},{3,2},{4,5},{5,4},{6,7},{7,6},{8,9},{9,8},{10,11... | collective-permute-start | bytes 3145736 | tf_op jit(solution)/shard_map/ppermute | solution.py:472
  202.2 9.7 %collective-permute-start.9 = (bf16[512,1024]{1,0:T(8,128)(2,1)S(1)}, bf16[512,1024]{1,0:T(8,128)(2,1)S(1)}, u32[]{:S(2)}, u32[]{:S(2)}) collective-permute-start(bf16[512,1024]{1,0:T(8,128)(2,1)S(1)} %collective-permute-done.7), channel_id=1, source_target_pairs={{0,1},{1,0},{2,3},{3,2},{4,5},{5,4},{6,7},{7,6},{8,9},{9,8},{10,11... | collective-permute-start | bytes 3145736 | tf_op jit(solution)/shard_map/ppermute | solution.py:472
  209.8 3.1 collective-permute-start.12
  212.0 4.6 collective-permute-start.13
  260.4 8.4 %copy-start.1 = (bf16[512,1024]{1,0:T(8,128)(2,1)S(1)}, bf16[512,1024]{1,0:T(8,128)(2,1)}, u32[]{:S(2)}) copy-start(bf16[512,1024]{1,0:T(8,128)(2,1)} %param.20) | copy-start | bytes 3145732
  262.7 30.4 %all-to-all-start.1 = ((bf16[8,512,128]{1,2,0:T(8,128)(2,1)}), bf16[8,512,128]{1,2,0:T(8,128)(2,1)S(1)}, u32[]{:S(2)}, u32[]{:S(2)}) async-start(bf16[8,512,128]{1,2,0:T(8,128)(2,1)} %copy.87), calls=%async_computation.1 | async-start | bytes 2097152 | tf_op jit(solution)/shard_map/all_to_all | solution.py:674
  266.6 7.8 %copy-start.39 = (f32[512]{0:T(512)}, f32[512]{0:T(512)S(1)}, u32[]{:S(2)}) copy-start(f32[512]{0:T(512)S(1)} %convert_element_type.243) | copy-start | bytes 6148
  270.7 35.0 %collective-permute-start.16 = (bf16[512,1024]{1,0:T(8,128)(2,1)}, bf16[512,1024]{1,0:T(8,128)(2,1)}, u32[]{:S(2)}, u32[]{:S(2)}) collective-permute-start(bf16[512,1024]{1,0:T(8,128)(2,1)} %get-tuple-element.75), channel_id=1, source_target_pairs={{0,1},{1,0},{2,3},{3,2},{4,5},{5,4},{6,7},{7,6},{8,9},{9,8},{10,11... | collective-permute-start | bytes 3145736 | tf_op jit(solution)/shard_map/ppermute | solution.py:472
  271.2 22.9 %copy-start.44 = (f32[1024]{0:T(1024)S(1)}, f32[1024]{0:T(1024)}, u32[]{:S(2)}) copy-start(f32[1024]{0:T(1024)} %mul.321) | copy-start | bytes 12292
  271.2 22.9 %copy-start.46 = (f32[1024]{0:T(1024)S(1)}, f32[1024]{0:T(1024)}, u32[]{:S(2)}) copy-start(f32[1024]{0:T(1024)} %add.291) | copy-start | bytes 12292
  301.3 7.5 %collective-permute-start.15 = (bf16[512,1024]{1,0:T(8,128)(2,1)}, bf16[512,1024]{1,0:T(8,128)(2,1)}, u32[]{:S(2)}, u32[]{:S(2)}) collective-permute-start(bf16[512,1024]{1,0:T(8,128)(2,1)} %add_convert_fusion.1), channel_id=1, source_target_pairs={{0,1},{1,0},{2,3},{3,2},{4,5},{5,4},{6,7},{7,6},{8,9},{9,8},{10,11... | collective-permute-start | bytes 3145736 | tf_op jit(solution)/shard_map/ppermute | solution.py:472
  353.8 4.6 collective-permute-start.18
  355.8 6.3 %collective-permute-start.17 = (f32[512,1024]{1,0:T(8,128)}, f32[512,1024]{1,0:T(8,128)}, u32[]{:S(2)}, u32[]{:S(2)}) collective-permute-start(f32[512,1024]{1,0:T(8,128)} %slice.150), channel_id=1, source_target_pairs={{0,1},{1,0},{2,3},{3,2},{4,5},{5,4},{6,7},{7,6},{8,9},{9,8},{10,11... | collective-permute-start | bytes 6291464 | tf_op jit(solution)/shard_map/ppermute | solution.py:472
  371.7 8.1 %slice-start = ((s8[6291456]{0:T(1024)(128)(4,1)}), s8[2097152]{0:T(1024)(128)(4,1)S(1)}, s32[]{:S(2)}) async-start(s8[6291456]{0:T(1024)(128)(4,1)} %bitcast.194), calls=%async_computation.7 | async-start | bytes 4194304
  372.9 30.9 %all-to-all-start.2 = ((bf16[8,512,128]{2,1,0:T(8,128)(2,1)}), bf16[8,512,128]{2,1,0:T(8,128)(2,1)}, u32[]{:S(2)}, u32[]{:S(2)}) async-start(bf16[8,512,128]{2,1,0:T(8,128)(2,1)} %bitcast.185), calls=%async_computation.2 | async-start | bytes 2097152 | tf_op jit(solution)/shard_map/all_to_all | solution.py:698
  383.7 71.2 %collective-permute-start.21 = (bf16[2,4,192,1024]{3,2,1,0:T(8,128)(2,1)}, bf16[2,4,192,1024]{3,2,1,0:T(8,128)(2,1)}, u32[]{:S(2)}, u32[]{:S(2)}) collective-permute-start(bf16[2,4,192,1024]{3,2,1,0:T(8,128)(2,1)} %dynamic-slice_bitcast_fusion), channel_id=1, source_target_pairs={{0,8},{8,0},{1,9},{9,1},{2,10},{10,2},{3,11},{11,3},{4,12},{12,4},... | collective-permute-start | bytes 9437192 | tf_op jit(solution)/shard_map/ppermute | solution.py:519
  388.5 54.6 %collective-permute-start.23 = (bf16[2,4,128,1024]{3,2,1,0:T(8,128)(2,1)}, bf16[2,4,128,1024]{3,2,1,0:T(8,128)(2,1)S(1)}, u32[]{:S(2)}, u32[]{:S(2)}) collective-permute-start(bf16[2,4,128,1024]{3,2,1,0:T(8,128)(2,1)} %dynamic-slice_bitcast_fusion.1), channel_id=1, source_target_pairs={{0,16},{16,0},{1,17},{17,1},{2,18},{18,2},{3,19},{19,3},{4,20},{20... | collective-permute-start | bytes 6291464 | tf_op jit(solution)/shard_map/ppermute | solution.py:519
  438.4 76.2 %all-to-all-start.3 = ((bf16[8,512,384]{2,1,0:T(8,128)(2,1)}), bf16[8,512,384]{2,1,0:T(8,128)(2,1)}, u32[]{:S(2)}, u32[]{:S(2)}) async-start(bf16[8,512,384]{2,1,0:T(8,128)(2,1)} %bitcast.204), calls=%async_computation.3 | async-start | bytes 6291456 | tf_op jit(solution)/shard_map/all_to_all | solution.py:714
  443.1 19.3 %slice-start.2 = ((s8[8388608]{0:T(1024)(128)(4,1)}), s8[4194304]{0:T(1024)(128)(4,1)S(1)}, s32[]{:S(2)}) async-start(s8[8388608]{0:T(1024)(128)(4,1)} %bitcast.235), calls=%async_computation.9 | async-start | bytes 8388608
  447.0 15.3 %slice-start.3 = ((s8[8388608]{0:T(1024)(128)(4,1)}), s8[4194304]{0:T(1024)(128)(4,1)S(1)}, s32[]{:S(2)}) async-start(s8[8388608]{0:T(1024)(128)(4,1)} %bitcast.235), calls=%async_computation.10 | async-start | bytes 8388608
  447.0 41.3 %collective-permute-start.24 = (bf16[4,128,1024]{2,1,0:T(8,128)(2,1)}, bf16[4,128,1024]{2,1,0:T(8,128)(2,1)}, u32[]{:S(2)}, u32[]{:S(2)}) collective-permute-start(bf16[4,128,1024]{2,1,0:T(8,128)(2,1)} %dynamic-slice_bitcast_fusion.3), channel_id=1, source_target_pairs={{0,8},{8,0},{1,9},{9,1},{2,10},{10,2},{3,11},{11,3},{4,12},{12,4},... | collective-permute-start | bytes 3145736 | tf_op jit(solution)/shard_map/ppermute | solution.py:519
  460.7 40.6 %collective-permute-start.22 = (bf16[4,192,1024]{2,1,0:T(8,128)(2,1)}, bf16[4,192,1024]{2,1,0:T(8,128)(2,1)}, u32[]{:S(2)}, u32[]{:S(2)}) collective-permute-start(bf16[4,192,1024]{2,1,0:T(8,128)(2,1)} %dynamic-slice_bitcast_fusion.2), channel_id=1, source_target_pairs={{0,16},{16,0},{1,17},{17,1},{2,18},{18,2},{3,19},{19,3},{4,20},{20... | collective-permute-start | bytes 4718600 | tf_op jit(solution)/shard_map/ppermute | solution.py:519
  462.3 8.4 %copy-start.43 = (f32[1024]{0:T(1024)S(1)}, f32[1024]{0:T(1024)}, u32[]{:S(2)}) copy-start(f32[1024]{0:T(1024)} %get-tuple-element.74) | copy-start | bytes 12292
  468.6 16.8 %collective-permute-start.19 = (bf16[2,256,384]{2,1,0:T(8,128)(2,1)}, bf16[2,256,384]{2,1,0:T(8,128)(2,1)}, u32[]{:S(2)}, u32[]{:S(2)}) collective-permute-start(bf16[2,256,384]{2,1,0:T(8,128)(2,1)} %dynamic-slice_bitcast_fusion.6), channel_id=1, source_target_pairs={{0,8},{8,0},{1,9},{9,1},{2,10},{10,2},{3,11},{11,3},{4,12},{12,4},... | collective-permute-start | bytes 1179656 | tf_op jit(solution)/shard_map/ppermute | solution.py:519
  486.6 14.0 %collective-permute-start.20 = (bf16[256,384]{1,0:T(8,128)(2,1)S(1)}, bf16[256,384]{1,0:T(8,128)(2,1)S(1)}, u32[]{:S(2)}, u32[]{:S(2)}) collective-permute-start(bf16[256,384]{1,0:T(8,128)(2,1)S(1)} %dynamic-slice_bitcast_fusion.7), channel_id=1, source_target_pairs={{0,16},{16,0},{1,17},{17,1},{2,18},{18,2},{3,19},{19,3},{4,20},{20... | collective-permute-start | bytes 589832 | tf_op jit(solution)/shard_map/ppermute | solution.py:519
  515.7 17.9 %collective-permute-start.25 = (bf16[320,1024]{1,0:T(8,128)(2,1)}, bf16[320,1024]{1,0:T(8,128)(2,1)}, u32[]{:S(2)}, u32[]{:S(2)}) collective-permute-start(bf16[320,1024]{1,0:T(8,128)(2,1)} %get-tuple-element.101), channel_id=1, source_target_pairs={{0,2},{1,3},{8,10},{9,11},{16,18},{17,19},{24,26},{25,27}} | collective-permute-start | bytes 1966088 | tf_op jit(solution)/shard_map/ppermute | solution.py:529
  528.4 8.9 %copy-start.35 = (f32[1,32,32]{2,1,0:T(8,128)S(1)}, f32[1,32,32]{2,1,0:T(8,128)}, u32[]{:S(2)}) copy-start(f32[1,32,32]{2,1,0:T(8,128)} %concatenate.78) | copy-start | bytes 12292
  528.5 8.9 %copy-start.36 = (f32[1,32,32]{2,1,0:T(8,128)S(1)}, f32[1,32,32]{2,1,0:T(8,128)}, u32[]{:S(2)}) copy-start(f32[1,32,32]{2,1,0:T(8,128)} %concatenate.79) | copy-start | bytes 12292
  528.5 8.9 %copy-start.33 = (f32[1,32,32]{2,1,0:T(8,128)S(1)}, f32[1,32,32]{2,1,0:T(8,128)}, u32[]{:S(2)}) copy-start(f32[1,32,32]{2,1,0:T(8,128)} %concatenate.80) | copy-start | bytes 12292
  528.5 8.9 %copy-start.34 = (f32[1,32,32]{2,1,0:T(8,128)S(1)}, f32[1,32,32]{2,1,0:T(8,128)}, u32[]{:S(2)}) copy-start(f32[1,32,32]{2,1,0:T(8,128)} %concatenate.81) | copy-start | bytes 12292
  528.5 8.9 %copy-start.32 = (f32[1,32,32]{2,1,0:T(8,128)S(1)}, f32[1,32,32]{2,1,0:T(8,128)}, u32[]{:S(2)}) copy-start(f32[1,32,32]{2,1,0:T(8,128)} %concatenate.82) | copy-start | bytes 12292
  532.7 4.8 collective-permute-start.28
  535.0 18.6 %copy-start.27 = (f32[4,32,32]{2,1,0:T(8,128)S(1)}, f32[4,32,32]{2,1,0:T(8,128)}, u32[]{:S(2)}) copy-start(f32[4,32,32]{2,1,0:T(8,128)} %select_n.194) | copy-start | bytes 49156
  535.0 15.5 %collective-permute-start.26 = (bf16[320,1024]{1,0:T(8,128)(2,1)S(1)}, bf16[320,1024]{1,0:T(8,128)(2,1)S(1)}, u32[]{:S(2)}, u32[]{:S(2)}) collective-permute-start(bf16[320,1024]{1,0:T(8,128)(2,1)S(1)} %fusion.7), channel_id=1, source_target_pairs={{0,2},{2,4},{1,3},{3,5},{8,10},{10,12},{9,11},{11,13},{16,18},{18,... | collective-permute-start | bytes 1966088 | tf_op jit(solution)/shard_map/ppermute | solution.py:529
  537.4 41.4 %copy-start.38 = (f32[14,32]{1,0:T(8,128)S(1)}, f32[14,32]{1,0:T(8,128)}, u32[]{:S(2)}) copy-start(f32[14,32]{1,0:T(8,128)} %param.27) | copy-start | bytes 5380
  537.5 41.4 %copy-start.50 = (f32[14,32]{1,0:T(8,128)S(1)}, f32[14,32]{1,0:T(8,128)}, u32[]{:S(2)}) copy-start(f32[14,32]{1,0:T(8,128)} %param.32) | copy-start | bytes 5380
  537.5 41.4 %copy-start.51 = (f32[14,32]{1,0:T(8,128)S(1)}, f32[14,32]{1,0:T(8,128)}, u32[]{:S(2)}) copy-start(f32[14,32]{1,0:T(8,128)} %param.37) | copy-start | bytes 5380
  552.2 38.1 %collective-permute-start.29 = (bf16[320,1024]{1,0:T(8,128)(2,1)}, bf16[320,1024]{1,0:T(8,128)(2,1)}, u32[]{:S(2)}, u32[]{:S(2)}) collective-permute-start(bf16[320,1024]{1,0:T(8,128)(2,1)} %get-tuple-element.100), channel_id=1, source_target_pairs={{4,2},{6,4},{5,3},{7,5},{12,10},{14,12},{13,11},{15,13},{20,18},{2... | collective-permute-start | bytes 1966088 | tf_op jit(solution)/shard_map/ppermute | solution.py:529
  574.1 12.4 %all-to-all-start.4 = ((bf16[8,32,384]{2,1,0:T(8,128)(2,1)}), bf16[8,32,384]{2,1,0:T(8,128)(2,1)}, u32[]{:S(2)}, u32[]{:S(2)}) async-start(bf16[8,32,384]{2,1,0:T(8,128)(2,1)} %bitcast.58), calls=%async_computation.4 | async-start | bytes 393216 | tf_op jit(solution)/shard_map/all_to_all | solution.py:724
  587.8 16.3 %collective-permute-start.27 = (bf16[320,1024]{1,0:T(8,128)(2,1)}, bf16[320,1024]{1,0:T(8,128)(2,1)S(1)}, u32[]{:S(2)}, u32[]{:S(2)}) collective-permute-start(bf16[320,1024]{1,0:T(8,128)(2,1)} %get-tuple-element.99), channel_id=1, source_target_pairs={{0,2},{2,4},{4,6},{1,3},{3,5},{5,7},{8,10},{10,12},{12,14},{9,11},... | collective-permute-start | bytes 1966088 | tf_op jit(solution)/shard_map/ppermute | solution.py:529
  591.6 17.8 %collective-permute-start.30 = (bf16[320,1024]{1,0:T(8,128)(2,1)S(1)}, bf16[320,1024]{1,0:T(8,128)(2,1)S(1)}, u32[]{:S(2)}, u32[]{:S(2)}) collective-permute-start(bf16[320,1024]{1,0:T(8,128)(2,1)S(1)} %fusion.6), channel_id=1, source_target_pairs={{2,0},{4,2},{6,4},{3,1},{5,3},{7,5},{10,8},{12,10},{14,12},{11,9},... | collective-permute-start | bytes 1966088 | tf_op jit(solution)/shard_map/ppermute | solution.py:529
  594.1 15.8 %copy-start.14 = (f32[128,1024]{1,0:T(8,128)S(1)}, f32[128,1024]{1,0:T(8,128)}, u32[]{:S(2)}) copy-start(f32[128,1024]{1,0:T(8,128)} %param.26) | copy-start | bytes 1572868
  594.1 15.8 %copy-start.23 = (f32[128,1024]{1,0:T(8,128)S(1)}, f32[128,1024]{1,0:T(8,128)}, u32[]{:S(2)}) copy-start(f32[128,1024]{1,0:T(8,128)} %param.31) | copy-start | bytes 1572868
  594.1 15.8 %copy-start.24 = (f32[128,1024]{1,0:T(8,128)S(1)}, f32[128,1024]{1,0:T(8,128)}, u32[]{:S(2)}) copy-start(f32[128,1024]{1,0:T(8,128)} %param.36) | copy-start | bytes 1572868
  609.8 1.5 collective-permute-start.31
  (33 other events, 99.8 us)
Sparse Core Ops, SparseCore 0:
  11.1 207.0 all-gather.2

commit v5 on v4

--- a/solution.py
+++ b/solution.py
@@ -262,17 +262,26 @@
 
 
 def mlp_kernel(
-    pieces,
-    core_ref,
+    own_ref,
+    other_ref,
+    gm_own_ref,
+    gm_other_ref,
+    bias_ref,
+    up_ref,
+    down_ref,
+    up_grad_ref,
+    down_grad_ref,
+    m_own_ref,
+    m_other_ref,
+    gh_own_ref,
+    gh_other_ref,
+    bias_grad_ref,
     h_ref,
     gm_ref,
-    bias_ref,
-    *refs,
+    turned_ref,
 ):
-    up_refs, down_refs = refs[:pieces], refs[pieces : 2 * pieces]
-    up_grad_ref, down_grad_ref, m_ref, gh_ref, bias_grad_ref, turned_ref = refs[2 * pieces :]
     tile = pl.program_id(0)
-    width = h_ref.shape[1]
+    rows, width = own_ref.shape
     chips = up_grad_ref.shape[0]
     up_rows = width // chips
     units = bias_ref.shape[1]
@@ -280,12 +289,16 @@
 
     @pl.when(tile == 0)
     def clear():
-        m_ref[...] = jnp.zeros_like(m_ref)
-        gh_ref[...] = jnp.zeros_like(gh_ref)
+        for ref in (m_own_ref, m_other_ref, gh_own_ref, gh_other_ref):
+            ref[...] = jnp.zeros_like(ref)
+        h_ref[:rows] = own_ref[...]
+        h_ref[rows:] = other_ref[...]
+        gm_ref[:rows] = gm_own_ref[...]
+        gm_ref[rows:] = gm_other_ref[...]
         turned_ref[...] = h_ref[...].T
 
-    weight_up = jnp.concatenate([ref[...].reshape(width, -1) for ref in up_refs], axis=1)
-    weight_down = jnp.concatenate([ref[...].reshape(-1, width) for ref in down_refs], axis=0)
+    weight_up = up_ref[...].reshape(width, units)
+    weight_down = down_ref[...].reshape(units, width)
     gm = gm_ref[...]
     upward = plain_product(h_ref[...], weight_up) + bias_ref[...]
     normal = 0.5 * (1.0 + lax.erf(upward * 0.5**0.5))
@@ -293,8 +306,12 @@
     active = (upward * normal).astype(jnp.bfloat16)
     grad_up = (inner_cols(gm, weight_down) * slope).astype(jnp.bfloat16)
     bias_grad_ref[...] = jnp.sum(grad_up.astype(jnp.float32), axis=0, keepdims=True)
-    m_ref[...] += plain_product(active, weight_down)
-    gh_ref[...] += inner_cols(grad_up, weight_up)
+    branch = plain_product(active, weight_down)
+    m_own_ref[...] += branch[:rows]
+    m_other_ref[...] += branch[rows:]
+    grad_norm = inner_cols(grad_up, weight_up)
+    gh_own_ref[...] += grad_norm[:rows]
+    gh_other_ref[...] += grad_norm[rows:]
     up_grad = plain_product(turned_ref[...], grad_up).astype(jnp.bfloat16)
     row = pl.multiple_of(tile // folds * up_rows, up_rows)
     column = pl.multiple_of(lax.rem(tile, folds) * units, units)
@@ -304,86 +321,60 @@
     down_grad_ref[...] = down_grad.reshape(down_grad_ref.shape)
 
 
-def mlp(core, normed, gm, weights, bias, chips):
-    rows, width = normed.shape
-    count = 2 * chips
-    share = width // count
+def mlp(own, other, gm_own, gm_other, up, down, bias, chips):
+    rows, width = own.shape
+    up_rows = width // chips
     half = bias.shape[0]
-    unit_block = half // chips
     units = 256
     folds = width // units
     once = dict(pipeline_mode=pl.Buffered(1))
-    fixed = pl.BlockSpec((rows, width), lambda j, core: (0, 0), **once)
-    if len(weights) == 1:
-        pieces = units // unit_block
-        lane_blocks = width // unit_block
-
-        def up_spec(piece):
-            def place(j, core):
-                block = 2 * (j * pieces + piece) + core[0]
-                return (0, block // lane_blocks, lax.rem(block, lane_blocks))
-
-            return pl.BlockSpec((count, share, unit_block), place)
-
-        def down_spec(piece):
-            return pl.BlockSpec(
-                (1, unit_block, width), lambda j, core: (2 * (j * pieces + piece) + core[0], 1, 0)
-            )
-
-        weights = list(weights) * (2 * pieces)
-        weight_specs = [up_spec(n) for n in range(pieces)] + [down_spec(n) for n in range(pieces)]
-        up_grad_shape = (chips, 2 * share * (half // width) + 2 * share, width)
-        down_grad_shape = (chips, unit_block, width)
-        down_grad_spec = pl.BlockSpec((pieces, unit_block, width), lambda j, core: (j, 0, 0))
+    fixed = pl.BlockSpec((rows, width), lambda j: (0, 0), **once)
+    if up.ndim == 3:
+        pieces = units * chips // half
+        up_spec = pl.BlockSpec((chips, up_rows, units), lambda j: (0, j // folds, lax.rem(j, folds)))
+        down_spec = pl.BlockSpec((pieces, units // pieces, width), lambda j: (j, 0, 0))
+        up_shape, down_shape = (chips, half // chips, width), (chips, half // chips, width)
+        down_grad_spec = down_spec
     else:
-        pieces = 1
-        block = jnp.arange(half) // unit_block * 2 + core[0]
-        index = block * unit_block + lax.rem(jnp.arange(half), unit_block)
-        weights = [jnp.take(weights[0], index, axis=1), jnp.take(weights[1], index, axis=0)]
-        weight_specs = [
-            pl.BlockSpec((width, units), lambda j, core: (0, j)),
-            pl.BlockSpec((units, width), lambda j, core: (j, 0)),
-        ]
-        up_grad_shape = (1, half // width * width, width)
-        down_grad_shape = (1, half, width)
-        down_grad_spec = pl.BlockSpec((1, units, width), lambda j, core: (0, j, 0))
+        up_spec = pl.BlockSpec((width, units), lambda j: (0, j))
+        down_spec = pl.BlockSpec((units, width), lambda j: (j, 0))
+        up_shape, down_shape = (1, half // width * width, width), (1, half, width)
+        down_grad_spec = pl.BlockSpec((1, units, width), lambda j: (0, j, 0))
     total = jax.ShapeDtypeStruct((rows, width), jnp.float32)
     outs = pl.pallas_call(
-        functools.partial(mlp_kernel, pieces),
-        grid_spec=pltpu.PrefetchScalarGridSpec(
-            num_scalar_prefetch=1,
-            grid=(half // units,),
-            in_specs=[fixed, fixed, pl.BlockSpec((1, units), lambda j, core: (0, j)), *weight_specs],
-            out_specs=[
-                pl.BlockSpec(up_grad_shape, lambda j, core: (0, 0, 0), **once),
-                down_grad_spec,
-                fixed,
-                fixed,
-                pl.BlockSpec((1, units), lambda j, core: (0, j)),
-            ],
-            scratch_shapes=[pltpu.VMEM((width, rows), jnp.bfloat16)],
-        ),
+        mlp_kernel,
+        grid=(half // units,),
+        in_specs=[fixed] * 4 + [pl.BlockSpec((1, units), lambda j: (0, j)), up_spec, down_spec],
+        out_specs=[
+            pl.BlockSpec(up_shape, lambda j: (0, 0, 0), **once),
+            down_grad_spec,
+            *[fixed] * 4,
+            pl.BlockSpec((1, units), lambda j: (0, j)),
+        ],
         out_shape=(
-            jax.ShapeDtypeStruct(up_grad_shape, jnp.bfloat16),
-            jax.ShapeDtypeStruct(down_grad_shape, jnp.bfloat16),
-            total,
-            total,
+            jax.ShapeDtypeStruct(up_shape, jnp.bfloat16),
+            jax.ShapeDtypeStruct(down_shape, jnp.bfloat16),
+            *[total] * 4,
             jax.ShapeDtypeStruct((1, half), jnp.float32),
         ),
+        scratch_shapes=[
+            pltpu.VMEM((2 * rows, width), jnp.bfloat16),
+            pltpu.VMEM((2 * rows, width), jnp.bfloat16),
+            pltpu.VMEM((width, 2 * rows), jnp.bfloat16),
+        ],
         compiler_params=pltpu.CompilerParams(vmem_limit_bytes=VMEM_BYTES),
         cost_estimate=pl.CostEstimate(
-            flops=rows * width * half * 12,
-            bytes_accessed=half * width * 8 + rows * width * 12,
-            transcendentals=rows * half * 2,
+            flops=2 * rows * width * half * 12,
+            bytes_accessed=half * width * 8 + rows * width * 24,
+            transcendentals=rows * half * 4,
         ),
         name="mlp_both_ways",
-    )(core, normed, gm, bias[None], *weights)
+    )(own, other, gm_own, gm_other, bias[None], up, down)
     up_grad, down_grad = outs[0], outs[1]
-    if pieces == 1:
-        up_grad = up_grad.reshape(half // width, chips, 2 * share, width).swapaxes(0, 1)
+    if up.ndim == 2:
+        up_grad = up_grad.reshape(half // width, chips, up_rows, width).swapaxes(0, 1)
         up_grad = up_grad.reshape(chips, -1, width)
-        up_grad = jnp.pad(up_grad, ((0, 0), (0, 2 * share), (0, 0)))
-        down_grad = down_grad.reshape(chips, unit_block, width)
+        down_grad = down_grad.reshape(chips, -1, width)
     return (up_grad, down_grad, *outs[2:])
 
 
@@ -488,6 +479,27 @@
     return pieces
 
 
+def line_pieces_two(first, second, axis):
+    size = lax.axis_size(axis)
+    pieces = ([], [])
+    moving = {-1: (first, second), 1: (first, second)}
+    for step in range(1, size):
+        arrived = []
+        for sign in (-1, 1):
+            pairs = [(i, i - sign) for i in range(size) if 0 <= i - sign < size]
+            pairs = [(i, j) for i, j in pairs if 0 <= i + sign * (step - 1) < size]
+            arrived.append((sign, pairs, lax.ppermute(moving[sign][0], axis, pairs)))
+        tied = lax.optimization_barrier(
+            tuple(item[2] for item in arrived) + tuple(moving[item[0]][1] for item in arrived)
+        )
+        for n, (sign, pairs, _) in enumerate(arrived):
+            later = lax.ppermute(tied[2 + n], axis, pairs)
+            moving[sign] = (tied[n], later)
+            pieces[0].append((sign * step, tied[n]))
+            pieces[1].append((sign * step, later))
+    return pieces
+
+
 def line_order(value, pieces, axis):
     place = lax.axis_index(axis)
     size = lax.axis_size(axis)
@@ -573,28 +585,53 @@
             [jnp.where(first_core, own, other), jnp.where(first_core, other, own)], axis=axis
         )
 
+    half = FF // 2
     unit_block = FF // count
+    folds = half // width
+    up_end = 2 * share * folds
     low = lambda value: value.astype(jnp.bfloat16)
-    if share % 16 == 0 and unit_block == 128:
-        fold = lambda value: low(value).reshape(share, -1, width).swapaxes(0, 1).reshape(-1, width)
+    direct = share % 16 == 0 and unit_block == 128
+    if direct:
+        up_blocks = low(hidden_up).reshape(share, chips, 2, unit_block)
+        up_first = up_blocks[:, :, 0].reshape(share, half)
+        up_second = up_blocks[:, :, 1].reshape(share, half)
+        out_rows = low(project_out)
+        received = swap_cores(
+            jnp.concatenate(
+                [jnp.where(first_core, up_second, up_first).reshape(-1, width), out_rows], axis=0
+            )
+        )
+        up_rows = in_order(
+            jnp.where(first_core, up_first, up_second),
+            received[: share * folds].reshape(share, half),
+            0,
+        )
         packed = jnp.concatenate(
-            [fold(hidden_up), low(hidden_down), low(project_out), fold(project_in)], axis=0
+            [
+                up_rows.reshape(2 * share, folds, width).transpose(1, 0, 2).reshape(-1, width),
+                in_order(out_rows, received[share * folds :], 0),
+                low(hidden_down),
+            ],
+            axis=0,
         )
-        gathered = lax.all_gather(packed, everyone, axis=0, tiled=False)
-        out_at = FF // width * share + unit_block
-        whole_out = gathered[:, out_at : out_at + share].reshape(width, width)
-        mlp_weights, whole_in = (gathered,), gathered
+        weight_pieces, pieces = line_pieces_two(packed, tokens, "line")
+        line_packed = line_order(packed, weight_pieces, "line")
+        middle = up_end + share
+        inner_first, outer_first = line_packed[:, :middle], line_packed[:, middle:]
+        inner_first = gather_line(inner_first, "inner")
+        outer_first = gather_line(outer_first, "outer")
     else:
-        whole_in, whole_out, whole_up, whole_down = (
-            lax.all_gather(low(value), everyone, axis=0, tiled=True)
-            for value in (project_in, project_out, hidden_up, hidden_down)
-        )
-        mlp_weights = (whole_up, whole_down)
-
-    pieces = line_pieces(tokens, "line")
+        pieces = line_pieces(tokens, "line")
+
     own_tokens = line_order(tokens, pieces, "line").reshape(-1, width)
     swapped = [(distance, swap_cores(piece)) for distance, piece in pieces]
     other_tokens = line_order(swap_cores(tokens), swapped, "line").reshape(-1, width)
+    if direct:
+        inner_first, outer_first, own_tokens = lax.optimization_barrier(
+            (inner_first, outer_first, own_tokens)
+        )
+        inner_first = gather_line(inner_first, "outer").reshape(chips, -1, width)
+        outer_first = gather_line(outer_first, "inner").swapaxes(0, 1).reshape(chips, -1, width)
 
     owned = project_in.astype(jnp.bfloat16).reshape(share, 3, group, lanes)
     owned = owned.transpose(2, 0, 1, 3).reshape(group, share, 3 * lanes)
@@ -627,10 +664,6 @@
     offsets = lax.broadcasted_iota(jnp.int32, (group, images), 0) * rows
     starts = jnp.min(jnp.where(first < rows, first + offsets, length), axis=0)
 
-    half = FF // 2
-    folds = half // width
-    up_end = 2 * share * folds
-
     gain_one, shift_one, bias_query, bias_value, bias_out = (
         vectors[0],
         vectors[1],
@@ -658,7 +691,6 @@
     )
     grad_rows = cotangent.astype(jnp.float32) * valid.astype(jnp.float32)[:, None]
     grad_branch = (scale_two * grad_rows).astype(jnp.bfloat16)
-    grad_branch_chip = jnp.concatenate([grad_branch, swap_cores(grad_branch)], axis=0)
 
     normed_one, query, keys, values = norm_mix(
         core.reshape(1),
@@ -671,21 +703,46 @@
         bias_in,
     )
     wide, attended, logs = attend(starts, query, keys, values)
+    if direct:
+        inner_first, outer_first, attended = lax.optimization_barrier(
+            (inner_first, outer_first, attended)
+        )
+        mlp_up, mlp_down = inner_first, outer_first[:, share:]
+        whole_out = jnp.concatenate([inner_first[:, up_end:], outer_first[:, :share]], axis=1)
+        whole_out = whole_out.reshape(width, width)
+    else:
+        whole_out, whole_up, whole_down = (
+            lax.all_gather(low(value), everyone, axis=0, tiled=True)
+            for value in (project_out, hidden_up, hidden_down)
+        )
+        block = jnp.arange(half) // unit_block * 2 + core
+        index = block * unit_block + lax.rem(jnp.arange(half), unit_block)
+        mlp_up, mlp_down = jnp.take(whole_up, index, axis=1), jnp.take(whole_down, index, axis=0)
     returned = lax.all_to_all(
         attended.reshape(group, rows, lanes), seq, split_axis=0, concat_axis=0, tiled=True
     )
+    in_rows, returned = lax.optimization_barrier((low(project_in), returned))
+    if direct:
+        in_rows = in_rows.reshape(share, 3, width).swapaxes(0, 1).reshape(-1, width)
+    whole_in = lax.all_gather(in_rows, everyone, axis=0, tiled=not direct)
     attended_rows = returned.transpose(1, 0, 2).reshape(rows, width)
     inputs = tokens.astype(jnp.float32)
     projected = plain_product(attended_rows, whole_out) + bias_out
     second = inputs + scale_one * projected
     norm_two, norm_two_back = jax.vjp(layer_norm, second, gain_two, shift_two)
     normed_two = norm_two.astype(jnp.bfloat16)
-    normed_chip = jnp.concatenate([normed_two, swap_cores(normed_two)], axis=0)
-    grad_up, grad_down, branch_part, grad_norm_part, grad_bias_up = mlp(
-        core.reshape(1), normed_chip, grad_branch_chip, mlp_weights, bias_up, chips
-    )
-    grad_norm_two = grad_norm_part[:rows] + swap_cores(grad_norm_part[rows:])
-    branch = branch_part[:rows] + swap_cores(branch_part[rows:]) + bias_down
+    grad_up, grad_down, branch, branch_other, grad_norm_two, grad_norm_other, grad_bias_up = mlp(
+        normed_two,
+        swap_cores(normed_two),
+        grad_branch,
+        swap_cores(grad_branch),
+        mlp_up,
+        mlp_down,
+        bias_up,
+        chips,
+    )
+    grad_norm_two = grad_norm_two + swap_cores(grad_norm_other)
+    branch = branch + swap_cores(branch_other) + bias_down
     block_output = (second + scale_two * branch).astype(jnp.bfloat16)
     grad_scale_two = jnp.sum(grad_rows * branch, axis=0)
     grad_bias_down = jnp.sum(grad_branch.astype(jnp.float32), axis=0)
@@ -704,22 +761,24 @@
     ).reshape(length, lanes)
     grad_out = inner_rows(attended_rows, grad_projected).astype(jnp.bfloat16)
     grad_out = grad_out.reshape(chips, 2 * share, width)
-    grad_up = lax.dynamic_update_slice_in_dim(grad_up, grad_out, up_end, 1)
     outer, inner = lax.axis_size("outer"), lax.axis_size("inner")
-    grad_up = grad_up.reshape(outer, inner, line, -1, width)
-    grad_down = grad_down.reshape(outer, inner, line, -1, width)
+    grad_up, grad_out, grad_down = (
+        value.reshape(outer, inner, line, -1, width) for value in (grad_up, grad_out, grad_down)
+    )
     grad_down = scatter_line(scatter_line(grad_down, "outer", 0), "inner", 0)
     grad_up = scatter_line(scatter_line(grad_up, "inner", 1), "outer", 0)
+    grad_out = scatter_line(scatter_line(grad_out, "inner", 1), "outer", 0)
+
     grad_mixed_stream = attend_back(starts, query, keys, values, wide, logs, grad_stream)
     grad_mixed = lax.all_to_all(
         grad_mixed_stream.reshape(group, rows, 3 * lanes), seq, split_axis=0, concat_axis=0, tiled=True
     )
-    plane_sums = jnp.concatenate([grad_up, grad_down], axis=1)
+    plane_sums = jnp.concatenate([grad_up, grad_out, grad_down], axis=1)
+    summed = scatter_line(plane_sums, "line", 0)
     grad_in = inner_rows(normed_one, grad_mixed_stream).astype(jnp.bfloat16)
     parts = grad_in.reshape(outer, inner, group * share, 3 * lanes)
     parts = scatter_line(scatter_line(parts, "inner", 1), "outer", 0)
-    parts, plane_sums, grad_mixed = lax.optimization_barrier((parts, plane_sums, grad_mixed))
-    summed = scatter_line(plane_sums, "line", 0)
+    parts, grad_mixed = lax.optimization_barrier((parts, grad_mixed))
     parts = parts.reshape(group, share, 3 * lanes)
     parts = lax.all_to_all(parts, seq, split_axis=0, concat_axis=0, tiled=True)
     parts = parts.astype(jnp.float32)

time: 632 us -> 678 us (1.073)
  starting transfers between devices: 61.9 us -> 98.4 us
  blocking collectives: 20.1 us -> 0 us
  waiting for transfers between devices: 265 us -> 283 us
  local copies, waits for them, and re-layouts: 65.9 us -> 73.8 us
    ppermute x6 -> x8, waiting for transfers between devices: 22.8 us -> 90.9 us  [scatter_line(): lax.ppermute(pick(1 - place), axis, [(0, 1), (1, 0)])]
    ppermute x6 -> x12, waiting for transfers between devices: 135 us -> 70 us  [the longest x6 59.5 us: line_pieces_two(): arrived.append((sign, pairs, lax.ppermute(moving[sign][0], axis, pairs)))]
    ppermute x6, waiting for transfers between devices: 28.3 us -> 70.9 us  [scatter_line(): moving = lax.ppermute(payload, axis, pairs)]
    ppermute x6, starting transfers between devices: 10.5 us -> 30.8 us  [scatter_line(): moving = lax.ppermute(payload, axis, pairs)]
    all_to_all x1 -> x0, blocking collectives: 20.1 us -> none  [on_device(): lax.all_to_all(parts.reshape(count, small_rows * share), everyone, split_...]
    all_to_all x1, waiting for transfers between devices: 13.7 us -> 0.01 us  [on_device(): lax.all_to_all(grad_attended.reshape(rows, group, lanes).transpose(1, 0,...]
    select_n x3 -> x7, other arithmetic: 1.65 us -> 14.3 us  [line_order(): jnp.where(place == 0, jnp.stack([value, other]), jnp.stack([other, value]))]
    all_to_all x1, waiting for transfers between devices: 10.9 us -> 0.01 us  [on_device(): lax.all_to_all(grad_mixed_stream.reshape(group, rows, 3 * lanes), seq, sp...]
  transfers between devices with their start and end apart: 38 -> 52, of which waited for: 19 -> 20; matrix products, arithmetic and copies ran while one was open for 16% -> 19% of each run, Pallas kernels for 14% -> 11%
where the time goes in v5:
time: 678 us; the launch traced here: 671 us
  waiting for transfers between devices  283 us (42%)
  Pallas kernels  123 us (18%)
  starting transfers between devices  98.4 us (15%)
  local copies, waits for them, and re-layouts  73.8 us (11%)
  other arithmetic  62.3 us (9%)
  between operations  16 us (2%)
  matrix products  14.6 us (2%)
    ppermute x8, waiting for transfers between devices, scatter_line(): lax.ppermute(pick(1 - place), axis, [(0, 1), (1, 0)])  90.9 us
    ppermute x6, waiting for transfers between devices, scatter_line(): moving = lax.ppermute(payload, axis, pairs)  70.9 us
    ppermute x6, waiting for transfers between devices, line_pieces_two(): arrived.append((sign, pairs, lax.ppermute(moving[sign][0], axis, pairs)))  59.5 us
    pallas_call x1, Pallas kernels, mlp(): pl.pallas_call(mlp_kernel, grid=(half // units,), in_specs=[fixed] * 4 +...  37.5 us
    pallas_call x1, Pallas kernels, attend_back(): pl.pallas_call(attend_back_kernel, grid_spec=pltpu.PrefetchScalarGridSpec...  34.7 us
    ppermute x6, starting transfers between devices, scatter_line(): moving = lax.ppermute(payload, axis, pairs)  30.8 us
    pallas_call x1, Pallas kernels, attend(): pl.pallas_call(attend_kernel, grid_spec=pltpu.PrefetchScalarGridSpec(num_...  26.3 us
    ppermute x6, waiting for transfers between devices, line_pieces(): other = lax.ppermute(value, axis, [(0, 1), (1, 0)])  22.2 us
  transfers between devices with their start and end apart: 52, of which 20 were waited for; matrix products, arithmetic and copies ran while one was open for 19% of the time, Pallas kernels for 11%

profile of v5, /device:TPU:0, one launch (start us, length us, event | category | flops | bytes accessed | tf_op | source)
XLA Modules:
  0.0 671.4 jit_solution(4361176632181038132)
XLA Ops:
  12.2 5.9 collective-permute-start.3
  20.6 5.9 all-to-all-start
  26.5 5.8 collective-permute-done.3
  32.3 5.3 collective-permute-done.4
  37.5 4.3 collective-permute-start.7
  43.1 1.6 collective-permute-start
  47.5 1.9 collective-permute-done
  49.5 1.6 collective-permute-start.1
  51.2 7.9 %collective-permute-done.1 = bf16[2,8,34,384]{3,2,1,0:T(8,128)(2,1)} collective-permute-done((bf16[2,8,34,384]{3,2,1,0:T(8,128)(2,1)S(1)}, bf16[2,8,34,384]{3,2,1,0:T(8,128)(2,1)}, u32[]{:S(2)}, u32[]{:S(2)}) %collective-permute-start.1) | collective-permute-done | bytes 417824 | tf_op jit(solution)/shard_map/ppermute | solution.py:469
  60.6 19.3 %collective-permute-done.6 = bf16[320,1024]{1,0:T(8,128)(2,1)} collective-permute-done((bf16[320,1024]{1,0:T(8,128)(2,1)}, bf16[320,1024]{1,0:T(8,128)(2,1)}, u32[]{:S(2)}, u32[]{:S(2)}) %collective-permute-start.6) | collective-permute-done | bytes 655392 | tf_op jit(solution)/shard_map/ppermute | solution.py:491
  80.0 1.6 collective-permute-start.11
  89.9 29.1 %collective-permute-done.10 = bf16[320,1024]{1,0:T(8,128)(2,1)S(1)} collective-permute-done((bf16[320,1024]{1,0:T(8,128)(2,1)}, bf16[320,1024]{1,0:T(8,128)(2,1)S(1)}, u32[]{:S(2)}, u32[]{:S(2)}) %collective-permute-start.10) | collective-permute-done | bytes 655392 | tf_op jit(solution)/shard_map/ppermute | solution.py:491
  119.7 1.8 collective-permute-start.16
  127.4 1.6 collective-permute-start.13
  131.6 10.5 %collective-permute-done.16 = bf16[512,1024]{1,0:T(8,128)(2,1)S(1)} collective-permute-done((bf16[512,1024]{1,0:T(8,128)(2,1)}, bf16[512,1024]{1,0:T(8,128)(2,1)S(1)}, u32[]{:S(2)}, u32[]{:S(2)}) %collective-permute-start.16) | collective-permute-done | bytes 1048608 | tf_op jit(solution)/shard_map/ppermute | solution.py:496
  147.8 5.6 collective-permute-done.13
  155.0 1.6 collective-permute-start.17
  156.6 2.5 broadcast.139.clone.1
  168.0 14.2 %norm_mix.1 = (bf16[4096,1024]{1,0:T(8,128)(2,1)}, bf16[4096,128]{1,0:T(8,128)(2,1)}, bf16[4096,128]{1,0:T(8,128)(2,1)}, bf16[4096,128]{1,0:T(8,128)(2,1)}) custom-call(s32[1]{0:T(128)} %bitcast.36.core_ref, bf16[2048,1024]{1,0:T(8,128)(2,1)} %bitcast.245, bf16[2048,1024]{1,0:T(8,128)(2,1)} %bitcast.44.other_ref, f32[1,1024]{1,0:T(1,128)} %slice.153.gain_ref, ...), custom_call_target="tpu_custom_call" | custom-call | flops 3221225472 | bytes 16777216 | tf_op jit(solution)/shard_map/norm_mix/pallas_call | solution.py:240
  182.2 26.3 %attend_forward.1 = (f32[4096,128]{1,0:T(8,128)}, bf16[4096,128]{1,0:T(8,128)(2,1)}, f32[4096,128]{1,0:T(8,128)}) custom-call(s32[2]{0:T(128)} %select_reduce_fusion.starts_ref, bf16[4096,128]{1,0:T(8,128)(2,1)} %get-tuple-element.73.q_ref, bf16[4096,128]{1,0:T(8,128)(2,1)} %get-tuple-element.74.k_ref, bf16[4096,128]{1,0:T(8,128)(2,1)} %get-tuple-element.75.v_ref), custom_call_target="tpu_custom_call" | custom-call | flops 4060086272 | bytes 8388608 | tf_op jit(solution)/shard_map/attend_forward/pallas_call | solution.py:116
  208.5 6.0 collective-permute-done.17
  214.5 5.9 maximum_select_fusion
  220.4 5.9 maximum_select_fusion.1
  227.7 3.7 all-to-all-start.1
  234.4 2.0 convert_reduce_fusion
  241.1 16.8 %all-to-all-done.1 = bf16[8,512,128]{1,2,0:T(8,128)(2,1)S(1)} async-done(((bf16[8,512,128]{1,2,0:T(8,128)(2,1)}), bf16[8,512,128]{1,2,0:T(8,128)(2,1)S(1)}, u32[]{:S(2)}, u32[]{:S(2)}) %all-to-all-start.1) | async-done | bytes 1048608 | tf_op jit(solution)/shard_map/all_to_all | solution.py:721
  258.9 4.8 fusion.46
  270.5 4.8 slice.168.down_ref
  275.4 37.5 %mlp_both_ways.1 = (bf16[16,128,1024]{2,1,0:T(8,128)(2,1)}, bf16[16,128,1024]{2,1,0:T(8,128)(2,1)}, f32[512,1024]{1,0:T(8,128)}, f32[512,1024]{1,0:T(8,128)}, f3...) custom-call(bf16[512,1024]{1,0:T(8,128)(2,1)} %add_convert_fusion.1.own_ref, ...), custom_call_target="tpu_custom_call" | custom-call | flops 25769803776 | bytes 29360128 | tf_op jit(solution)/shard_map/mlp_both_ways/pallas_call | solution.py:344
  312.9 3.1 dynamic-slice_bitcast_fusion
  319.5 1.9 reshape.419
  321.4 1.7 copy.123
  323.1 2.0 dynamic-slice_bitcast_fusion.1
  326.1 42.6 %collective-permute-done.36 = bf16[2,4,128,1024]{3,2,1,0:T(8,128)(2,1)} collective-permute-done((bf16[2,4,128,1024]{3,2,1,0:T(8,128)(2,1)}, bf16[2,4,128,1024]{3,2,1,0:T(8,128)(2,1)}, u32[]{:S(2)}, u32[]{:S(2)}) %collective-permute-start.36) | collective-permute-done | bytes 2097184 | tf_op jit(solution)/shard_map/ppermute | solution.py:531
  368.6 2.6 fusion
  374.5 3.2 multiply_reduce_fusion.1
  377.8 4.4 multiply_reduce_fusion
  390.9 1.5 collective-permute-start.33
  394.9 4.2 all-to-all-start.2
  399.2 37.1 %collective-permute-done.34 = bf16[2,4,64,1024]{3,2,1,0:T(8,128)(2,1)} collective-permute-done((bf16[2,4,64,1024]{3,2,1,0:T(8,128)(2,1)}, bf16[2,4,64,1024]{3,2,1,0:T(8,128)(2,1)}, u32[]{:S(2)}, u32[]{:S(2)}) %collective-permute-start.34) | collective-permute-done | bytes 1048608 | tf_op jit(solution)/shard_map/ppermute | solution.py:531
  436.3 1.9 fusion.3
  438.9 1.6 fusion.2
  440.5 1.6 fusion.4
  442.1 9.4 %collective-permute-done.35 = bf16[4,64,1024]{2,1,0:T(8,128)(2,1)S(1)} collective-permute-done((bf16[4,64,1024]{2,1,0:T(8,128)(2,1)S(1)}, bf16[4,64,1024]{2,1,0:T(8,128)(2,1)S(1)}, u32[]{:S(2)}, u32[]{:S(2)}) %collective-permute-start.35) | collective-permute-done | bytes 524320 | tf_op jit(solution)/shard_map/ppermute | solution.py:531
  453.2 2.2 collective-permute-start.38
  455.4 34.7 %attend_backward.1 = bf16[4096,384]{1,0:T(8,128)(2,1)} custom-call(s32[2]{0:T(128)} %select_reduce_fusion.starts_ref, bf16[4096,128]{1,0:T(8,128)(2,1)} %get-tuple-element.73.q_ref, bf16[4096,128]{1,0:T(8,128)(2,1)} %get-tuple-element.74.k_ref, bf16[4096,128]{1,0:T(8,128)(2,1)} %get-tuple-element.75.v_ref, f32[4096,128]{1,0:T(8,128)} %get-tuple-element.84.wide_ref, ...), custom_call_target="tpu_custom_call" | custom-call | flops 10150215680 | bytes 11534336 | tf_op jit(solution)/shard_map/attend_backward/pallas_call | solution.py:196
  490.1 4.4 all-to-all-start.3
  496.6 4.1 collective-permute-start.39
  500.7 59.5 %collective-permute-done.39 = bf16[320,1024]{1,0:T(8,128)(2,1)S(1)} collective-permute-done((bf16[320,1024]{1,0:T(8,128)(2,1)S(1)}, bf16[320,1024]{1,0:T(8,128)(2,1)S(1)}, u32[]{:S(2)}, u32[]{:S(2)}) %collective-permute-start.39) | collective-permute-done | bytes 655392 | tf_op jit(solution)/shard_map/ppermute | solution.py:541
  560.2 1.7 fusion.9
  561.9 1.6 collective-permute-start.42
  563.5 7.2 %convolution_convert_fusion.2 = bf16[1024,384]{1,0:T(8,128)(2,1)S(1)} fusion(bf16[4096,1024]{1,0:T(8,128)(2,1)} %get-tuple-element.83, bf16[4096,384]{1,0:T(8,128)(2,1)S(1)} %copy-done.9), kind=kOutput, calls=%fused_computation.36 | convolution fusion | flops 3221618688 | bytes 12320768 | tf_op jit(solution)/shard_map/dot_general | solution.py:41
  572.7 20.9 %collective-permute-start.40 = (bf16[320,1024]{1,0:T(8,128)(2,1)}, bf16[320,1024]{1,0:T(8,128)(2,1)}, u32[]{:S(2)}, u32[]{:S(2)}) collective-permute-start(bf16[320,1024]{1,0:T(8,128)(2,1)} %get-tuple-element.141), channel_id=1, source_target_pairs={{0,2},{2,4},{4,6},{1,3},{3,5},{5,7},{8,10},{10,12},{12,14},{9,11},... | collective-permute-start | bytes 1966088 | tf_op jit(solution)/shard_map/ppermute | solution.py:541
  593.6 2.2 fusion.7
  603.8 1.7 collective-permute-done.31
  605.5 1.7 fusion.19
  607.2 11.4 %collective-permute-done.43 = bf16[320,1024]{1,0:T(8,128)(2,1)} collective-permute-done((bf16[320,1024]{1,0:T(8,128)(2,1)}, bf16[320,1024]{1,0:T(8,128)(2,1)}, u32[]{:S(2)}, u32[]{:S(2)}) %collective-permute-start.43) | collective-permute-done | bytes 655392 | tf_op jit(solution)/shard_map/ppermute | solution.py:541
  618.6 1.6 fusion.11
  624.0 4.1 all-to-all-start.4
  629.5 1.7 multiply_subtract_fusion.3
  631.1 5.3 all-to-all-done.4
  636.9 10.6 %finish_input.1 = (f32[512,1024]{1,0:T(8,128)}, f32[1,1024]{1,0:T(1,128)}, f32[1,1024]{1,0:T(1,128)}, f32[3,1,1024]{2,1,0:T(1,128)}) custom-call(bf16[8,512,384]{2,1,0:T(8,128)(2,1)} %all-to-all-done.3.grad_ref, bf16[32,96,1024]{2,1,0:T(8,128)(2,1)} %all-gather.2.cloned.1.call-done.weight_ref, bf16[512,1024]{1,0:T(8,128)(2,1)} %x_ref.1, ...), custom_call_target="tpu_custom_call" | custom-call | flops 3221225472 | bytes 16777216 | tf_op jit(solution)/shard_map/finish_input/pallas_call | solution.py:431
  652.9 2.6 all-to-all-start.5
  656.8 6.1 all-to-all-done.5
  (371 shorter events, 109.5 us)
Async XLA Ops:
  10.0 1.6 collective-permute-start.2
  12.1 25.4 %copy-start.4 = (bf16[512,1024]{1,0:T(8,128)(2,1)S(1)}, bf16[512,1024]{1,0:T(8,128)(2,1)}, u32[]{:S(2)}) copy-start(bf16[512,1024]{1,0:T(8,128)(2,1)} %x_ref.1) | copy-start | bytes 3145732
  12.2 20.1 %collective-permute-start.3 = (bf16[320,1024]{1,0:T(8,128)(2,1)S(1)}, bf16[320,1024]{1,0:T(8,128)(2,1)}, u32[]{:S(2)}, u32[]{:S(2)}) collective-permute-start(bf16[320,1024]{1,0:T(8,128)(2,1)S(1)} %pad_maximum_fusion.2), channel_id=1, source_target_pairs={{0,2},{2,4},{4,6},{1,3},{3,5},{5,7},{8,10},{10,12},{12,14},{9,11},... | collective-permute-start | bytes 1966088 | tf_op jit(solution)/shard_map/ppermute | solution.py:491
  18.1 19.5 %collective-permute-start.4 = (bf16[320,1024]{1,0:T(8,128)(2,1)S(1)}, bf16[320,1024]{1,0:T(8,128)(2,1)}, u32[]{:S(2)}, u32[]{:S(2)}) collective-permute-start(bf16[320,1024]{1,0:T(8,128)(2,1)S(1)} %pad_maximum_fusion.2), channel_id=1, source_target_pairs={{2,0},{4,2},{6,4},{3,1},{5,3},{7,5},{10,8},{12,10},{14,12},{11,9},... | collective-permute-start | bytes 1966088 | tf_op jit(solution)/shard_map/ppermute | solution.py:491
  20.6 22.6 %all-to-all-start = ((bf16[8,34,384]{2,1,0:T(8,128)(2,1)}), bf16[8,34,384]{2,1,0:T(8,128)(2,1)S(1)}, u32[]{:S(2)}, u32[]{:S(2)}) async-start(bf16[8,34,384]{2,1,0:T(8,128)(2,1)} %pad_maximum_fusion.3), calls=%async_computation | async-start | bytes 491520 | tf_op jit(solution)/shard_map/all_to_all | solution.py:654
  37.5 42.4 %collective-permute-start.7 = (bf16[512,1024]{1,0:T(8,128)(2,1)S(1)}, bf16[512,1024]{1,0:T(8,128)(2,1)}, u32[]{:S(2)}, u32[]{:S(2)}) collective-permute-start(bf16[512,1024]{1,0:T(8,128)(2,1)S(1)} %copy-done.4), channel_id=1, source_target_pairs={{0,2},{2,4},{4,6},{1,3},{3,5},{5,7},{8,10},{10,12},{12,14},{9,11},... | collective-permute-start | bytes 3145736 | tf_op jit(solution)/shard_map/ppermute | solution.py:496
  41.8 38.1 %collective-permute-start.8 = (bf16[512,1024]{1,0:T(8,128)(2,1)S(1)}, bf16[512,1024]{1,0:T(8,128)(2,1)}, u32[]{:S(2)}, u32[]{:S(2)}) collective-permute-start(bf16[512,1024]{1,0:T(8,128)(2,1)S(1)} %copy-done.4), channel_id=1, source_target_pairs={{2,0},{4,2},{6,4},{3,1},{5,3},{7,5},{10,8},{12,10},{14,12},{11,9},... | collective-permute-start | bytes 3145736 | tf_op jit(solution)/shard_map/ppermute | solution.py:496
  43.1 6.3 collective-permute-start
  44.7 15.9 %collective-permute-start.5 = (bf16[320,1024]{1,0:T(8,128)(2,1)}, bf16[320,1024]{1,0:T(8,128)(2,1)}, u32[]{:S(2)}, u32[]{:S(2)}) collective-permute-start(bf16[320,1024]{1,0:T(8,128)(2,1)} %collective-permute-done.3), channel_id=1, source_target_pairs={{2,4},{4,6},{3,5},{5,7},{10,12},{12,14},{11,13},{13,15},{18,20},{2... | collective-permute-start | bytes 1966088 | tf_op jit(solution)/shard_map/ppermute | solution.py:491
  46.2 33.8 %collective-permute-start.6 = (bf16[320,1024]{1,0:T(8,128)(2,1)}, bf16[320,1024]{1,0:T(8,128)(2,1)}, u32[]{:S(2)}, u32[]{:S(2)}) collective-permute-start(bf16[320,1024]{1,0:T(8,128)(2,1)} %collective-permute-done.4), channel_id=1, source_target_pairs={{2,0},{4,2},{3,1},{5,3},{10,8},{12,10},{11,9},{13,11},{18,16},{20,... | collective-permute-start | bytes 1966088 | tf_op jit(solution)/shard_map/ppermute | solution.py:491
  49.5 9.6 %collective-permute-start.1 = (bf16[2,8,34,384]{3,2,1,0:T(8,128)(2,1)S(1)}, bf16[2,8,34,384]{3,2,1,0:T(8,128)(2,1)}, u32[]{:S(2)}, u32[]{:S(2)}) collective-permute-start(bf16[2,8,34,384]{3,2,1,0:T(8,128)(2,1)S(1)} %maximum_select_fusion.6), channel_id=1, source_target_pairs={{0,16},{16,0},{1,17},{17,1},{2,18},{18,2},{3,19},{19,3},{4,20},{20... | collective-permute-start | bytes 1253384 | tf_op jit(solution)/shard_map/ppermute | solution.py:469
  80.0 39.0 %collective-permute-start.11 = (bf16[512,1024]{1,0:T(8,128)(2,1)}, bf16[512,1024]{1,0:T(8,128)(2,1)}, u32[]{:S(2)}, u32[]{:S(2)}) collective-permute-start(bf16[512,1024]{1,0:T(8,128)(2,1)} %collective-permute-done.7), channel_id=1, source_target_pairs={{2,4},{4,6},{3,5},{5,7},{10,12},{12,14},{11,13},{13,15},{18,20},{2... | collective-permute-start | bytes 3145736 | tf_op jit(solution)/shard_map/ppermute | solution.py:496
  81.6 37.4 %collective-permute-start.12 = (bf16[512,1024]{1,0:T(8,128)(2,1)}, bf16[512,1024]{1,0:T(8,128)(2,1)}, u32[]{:S(2)}, u32[]{:S(2)}) collective-permute-start(bf16[512,1024]{1,0:T(8,128)(2,1)} %collective-permute-done.8), channel_id=1, source_target_pairs={{2,0},{4,2},{3,1},{5,3},{10,8},{12,10},{11,9},{13,11},{18,16},{20,... | collective-permute-start | bytes 3145736 | tf_op jit(solution)/shard_map/ppermute | solution.py:496
  84.0 37.9 %copy-start.23 = (f32[32,14,32]{2,1,0:T(8,128)}, f32[32,14,32]{2,1,0:T(8,128)S(1)}, u32[]{:S(2)}) copy-start(f32[32,14,32]{2,1,0:T(8,128)S(1)} %reshape.446) | copy-start | bytes 172036
  86.5 3.3 collective-permute-start.9
  87.2 31.7 %collective-permute-start.10 = (bf16[320,1024]{1,0:T(8,128)(2,1)}, bf16[320,1024]{1,0:T(8,128)(2,1)S(1)}, u32[]{:S(2)}, u32[]{:S(2)}) collective-permute-start(bf16[320,1024]{1,0:T(8,128)(2,1)} %collective-permute-done.6), channel_id=1, source_target_pairs={{2,0},{3,1},{10,8},{11,9},{18,16},{19,17},{26,24},{27,25}} | collective-permute-start | bytes 1966088 | tf_op jit(solution)/shard_map/ppermute | solution.py:491
  119.0 11.5 %collective-permute-start.15 = (bf16[512,1024]{1,0:T(8,128)(2,1)}, bf16[512,1024]{1,0:T(8,128)(2,1)S(1)}, u32[]{:S(2)}, u32[]{:S(2)}) collective-permute-start(bf16[512,1024]{1,0:T(8,128)(2,1)} %collective-permute-done.11), channel_id=1, source_target_pairs={{4,6},{5,7},{12,14},{13,15},{20,22},{21,23},{28,30},{29,31}} | collective-permute-start | bytes 3145736 | tf_op jit(solution)/shard_map/ppermute | solution.py:496
  119.7 22.4 %collective-permute-start.16 = (bf16[512,1024]{1,0:T(8,128)(2,1)}, bf16[512,1024]{1,0:T(8,128)(2,1)S(1)}, u32[]{:S(2)}, u32[]{:S(2)}) collective-permute-start(bf16[512,1024]{1,0:T(8,128)(2,1)} %collective-permute-done.12), channel_id=1, source_target_pairs={{2,0},{3,1},{10,8},{11,9},{18,16},{19,17},{26,24},{27,25}} | collective-permute-start | bytes 3145736 | tf_op jit(solution)/shard_map/ppermute | solution.py:496
  127.4 26.0 %collective-permute-start.13 = (bf16[4,160,1024]{2,1,0:T(8,128)(2,1)S(1)}, bf16[4,160,1024]{2,1,0:T(8,128)(2,1)S(1)}, u32[]{:S(2)}, u32[]{:S(2)}) collective-permute-start(bf16[4,160,1024]{2,1,0:T(8,128)(2,1)S(1)} %get-tuple-element.148), channel_id=1, source_target_pairs={{0,8},{8,0},{1,9},{9,1},{2,10},{10,2},{3,11},{11,3},{4,12},{12,4},... | collective-permute-start | bytes 3932168 | tf_op jit(solution)/shard_map/ppermute | solution.py:469
  128.9 25.7 %collective-permute-start.14 = (bf16[4,160,1024]{2,1,0:T(8,128)(2,1)S(1)}, bf16[4,160,1024]{2,1,0:T(8,128)(2,1)S(1)}, u32[]{:S(2)}, u32[]{:S(2)}) collective-permute-start(bf16[4,160,1024]{2,1,0:T(8,128)(2,1)S(1)} %get-tuple-element.147), channel_id=1, source_target_pairs={{0,16},{16,0},{1,17},{17,1},{2,18},{18,2},{3,19},{19,3},{4,20},{20... | collective-permute-start | bytes 3932168 | tf_op jit(solution)/shard_map/ppermute | solution.py:469
  130.4 29.7 %collective-permute-start.21 = (bf16[512,1024]{1,0:T(8,128)(2,1)}, bf16[512,1024]{1,0:T(8,128)(2,1)S(1)}, u32[]{:S(2)}, u32[]{:S(2)}) collective-permute-start(bf16[512,1024]{1,0:T(8,128)(2,1)} %collective-permute-done.11), channel_id=1, source_target_pairs={{0,1},{1,0},{2,3},{3,2},{4,5},{5,4},{6,7},{7,6},{8,9},{9,8},{10,11... | collective-permute-start | bytes 3145736 | tf_op jit(solution)/shard_map/ppermute | solution.py:463
  130.4 24.6 %collective-permute-start.19 = (bf16[512,1024]{1,0:T(8,128)(2,1)S(1)}, bf16[512,1024]{1,0:T(8,128)(2,1)S(1)}, u32[]{:S(2)}, u32[]{:S(2)}) collective-permute-start(bf16[512,1024]{1,0:T(8,128)(2,1)S(1)} %collective-permute-done.15), channel_id=1, source_target_pairs={{0,1},{1,0},{2,3},{3,2},{4,5},{5,4},{6,7},{7,6},{8,9},{9,8},{10,11... | collective-permute-start | bytes 3145736 | tf_op jit(solution)/shard_map/ppermute | solution.py:463
  142.1 18.2 %collective-permute-start.20 = (bf16[512,1024]{1,0:T(8,128)(2,1)S(1)}, bf16[512,1024]{1,0:T(8,128)(2,1)S(1)}, u32[]{:S(2)}, u32[]{:S(2)}) collective-permute-start(bf16[512,1024]{1,0:T(8,128)(2,1)S(1)} %collective-permute-done.16), channel_id=1, source_target_pairs={{0,1},{1,0},{2,3},{3,2},{4,5},{5,4},{6,7},{7,6},{8,9},{9,8},{10,11... | collective-permute-start | bytes 3145736 | tf_op jit(solution)/shard_map/ppermute | solution.py:463
  153.4 9.2 %collective-permute-start.22 = (bf16[512,1024]{1,0:T(8,128)(2,1)}, bf16[512,1024]{1,0:T(8,128)(2,1)S(1)}, u32[]{:S(2)}, u32[]{:S(2)}) collective-permute-start(bf16[512,1024]{1,0:T(8,128)(2,1)} %collective-permute-done.12), channel_id=1, source_target_pairs={{0,1},{1,0},{2,3},{3,2},{4,5},{5,4},{6,7},{7,6},{8,9},{9,8},{10,11... | collective-permute-start | bytes 3145736 | tf_op jit(solution)/shard_map/ppermute | solution.py:463
  154.6 10.3 %collective-permute-start.23 = (bf16[512,1024]{1,0:T(8,128)(2,1)}, bf16[512,1024]{1,0:T(8,128)(2,1)S(1)}, u32[]{:S(2)}, u32[]{:S(2)}) collective-permute-start(bf16[512,1024]{1,0:T(8,128)(2,1)} %collective-permute-done.7), channel_id=1, source_target_pairs={{0,1},{1,0},{2,3},{3,2},{4,5},{5,4},{6,7},{7,6},{8,9},{9,8},{10,11... | collective-permute-start | bytes 3145736 | tf_op jit(solution)/shard_map/ppermute | solution.py:463
  155.0 59.4 %collective-permute-start.17 = (bf16[2,4,160,1024]{3,2,1,0:T(8,128)(2,1)S(1)}, bf16[2,4,160,1024]{3,2,1,0:T(8,128)(2,1)}, u32[]{:S(2)}, u32[]{:S(2)}) collective-permute-start(bf16[2,4,160,1024]{3,2,1,0:T(8,128)(2,1)S(1)} %maximum_select_fusion.2), channel_id=1, source_target_pairs={{0,16},{16,0},{1,17},{17,1},{2,18},{18,2},{3,19},{19,3},{4,20},{20... | collective-permute-start | bytes 7864328 | tf_op jit(solution)/shard_map/ppermute | solution.py:469
  160.2 5.7 collective-permute-start.24
  160.4 60.0 %collective-permute-start.18 = (bf16[2,4,160,1024]{3,2,1,0:T(8,128)(2,1)S(1)}, bf16[2,4,160,1024]{3,2,1,0:T(8,128)(2,1)}, u32[]{:S(2)}, u32[]{:S(2)}) collective-permute-start(bf16[2,4,160,1024]{3,2,1,0:T(8,128)(2,1)S(1)} %maximum_select_fusion.3), channel_id=1, source_target_pairs={{0,8},{8,0},{1,9},{9,1},{2,10},{10,2},{3,11},{11,3},{4,12},{12,4},... | collective-permute-start | bytes 7864328 | tf_op jit(solution)/shard_map/ppermute | solution.py:469
  162.6 4.4 collective-permute-start.25
  227.7 30.3 %all-to-all-start.1 = ((bf16[8,512,128]{1,2,0:T(8,128)(2,1)}), bf16[8,512,128]{1,2,0:T(8,128)(2,1)S(1)}, u32[]{:S(2)}, u32[]{:S(2)}) async-start(bf16[8,512,128]{1,2,0:T(8,128)(2,1)} %copy.120), calls=%async_computation.1 | async-start | bytes 2097152 | tf_op jit(solution)/shard_map/all_to_all | solution.py:721
  231.4 405.6 %all-gather.2.cloned.1.call-start = ((), (), s32[]{:S(2)}) async-start(), calls=%async_computation.6 | async-start | bytes 6488064 | tf_op jit(solution)/shard_map/all_gather | solution.py:727
  236.5 38.9 %collective-permute-start.27 = (bf16[512,1024]{1,0:T(8,128)(2,1)}, bf16[512,1024]{1,0:T(8,128)(2,1)}, u32[]{:S(2)}, u32[]{:S(2)}) collective-permute-start(bf16[512,1024]{1,0:T(8,128)(2,1)} %get-tuple-element.117.gm_own_ref), channel_id=1, source_target_pairs={{0,1},{1,0},{2,3},{3,2},{4,5},{5,4},{6,7},{7,6},{8,9},{9,8},{10,11... | collective-permute-start | bytes 3145736 | tf_op jit(solution)/shard_map/ppermute | solution.py:463
  266.1 9.3 %collective-permute-start.26 = (bf16[512,1024]{1,0:T(8,128)(2,1)}, bf16[512,1024]{1,0:T(8,128)(2,1)}, u32[]{:S(2)}, u32[]{:S(2)}) collective-permute-start(bf16[512,1024]{1,0:T(8,128)(2,1)} %add_convert_fusion.1.own_ref), channel_id=1, source_target_pairs={{0,1},{1,0},{2,3},{3,2},{4,5},{5,4},{6,7},{7,6},{8,9},{9,8},{10,11... | collective-permute-start | bytes 3145736 | tf_op jit(solution)/shard_map/ppermute | solution.py:463
  316.1 52.6 %collective-permute-start.36 = (bf16[2,4,128,1024]{3,2,1,0:T(8,128)(2,1)}, bf16[2,4,128,1024]{3,2,1,0:T(8,128)(2,1)}, u32[]{:S(2)}, u32[]{:S(2)}) collective-permute-start(bf16[2,4,128,1024]{3,2,1,0:T(8,128)(2,1)} %dynamic-slice_bitcast_fusion), channel_id=1, source_target_pairs={{0,16},{16,0},{1,17},{17,1},{2,18},{18,2},{3,19},{19,3},{4,20},{20... | collective-permute-start | bytes 6291464 | tf_op jit(solution)/shard_map/ppermute | solution.py:531
  317.6 56.8 %collective-permute-start.29 = (f32[512,1024]{1,0:T(8,128)}, f32[512,1024]{1,0:T(8,128)}, u32[]{:S(2)}, u32[]{:S(2)}) collective-permute-start(f32[512,1024]{1,0:T(8,128)} %get-tuple-element.87), channel_id=1, source_target_pairs={{0,1},{1,0},{2,3},{3,2},{4,5},{5,4},{6,7},{7,6},{8,9},{9,8},{10,11... | collective-permute-start | bytes 6291464 | tf_op jit(solution)/shard_map/ppermute | solution.py:463
  317.8 59.9 %collective-permute-start.28 = (f32[512,1024]{1,0:T(8,128)}, f32[512,1024]{1,0:T(8,128)}, u32[]{:S(2)}, u32[]{:S(2)}) collective-permute-start(f32[512,1024]{1,0:T(8,128)} %get-tuple-element.82), channel_id=1, source_target_pairs={{0,1},{1,0},{2,3},{3,2},{4,5},{5,4},{6,7},{7,6},{8,9},{9,8},{10,11... | collective-permute-start | bytes 6291464 | tf_op jit(solution)/shard_map/ppermute | solution.py:463
  323.1 45.5 %copy-start.6 = (bf16[16,128,1024]{2,1,0:T(8,128)(2,1)S(1)}, bf16[16,128,1024]{2,1,0:T(8,128)(2,1)}, u32[]{:S(2)}) copy-start(bf16[16,128,1024]{2,1,0:T(8,128)(2,1)} %get-tuple-element.93) | copy-start | bytes 12582916
  325.2 63.7 %collective-permute-start.32 = (bf16[2,4,128,1024]{3,2,1,0:T(8,128)(2,1)S(1)}, bf16[2,4,128,1024]{3,2,1,0:T(8,128)(2,1)S(1)}, u32[]{:S(2)}, u32[]{:S(2)}) collective-permute-start(bf16[2,4,128,1024]{3,2,1,0:T(8,128)(2,1)S(1)} %dynamic-slice_bitcast_fusion.1), channel_id=1, source_target_pairs={{0,8},{8,0},{1,9},{9,1},{2,10},{10,2},{3,11},{11,3},{4,12},{12,4},... | collective-permute-start | bytes 6291464 | tf_op jit(solution)/shard_map/ppermute | solution.py:531
  373.6 65.3 %collective-permute-start.37 = (bf16[4,128,1024]{2,1,0:T(8,128)(2,1)}, bf16[4,128,1024]{2,1,0:T(8,128)(2,1)}, u32[]{:S(2)}, u32[]{:S(2)}) collective-permute-start(bf16[4,128,1024]{2,1,0:T(8,128)(2,1)} %dynamic-slice_bitcast_fusion.2), channel_id=1, source_target_pairs={{0,8},{8,0},{1,9},{9,1},{2,10},{10,2},{3,11},{11,3},{4,12},{12,4},... | collective-permute-start | bytes 3145736 | tf_op jit(solution)/shard_map/ppermute | solution.py:531
  387.7 48.6 %collective-permute-start.34 = (bf16[2,4,64,1024]{3,2,1,0:T(8,128)(2,1)}, bf16[2,4,64,1024]{3,2,1,0:T(8,128)(2,1)}, u32[]{:S(2)}, u32[]{:S(2)}) collective-permute-start(bf16[2,4,64,1024]{3,2,1,0:T(8,128)(2,1)} %dynamic-slice_bitcast_fusion.3), channel_id=1, source_target_pairs={{0,8},{8,0},{1,9},{9,1},{2,10},{10,2},{3,11},{11,3},{4,12},{12,4},... | collective-permute-start | bytes 3145736 | tf_op jit(solution)/shard_map/ppermute | solution.py:531
  390.9 49.6 %collective-permute-start.33 = (bf16[4,128,1024]{2,1,0:T(8,128)(2,1)}, bf16[4,128,1024]{2,1,0:T(8,128)(2,1)}, u32[]{:S(2)}, u32[]{:S(2)}) collective-permute-start(bf16[4,128,1024]{2,1,0:T(8,128)(2,1)} %dynamic-slice_bitcast_fusion.4), channel_id=1, source_target_pairs={{0,16},{16,0},{1,17},{17,1},{2,18},{18,2},{3,19},{19,3},{4,20},{20... | collective-permute-start | bytes 3145736 | tf_op jit(solution)/shard_map/ppermute | solution.py:531
  394.9 60.5 %all-to-all-start.2 = ((bf16[8,512,128]{2,1,0:T(8,128)(2,1)}), bf16[8,512,128]{2,1,0:T(8,128)(2,1)}, u32[]{:S(2)}, u32[]{:S(2)}) async-start(bf16[8,512,128]{2,1,0:T(8,128)(2,1)} %bitcast.229), calls=%async_computation.2 | async-start | bytes 2097152 | tf_op jit(solution)/shard_map/all_to_all | solution.py:755
  399.2 39.7 %copy-start.3 = (bf16[2,4,128,1024]{3,2,1,0:T(8,128)(2,1)S(1)}, bf16[2,4,128,1024]{3,2,1,0:T(8,128)(2,1)}, u32[]{:S(2)}) copy-start(bf16[2,4,128,1024]{3,2,1,0:T(8,128)(2,1)} %copy-done.2) | copy-start | bytes 6291460
  438.3 13.3 %collective-permute-start.35 = (bf16[4,64,1024]{2,1,0:T(8,128)(2,1)S(1)}, bf16[4,64,1024]{2,1,0:T(8,128)(2,1)S(1)}, u32[]{:S(2)}, u32[]{:S(2)}) collective-permute-start(bf16[4,64,1024]{2,1,0:T(8,128)(2,1)S(1)} %dynamic-slice_bitcast_fusion.7), channel_id=1, source_target_pairs={{0,16},{16,0},{1,17},{17,1},{2,18},{18,2},{3,19},{19,3},{4,20},{20... | collective-permute-start | bytes 1572872 | tf_op jit(solution)/shard_map/ppermute | solution.py:531
  453.2 42.0 %collective-permute-start.38 = (bf16[320,1024]{1,0:T(8,128)(2,1)}, bf16[320,1024]{1,0:T(8,128)(2,1)}, u32[]{:S(2)}, u32[]{:S(2)}) collective-permute-start(bf16[320,1024]{1,0:T(8,128)(2,1)} %get-tuple-element.143), channel_id=1, source_target_pairs={{0,2},{1,3},{8,10},{9,11},{16,18},{17,19},{24,26},{25,27}} | collective-permute-start | bytes 1966088 | tf_op jit(solution)/shard_map/ppermute | solution.py:541
  490.1 133.9 %all-to-all-start.3 = ((bf16[8,512,384]{2,1,0:T(8,128)(2,1)}), bf16[8,512,384]{2,1,0:T(8,128)(2,1)}, u32[]{:S(2)}, u32[]{:S(2)}) async-start(bf16[8,512,384]{2,1,0:T(8,128)(2,1)} %bitcast.248), calls=%async_computation.3 | async-start | bytes 6291456 | tf_op jit(solution)/shard_map/all_to_all | solution.py:773
  494.5 6.2 collective-permute-start.41
  496.6 66.9 %copy-start.9 = (bf16[4096,384]{1,0:T(8,128)(2,1)S(1)}, bf16[4096,384]{1,0:T(8,128)(2,1)}, u32[]{:S(2)}) copy-start(bf16[4096,384]{1,0:T(8,128)(2,1)} %attend_backward.1) | copy-start | bytes 9437188
  496.6 63.6 %collective-permute-start.39 = (bf16[320,1024]{1,0:T(8,128)(2,1)S(1)}, bf16[320,1024]{1,0:T(8,128)(2,1)S(1)}, u32[]{:S(2)}, u32[]{:S(2)}) collective-permute-start(bf16[320,1024]{1,0:T(8,128)(2,1)S(1)} %fusion.8), channel_id=1, source_target_pairs={{0,2},{2,4},{1,3},{3,5},{8,10},{10,12},{9,11},{11,13},{16,18},{18,... | collective-permute-start | bytes 1966088 | tf_op jit(solution)/shard_map/ppermute | solution.py:541
  561.9 31.7 %collective-permute-start.42 = (bf16[320,1024]{1,0:T(8,128)(2,1)}, bf16[320,1024]{1,0:T(8,128)(2,1)}, u32[]{:S(2)}, u32[]{:S(2)}) collective-permute-start(bf16[320,1024]{1,0:T(8,128)(2,1)} %get-tuple-element.142), channel_id=1, source_target_pairs={{4,2},{6,4},{5,3},{7,5},{12,10},{14,12},{13,11},{15,13},{20,18},{2... | collective-permute-start | bytes 1966088 | tf_op jit(solution)/shard_map/ppermute | solution.py:541
  571.6 28.0 %copy-start.65 = (f32[1,2048]{1,0:T(1,128)S(1)}, f32[1,2048]{1,0:T(1,128)}, u32[]{:S(2)}) copy-start(f32[1,2048]{1,0:T(1,128)} %get-tuple-element.97) | copy-start | bytes 24580
  571.6 28.8 %copy-start.60 = (f32[1024]{0:T(1024)S(1)}, f32[1024]{0:T(1024)}, u32[]{:S(2)}) copy-start(f32[1024]{0:T(1024)} %get-tuple-element.120) | copy-start | bytes 12292
  571.6 29.5 %copy-start.55 = (f32[1024]{0:T(1024)S(1)}, f32[1024]{0:T(1024)}, u32[]{:S(2)}) copy-start(f32[1024]{0:T(1024)} %get-tuple-element.118) | copy-start | bytes 12292
  571.6 30.1 %copy-start.53 = (f32[1024]{0:T(1024)S(1)}, f32[1024]{0:T(1024)}, u32[]{:S(2)}) copy-start(f32[1024]{0:T(1024)} %get-tuple-element.98) | copy-start | bytes 12292
  571.6 30.8 %copy-start.52 = (f32[1024]{0:T(1024)S(1)}, f32[1024]{0:T(1024)}, u32[]{:S(2)}) copy-start(f32[1024]{0:T(1024)} %get-tuple-element.100) | copy-start | bytes 12292
  571.6 31.5 %copy-start.54 = (f32[1024]{0:T(1024)S(1)}, f32[1024]{0:T(1024)}, u32[]{:S(2)}) copy-start(f32[1024]{0:T(1024)} %get-tuple-element.139) | copy-start | bytes 12292
  571.7 25.4 %collective-permute-start.30 = (bf16[2,256,384]{2,1,0:T(8,128)(2,1)S(1)}, bf16[2,256,384]{2,1,0:T(8,128)(2,1)}, u32[]{:S(2)}, u32[]{:S(2)}) collective-permute-start(bf16[2,256,384]{2,1,0:T(8,128)(2,1)S(1)} %dynamic-slice_bitcast_fusion.8), channel_id=1, source_target_pairs={{0,8},{8,0},{1,9},{9,1},{2,10},{10,2},{3,11},{11,3},{4,12},{12,4},... | collective-permute-start | bytes 1179656 | tf_op jit(solution)/shard_map/ppermute | solution.py:531
  572.7 24.4 %copy-start.25 = (bf16[1024,384]{1,0:T(8,128)(2,1)S(1)}, bf16[1024,384]{1,0:T(8,128)(2,1)}, u32[]{:S(2)}) copy-start(bf16[1024,384]{1,0:T(8,128)(2,1)} %copy-done.24) | copy-start | bytes 2359300
  572.7 34.5 %collective-permute-start.40 = (bf16[320,1024]{1,0:T(8,128)(2,1)}, bf16[320,1024]{1,0:T(8,128)(2,1)}, u32[]{:S(2)}, u32[]{:S(2)}) collective-permute-start(bf16[320,1024]{1,0:T(8,128)(2,1)} %get-tuple-element.141), channel_id=1, source_target_pairs={{0,2},{2,4},{4,6},{1,3},{3,5},{5,7},{8,10},{10,12},{12,14},{9,11},... | collective-permute-start | bytes 1966088 | tf_op jit(solution)/shard_map/ppermute | solution.py:541
  595.8 22.8 %collective-permute-start.43 = (bf16[320,1024]{1,0:T(8,128)(2,1)}, bf16[320,1024]{1,0:T(8,128)(2,1)}, u32[]{:S(2)}, u32[]{:S(2)}) collective-permute-start(bf16[320,1024]{1,0:T(8,128)(2,1)} %fusion.7), channel_id=1, source_target_pairs={{2,0},{4,2},{6,4},{3,1},{5,3},{7,5},{10,8},{12,10},{14,12},{11,9},... | collective-permute-start | bytes 1966088 | tf_op jit(solution)/shard_map/ppermute | solution.py:541
  598.9 6.6 collective-permute-start.31
  620.3 1.5 collective-permute-start.44
  624.0 12.4 %all-to-all-start.4 = ((bf16[8,32,384]{2,1,0:T(8,128)(2,1)}), bf16[8,32,384]{2,1,0:T(8,128)(2,1)S(1)}, u32[]{:S(2)}, u32[]{:S(2)}) async-start(bf16[8,32,384]{2,1,0:T(8,128)(2,1)} %bitcast.63), calls=%async_computation.4 | async-start | bytes 393216 | tf_op jit(solution)/shard_map/all_to_all | solution.py:783
  652.9 10.0 %all-to-all-start.5 = ((f32[32,1,448]{2,1,0:T(1,128)}), f32[32,1,448]{2,1,0:T(1,128)S(1)}, u32[]{:S(2)}, u32[]{:S(2)}) async-start(f32[32,1,448]{2,1,0:T(1,128)} %all_to_all.28), calls=%async_computation.5 | async-start | bytes 131072 | tf_op jit(solution)/shard_map/all_to_all | solution.py:816
  (57 other events, 405.2 us)
Sparse Core Ops, SparseCore 0:
  323.2 86.9 all-gather.1

commit v6 on v4

--- a/solution.py
+++ b/solution.py
@@ -261,18 +261,14 @@
     )(core, own, other, gain[None], shift[None], weight, bias[None])
 
 
-def mlp_kernel(
-    pieces,
-    core_ref,
-    h_ref,
-    gm_ref,
-    bias_ref,
-    *refs,
-):
+def mlp_kernel(pieces, core_ref, own_ref, other_ref, gm_own_ref, gm_other_ref, bias_ref, *refs):
     up_refs, down_refs = refs[:pieces], refs[pieces : 2 * pieces]
-    up_grad_ref, down_grad_ref, m_ref, gh_ref, bias_grad_ref, turned_ref = refs[2 * pieces :]
+    up_grad_ref, down_grad_ref, m_own_ref, m_other_ref, gh_own_ref, gh_other_ref = refs[
+        2 * pieces : 2 * pieces + 6
+    ]
+    bias_grad_ref, h_ref, gm_ref, turned_ref = refs[2 * pieces + 6 :]
     tile = pl.program_id(0)
-    width = h_ref.shape[1]
+    rows, width = own_ref.shape
     chips = up_grad_ref.shape[0]
     up_rows = width // chips
     units = bias_ref.shape[1]
@@ -280,8 +276,12 @@
 
     @pl.when(tile == 0)
     def clear():
-        m_ref[...] = jnp.zeros_like(m_ref)
-        gh_ref[...] = jnp.zeros_like(gh_ref)
+        for ref in (m_own_ref, m_other_ref, gh_own_ref, gh_other_ref):
+            ref[...] = jnp.zeros_like(ref)
+        h_ref[:rows] = own_ref[...]
+        h_ref[rows:] = other_ref[...]
+        gm_ref[:rows] = gm_own_ref[...]
+        gm_ref[rows:] = gm_other_ref[...]
         turned_ref[...] = h_ref[...].T
 
     weight_up = jnp.concatenate([ref[...].reshape(width, -1) for ref in up_refs], axis=1)
@@ -293,8 +293,12 @@
     active = (upward * normal).astype(jnp.bfloat16)
     grad_up = (inner_cols(gm, weight_down) * slope).astype(jnp.bfloat16)
     bias_grad_ref[...] = jnp.sum(grad_up.astype(jnp.float32), axis=0, keepdims=True)
-    m_ref[...] += plain_product(active, weight_down)
-    gh_ref[...] += inner_cols(grad_up, weight_up)
+    branch = plain_product(active, weight_down)
+    m_own_ref[...] += branch[:rows]
+    m_other_ref[...] += branch[rows:]
+    grad_norm = inner_cols(grad_up, weight_up)
+    gh_own_ref[...] += grad_norm[:rows]
+    gh_other_ref[...] += grad_norm[rows:]
     up_grad = plain_product(turned_ref[...], grad_up).astype(jnp.bfloat16)
     row = pl.multiple_of(tile // folds * up_rows, up_rows)
     column = pl.multiple_of(lax.rem(tile, folds) * units, units)
@@ -304,10 +308,8 @@
     down_grad_ref[...] = down_grad.reshape(down_grad_ref.shape)
 
 
-def mlp(core, normed, gm, weights, bias, chips):
-    rows, width = normed.shape
-    count = 2 * chips
-    share = width // count
+def mlp(core, own, other, gm_own, gm_other, weights, bias, chips):
+    rows, width = own.shape
     half = bias.shape[0]
     unit_block = half // chips
     units = 256
@@ -315,6 +317,8 @@
     once = dict(pipeline_mode=pl.Buffered(1))
     fixed = pl.BlockSpec((rows, width), lambda j, core: (0, 0), **once)
     if len(weights) == 1:
+        count = 2 * chips
+        share = width // count
         pieces = units // unit_block
         lane_blocks = width // unit_block
 
@@ -332,20 +336,15 @@
 
         weights = list(weights) * (2 * pieces)
         weight_specs = [up_spec(n) for n in range(pieces)] + [down_spec(n) for n in range(pieces)]
-        up_grad_shape = (chips, 2 * share * (half // width) + 2 * share, width)
-        down_grad_shape = (chips, unit_block, width)
+        up_shape, down_shape = (chips, half // chips, width), (chips, half // chips, width)
         down_grad_spec = pl.BlockSpec((pieces, unit_block, width), lambda j, core: (j, 0, 0))
     else:
         pieces = 1
-        block = jnp.arange(half) // unit_block * 2 + core[0]
-        index = block * unit_block + lax.rem(jnp.arange(half), unit_block)
-        weights = [jnp.take(weights[0], index, axis=1), jnp.take(weights[1], index, axis=0)]
         weight_specs = [
             pl.BlockSpec((width, units), lambda j, core: (0, j)),
             pl.BlockSpec((units, width), lambda j, core: (j, 0)),
         ]
-        up_grad_shape = (1, half // width * width, width)
-        down_grad_shape = (1, half, width)
+        up_shape, down_shape = (1, half // width * width, width), (1, half, width)
         down_grad_spec = pl.BlockSpec((1, units, width), lambda j, core: (0, j, 0))
     total = jax.ShapeDtypeStruct((rows, width), jnp.float32)
     outs = pl.pallas_call(
@@ -353,37 +352,38 @@
         grid_spec=pltpu.PrefetchScalarGridSpec(
             num_scalar_prefetch=1,
             grid=(half // units,),
-            in_specs=[fixed, fixed, pl.BlockSpec((1, units), lambda j, core: (0, j)), *weight_specs],
+            in_specs=[fixed] * 4 + [pl.BlockSpec((1, units), lambda j, core: (0, j)), *weight_specs],
             out_specs=[
-                pl.BlockSpec(up_grad_shape, lambda j, core: (0, 0, 0), **once),
+                pl.BlockSpec(up_shape, lambda j, core: (0, 0, 0), **once),
                 down_grad_spec,
-                fixed,
-                fixed,
+                *[fixed] * 4,
                 pl.BlockSpec((1, units), lambda j, core: (0, j)),
             ],
-            scratch_shapes=[pltpu.VMEM((width, rows), jnp.bfloat16)],
+            scratch_shapes=[
+                pltpu.VMEM((2 * rows, width), jnp.bfloat16),
+                pltpu.VMEM((2 * rows, width), jnp.bfloat16),
+                pltpu.VMEM((width, 2 * rows), jnp.bfloat16),
+            ],
         ),
         out_shape=(
-            jax.ShapeDtypeStruct(up_grad_shape, jnp.bfloat16),
-            jax.ShapeDtypeStruct(down_grad_shape, jnp.bfloat16),
-            total,
-            total,
+            jax.ShapeDtypeStruct(up_shape, jnp.bfloat16),
+            jax.ShapeDtypeStruct(down_shape, jnp.bfloat16),
+            *[total] * 4,
             jax.ShapeDtypeStruct((1, half), jnp.float32),
         ),
         compiler_params=pltpu.CompilerParams(vmem_limit_bytes=VMEM_BYTES),
         cost_estimate=pl.CostEstimate(
-            flops=rows * width * half * 12,
-            bytes_accessed=half * width * 8 + rows * width * 12,
-            transcendentals=rows * half * 2,
+            flops=2 * rows * width * half * 12,
+            bytes_accessed=half * width * 8 + rows * width * 24,
+            transcendentals=rows * half * 4,
         ),
         name="mlp_both_ways",
-    )(core, normed, gm, bias[None], *weights)
+    )(core, own, other, gm_own, gm_other, bias[None], *weights)
     up_grad, down_grad = outs[0], outs[1]
     if pieces == 1:
-        up_grad = up_grad.reshape(half // width, chips, 2 * share, width).swapaxes(0, 1)
+        up_grad = up_grad.reshape(half // width, chips, width // chips, width).swapaxes(0, 1)
         up_grad = up_grad.reshape(chips, -1, width)
-        up_grad = jnp.pad(up_grad, ((0, 0), (0, 2 * share), (0, 0)))
-        down_grad = down_grad.reshape(chips, unit_block, width)
+        down_grad = down_grad.reshape(chips, -1, width)
     return (up_grad, down_grad, *outs[2:])
 
 
@@ -509,6 +509,28 @@
     return sum(term.astype(jnp.float32) for term in terms).astype(jnp.bfloat16)
 
 
+def scatter_terms(value, axis, dim):
+    if lax.axis_size(axis) != 2:
+        return (scatter_line(value, axis, dim),)
+    place = lax.axis_index(axis)
+    pick = lambda slot: lax.dynamic_index_in_dim(value, slot, dim, keepdims=False)
+    return (pick(place), lax.ppermute(pick(1 - place), axis, [(0, 1), (1, 0)]))
+
+
+def scatter_direct(value, axis, dim):
+    place = lax.axis_index(axis)
+    size = lax.axis_size(axis)
+    pick = lambda slot: lax.dynamic_index_in_dim(
+        value, jnp.clip(slot, 0, size - 1), dim, keepdims=False
+    )
+    terms = [pick(place)]
+    for distance in range(size - 1, 0, -1):
+        for move in (-distance, distance):
+            pairs = [(i, i + move) for i in range(size) if 0 <= i + move < size]
+            terms.append(lax.ppermute(pick(place + move), axis, pairs))
+    return rounded_sum(*terms)
+
+
 def scatter_line(value, axis, dim):
     place = lax.axis_index(axis)
     size = lax.axis_size(axis)
@@ -573,25 +595,23 @@
             [jnp.where(first_core, own, other), jnp.where(first_core, other, own)], axis=axis
         )
 
+    half = FF // 2
     unit_block = FF // count
+    folds = half // width
+    up_end = 2 * share * folds
     low = lambda value: value.astype(jnp.bfloat16)
-    if share % 16 == 0 and unit_block == 128:
+    direct = share % 16 == 0 and unit_block == 128
+    pieces = line_pieces(tokens, "line")
+    if direct:
         fold = lambda value: low(value).reshape(share, -1, width).swapaxes(0, 1).reshape(-1, width)
-        packed = jnp.concatenate(
-            [fold(hidden_up), low(hidden_down), low(project_out), fold(project_in)], axis=0
-        )
+        packed = jnp.concatenate([fold(hidden_up), low(hidden_down), low(project_out)], axis=0)
+        pieces = dict(pieces)
+        begun = sorted(pieces, key=abs)[:4]
+        packed, *tied = lax.optimization_barrier((packed, *[pieces[n] for n in begun]))
+        pieces = list((pieces | dict(zip(begun, tied))).items())
         gathered = lax.all_gather(packed, everyone, axis=0, tiled=False)
-        out_at = FF // width * share + unit_block
-        whole_out = gathered[:, out_at : out_at + share].reshape(width, width)
-        mlp_weights, whole_in = (gathered,), gathered
-    else:
-        whole_in, whole_out, whole_up, whole_down = (
-            lax.all_gather(low(value), everyone, axis=0, tiled=True)
-            for value in (project_in, project_out, hidden_up, hidden_down)
-        )
-        mlp_weights = (whole_up, whole_down)
-
-    pieces = line_pieces(tokens, "line")
+        whole_out = gathered[:, packed.shape[0] - share :].reshape(width, width)
+        mlp_weights = (gathered,)
     own_tokens = line_order(tokens, pieces, "line").reshape(-1, width)
     swapped = [(distance, swap_cores(piece)) for distance, piece in pieces]
     other_tokens = line_order(swap_cores(tokens), swapped, "line").reshape(-1, width)
@@ -627,10 +647,6 @@
     offsets = lax.broadcasted_iota(jnp.int32, (group, images), 0) * rows
     starts = jnp.min(jnp.where(first < rows, first + offsets, length), axis=0)
 
-    half = FF // 2
-    folds = half // width
-    up_end = 2 * share * folds
-
     gain_one, shift_one, bias_query, bias_value, bias_out = (
         vectors[0],
         vectors[1],
@@ -658,7 +674,6 @@
     )
     grad_rows = cotangent.astype(jnp.float32) * valid.astype(jnp.float32)[:, None]
     grad_branch = (scale_two * grad_rows).astype(jnp.bfloat16)
-    grad_branch_chip = jnp.concatenate([grad_branch, swap_cores(grad_branch)], axis=0)
 
     normed_one, query, keys, values = norm_mix(
         core.reshape(1),
@@ -671,21 +686,39 @@
         bias_in,
     )
     wide, attended, logs = attend(starts, query, keys, values)
+    if not direct:
+        whole_out, whole_up, whole_down = (
+            lax.all_gather(low(value), everyone, axis=0, tiled=True)
+            for value in (project_out, hidden_up, hidden_down)
+        )
+        block = jnp.arange(half) // unit_block * 2 + core
+        index = block * unit_block + lax.rem(jnp.arange(half), unit_block)
+        mlp_weights = (jnp.take(whole_up, index, axis=1), jnp.take(whole_down, index, axis=0))
     returned = lax.all_to_all(
         attended.reshape(group, rows, lanes), seq, split_axis=0, concat_axis=0, tiled=True
     )
+    in_rows, returned = lax.optimization_barrier((low(project_in), returned))
+    if direct:
+        in_rows = in_rows.reshape(share, 3, width).swapaxes(0, 1).reshape(-1, width)
+    whole_in = lax.all_gather(in_rows, everyone, axis=0, tiled=not direct)
     attended_rows = returned.transpose(1, 0, 2).reshape(rows, width)
     inputs = tokens.astype(jnp.float32)
     projected = plain_product(attended_rows, whole_out) + bias_out
     second = inputs + scale_one * projected
     norm_two, norm_two_back = jax.vjp(layer_norm, second, gain_two, shift_two)
     normed_two = norm_two.astype(jnp.bfloat16)
-    normed_chip = jnp.concatenate([normed_two, swap_cores(normed_two)], axis=0)
-    grad_up, grad_down, branch_part, grad_norm_part, grad_bias_up = mlp(
-        core.reshape(1), normed_chip, grad_branch_chip, mlp_weights, bias_up, chips
-    )
-    grad_norm_two = grad_norm_part[:rows] + swap_cores(grad_norm_part[rows:])
-    branch = branch_part[:rows] + swap_cores(branch_part[rows:]) + bias_down
+    grad_up, grad_down, branch, branch_other, grad_norm_two, grad_norm_other, grad_bias_up = mlp(
+        core.reshape(1),
+        normed_two,
+        swap_cores(normed_two),
+        grad_branch,
+        swap_cores(grad_branch),
+        mlp_weights,
+        bias_up,
+        chips,
+    )
+    grad_norm_two = grad_norm_two + swap_cores(grad_norm_other)
+    branch = branch + swap_cores(branch_other) + bias_down
     block_output = (second + scale_two * branch).astype(jnp.bfloat16)
     grad_scale_two = jnp.sum(grad_rows * branch, axis=0)
     grad_bias_down = jnp.sum(grad_branch.astype(jnp.float32), axis=0)
@@ -704,30 +737,38 @@
     ).reshape(length, lanes)
     grad_out = inner_rows(attended_rows, grad_projected).astype(jnp.bfloat16)
     grad_out = grad_out.reshape(chips, 2 * share, width)
-    grad_up = lax.dynamic_update_slice_in_dim(grad_up, grad_out, up_end, 1)
     outer, inner = lax.axis_size("outer"), lax.axis_size("inner")
-    grad_up = grad_up.reshape(outer, inner, line, -1, width)
-    grad_down = grad_down.reshape(outer, inner, line, -1, width)
-    grad_down = scatter_line(scatter_line(grad_down, "outer", 0), "inner", 0)
-    grad_up = scatter_line(scatter_line(grad_up, "inner", 1), "outer", 0)
+    grad_up, grad_out, grad_down = (
+        value.reshape(outer, inner, line, -1, width) for value in (grad_up, grad_out, grad_down)
+    )
+    begun = (
+        scatter_terms(grad_up, "inner", 1),
+        scatter_terms(grad_out, "inner", 1),
+        scatter_terms(grad_down, "outer", 0),
+    )
+
     grad_mixed_stream = attend_back(starts, query, keys, values, wide, logs, grad_stream)
     grad_mixed = lax.all_to_all(
         grad_mixed_stream.reshape(group, rows, 3 * lanes), seq, split_axis=0, concat_axis=0, tiled=True
     )
-    plane_sums = jnp.concatenate([grad_up, grad_down], axis=1)
+    begun, grad_mixed_stream = lax.optimization_barrier((begun, grad_mixed_stream))
+    grad_up, grad_out, grad_down = (rounded_sum(*terms) for terms in begun)
+    grad_down = scatter_line(grad_down, "inner", 0)
+    grad_up, grad_out = (scatter_line(value, "outer", 0) for value in (grad_up, grad_out))
+    plane_sums = jnp.concatenate([grad_up, grad_out, grad_down], axis=1)
+    plane_sums, grad_mixed = lax.optimization_barrier((plane_sums, grad_mixed))
+    summed = scatter_direct(plane_sums, "line", 0)
     grad_in = inner_rows(normed_one, grad_mixed_stream).astype(jnp.bfloat16)
     parts = grad_in.reshape(outer, inner, group * share, 3 * lanes)
     parts = scatter_line(scatter_line(parts, "inner", 1), "outer", 0)
-    parts, plane_sums, grad_mixed = lax.optimization_barrier((parts, plane_sums, grad_mixed))
-    summed = scatter_line(plane_sums, "line", 0)
+    input_grad, grad_gain_one, grad_shift_one, mixed_sums = finish(
+        grad_mixed, whole_in, tokens, grad_second, gain_one
+    )
+    parts, grad_gain_one = lax.optimization_barrier((parts, grad_gain_one))
     parts = parts.reshape(group, share, 3 * lanes)
     parts = lax.all_to_all(parts, seq, split_axis=0, concat_axis=0, tiled=True)
     parts = parts.astype(jnp.float32)
     summed_in = parts.reshape(group, share, 3, lanes).transpose(1, 2, 0, 3).reshape(share, 3 * width)
-
-    input_grad, grad_gain_one, grad_shift_one, mixed_sums = finish(
-        grad_mixed, whole_in, tokens, grad_second, gain_one
-    )
     up_sums = grad_bias_up.reshape(chips, unit_block)
     up_sums = jnp.where(
         (lax.broadcasted_iota(jnp.int32, (1, 2, 1), 1) == core), up_sums[:, None, :], 0.0

time: 632 us -> 606 us (0.959)
  waiting for transfers between devices: 265 us -> 242 us
  other arithmetic: 56.4 us -> 43.6 us
  starting transfers between devices: 61.9 us -> 71.4 us
    ppermute x6, waiting for transfers between devices: 135 us -> 101 us  [line_pieces(): moving = lax.ppermute(moving, axis, pairs)]
    ppermute x6 -> x9, waiting for transfers between devices: 28.3 us -> 54.8 us  [the longest x6 39.1 us: scatter_direct(): terms.append(lax.ppermute(pick(place + move), axis, pairs))]
    ppermute x6 -> x9, starting transfers between devices: 10.5 us -> 27.7 us  [the longest x6 23.9 us: scatter_direct(): terms.append(lax.ppermute(pick(place + move), axis, pairs))]
    all_to_all x0 -> x1, blocking collectives: none -> 13.6 us  [on_device(): lax.all_to_all(blocks, seq, split_axis=0, concat_axis=0, tiled=True)]
    squeeze x0 -> x4, local copies, waits for them, and re-layouts: none -> 11.7 us  [the longest x3 9.72 us: scatter_terms(): lax.dynamic_index_in_dim(value, slot, dim, keepdims=False)]
    all_to_all x1, waiting for transfers between devices: 10.9 us -> 0.01 us  [on_device(): lax.all_to_all(grad_mixed_stream.reshape(group, rows, 3 * lanes), seq, sp...]
    all_to_all x1, blocking collectives: 20.1 us -> 10 us  [on_device(): lax.all_to_all(parts.reshape(count, small_rows * share), everyone, split_...]
    squeeze x7 -> x5, local copies, waits for them, and re-layouts: 10.1 us -> 0.28 us  [scatter_line(): lax.dynamic_index_in_dim(value, jnp.clip(slot, 0, size - 1), dim, keepdim...]
  transfers between devices with their start and end apart: 38 -> 40, of which waited for: 19 -> 13; matrix products, arithmetic and copies ran while one was open for 16% -> 18% of each run, Pallas kernels for 14% -> 13%
where the time goes in v6:
time: 606 us; the launch traced here: 597 us
  waiting for transfers between devices  242 us (40%)
  Pallas kernels  124 us (20%)
  starting transfers between devices  71.4 us (12%)
  local copies, waits for them, and re-layouts  60.5 us (10%)
  other arithmetic  43.6 us (7%)
  blocking collectives  23.7 us (4%)
  matrix products  15.6 us (3%)
  between operations  15.6 us (3%)
    ppermute x6, waiting for transfers between devices, line_pieces(): moving = lax.ppermute(moving, axis, pairs)  101 us
    ppermute x6, waiting for transfers between devices, scatter_direct(): terms.append(lax.ppermute(pick(place + move), axis, pairs))  39.1 us
    pallas_call x1, Pallas kernels, mlp(): pl.pallas_call(functools.partial(mlp_kernel, pieces), grid_spec=pltpu.Pre...  38 us
    pallas_call x1, Pallas kernels, attend_back(): pl.pallas_call(attend_back_kernel, grid_spec=pltpu.PrefetchScalarGridSpec...  34.9 us
    pallas_call x1, Pallas kernels, attend(): pl.pallas_call(attend_kernel, grid_spec=pltpu.PrefetchScalarGridSpec(num_...  26.3 us
    ppermute x5, waiting for transfers between devices, scatter_line(): lax.ppermute(pick(1 - place), axis, [(0, 1), (1, 0)])  25.8 us
    ppermute x6, starting transfers between devices, scatter_direct(): terms.append(lax.ppermute(pick(place + move), axis, pairs))  23.9 us
    all_to_all x1, waiting for transfers between devices, on_device(): lax.all_to_all(grad_attended.reshape(rows, group, lanes).transpose(1, 0,...  22.8 us
  transfers between devices with their start and end apart: 40, of which 13 were waited for; matrix products, arithmetic and copies ran while one was open for 18% of the time, Pallas kernels for 13%

profile of v6, /device:TPU:0, one launch (start us, length us, event | category | flops | bytes accessed | tf_op | source)
XLA Modules:
  0.0 596.7 jit_solution(12782039475639340844)
XLA Ops:
  7.3 6.1 %collective-permute-start.2 = (bf16[512,1024]{1,0:T(8,128)(2,1)}, bf16[512,1024]{1,0:T(8,128)(2,1)}, u32[]{:S(2)}, u32[]{:S(2)}) collective-permute-start(bf16[512,1024]{1,0:T(8,128)(2,1)} %x_ref.1), channel_id=1, source_target_pairs={{0,2},{2,4},{4,6},{1,3},{3,5},{5,7},{8,10},{10,12},{12,14},{9,11},... | collective-permute-start | bytes 3145736 | tf_op jit(solution)/shard_map/ppermute | solution.py:486
  14.6 20.4 %collective-permute-done.2 = bf16[512,1024]{1,0:T(8,128)(2,1)} collective-permute-done((bf16[512,1024]{1,0:T(8,128)(2,1)}, bf16[512,1024]{1,0:T(8,128)(2,1)}, u32[]{:S(2)}, u32[]{:S(2)}) %collective-permute-start.2) | collective-permute-done | bytes 1048608 | tf_op jit(solution)/shard_map/ppermute | solution.py:486
  35.1 1.7 collective-permute-start.3
  36.7 3.3 collective-permute-done.5
  45.3 20.7 %collective-permute-done.6 = bf16[512,1024]{1,0:T(8,128)(2,1)} collective-permute-done((bf16[512,1024]{1,0:T(8,128)(2,1)S(1)}, bf16[512,1024]{1,0:T(8,128)(2,1)}, u32[]{:S(2)}, u32[]{:S(2)}) %collective-permute-start.6) | collective-permute-done | bytes 1048608 | tf_op jit(solution)/shard_map/ppermute | solution.py:486
  66.8 13.6 %all_to_all.35 = bf16[8,34,384]{2,1,0:T(8,128)(2,1)S(1)} all-to-all(bf16[8,34,384]{2,1,0:T(8,128)(2,1)S(1)} %pad_maximum_fusion.2), channel_id=1, replica_groups=mesh['outer'=2,'inner'=2,'line'=4,'core'=2] {'line','core'}, dimensions={0} | all-to-all | bytes 417792 | tf_op jit(solution)/shard_map/all_to_all | solution.py:637
  80.5 1.6 collective-permute-start
  82.1 4.6 collective-permute-done
  86.8 1.7 collective-permute-start.1
  88.6 8.9 %collective-permute-done.1 = bf16[2,8,34,384]{3,2,1,0:T(8,128)(2,1)} collective-permute-done((bf16[2,8,34,384]{3,2,1,0:T(8,128)(2,1)S(1)}, bf16[2,8,34,384]{3,2,1,0:T(8,128)(2,1)}, u32[]{:S(2)}, u32[]{:S(2)}) %collective-permute-start.1) | collective-permute-done | bytes 417824 | tf_op jit(solution)/shard_map/ppermute | solution.py:478
  97.5 1.5 maximum_select_fusion
  99.0 1.6 collective-permute-start.4
  107.4 57.0 %collective-permute-done.7 = bf16[512,1024]{1,0:T(8,128)(2,1)} collective-permute-done((bf16[512,1024]{1,0:T(8,128)(2,1)}, bf16[512,1024]{1,0:T(8,128)(2,1)}, u32[]{:S(2)}, u32[]{:S(2)}) %collective-permute-start.7) | collective-permute-done | bytes 1048608 | tf_op jit(solution)/shard_map/ppermute | solution.py:486
  168.9 1.4 bitcast_dynamic-update-slice_fusion.10
  175.1 2.0 collective-permute-done.13
  178.6 2.0 copy-done.5
  180.6 14.6 %norm_mix.1 = (bf16[4096,1024]{1,0:T(8,128)(2,1)}, bf16[4096,128]{1,0:T(8,128)(2,1)}, bf16[4096,128]{1,0:T(8,128)(2,1)}, bf16[4096,128]{1,0:T(8,128)(2,1)}) custom-call(s32[1]{0:T(128)} %bitcast.8.core_ref, bf16[2048,1024]{1,0:T(8,128)(2,1)} %bitcast.192, bf16[2048,1024]{1,0:T(8,128)(2,1)} %bitcast.191, f32[1,1024]{1,0:T(1,128)} %slice.123.gain_ref, ...), custom_call_target="tpu_custom_call" | custom-call | flops 3221225472 | bytes 16777216 | tf_op jit(solution)/shard_map/norm_mix/pallas_call | solution.py:240
  195.2 26.3 %attend_forward.1 = (f32[4096,128]{1,0:T(8,128)}, bf16[4096,128]{1,0:T(8,128)(2,1)}, f32[4096,128]{1,0:T(8,128)}) custom-call(s32[2]{0:T(128)} %select_reduce_fusion.starts_ref, bf16[4096,128]{1,0:T(8,128)(2,1)} %get-tuple-element.58.q_ref, bf16[4096,128]{1,0:T(8,128)(2,1)} %get-tuple-element.59.k_ref, bf16[4096,128]{1,0:T(8,128)(2,1)} %get-tuple-element.60.v_ref), custom_call_target="tpu_custom_call" | custom-call | flops 4060086272 | bytes 8388608 | tf_op jit(solution)/shard_map/attend_forward/pallas_call | solution.py:116
  221.4 2.4 copy.98
  223.8 3.6 all-to-all-start.1
  229.9 1.9 convert_reduce_fusion
  232.2 21.7 %all-to-all-done.1 = bf16[8,512,128]{1,2,0:T(8,128)(2,1)S(1)} async-done(((bf16[8,512,128]{1,2,0:T(8,128)(2,1)}), bf16[8,512,128]{1,2,0:T(8,128)(2,1)S(1)}, u32[]{:S(2)}, u32[]{:S(2)}) %all-to-all-start.1) | async-done | bytes 1048608 | tf_op jit(solution)/shard_map/all_to_all | solution.py:697
  253.9 2.2 slice.162
  256.1 4.7 fusion.43
  261.8 1.4 add_convert_fusion.4.own_ref
  264.7 1.5 reshape.372
  267.6 38.0 %mlp_both_ways.1 = (bf16[16,128,1024]{2,1,0:T(8,128)(2,1)}, bf16[16,128,1024]{2,1,0:T(8,128)(2,1)}, f32[512,1024]{1,0:T(8,128)}, f32[512,1024]{1,0:T(8,128)}, f3...) custom-call(s32[1]{0:T(128)} %bitcast.8.core_ref, bf16[512,1024]{1,0:T(8,128)(2,1)} %add_convert_fusion.4.own_ref, ...), custom_call_target="tpu_custom_call" | custom-call | flops 25769803776 | bytes 29360128 | tf_op jit(solution)/shard_map/mlp_both_ways/pallas_call | solution.py:350
  306.2 1.9 reshape.378
  308.1 1.7 copy.101
  309.9 1.4 add.323
  311.3 3.8 multiply_reduce_fusion.1
  315.1 4.2 multiply_reduce_fusion
  321.4 1.4 copy-done.11
  325.3 4.6 all-to-all-start.2
  330.0 4.4 dynamic-slice_bitcast_fusion.2
  335.6 2.6 dynamic-slice_bitcast_fusion
  338.2 1.4 collective-permute-start.21
  339.6 2.6 convolution_convert_fusion
  342.2 22.8 %all-to-all-done.2 = bf16[8,512,128]{2,1,0:T(8,128)(2,1)} async-done(((bf16[8,512,128]{2,1,0:T(8,128)(2,1)}), bf16[8,512,128]{2,1,0:T(8,128)(2,1)}, u32[]{:S(2)}, u32[]{:S(2)}) %all-to-all-start.2) | async-done | bytes 1048608 | tf_op jit(solution)/shard_map/all_to_all | solution.py:731
  365.0 34.9 %attend_backward.1 = bf16[4096,384]{1,0:T(8,128)(2,1)} custom-call(s32[2]{0:T(128)} %select_reduce_fusion.starts_ref, bf16[4096,128]{1,0:T(8,128)(2,1)} %get-tuple-element.58.q_ref, bf16[4096,128]{1,0:T(8,128)(2,1)} %get-tuple-element.59.k_ref, bf16[4096,128]{1,0:T(8,128)(2,1)} %get-tuple-element.60.v_ref, f32[4096,128]{1,0:T(8,128)} %get-tuple-element.70.wide_ref, ...), custom_call_target="tpu_custom_call" | custom-call | flops 10150215680 | bytes 11534336 | tf_op jit(solution)/shard_map/attend_backward/pallas_call | solution.py:196
  399.9 4.6 all-to-all-start.3
  404.5 2.8 dynamic-slice_bitcast_fusion.6
  411.2 1.4 concatenate.70
  412.6 1.4 concatenate.71
  414.0 1.4 concatenate.72
  417.5 15.7 %collective-permute-done.20 = bf16[2,4,64,1024]{3,2,1,0:T(8,128)(2,1)} collective-permute-done((bf16[2,4,64,1024]{3,2,1,0:T(8,128)(2,1)}, bf16[2,4,64,1024]{3,2,1,0:T(8,128)(2,1)}, u32[]{:S(2)}, u32[]{:S(2)}) %collective-permute-start.20) | collective-permute-done | bytes 1048608 | tf_op jit(solution)/shard_map/ppermute | solution.py:517
  433.1 3.2 add_convert_fusion
  437.8 1.6 add_convert_fusion.2
  440.7 7.0 %convolution_convert_fusion.2 = bf16[1024,384]{1,0:T(8,128)(2,1)S(1)} fusion(bf16[4096,1024]{1,0:T(8,128)(2,1)} %get-tuple-element.81, bf16[4096,384]{1,0:T(8,128)(2,1)S(1)} %copy-done.8), kind=kOutput, calls=%fused_computation.30 | convolution fusion | flops 3221618688 | bytes 12320768 | tf_op jit(solution)/shard_map/dot_general | solution.py:41
  448.8 2.6 add_convert_fusion.1
  452.3 17.4 %collective-permute-done.25 = bf16[2,256,384]{2,1,0:T(8,128)(2,1)S(1)} collective-permute-done((bf16[2,256,384]{2,1,0:T(8,128)(2,1)S(1)}, bf16[2,256,384]{2,1,0:T(8,128)(2,1)S(1)}, u32[]{:S(2)}, u32[]{:S(2)}) %collective-permute-start.25) | collective-permute-done | bytes 393248 | tf_op jit(solution)/shard_map/ppermute | solution.py:541
  471.1 8.3 %collective-permute-done.26 = bf16[256,384]{1,0:T(8,128)(2,1)S(1)} collective-permute-done((bf16[256,384]{1,0:T(8,128)(2,1)S(1)}, bf16[256,384]{1,0:T(8,128)(2,1)S(1)}, u32[]{:S(2)}, u32[]{:S(2)}) %collective-permute-start.26) | collective-permute-done | bytes 196640 | tf_op jit(solution)/shard_map/ppermute | solution.py:541
  481.3 10.5 %finish_input.1 = (f32[512,1024]{1,0:T(8,128)}, f32[1,1024]{1,0:T(1,128)}, f32[1,1024]{1,0:T(1,128)}, f32[3,1,1024]{2,1,0:T(1,128)}) custom-call(bf16[8,512,384]{2,1,0:T(8,128)(2,1)} %all-to-all-done.3.grad_ref, bf16[32,96,1024]{2,1,0:T(8,128)(2,1)} %all-gather.4.cloned.1.call-done.weight_ref, bf16[512,1024]{1,0:T(8,128)(2,1)} %x_ref.1, ...), custom_call_target="tpu_custom_call" | custom-call | flops 3221225472 | bytes 16777216 | tf_op jit(solution)/shard_map/finish_input/pallas_call | solution.py:440
  492.0 2.0 dynamic-slice_bitcast_fusion.13
  493.9 4.1 collective-permute-start.32
  500.7 10.0 %all_to_all.36 = f32[32,1,448]{2,1,0:T(1,128)S(1)} all-to-all(f32[32,1,448]{2,1,0:T(1,128)S(1)} %all_to_all.28), channel_id=1, replica_groups=mesh['outer'=2,'inner'=2,'line'=4,'core'=2] {'outer','inner','line','core'}, dimensions={0} | all-to-all | bytes 114688 | tf_op jit(solution)/shard_map/all_to_all | solution.py:798
  510.7 6.0 %all-to-all-start.4 = ((bf16[8,32,384]{2,1,0:T(8,128)(2,1)}), bf16[8,32,384]{2,1,0:T(8,128)(2,1)}, u32[]{:S(2)}, u32[]{:S(2)}) async-start(bf16[8,32,384]{2,1,0:T(8,128)(2,1)} %bitcast.62), calls=%async_computation.4 | async-start | bytes 393216 | tf_op jit(solution)/shard_map/all_to_all | solution.py:769
  518.0 6.9 %collective-permute-start.30 = (bf16[320,1024]{1,0:T(8,128)(2,1)}, bf16[320,1024]{1,0:T(8,128)(2,1)}, u32[]{:S(2)}, u32[]{:S(2)}) collective-permute-start(bf16[320,1024]{1,0:T(8,128)(2,1)} %get-tuple-element.140), channel_id=1, source_target_pairs={{0,4},{2,6},{1,5},{3,7},{8,12},{10,14},{9,13},{11,15},{16,20},{18,... | collective-permute-start | bytes 1966088 | tf_op jit(solution)/shard_map/ppermute | solution.py:530
  526.2 9.1 %collective-permute-start.28 = (bf16[320,1024]{1,0:T(8,128)(2,1)}, bf16[320,1024]{1,0:T(8,128)(2,1)}, u32[]{:S(2)}, u32[]{:S(2)}) collective-permute-start(bf16[320,1024]{1,0:T(8,128)(2,1)} %get-tuple-element.142), channel_id=1, source_target_pairs={{0,6},{1,7},{8,14},{9,15},{16,22},{17,23},{24,30},{25,31}} | collective-permute-start | bytes 1966088 | tf_op jit(solution)/shard_map/ppermute | solution.py:530
  539.9 2.4 multiply_subtract_fusion.2
  542.3 39.1 %collective-permute-done.29 = bf16[320,1024]{1,0:T(8,128)(2,1)} collective-permute-done((bf16[320,1024]{1,0:T(8,128)(2,1)}, bf16[320,1024]{1,0:T(8,128)(2,1)}, u32[]{:S(2)}, u32[]{:S(2)}) %collective-permute-start.29) | collective-permute-done | bytes 655392 | tf_op jit(solution)/shard_map/ppermute | solution.py:530
  581.4 2.9 fusion.8
  584.5 1.4 multiply_subtract_fusion
  587.4 1.4 multiply_subtract_fusion.1
  (278 shorter events, 64.1 us)
Async XLA Ops:
  7.2 58.9 %copy-start.31 = (f32[14,32]{1,0:T(8,128)S(1)}, f32[14,32]{1,0:T(8,128)}, u32[]{:S(2)}) copy-start(f32[14,32]{1,0:T(8,128)} %param.27) | copy-start | bytes 5380
  7.2 59.0 %copy-start.43 = (s32[512]{0:T(512)S(1)}, s32[512]{0:T(512)}, u32[]{:S(2)}) copy-start(s32[512]{0:T(512)} %param.22) | copy-start | bytes 6148
  7.2 59.0 %copy-start.47 = (s32[512]{0:T(512)S(1)}, s32[512]{0:T(512)}, u32[]{:S(2)}) copy-start(s32[512]{0:T(512)} %param.21) | copy-start | bytes 6148
  7.2 59.2 %copy-start.7 = (f32[32,3072]{1,0:T(8,128)S(1)}, f32[32,3072]{1,0:T(8,128)}, u32[]{:S(2)}) copy-start(f32[32,3072]{1,0:T(8,128)} %param.23) | copy-start | bytes 1179652
  7.2 246.7 %all-gather.6.cloned.1.call-start = ((), (), s32[]{:S(2)}) async-start(), calls=%async_computation.7 | async-start | bytes 19464192 | tf_op jit(solution)/shard_map/all_gather | solution.py:612
  7.3 27.8 %collective-permute-start.2 = (bf16[512,1024]{1,0:T(8,128)(2,1)}, bf16[512,1024]{1,0:T(8,128)(2,1)}, u32[]{:S(2)}, u32[]{:S(2)}) collective-permute-start(bf16[512,1024]{1,0:T(8,128)(2,1)} %x_ref.1), channel_id=1, source_target_pairs={{0,2},{2,4},{4,6},{1,3},{3,5},{5,7},{8,10},{10,12},{12,14},{9,11},... | collective-permute-start | bytes 3145736 | tf_op jit(solution)/shard_map/ppermute | solution.py:486
  13.3 26.7 %collective-permute-start.5 = (bf16[512,1024]{1,0:T(8,128)(2,1)}, bf16[512,1024]{1,0:T(8,128)(2,1)S(1)}, u32[]{:S(2)}, u32[]{:S(2)}) collective-permute-start(bf16[512,1024]{1,0:T(8,128)(2,1)} %x_ref.1), channel_id=1, source_target_pairs={{2,0},{4,2},{6,4},{3,1},{5,3},{7,5},{10,8},{12,10},{14,12},{11,9},... | collective-permute-start | bytes 3145736 | tf_op jit(solution)/shard_map/ppermute | solution.py:486
  35.1 10.3 %collective-permute-start.3 = (bf16[512,1024]{1,0:T(8,128)(2,1)}, bf16[512,1024]{1,0:T(8,128)(2,1)}, u32[]{:S(2)}, u32[]{:S(2)}) collective-permute-start(bf16[512,1024]{1,0:T(8,128)(2,1)} %collective-permute-done.2), channel_id=1, source_target_pairs={{2,4},{4,6},{3,5},{5,7},{10,12},{12,14},{11,13},{13,15},{18,20},{2... | collective-permute-start | bytes 3145736 | tf_op jit(solution)/shard_map/ppermute | solution.py:486
  40.1 26.0 %collective-permute-start.6 = (bf16[512,1024]{1,0:T(8,128)(2,1)S(1)}, bf16[512,1024]{1,0:T(8,128)(2,1)}, u32[]{:S(2)}, u32[]{:S(2)}) collective-permute-start(bf16[512,1024]{1,0:T(8,128)(2,1)S(1)} %collective-permute-done.5), channel_id=1, source_target_pairs={{2,0},{4,2},{3,1},{5,3},{10,8},{12,10},{11,9},{13,11},{18,16},{20,... | collective-permute-start | bytes 3145736 | tf_op jit(solution)/shard_map/ppermute | solution.py:486
  45.3 43.2 %copy-start.2 = (bf16[512,1024]{1,0:T(8,128)(2,1)S(1)}, bf16[512,1024]{1,0:T(8,128)(2,1)}, u32[]{:S(2)}) copy-start(bf16[512,1024]{1,0:T(8,128)(2,1)} %x_ref.1) | copy-start | bytes 3145732
  80.5 6.2 %collective-permute-start = (bf16[8,34,384]{2,1,0:T(8,128)(2,1)S(1)}, bf16[8,34,384]{2,1,0:T(8,128)(2,1)S(1)}, u32[]{:S(2)}, u32[]{:S(2)}) collective-permute-start(bf16[8,34,384]{2,1,0:T(8,128)(2,1)S(1)} %all_to_all.35), channel_id=1, source_target_pairs={{0,8},{8,0},{1,9},{9,1},{2,10},{10,2},{3,11},{11,3},{4,12},{12,4},... | collective-permute-start | bytes 626696 | tf_op jit(solution)/shard_map/ppermute | solution.py:478
  86.8 10.7 %collective-permute-start.1 = (bf16[2,8,34,384]{3,2,1,0:T(8,128)(2,1)S(1)}, bf16[2,8,34,384]{3,2,1,0:T(8,128)(2,1)}, u32[]{:S(2)}, u32[]{:S(2)}) collective-permute-start(bf16[2,8,34,384]{3,2,1,0:T(8,128)(2,1)S(1)} %maximum_select_fusion.2), channel_id=1, source_target_pairs={{0,16},{16,0},{1,17},{17,1},{2,18},{18,2},{3,19},{19,3},{4,20},{20... | collective-permute-start | bytes 1253384 | tf_op jit(solution)/shard_map/ppermute | solution.py:478
  88.5 88.7 %collective-permute-start.14 = (bf16[512,1024]{1,0:T(8,128)(2,1)S(1)}, bf16[512,1024]{1,0:T(8,128)(2,1)}, u32[]{:S(2)}, u32[]{:S(2)}) collective-permute-start(bf16[512,1024]{1,0:T(8,128)(2,1)S(1)} %copy-done.2), channel_id=1, source_target_pairs={{0,1},{1,0},{2,3},{3,2},{4,5},{5,4},{6,7},{7,6},{8,9},{9,8},{10,11... | collective-permute-start | bytes 3145736 | tf_op jit(solution)/shard_map/ppermute | solution.py:472
  99.0 8.4 %collective-permute-start.4 = (bf16[512,1024]{1,0:T(8,128)(2,1)}, bf16[512,1024]{1,0:T(8,128)(2,1)}, u32[]{:S(2)}, u32[]{:S(2)}) collective-permute-start(bf16[512,1024]{1,0:T(8,128)(2,1)} %collective-permute-done.3), channel_id=1, source_target_pairs={{4,6},{5,7},{12,14},{13,15},{20,22},{21,23},{28,30},{29,31}} | collective-permute-start | bytes 3145736 | tf_op jit(solution)/shard_map/ppermute | solution.py:486
  100.7 63.7 %collective-permute-start.7 = (bf16[512,1024]{1,0:T(8,128)(2,1)}, bf16[512,1024]{1,0:T(8,128)(2,1)}, u32[]{:S(2)}, u32[]{:S(2)}) collective-permute-start(bf16[512,1024]{1,0:T(8,128)(2,1)} %collective-permute-done.6), channel_id=1, source_target_pairs={{2,0},{3,1},{10,8},{11,9},{18,16},{19,17},{26,24},{27,25}} | collective-permute-start | bytes 3145736 | tf_op jit(solution)/shard_map/ppermute | solution.py:486
  103.0 61.8 %copy-start.17 = (f32[32,14,32]{2,1,0:T(8,128)}, f32[32,14,32]{2,1,0:T(8,128)S(1)}, u32[]{:S(2)}) copy-start(f32[32,14,32]{2,1,0:T(8,128)S(1)} %reshape.397) | copy-start | bytes 172036
  106.9 67.9 %collective-permute-start.10 = (bf16[512,1024]{1,0:T(8,128)(2,1)}, bf16[512,1024]{1,0:T(8,128)(2,1)S(1)}, u32[]{:S(2)}, u32[]{:S(2)}) collective-permute-start(bf16[512,1024]{1,0:T(8,128)(2,1)} %collective-permute-done.3), channel_id=1, source_target_pairs={{0,1},{1,0},{2,3},{3,2},{4,5},{5,4},{6,7},{7,6},{8,9},{9,8},{10,11... | collective-permute-start | bytes 3145736 | tf_op jit(solution)/shard_map/ppermute | solution.py:472
  106.9 68.0 %collective-permute-start.11 = (bf16[512,1024]{1,0:T(8,128)(2,1)}, bf16[512,1024]{1,0:T(8,128)(2,1)S(1)}, u32[]{:S(2)}, u32[]{:S(2)}) collective-permute-start(bf16[512,1024]{1,0:T(8,128)(2,1)} %collective-permute-done.6), channel_id=1, source_target_pairs={{0,1},{1,0},{2,3},{3,2},{4,5},{5,4},{6,7},{7,6},{8,9},{9,8},{10,11... | collective-permute-start | bytes 3145736 | tf_op jit(solution)/shard_map/ppermute | solution.py:472
  107.4 64.5 %collective-permute-start.8 = (bf16[512,1024]{1,0:T(8,128)(2,1)}, bf16[512,1024]{1,0:T(8,128)(2,1)S(1)}, u32[]{:S(2)}, u32[]{:S(2)}) collective-permute-start(bf16[512,1024]{1,0:T(8,128)(2,1)} %collective-permute-done.4), channel_id=1, source_target_pairs={{0,1},{1,0},{2,3},{3,2},{4,5},{5,4},{6,7},{7,6},{8,9},{9,8},{10,11... | collective-permute-start | bytes 3145736 | tf_op jit(solution)/shard_map/ppermute | solution.py:472
  164.3 9.8 %collective-permute-start.9 = (bf16[512,1024]{1,0:T(8,128)(2,1)}, bf16[512,1024]{1,0:T(8,128)(2,1)S(1)}, u32[]{:S(2)}, u32[]{:S(2)}) collective-permute-start(bf16[512,1024]{1,0:T(8,128)(2,1)} %collective-permute-done.7), channel_id=1, source_target_pairs={{0,1},{1,0},{2,3},{3,2},{4,5},{5,4},{6,7},{7,6},{8,9},{9,8},{10,11... | collective-permute-start | bytes 3145736 | tf_op jit(solution)/shard_map/ppermute | solution.py:472
  171.9 3.1 collective-permute-start.12
  174.1 3.0 collective-permute-start.13
  221.4 8.5 %copy-start.1 = (bf16[512,1024]{1,0:T(8,128)(2,1)S(1)}, bf16[512,1024]{1,0:T(8,128)(2,1)}, u32[]{:S(2)}) copy-start(bf16[512,1024]{1,0:T(8,128)(2,1)} %param.20) | copy-start | bytes 3145732
  223.8 30.1 %all-to-all-start.1 = ((bf16[8,512,128]{1,2,0:T(8,128)(2,1)}), bf16[8,512,128]{1,2,0:T(8,128)(2,1)S(1)}, u32[]{:S(2)}, u32[]{:S(2)}) async-start(bf16[8,512,128]{1,2,0:T(8,128)(2,1)} %copy.98), calls=%async_computation.1 | async-start | bytes 2097152 | tf_op jit(solution)/shard_map/all_to_all | solution.py:697
  227.4 253.9 %all-gather.4.cloned.1.call-start = ((), (), s32[]{:S(2)}) async-start(), calls=%async_computation.6 | async-start | bytes 6488064 | tf_op jit(solution)/shard_map/all_gather | solution.py:703
  227.6 28.4 %copy-start.32 = (f32[512]{0:T(512)}, f32[512]{0:T(512)S(1)}, u32[]{:S(2)}) copy-start(f32[512]{0:T(512)S(1)} %convert_element_type.222) | copy-start | bytes 6148
  229.1 27.0 %copy-start.37 = (f32[1024]{0:T(1024)}, f32[1024]{0:T(1024)S(1)}, u32[]{:S(2)}) copy-start(f32[1024]{0:T(1024)S(1)} %mul.321) | copy-start | bytes 12292
  231.8 35.8 %collective-permute-start.16 = (bf16[512,1024]{1,0:T(8,128)(2,1)}, bf16[512,1024]{1,0:T(8,128)(2,1)}, u32[]{:S(2)}, u32[]{:S(2)}) collective-permute-start(bf16[512,1024]{1,0:T(8,128)(2,1)} %get-tuple-element.109.gm_own_ref), channel_id=1, source_target_pairs={{0,1},{1,0},{2,3},{3,2},{4,5},{5,4},{6,7},{7,6},{8,9},{9,8},{10,11... | collective-permute-start | bytes 3145736 | tf_op jit(solution)/shard_map/ppermute | solution.py:472
  256.1 4.8 copy-start.10
  263.2 4.4 collective-permute-start.15
  305.6 5.7 collective-permute-start.19
  306.1 8.9 %collective-permute-start.17 = (f32[512,1024]{1,0:T(8,128)}, f32[512,1024]{1,0:T(8,128)}, u32[]{:S(2)}, u32[]{:S(2)}) collective-permute-start(f32[512,1024]{1,0:T(8,128)} %get-tuple-element.65), channel_id=1, source_target_pairs={{0,1},{1,0},{2,3},{3,2},{4,5},{5,4},{6,7},{7,6},{8,9},{9,8},{10,11... | collective-permute-start | bytes 6291464 | tf_op jit(solution)/shard_map/ppermute | solution.py:472
  325.3 39.7 %all-to-all-start.2 = ((bf16[8,512,128]{2,1,0:T(8,128)(2,1)}), bf16[8,512,128]{2,1,0:T(8,128)(2,1)}, u32[]{:S(2)}, u32[]{:S(2)}) async-start(bf16[8,512,128]{2,1,0:T(8,128)(2,1)} %bitcast.186), calls=%async_computation.2 | async-start | bytes 2097152 | tf_op jit(solution)/shard_map/all_to_all | solution.py:731
  330.0 5.6 copy-start.4
  334.4 83.1 %collective-permute-start.18 = (bf16[2,4,128,1024]{3,2,1,0:T(8,128)(2,1)}, bf16[2,4,128,1024]{3,2,1,0:T(8,128)(2,1)}, u32[]{:S(2)}, u32[]{:S(2)}) collective-permute-start(bf16[2,4,128,1024]{3,2,1,0:T(8,128)(2,1)} %get-tuple-element.135), channel_id=1, source_target_pairs={{0,8},{8,0},{1,9},{9,1},{2,10},{10,2},{3,11},{11,3},{4,12},{12,4},... | collective-permute-start | bytes 6291464 | tf_op jit(solution)/shard_map/ppermute | solution.py:517
  338.2 79.3 %collective-permute-start.21 = (bf16[2,4,128,1024]{3,2,1,0:T(8,128)(2,1)}, bf16[2,4,128,1024]{3,2,1,0:T(8,128)(2,1)}, u32[]{:S(2)}, u32[]{:S(2)}) collective-permute-start(bf16[2,4,128,1024]{3,2,1,0:T(8,128)(2,1)} %get-tuple-element.133), channel_id=1, source_target_pairs={{0,16},{16,0},{1,17},{17,1},{2,18},{18,2},{3,19},{19,3},{4,20},{20... | collective-permute-start | bytes 6291464 | tf_op jit(solution)/shard_map/ppermute | solution.py:517
  399.9 81.4 %all-to-all-start.3 = ((bf16[8,512,384]{2,1,0:T(8,128)(2,1)}), bf16[8,512,384]{2,1,0:T(8,128)(2,1)}, u32[]{:S(2)}, u32[]{:S(2)}) async-start(bf16[8,512,384]{2,1,0:T(8,128)(2,1)} %bitcast.195), calls=%async_computation.3 | async-start | bytes 6291456 | tf_op jit(solution)/shard_map/all_to_all | solution.py:751
  404.5 4.5 copy-start.36
  407.3 25.8 %collective-permute-start.20 = (bf16[2,4,64,1024]{3,2,1,0:T(8,128)(2,1)}, bf16[2,4,64,1024]{3,2,1,0:T(8,128)(2,1)}, u32[]{:S(2)}, u32[]{:S(2)}) collective-permute-start(bf16[2,4,64,1024]{3,2,1,0:T(8,128)(2,1)} %get-tuple-element.145), channel_id=1, source_target_pairs={{0,8},{8,0},{1,9},{9,1},{2,10},{10,2},{3,11},{11,3},{4,12},{12,4},... | collective-permute-start | bytes 3145736 | tf_op jit(solution)/shard_map/ppermute | solution.py:517
  436.5 43.7 %collective-permute-start.24 = (bf16[4,128,1024]{2,1,0:T(8,128)(2,1)S(1)}, bf16[4,128,1024]{2,1,0:T(8,128)(2,1)S(1)}, u32[]{:S(2)}, u32[]{:S(2)}) collective-permute-start(bf16[4,128,1024]{2,1,0:T(8,128)(2,1)S(1)} %dynamic-slice_bitcast_fusion.4), channel_id=1, source_target_pairs={{0,8},{8,0},{1,9},{9,1},{2,10},{10,2},{3,11},{11,3},{4,12},{12,4},... | collective-permute-start | bytes 3145736 | tf_op jit(solution)/shard_map/ppermute | solution.py:541
  439.5 31.5 %collective-permute-start.23 = (bf16[4,64,1024]{2,1,0:T(8,128)(2,1)S(1)}, bf16[4,64,1024]{2,1,0:T(8,128)(2,1)S(1)}, u32[]{:S(2)}, u32[]{:S(2)}) collective-permute-start(bf16[4,64,1024]{2,1,0:T(8,128)(2,1)S(1)} %dynamic-slice_bitcast_fusion.14), channel_id=1, source_target_pairs={{0,16},{16,0},{1,17},{17,1},{2,18},{18,2},{3,19},{19,3},{4,20},{20... | collective-permute-start | bytes 1572872 | tf_op jit(solution)/shard_map/ppermute | solution.py:541
  447.8 21.9 %collective-permute-start.25 = (bf16[2,256,384]{2,1,0:T(8,128)(2,1)S(1)}, bf16[2,256,384]{2,1,0:T(8,128)(2,1)S(1)}, u32[]{:S(2)}, u32[]{:S(2)}) collective-permute-start(bf16[2,256,384]{2,1,0:T(8,128)(2,1)S(1)} %dynamic-slice_bitcast_fusion.15), channel_id=1, source_target_pairs={{0,8},{8,0},{1,9},{9,1},{2,10},{10,2},{3,11},{11,3},{4,12},{12,4},... | collective-permute-start | bytes 1179656 | tf_op jit(solution)/shard_map/ppermute | solution.py:541
  451.4 29.2 %collective-permute-start.22 = (bf16[4,128,1024]{2,1,0:T(8,128)(2,1)S(1)}, bf16[4,128,1024]{2,1,0:T(8,128)(2,1)S(1)}, u32[]{:S(2)}, u32[]{:S(2)}) collective-permute-start(bf16[4,128,1024]{2,1,0:T(8,128)(2,1)S(1)} %dynamic-slice_bitcast_fusion.5), channel_id=1, source_target_pairs={{0,16},{16,0},{1,17},{17,1},{2,18},{18,2},{3,19},{19,3},{4,20},{20... | collective-permute-start | bytes 3145736 | tf_op jit(solution)/shard_map/ppermute | solution.py:541
  469.8 9.6 %collective-permute-start.26 = (bf16[256,384]{1,0:T(8,128)(2,1)S(1)}, bf16[256,384]{1,0:T(8,128)(2,1)S(1)}, u32[]{:S(2)}, u32[]{:S(2)}) collective-permute-start(bf16[256,384]{1,0:T(8,128)(2,1)S(1)} %dynamic-slice_bitcast_fusion.16), channel_id=1, source_target_pairs={{0,16},{16,0},{1,17},{17,1},{2,18},{18,2},{3,19},{19,3},{4,20},{20... | collective-permute-start | bytes 589832 | tf_op jit(solution)/shard_map/ppermute | solution.py:541
  491.9 6.7 %copy-start.46 = (f32[1,1024]{1,0:T(1,128)S(1)}, f32[1,1024]{1,0:T(1,128)}, u32[]{:S(2)}) copy-start(f32[1,1024]{1,0:T(1,128)} %get-tuple-element.86) | copy-start | bytes 12292
  491.9 7.4 %copy-start.45 = (f32[1,1024]{1,0:T(1,128)S(1)}, f32[1,1024]{1,0:T(1,128)}, u32[]{:S(2)}) copy-start(f32[1,1024]{1,0:T(1,128)} %get-tuple-element.87) | copy-start | bytes 12292
  491.9 8.1 %copy-start.44 = (f32[3,1,1024]{2,1,0:T(1,128)S(1)}, f32[3,1,1024]{2,1,0:T(1,128)}, u32[]{:S(2)}) copy-start(f32[3,1,1024]{2,1,0:T(1,128)} %get-tuple-element.88) | copy-start | bytes 36868
  491.9 8.3 %copy-start.29 = (f32[1,32,32]{2,1,0:T(8,128)S(1)}, f32[1,32,32]{2,1,0:T(8,128)}, u32[]{:S(2)}) copy-start(f32[1,32,32]{2,1,0:T(8,128)} %concatenate.70) | copy-start | bytes 12292
  491.9 8.3 %copy-start.30 = (f32[1,32,32]{2,1,0:T(8,128)S(1)}, f32[1,32,32]{2,1,0:T(8,128)}, u32[]{:S(2)}) copy-start(f32[1,32,32]{2,1,0:T(8,128)} %concatenate.71) | copy-start | bytes 12292
  491.9 8.3 %copy-start.27 = (f32[1,32,32]{2,1,0:T(8,128)S(1)}, f32[1,32,32]{2,1,0:T(8,128)}, u32[]{:S(2)}) copy-start(f32[1,32,32]{2,1,0:T(8,128)} %concatenate.72) | copy-start | bytes 12292
  491.9 8.3 %copy-start.28 = (f32[1,32,32]{2,1,0:T(8,128)S(1)}, f32[1,32,32]{2,1,0:T(8,128)}, u32[]{:S(2)}) copy-start(f32[1,32,32]{2,1,0:T(8,128)} %concatenate.73) | copy-start | bytes 12292
  491.9 8.3 %copy-start.26 = (f32[1,32,32]{2,1,0:T(8,128)S(1)}, f32[1,32,32]{2,1,0:T(8,128)}, u32[]{:S(2)}) copy-start(f32[1,32,32]{2,1,0:T(8,128)} %concatenate.74) | copy-start | bytes 12292
  492.0 8.4 %copy-start.23 = (f32[4,32,32]{2,1,0:T(8,128)S(1)}, f32[4,32,32]{2,1,0:T(8,128)}, u32[]{:S(2)}) copy-start(f32[4,32,32]{2,1,0:T(8,128)} %select_n.211) | copy-start | bytes 49156
  493.9 44.7 %collective-permute-start.32 = (bf16[320,1024]{1,0:T(8,128)(2,1)}, bf16[320,1024]{1,0:T(8,128)(2,1)}, u32[]{:S(2)}, u32[]{:S(2)}) collective-permute-start(bf16[320,1024]{1,0:T(8,128)(2,1)} %get-tuple-element.138), channel_id=1, source_target_pairs={{0,2},{2,4},{4,6},{1,3},{3,5},{5,7},{8,10},{10,12},{12,14},{9,11},... | collective-permute-start | bytes 1966088 | tf_op jit(solution)/shard_map/ppermute | solution.py:530
  510.7 26.6 %all-to-all-start.4 = ((bf16[8,32,384]{2,1,0:T(8,128)(2,1)}), bf16[8,32,384]{2,1,0:T(8,128)(2,1)}, u32[]{:S(2)}, u32[]{:S(2)}) async-start(bf16[8,32,384]{2,1,0:T(8,128)(2,1)} %bitcast.62), calls=%async_computation.4 | async-start | bytes 393216 | tf_op jit(solution)/shard_map/all_to_all | solution.py:769
  516.8 25.5 %collective-permute-start.31 = (bf16[320,1024]{1,0:T(8,128)(2,1)}, bf16[320,1024]{1,0:T(8,128)(2,1)}, u32[]{:S(2)}, u32[]{:S(2)}) collective-permute-start(bf16[320,1024]{1,0:T(8,128)(2,1)} %get-tuple-element.139), channel_id=1, source_target_pairs={{2,0},{4,2},{6,4},{3,1},{5,3},{7,5},{10,8},{12,10},{14,12},{11,9},... | collective-permute-start | bytes 1966088 | tf_op jit(solution)/shard_map/ppermute | solution.py:530
  518.0 24.2 %collective-permute-start.30 = (bf16[320,1024]{1,0:T(8,128)(2,1)}, bf16[320,1024]{1,0:T(8,128)(2,1)}, u32[]{:S(2)}, u32[]{:S(2)}) collective-permute-start(bf16[320,1024]{1,0:T(8,128)(2,1)} %get-tuple-element.140), channel_id=1, source_target_pairs={{0,4},{2,6},{1,5},{3,7},{8,12},{10,14},{9,13},{11,15},{16,20},{18,... | collective-permute-start | bytes 1966088 | tf_op jit(solution)/shard_map/ppermute | solution.py:530
  524.9 56.5 %collective-permute-start.29 = (bf16[320,1024]{1,0:T(8,128)(2,1)}, bf16[320,1024]{1,0:T(8,128)(2,1)}, u32[]{:S(2)}, u32[]{:S(2)}) collective-permute-start(bf16[320,1024]{1,0:T(8,128)(2,1)} %get-tuple-element.141), channel_id=1, source_target_pairs={{4,0},{6,2},{5,1},{7,3},{12,8},{14,10},{13,9},{15,11},{20,16},{22,... | collective-permute-start | bytes 1966088 | tf_op jit(solution)/shard_map/ppermute | solution.py:530
  526.2 55.2 %collective-permute-start.28 = (bf16[320,1024]{1,0:T(8,128)(2,1)}, bf16[320,1024]{1,0:T(8,128)(2,1)}, u32[]{:S(2)}, u32[]{:S(2)}) collective-permute-start(bf16[320,1024]{1,0:T(8,128)(2,1)} %get-tuple-element.142), channel_id=1, source_target_pairs={{0,6},{1,7},{8,14},{9,15},{16,22},{17,23},{24,30},{25,31}} | collective-permute-start | bytes 1966088 | tf_op jit(solution)/shard_map/ppermute | solution.py:530
  538.6 42.8 %collective-permute-start.27 = (bf16[320,1024]{1,0:T(8,128)(2,1)}, bf16[320,1024]{1,0:T(8,128)(2,1)S(1)}, u32[]{:S(2)}, u32[]{:S(2)}) collective-permute-start(bf16[320,1024]{1,0:T(8,128)(2,1)} %get-tuple-element.137), channel_id=1, source_target_pairs={{6,0},{7,1},{14,8},{15,9},{22,16},{23,17},{30,24},{31,25}} | collective-permute-start | bytes 1966088 | tf_op jit(solution)/shard_map/ppermute | solution.py:530
  542.3 42.2 %copy-start.12 = (f32[128,1024]{1,0:T(8,128)S(1)}, f32[128,1024]{1,0:T(8,128)}, u32[]{:S(2)}) copy-start(f32[128,1024]{1,0:T(8,128)} %param.26) | copy-start | bytes 1572868
  542.3 42.2 %copy-start.21 = (f32[128,1024]{1,0:T(8,128)S(1)}, f32[128,1024]{1,0:T(8,128)}, u32[]{:S(2)}) copy-start(f32[128,1024]{1,0:T(8,128)} %param.31) | copy-start | bytes 1572868
  542.3 42.2 %copy-start.22 = (f32[128,1024]{1,0:T(8,128)S(1)}, f32[128,1024]{1,0:T(8,128)}, u32[]{:S(2)}) copy-start(f32[128,1024]{1,0:T(8,128)} %param.36) | copy-start | bytes 1572868
  584.4 1.5 collective-permute-start.33
  (24 other events, 59.9 us)
Sparse Core Ops, SparseCore 0:
  66.2 133.6 all-gather.5
  310.0 89.6 all-gather.3

commit v7 on v6

--- a/solution.py
+++ b/solution.py
@@ -215,30 +215,40 @@
     )(starts, query, keys, values, wide, logs, grad_out)
 
 
-def norm_mix_kernel(
-    core_ref, own_ref, other_ref, gain_ref, shift_ref, weight_ref, bias_ref, a_ref, q_ref, k_ref, v_ref
-):
+def norm_mix_kernel(pieces, place_ref, own_ref, other_ref, gain_ref, shift_ref, bias_ref, *refs):
+    weight = jnp.concatenate(
+        [ref[...].reshape(own_ref.shape[1], -1) for ref in refs[:pieces]], axis=1
+    )
+    a_ref, q_ref, k_ref, v_ref = refs[pieces:]
     lanes = q_ref.shape[1]
-    mine = lax.rem(pl.program_id(0), 2) == core_ref[0]
+    mine = lax.rem(pl.program_id(0), 2) == lax.rem(place_ref[0], 2)
     own, other = own_ref[...].astype(jnp.float32), other_ref[...].astype(jnp.float32)
     normed = layer_norm(jnp.where(mine, own, other), gain_ref[...], shift_ref[...])
     normed = normed.astype(jnp.bfloat16)
     a_ref[...] = normed
-    mixed = (plain_product(normed, weight_ref[...]) + bias_ref[...]).astype(jnp.bfloat16)
+    mixed = (plain_product(normed, weight) + bias_ref[...]).astype(jnp.bfloat16)
     q_ref[...] = mixed[:, :lanes]
     k_ref[...] = mixed[:, lanes : 2 * lanes]
     v_ref[...] = mixed[:, 2 * lanes :]
 
 
-def norm_mix(core, own, other, block, gain, shift, weight, bias):
+def norm_mix(place, own, other, block, gain, shift, weight, bias):
     length, width = own.shape[0] * 2, own.shape[1]
-    lanes = weight.shape[1] // 3
-    row = lambda size: pl.BlockSpec((block, size), lambda i, core: (i, 0))
-    half = pl.BlockSpec((block, width), lambda i, core: (i // 2, 0))
-    fixed = lambda *shape: pl.BlockSpec(shape, lambda i, core: (0, 0))
+    lanes = bias.shape[0] // 3
+    row = lambda size: pl.BlockSpec((block, size), lambda i, place: (i, 0))
+    half = pl.BlockSpec((block, width), lambda i, place: (i // 2, 0))
+    fixed = lambda *shape: pl.BlockSpec(shape, lambda i, place: (0, 0))
     part = jax.ShapeDtypeStruct((length, lanes), jnp.bfloat16)
+    if weight.ndim == 3:
+        count = weight.shape[0]
+        columns = lambda k: pl.BlockSpec(
+            (count, width // count, lanes), lambda i, place: (0, k, place[0])
+        )
+        weights, weight_specs = [weight] * 3, [columns(k) for k in range(3)]
+    else:
+        weights, weight_specs = [weight], [fixed(width, 3 * lanes)]
     return pl.pallas_call(
-        norm_mix_kernel,
+        functools.partial(norm_mix_kernel, len(weights)),
         grid_spec=pltpu.PrefetchScalarGridSpec(
             num_scalar_prefetch=1,
             grid=(length // block,),
@@ -247,8 +257,8 @@
                 half,
                 fixed(1, width),
                 fixed(1, width),
-                fixed(width, 3 * lanes),
                 fixed(1, 3 * lanes),
+                *weight_specs,
             ],
             out_specs=[row(width), row(lanes), row(lanes), row(lanes)],
         ),
@@ -258,7 +268,7 @@
             flops=length * width * lanes * 6, bytes_accessed=length * width * 4, transcendentals=0
         ),
         name="norm_mix",
-    )(core, own, other, gain[None], shift[None], weight, bias[None])
+    )(place, own, other, gain[None], shift[None], bias[None], *weights)
 
 
 def mlp_kernel(pieces, core_ref, own_ref, other_ref, gm_own_ref, gm_other_ref, bias_ref, *refs):
@@ -517,18 +527,19 @@
     return (pick(place), lax.ppermute(pick(1 - place), axis, [(0, 1), (1, 0)]))
 
 
-def scatter_direct(value, axis, dim):
+def scatter_step(value, axis, moving, step):
     place = lax.axis_index(axis)
     size = lax.axis_size(axis)
-    pick = lambda slot: lax.dynamic_index_in_dim(
-        value, jnp.clip(slot, 0, size - 1), dim, keepdims=False
-    )
-    terms = [pick(place)]
-    for distance in range(size - 1, 0, -1):
-        for move in (-distance, distance):
-            pairs = [(i, i + move) for i in range(size) if 0 <= i + move < size]
-            terms.append(lax.ppermute(pick(place + move), axis, pairs))
-    return rounded_sum(*terms)
+    sums = []
+    for n, sign in enumerate((-1, 1)):
+        start = 0 if sign < 0 else size - 1
+        pairs = [(i, i - sign) for i in range(size) if 0 <= i - sign < size]
+        pairs = [(i, j) for i, j in pairs if abs(i - start) <= step - 1]
+        slot = jnp.clip(place - sign * (size - step), 0, size - 1)
+        own = lax.dynamic_index_in_dim(value, slot, 0, keepdims=False)
+        payload = own if moving is None else rounded_sum(own, moving[n])
+        sums.append(lax.ppermute(payload, axis, pairs))
+    return tuple(sums)
 
 
 def scatter_line(value, axis, dim):
@@ -601,44 +612,23 @@
     up_end = 2 * share * folds
     low = lambda value: value.astype(jnp.bfloat16)
     direct = share % 16 == 0 and unit_block == 128
-    pieces = line_pieces(tokens, "line")
-    if direct:
-        fold = lambda value: low(value).reshape(share, -1, width).swapaxes(0, 1).reshape(-1, width)
-        packed = jnp.concatenate([fold(hidden_up), low(hidden_down), low(project_out)], axis=0)
-        pieces = dict(pieces)
-        begun = sorted(pieces, key=abs)[:4]
-        packed, *tied = lax.optimization_barrier((packed, *[pieces[n] for n in begun]))
-        pieces = list((pieces | dict(zip(begun, tied))).items())
-        gathered = lax.all_gather(packed, everyone, axis=0, tiled=False)
-        whole_out = gathered[:, packed.shape[0] - share :].reshape(width, width)
-        mlp_weights = (gathered,)
-    own_tokens = line_order(tokens, pieces, "line").reshape(-1, width)
-    swapped = [(distance, swap_cores(piece)) for distance, piece in pieces]
-    other_tokens = line_order(swap_cores(tokens), swapped, "line").reshape(-1, width)
-
-    owned = project_in.astype(jnp.bfloat16).reshape(share, 3, group, lanes)
-    owned = owned.transpose(2, 0, 1, 3).reshape(group, share, 3 * lanes)
     position = lax.broadcasted_iota(jnp.int32, (images, rows), 1)
     found = (segment_ids[None, :] == lax.broadcasted_iota(jnp.int32, (images, rows), 0)) & (
         valid[None, :] == 1
     )
     first = jnp.min(jnp.where(found, position, rows), axis=1)
-    small = jnp.concatenate(
-        [
-            gains_biases.astype(jnp.bfloat16).reshape(-1),
-            (first // 32).astype(jnp.bfloat16),
-            (first % 32).astype(jnp.bfloat16),
-        ]
-    )
+    small = jnp.concatenate([low(gains_biases).reshape(-1), low(first // 32), low(first % 32)])
+    fold = lambda value: low(value).reshape(share, -1, width).swapaxes(0, 1).reshape(-1, width)
+    if direct:
+        small = jnp.pad(small, (0, 16 * width - small.shape[0])).reshape(16, width)
+        whole_in = lax.all_gather(
+            jnp.concatenate([fold(project_in), small], axis=0), everyone, axis=0, tiled=False
+        )
+        small = whole_in[:, 3 * share]
+    else:
+        whole_in = lax.all_gather(low(project_in), everyone, axis=0, tiled=True)
+        small = lax.all_gather(small, everyone, axis=0, tiled=False)
     vector_size = gains_biases.size
-    extra = -(-small.shape[0] // (3 * lanes))
-    small = jnp.pad(small, (0, extra * 3 * lanes - small.shape[0])).reshape(1, extra, 3 * lanes)
-    blocks = jnp.concatenate([owned, jnp.broadcast_to(small, (group, extra, 3 * lanes))], axis=1)
-    blocks = lax.all_to_all(blocks, seq, split_axis=0, concat_axis=0, tiled=True)
-    blocks = gather_line(gather_line(blocks, "inner"), "outer")
-    blocks = blocks.reshape(count, share + extra, 3 * lanes)
-    mine_in = blocks[:, :share].reshape(width, 3 * lanes)
-    small = blocks[:, share:].reshape(count, -1)
     vectors = small[:, :vector_size].reshape(count, -1, share).transpose(1, 0, 2)
     vectors = vectors.reshape(-1, width).astype(jnp.float32)
     first = small[:, vector_size : vector_size + 2 * images].astype(jnp.int32)
@@ -646,6 +636,18 @@
     first = lax.dynamic_slice_in_dim(first, lax.axis_index(planes) * group, group, 0)
     offsets = lax.broadcasted_iota(jnp.int32, (group, images), 0) * rows
     starts = jnp.min(jnp.where(first < rows, first + offsets, length), axis=0)
+
+    pieces = line_pieces(tokens, "line")
+    if direct:
+        packed = jnp.concatenate([fold(hidden_up), low(hidden_down), low(project_out)], axis=0)
+        packed, pieces_in = lax.optimization_barrier((packed, tuple(piece for _, piece in pieces)))
+        pieces = [(distance, piece) for (distance, _), piece in zip(pieces, pieces_in)]
+        gathered = lax.all_gather(packed, everyone, axis=0, tiled=False)
+        whole_out = gathered[:, packed.shape[0] - share :].reshape(width, width)
+        mlp_weights = (gathered,)
+    own_tokens = line_order(tokens, pieces, "line").reshape(-1, width)
+    swapped = [(distance, swap_cores(piece)) for distance, piece in pieces]
+    other_tokens = line_order(swap_cores(tokens), swapped, "line").reshape(-1, width)
 
     gain_one, shift_one, bias_query, bias_value, bias_out = (
         vectors[0],
@@ -675,15 +677,15 @@
     grad_rows = cotangent.astype(jnp.float32) * valid.astype(jnp.float32)[:, None]
     grad_branch = (scale_two * grad_rows).astype(jnp.bfloat16)
 
+    place = lax.axis_index(seq)
+    if direct:
+        mine_in = whole_in
+    else:
+        mine_in = lax.dynamic_index_in_dim(
+            whole_in.reshape(width, 3, group, lanes), place, axis=2, keepdims=False
+        ).reshape(width, 3 * lanes)
     normed_one, query, keys, values = norm_mix(
-        core.reshape(1),
-        own_tokens,
-        other_tokens,
-        rows,
-        gain_one,
-        shift_one,
-        mine_in,
-        bias_in,
+        place.reshape(1), own_tokens, other_tokens, rows, gain_one, shift_one, mine_in, bias_in
     )
     wide, attended, logs = attend(starts, query, keys, values)
     if not direct:
@@ -697,10 +699,6 @@
     returned = lax.all_to_all(
         attended.reshape(group, rows, lanes), seq, split_axis=0, concat_axis=0, tiled=True
     )
-    in_rows, returned = lax.optimization_barrier((low(project_in), returned))
-    if direct:
-        in_rows = in_rows.reshape(share, 3, width).swapaxes(0, 1).reshape(-1, width)
-    whole_in = lax.all_gather(in_rows, everyone, axis=0, tiled=not direct)
     attended_rows = returned.transpose(1, 0, 2).reshape(rows, width)
     inputs = tokens.astype(jnp.float32)
     projected = plain_product(attended_rows, whole_out) + bias_out
@@ -746,7 +744,8 @@
         scatter_terms(grad_out, "inner", 1),
         scatter_terms(grad_down, "outer", 0),
     )
-
+    out_terms, grad_stream = lax.optimization_barrier((begun[1], grad_stream))
+    begun = (begun[0], out_terms, begun[2])
     grad_mixed_stream = attend_back(starts, query, keys, values, wide, logs, grad_stream)
     grad_mixed = lax.all_to_all(
         grad_mixed_stream.reshape(group, rows, 3 * lanes), seq, split_axis=0, concat_axis=0, tiled=True
@@ -754,17 +753,23 @@
     begun, grad_mixed_stream = lax.optimization_barrier((begun, grad_mixed_stream))
     grad_up, grad_out, grad_down = (rounded_sum(*terms) for terms in begun)
     grad_down = scatter_line(grad_down, "inner", 0)
-    grad_up, grad_out = (scatter_line(value, "outer", 0) for value in (grad_up, grad_out))
-    plane_sums = jnp.concatenate([grad_up, grad_out, grad_down], axis=1)
-    plane_sums, grad_mixed = lax.optimization_barrier((plane_sums, grad_mixed))
-    summed = scatter_direct(plane_sums, "line", 0)
+    grad_up = scatter_line(jnp.concatenate([grad_up, grad_out], axis=2), "outer", 0)
+    plane_sums = jnp.concatenate([grad_up, grad_down], axis=1)
+    moving = scatter_step(plane_sums, "line", None, 1)
+    moving, grad_mixed = lax.optimization_barrier((moving, grad_mixed))
     grad_in = inner_rows(normed_one, grad_mixed_stream).astype(jnp.bfloat16)
     parts = grad_in.reshape(outer, inner, group * share, 3 * lanes)
     parts = scatter_line(scatter_line(parts, "inner", 1), "outer", 0)
     input_grad, grad_gain_one, grad_shift_one, mixed_sums = finish(
         grad_mixed, whole_in, tokens, grad_second, gain_one
     )
-    parts, grad_gain_one = lax.optimization_barrier((parts, grad_gain_one))
+    for step in range(2, line):
+        moving = scatter_step(plane_sums, "line", moving, step)
+        if step == 2:
+            moving, parts, grad_gain_one = lax.optimization_barrier((moving, parts, grad_gain_one))
+    summed = rounded_sum(
+        lax.dynamic_index_in_dim(plane_sums, lax.axis_index("line"), 0, keepdims=False), *moving
+    )
     parts = parts.reshape(group, share, 3 * lanes)
     parts = lax.all_to_all(parts, seq, split_axis=0, concat_axis=0, tiled=True)
     parts = parts.astype(jnp.float32)

time: 606 us -> 573 us (0.946)
  blocking collectives: 23.7 us -> 0 us
  waiting for transfers between devices: 242 us -> 253 us
  local copies, waits for them, and re-layouts: 60.5 us -> 49.9 us
  starting transfers between devices: 71.4 us -> 62.2 us
    all_gather x1, waiting for transfers between devices: 0.01 us -> 68.2 us  [on_device(): gathered = lax.all_gather(packed, everyone, axis=0, tiled=False)]
    ppermute x8 -> x6, waiting for transfers between devices: 52.6 us -> 19.4 us  [scatter_step(): sums.append(lax.ppermute(payload, axis, pairs))]
    all_to_all x2 -> x0, blocking collectives: 23.7 us -> none  [the longest x1 13.6 us: on_device(): lax.all_to_all(blocks, seq, split_axis=0, concat_axis=0, tiled=True)]
    all_to_all x1, waiting for transfers between devices: 22.8 us -> 0.01 us  [on_device(): lax.all_to_all(grad_attended.reshape(rows, group, lanes).transpose(1, 0,...]
    all_to_all x1, waiting for transfers between devices: 21.7 us -> 0.01 us  [on_device(): lax.all_to_all(attended.reshape(group, rows, lanes), seq, split_axis=0, c...]
    ppermute x8 -> x6, starting transfers between devices: 27.2 us -> 16.2 us  [scatter_step(): sums.append(lax.ppermute(payload, axis, pairs))]
    all_to_all x0 -> x1, waiting for transfers between devices: none -> 7.38 us  [on_device(): lax.all_to_all(parts.reshape(count, small_rows * share), everyone, split_...]
    convert_element_type x9 -> x10, other arithmetic: 12.1 us -> 17.6 us  [rounded_sum(): sum((term.astype(jnp.float32) for term in terms)).astype(jnp.bfloat16)]
  transfers between devices with their start and end apart: 40 -> 38, of which waited for: 13 -> 16; matrix products, arithmetic and copies ran while one was open for 18% -> 15% of each run, Pallas kernels for 13% -> 15%
where the time goes in v7:
time: 573 us; the launch traced here: 564 us
  waiting for transfers between devices  253 us (44%)
  Pallas kernels  125 us (22%)
  starting transfers between devices  62.2 us (11%)
  local copies, waits for them, and re-layouts  49.9 us (9%)
  other arithmetic  46.3 us (8%)
  between operations  15.4 us (3%)
  matrix products  11.9 us (2%)
    ppermute x6, waiting for transfers between devices, line_pieces(): moving = lax.ppermute(moving, axis, pairs)  102 us
    all_gather x1, waiting for transfers between devices, on_device(): gathered = lax.all_gather(packed, everyone, axis=0, tiled=False)  68.2 us
    pallas_call x1, Pallas kernels, mlp(): pl.pallas_call(functools.partial(mlp_kernel, pieces), grid_spec=pltpu.Pre...  38 us
    pallas_call x1, Pallas kernels, attend_back(): pl.pallas_call(attend_back_kernel, grid_spec=pltpu.PrefetchScalarGridSpec...  34.9 us
    pallas_call x1, Pallas kernels, attend(): pl.pallas_call(attend_kernel, grid_spec=pltpu.PrefetchScalarGridSpec(num_...  26.9 us
    ppermute x4, waiting for transfers between devices, scatter_line(): lax.ppermute(pick(1 - place), axis, [(0, 1), (1, 0)])  24.4 us
    ppermute x3, waiting for transfers between devices, scatter_terms(): return (pick(place), lax.ppermute(pick(1 - place), axis, [(0, 1), (1, 0)]))  20.1 us
    ppermute x6, waiting for transfers between devices, scatter_step(): sums.append(lax.ppermute(payload, axis, pairs))  19.4 us
  transfers between devices with their start and end apart: 38, of which 16 were waited for; matrix products, arithmetic and copies ran while one was open for 15% of the time, Pallas kernels for 15%

profile of v7, /device:TPU:0, one launch (start us, length us, event | category | flops | bytes accessed | tf_op | source)
XLA Modules:
  0.0 563.6 jit_solution(9786336879929134434)
XLA Ops:
  12.0 5.0 collective-permute-start
  18.3 28.1 %collective-permute-done = bf16[512,1024]{1,0:T(8,128)(2,1)S(1)} collective-permute-done((bf16[512,1024]{1,0:T(8,128)(2,1)S(1)}, bf16[512,1024]{1,0:T(8,128)(2,1)S(1)}, u32[]{:S(2)}, u32[]{:S(2)}) %collective-permute-start) | collective-permute-done | bytes 1048608 | tf_op jit(solution)/shard_map/ppermute | solution.py:496
  46.5 1.7 collective-permute-start.1
  48.1 5.1 collective-permute-done.3
  54.6 1.6 collective-permute-start.2
  56.2 44.8 %collective-permute-done.4 = bf16[512,1024]{1,0:T(8,128)(2,1)} collective-permute-done((bf16[512,1024]{1,0:T(8,128)(2,1)S(1)}, bf16[512,1024]{1,0:T(8,128)(2,1)}, u32[]{:S(2)}, u32[]{:S(2)}) %collective-permute-start.4) | collective-permute-done | bytes 1048608 | tf_op jit(solution)/shard_map/ppermute | solution.py:496
  103.3 23.9 %collective-permute-done.5 = bf16[512,1024]{1,0:T(8,128)(2,1)} collective-permute-done((bf16[512,1024]{1,0:T(8,128)(2,1)}, bf16[512,1024]{1,0:T(8,128)(2,1)}, u32[]{:S(2)}, u32[]{:S(2)}) %collective-permute-start.5) | collective-permute-done | bytes 1048608 | tf_op jit(solution)/shard_map/ppermute | solution.py:496
  131.6 1.4 bitcast_dynamic-update-slice_fusion.11
  133.0 1.4 bitcast_dynamic-update-slice_fusion.10
  135.3 2.8 broadcast.119.clone.1
  144.8 2.3 bitcast_dynamic-update-slice_fusion
  151.7 14.4 %norm_mix.1 = (bf16[4096,1024]{1,0:T(8,128)(2,1)}, bf16[4096,128]{1,0:T(8,128)(2,1)}, bf16[4096,128]{1,0:T(8,128)(2,1)}, bf16[4096,128]{1,0:T(8,128)(2,1)}) custom-call(s32[1]{0:T(128)} %bitcast.4.place_ref, bf16[2048,1024]{1,0:T(8,128)(2,1)} %bitcast.194, bf16[2048,1024]{1,0:T(8,128)(2,1)} %bitcast.22.other_ref, f32[1,1024]{1,0:T(1,128)} %slice.120.gain_ref, ...), custom_call_target="tpu_custom_call" | custom-call | flops 3221225472 | bytes 16777216 | tf_op jit(solution)/shard_map/norm_mix/pallas_call | solution.py:250
  166.1 26.9 %attend_forward.1 = (f32[4096,128]{1,0:T(8,128)}, bf16[4096,128]{1,0:T(8,128)(2,1)}, f32[4096,128]{1,0:T(8,128)}) custom-call(s32[2]{0:T(128)} %select_reduce_fusion.starts_ref, bf16[4096,128]{1,0:T(8,128)(2,1)} %get-tuple-element.66.q_ref, bf16[4096,128]{1,0:T(8,128)(2,1)} %get-tuple-element.67.k_ref, bf16[4096,128]{1,0:T(8,128)(2,1)} %get-tuple-element.68.v_ref), custom_call_target="tpu_custom_call" | custom-call | flops 4060086272 | bytes 8388608 | tf_op jit(solution)/shard_map/attend_forward/pallas_call | solution.py:116
  193.0 2.6 copy.82
  195.6 4.0 all-to-all-start
  200.1 1.4 convert_reduce_fusion
  201.9 68.2 %all-gather.7.cloned.1.call-done = bf16[9216,1024]{1,0:T(8,128)(2,1)} async-done(((bf16[288,1024]{1,0:T(8,128)(2,1)}), bf16[9216,1024]{1,0:T(8,128)(2,1)}) %all-gather.7.cloned.1.call-update) | async-done | bytes 18874384 | tf_op jit(solution)/shard_map/all_gather | solution.py:645
  270.1 3.2 slice.157
  274.3 4.8 fusion.60
  279.5 1.4 add_convert_fusion.4.own_ref
  281.9 2.0 collective-permute-done.13.other_ref
  283.9 38.0 %mlp_both_ways.1 = (bf16[16,128,1024]{2,1,0:T(8,128)(2,1)}, bf16[16,128,1024]{2,1,0:T(8,128)(2,1)}, f32[512,1024]{1,0:T(8,128)}, f32[512,1024]{1,0:T(8,128)}, f3...) custom-call(s32[1]{0:T(128)} %bitcast.30.core_ref, bf16[512,1024]{1,0:T(8,128)(2,1)} %add_convert_fusion.4.own_ref, ...), custom_call_target="tpu_custom_call" | custom-call | flops 25769803776 | bytes 29360128 | tf_op jit(solution)/shard_map/mlp_both_ways/pallas_call | solution.py:360
  322.5 3.9 collective-permute-done.17
  326.4 3.8 multiply_reduce_fusion.1
  330.2 4.2 multiply_reduce_fusion
  335.4 2.0 copy-done.9
  339.8 4.4 all-to-all-start.1
  346.7 1.4 collective-permute-start.18
  348.1 4.4 dynamic-slice_bitcast_fusion.2
  353.1 2.5 dynamic-slice_bitcast_fusion
  355.6 1.5 collective-permute-start.19
  357.1 15.9 %collective-permute-done.18 = bf16[2,4,64,1024]{3,2,1,0:T(8,128)(2,1)} collective-permute-done((bf16[2,4,64,1024]{3,2,1,0:T(8,128)(2,1)}, bf16[2,4,64,1024]{3,2,1,0:T(8,128)(2,1)}, u32[]{:S(2)}, u32[]{:S(2)}) %collective-permute-start.18) | collective-permute-done | bytes 1048608 | tf_op jit(solution)/shard_map/ppermute | solution.py:527
  373.0 34.9 %attend_backward.1 = bf16[4096,384]{1,0:T(8,128)(2,1)} custom-call(s32[2]{0:T(128)} %select_reduce_fusion.starts_ref, bf16[4096,128]{1,0:T(8,128)(2,1)} %get-tuple-element.66.q_ref, bf16[4096,128]{1,0:T(8,128)(2,1)} %get-tuple-element.67.k_ref, bf16[4096,128]{1,0:T(8,128)(2,1)} %get-tuple-element.68.v_ref, f32[4096,128]{1,0:T(8,128)} %get-tuple-element.79.wide_ref, ...), custom_call_target="tpu_custom_call" | custom-call | flops 10150215680 | bytes 11534336 | tf_op jit(solution)/shard_map/attend_backward/pallas_call | solution.py:196
  407.9 5.4 all-to-all-start.2
  413.3 4.2 collective-permute-done.16
  417.5 1.8 add_convert_fusion.2
  419.3 2.6 add_convert_fusion.1
  422.0 1.5 collective-permute-start.20
  423.5 2.8 add_convert_fusion
  426.4 1.5 collective-permute-start.21
  427.9 4.5 convolution_convert_fusion.2
  433.2 19.4 %collective-permute-done.21 = bf16[4,128,1024]{2,1,0:T(8,128)(2,1)S(1)} collective-permute-done((bf16[4,128,1024]{2,1,0:T(8,128)(2,1)S(1)}, bf16[4,128,1024]{2,1,0:T(8,128)(2,1)S(1)}, u32[]{:S(2)}, u32[]{:S(2)}) %collective-permute-start.21) | collective-permute-done | bytes 1048608 | tf_op jit(solution)/shard_map/ppermute | solution.py:552
  453.0 5.0 collective-permute-done.20
  459.9 4.1 collective-permute-start.22
  464.0 1.6 collective-permute-start.23
  466.8 1.5 collective-permute-start.27
  468.3 10.7 %collective-permute-done.22 = bf16[320,1024]{1,0:T(8,128)(2,1)} collective-permute-done((bf16[320,1024]{1,0:T(8,128)(2,1)}, bf16[320,1024]{1,0:T(8,128)(2,1)}, u32[]{:S(2)}, u32[]{:S(2)}) %collective-permute-start.22) | collective-permute-done | bytes 655392 | tf_op jit(solution)/shard_map/ppermute | solution.py:541
  479.1 5.8 %all-to-all-done.2.grad_ref = bf16[8,512,384]{2,1,0:T(8,128)(2,1)} async-done(((bf16[8,512,384]{2,1,0:T(8,128)(2,1)}), bf16[8,512,384]{2,1,0:T(8,128)(2,1)}, u32[]{:S(2)}, u32[]{:S(2)}) %all-to-all-start.2) | async-done | bytes 3145760 | tf_op jit(solution)/shard_map/all_to_all | solution.py:750
  484.9 2.9 fusion.11
  487.8 2.1 collective-permute-start.24
  489.9 1.7 collective-permute-start.25
  494.9 10.5 %finish_input.1 = (f32[512,1024]{1,0:T(8,128)}, f32[1,1024]{1,0:T(1,128)}, f32[1,1024]{1,0:T(1,128)}, f32[3,1,1024]{2,1,0:T(1,128)}) custom-call(bf16[8,512,384]{2,1,0:T(8,128)(2,1)} %all-to-all-done.2.grad_ref, bf16[32,112,1024]{2,1,0:T(8,128)(2,1)} %bitcast.193, bf16[512,1024]{1,0:T(8,128)(2,1)} %x_ref.1, f32[512,1024]{1,0:T(8,128)} %copy-done, ...), custom_call_target="tpu_custom_call" | custom-call | flops 3221225472 | bytes 16777216 | tf_op jit(solution)/shard_map/finish_input/pallas_call | solution.py:450
  506.0 1.3 reduce.56
  508.3 1.4 reduce.55
  510.8 3.9 all-to-all-start.4
  514.7 7.4 %all-to-all-done.4 = f32[32,1,448]{2,1,0:T(1,128)S(1)} async-done(((f32[32,1,448]{2,1,0:T(1,128)}), f32[32,1,448]{2,1,0:T(1,128)S(1)}, u32[]{:S(2)}, u32[]{:S(2)}) %all-to-all-start.4) | async-done | bytes 57376 | tf_op jit(solution)/shard_map/all_to_all | solution.py:803
  522.0 4.0 all-to-all-start.3
  526.1 3.0 fusion.8
  530.4 5.4 collective-permute-start.28
  538.4 2.4 multiply_subtract_fusion.2
  540.8 7.6 %collective-permute-done.29 = bf16[320,1024]{1,0:T(8,128)(2,1)} collective-permute-done((bf16[320,1024]{1,0:T(8,128)(2,1)}, bf16[320,1024]{1,0:T(8,128)(2,1)}, u32[]{:S(2)}, u32[]{:S(2)}) %collective-permute-start.29) | collective-permute-done | bytes 655392 | tf_op jit(solution)/shard_map/ppermute | solution.py:541
  549.5 1.6 fusion.10
  551.3 1.4 multiply_subtract_fusion
  554.3 1.4 multiply_subtract_fusion.1
  (239 shorter events, 53.6 us)
Async XLA Ops:
  7.2 4.8 copy-start.4
  7.2 95.1 %copy-start.22 = (f32[32,1024]{1,0:T(8,128)S(1)}, f32[32,1024]{1,0:T(8,128)}, u32[]{:S(2)}) copy-start(f32[32,1024]{1,0:T(8,128)} %param.24) | copy-start | bytes 393220
  7.2 95.1 %copy-start.10 = (f32[128,1024]{1,0:T(8,128)S(1)}, f32[128,1024]{1,0:T(8,128)}, u32[]{:S(2)}) copy-start(f32[128,1024]{1,0:T(8,128)} %param.26) | copy-start | bytes 1572868
  7.2 95.1 %copy-start.7 = (f32[32,4096]{1,0:T(8,128)S(1)}, f32[32,4096]{1,0:T(8,128)}, u32[]{:S(2)}) copy-start(f32[32,4096]{1,0:T(8,128)} %param.25) | copy-start | bytes 1572868
  7.2 139.9 %all-gather.5.cloned.1.call-start = ((), (), s32[]{:S(2)}) async-start(), calls=%async_computation.5 | async-start | bytes 7569408 | tf_op jit(solution)/shard_map/all_gather | solution.py:624
  12.0 258.1 %all-gather.7.cloned.1.call-start = ((), (), s32[]{:S(2)}) async-start(), calls=%async_computation.6 | async-start | bytes 19464192 | tf_op jit(solution)/shard_map/all_gather | solution.py:645
  12.0 34.4 %collective-permute-start = (bf16[512,1024]{1,0:T(8,128)(2,1)S(1)}, bf16[512,1024]{1,0:T(8,128)(2,1)S(1)}, u32[]{:S(2)}, u32[]{:S(2)}) collective-permute-start(bf16[512,1024]{1,0:T(8,128)(2,1)S(1)} %copy-done.4), channel_id=1, source_target_pairs={{0,2},{2,4},{4,6},{1,3},{3,5},{5,7},{8,10},{10,12},{12,14},{9,11},... | collective-permute-start | bytes 3145736 | tf_op jit(solution)/shard_map/ppermute | solution.py:496
  17.0 36.3 %collective-permute-start.3 = (bf16[512,1024]{1,0:T(8,128)(2,1)S(1)}, bf16[512,1024]{1,0:T(8,128)(2,1)S(1)}, u32[]{:S(2)}, u32[]{:S(2)}) collective-permute-start(bf16[512,1024]{1,0:T(8,128)(2,1)S(1)} %copy-done.4), channel_id=1, source_target_pairs={{2,0},{4,2},{6,4},{3,1},{5,3},{7,5},{10,8},{12,10},{14,12},{11,9},... | collective-permute-start | bytes 3145736 | tf_op jit(solution)/shard_map/ppermute | solution.py:496
  46.5 54.5 %copy-start.15 = (bf16[512,1024]{1,0:T(8,128)(2,1)}, bf16[512,1024]{1,0:T(8,128)(2,1)S(1)}, u32[]{:S(2)}) copy-start(bf16[512,1024]{1,0:T(8,128)(2,1)S(1)} %collective-permute-done) | copy-start | bytes 3145732
  46.5 8.1 %collective-permute-start.1 = (bf16[512,1024]{1,0:T(8,128)(2,1)S(1)}, bf16[512,1024]{1,0:T(8,128)(2,1)}, u32[]{:S(2)}, u32[]{:S(2)}) collective-permute-start(bf16[512,1024]{1,0:T(8,128)(2,1)S(1)} %collective-permute-done), channel_id=1, source_target_pairs={{2,4},{4,6},{3,5},{5,7},{10,12},{12,14},{11,13},{13,15},{18,20},{2... | collective-permute-start | bytes 3145736 | tf_op jit(solution)/shard_map/ppermute | solution.py:496
  53.3 47.7 %collective-permute-start.4 = (bf16[512,1024]{1,0:T(8,128)(2,1)S(1)}, bf16[512,1024]{1,0:T(8,128)(2,1)}, u32[]{:S(2)}, u32[]{:S(2)}) collective-permute-start(bf16[512,1024]{1,0:T(8,128)(2,1)S(1)} %collective-permute-done.3), channel_id=1, source_target_pairs={{2,0},{4,2},{3,1},{5,3},{10,8},{12,10},{11,9},{13,11},{18,16},{20,... | collective-permute-start | bytes 3145736 | tf_op jit(solution)/shard_map/ppermute | solution.py:496
  54.6 48.7 %collective-permute-start.2 = (bf16[512,1024]{1,0:T(8,128)(2,1)}, bf16[512,1024]{1,0:T(8,128)(2,1)}, u32[]{:S(2)}, u32[]{:S(2)}) collective-permute-start(bf16[512,1024]{1,0:T(8,128)(2,1)} %collective-permute-done.1), channel_id=1, source_target_pairs={{4,6},{5,7},{12,14},{13,15},{20,22},{21,23},{28,30},{29,31}} | collective-permute-start | bytes 3145736 | tf_op jit(solution)/shard_map/ppermute | solution.py:496
  101.0 26.1 %collective-permute-start.5 = (bf16[512,1024]{1,0:T(8,128)(2,1)}, bf16[512,1024]{1,0:T(8,128)(2,1)}, u32[]{:S(2)}, u32[]{:S(2)}) collective-permute-start(bf16[512,1024]{1,0:T(8,128)(2,1)} %collective-permute-done.4), channel_id=1, source_target_pairs={{2,0},{3,1},{10,8},{11,9},{18,16},{19,17},{26,24},{27,25}} | collective-permute-start | bytes 3145736 | tf_op jit(solution)/shard_map/ppermute | solution.py:496
  127.1 17.7 %collective-permute-start.12 = (bf16[512,1024]{1,0:T(8,128)(2,1)S(1)}, bf16[512,1024]{1,0:T(8,128)(2,1)}, u32[]{:S(2)}, u32[]{:S(2)}) collective-permute-start(bf16[512,1024]{1,0:T(8,128)(2,1)S(1)} %copy-done.4), channel_id=1, source_target_pairs={{0,1},{1,0},{2,3},{3,2},{4,5},{5,4},{6,7},{7,6},{8,9},{9,8},{10,11... | collective-permute-start | bytes 3145736 | tf_op jit(solution)/shard_map/ppermute | solution.py:482
  127.3 7.5 %collective-permute-start.6 = (bf16[512,1024]{1,0:T(8,128)(2,1)}, bf16[512,1024]{1,0:T(8,128)(2,1)S(1)}, u32[]{:S(2)}, u32[]{:S(2)}) collective-permute-start(bf16[512,1024]{1,0:T(8,128)(2,1)} %collective-permute-done.2), channel_id=1, source_target_pairs={{0,1},{1,0},{2,3},{3,2},{4,5},{5,4},{6,7},{7,6},{8,9},{9,8},{10,11... | collective-permute-start | bytes 3145736 | tf_op jit(solution)/shard_map/ppermute | solution.py:482
  127.7 11.4 %collective-permute-start.7 = (bf16[512,1024]{1,0:T(8,128)(2,1)}, bf16[512,1024]{1,0:T(8,128)(2,1)S(1)}, u32[]{:S(2)}, u32[]{:S(2)}) collective-permute-start(bf16[512,1024]{1,0:T(8,128)(2,1)} %collective-permute-done.5), channel_id=1, source_target_pairs={{0,1},{1,0},{2,3},{3,2},{4,5},{5,4},{6,7},{7,6},{8,9},{9,8},{10,11... | collective-permute-start | bytes 3145736 | tf_op jit(solution)/shard_map/ppermute | solution.py:482
  127.8 12.7 %collective-permute-start.8 = (bf16[512,1024]{1,0:T(8,128)(2,1)}, bf16[512,1024]{1,0:T(8,128)(2,1)S(1)}, u32[]{:S(2)}, u32[]{:S(2)}) collective-permute-start(bf16[512,1024]{1,0:T(8,128)(2,1)} %collective-permute-done.1), channel_id=1, source_target_pairs={{0,1},{1,0},{2,3},{3,2},{4,5},{5,4},{6,7},{7,6},{8,9},{9,8},{10,11... | collective-permute-start | bytes 3145736 | tf_op jit(solution)/shard_map/ppermute | solution.py:482
  128.2 13.4 %collective-permute-start.9 = (bf16[512,1024]{1,0:T(8,128)(2,1)}, bf16[512,1024]{1,0:T(8,128)(2,1)S(1)}, u32[]{:S(2)}, u32[]{:S(2)}) collective-permute-start(bf16[512,1024]{1,0:T(8,128)(2,1)} %collective-permute-done.4), channel_id=1, source_target_pairs={{0,1},{1,0},{2,3},{3,2},{4,5},{5,4},{6,7},{7,6},{8,9},{9,8},{10,11... | collective-permute-start | bytes 3145736 | tf_op jit(solution)/shard_map/ppermute | solution.py:482
  134.8 3.3 copy-start.1
  134.8 7.9 %collective-permute-start.10 = (bf16[512,1024]{1,0:T(8,128)(2,1)S(1)}, bf16[512,1024]{1,0:T(8,128)(2,1)S(1)}, u32[]{:S(2)}, u32[]{:S(2)}) collective-permute-start(bf16[512,1024]{1,0:T(8,128)(2,1)S(1)} %copy-done.16), channel_id=1, source_target_pairs={{0,1},{1,0},{2,3},{3,2},{4,5},{5,4},{6,7},{7,6},{8,9},{9,8},{10,11... | collective-permute-start | bytes 3145736 | tf_op jit(solution)/shard_map/ppermute | solution.py:482
  139.1 4.7 collective-permute-start.11
  193.0 6.6 %copy-start.33 = (s32[512]{0:T(512)S(1)}, s32[512]{0:T(512)}, u32[]{:S(2)}) copy-start(s32[512]{0:T(512)} %param.22) | copy-start | bytes 6148
  193.0 7.0 %copy-start.2 = (bf16[512,1024]{1,0:T(8,128)(2,1)S(1)}, bf16[512,1024]{1,0:T(8,128)(2,1)}, u32[]{:S(2)}) copy-start(bf16[512,1024]{1,0:T(8,128)(2,1)} %param.20) | copy-start | bytes 3145732
  195.6 77.7 %all-to-all-start = ((bf16[8,512,128]{1,2,0:T(8,128)(2,1)}), bf16[8,512,128]{1,2,0:T(8,128)(2,1)S(1)}, u32[]{:S(2)}, u32[]{:S(2)}) async-start(bf16[8,512,128]{1,2,0:T(8,128)(2,1)} %copy.82), calls=%async_computation | async-start | bytes 2097152 | tf_op jit(solution)/shard_map/all_to_all | solution.py:699
  201.4 80.4 %collective-permute-start.14 = (bf16[512,1024]{1,0:T(8,128)(2,1)}, bf16[512,1024]{1,0:T(8,128)(2,1)}, u32[]{:S(2)}, u32[]{:S(2)}) collective-permute-start(bf16[512,1024]{1,0:T(8,128)(2,1)} %get-tuple-element.121.gm_own_ref), channel_id=1, source_target_pairs={{0,1},{1,0},{2,3},{3,2},{4,5},{5,4},{6,7},{7,6},{8,9},{9,8},{10,11... | collective-permute-start | bytes 3145736 | tf_op jit(solution)/shard_map/ppermute | solution.py:482
  280.9 3.0 collective-permute-start.13
  321.8 4.6 collective-permute-start.17
  322.1 8.1 %collective-permute-start.15 = (f32[512,1024]{1,0:T(8,128)}, f32[512,1024]{1,0:T(8,128)}, u32[]{:S(2)}, u32[]{:S(2)}) collective-permute-start(f32[512,1024]{1,0:T(8,128)} %get-tuple-element.72), channel_id=1, source_target_pairs={{0,1},{1,0},{2,3},{3,2},{4,5},{5,4},{6,7},{7,6},{8,9},{9,8},{10,11... | collective-permute-start | bytes 6291464 | tf_op jit(solution)/shard_map/ppermute | solution.py:482
  326.4 3.8 copy-start.13
  330.2 4.2 copy-start.12
  335.0 3.7 copy-start
  338.6 5.6 copy-start.18
  339.8 33.2 %all-to-all-start.1 = ((bf16[8,512,128]{2,1,0:T(8,128)(2,1)}), bf16[8,512,128]{2,1,0:T(8,128)(2,1)}, u32[]{:S(2)}, u32[]{:S(2)}) async-start(bf16[8,512,128]{2,1,0:T(8,128)(2,1)} %bitcast.186), calls=%async_computation.1 | async-start | bytes 2097152 | tf_op jit(solution)/shard_map/all_to_all | solution.py:729
  346.7 26.3 %collective-permute-start.18 = (bf16[2,4,64,1024]{3,2,1,0:T(8,128)(2,1)}, bf16[2,4,64,1024]{3,2,1,0:T(8,128)(2,1)}, u32[]{:S(2)}, u32[]{:S(2)}) collective-permute-start(bf16[2,4,64,1024]{3,2,1,0:T(8,128)(2,1)} %get-tuple-element.157), channel_id=1, source_target_pairs={{0,8},{8,0},{1,9},{9,1},{2,10},{10,2},{3,11},{11,3},{4,12},{12,4},... | collective-permute-start | bytes 3145736 | tf_op jit(solution)/shard_map/ppermute | solution.py:527
  348.1 5.0 copy-start.5
  352.5 64.9 %collective-permute-start.16 = (bf16[2,4,128,1024]{3,2,1,0:T(8,128)(2,1)}, bf16[2,4,128,1024]{3,2,1,0:T(8,128)(2,1)}, u32[]{:S(2)}, u32[]{:S(2)}) collective-permute-start(bf16[2,4,128,1024]{3,2,1,0:T(8,128)(2,1)} %get-tuple-element.147), channel_id=1, source_target_pairs={{0,8},{8,0},{1,9},{9,1},{2,10},{10,2},{3,11},{11,3},{4,12},{12,4},... | collective-permute-start | bytes 6291464 | tf_op jit(solution)/shard_map/ppermute | solution.py:527
  355.6 61.8 %collective-permute-start.19 = (bf16[2,4,128,1024]{3,2,1,0:T(8,128)(2,1)}, bf16[2,4,128,1024]{3,2,1,0:T(8,128)(2,1)}, u32[]{:S(2)}, u32[]{:S(2)}) collective-permute-start(bf16[2,4,128,1024]{3,2,1,0:T(8,128)(2,1)} %get-tuple-element.145), channel_id=1, source_target_pairs={{0,16},{16,0},{1,17},{17,1},{2,18},{18,2},{3,19},{19,3},{4,20},{20... | collective-permute-start | bytes 6291464 | tf_op jit(solution)/shard_map/ppermute | solution.py:527
  407.9 77.0 %all-to-all-start.2 = ((bf16[8,512,384]{2,1,0:T(8,128)(2,1)}), bf16[8,512,384]{2,1,0:T(8,128)(2,1)}, u32[]{:S(2)}, u32[]{:S(2)}) async-start(bf16[8,512,384]{2,1,0:T(8,128)(2,1)} %bitcast.197), calls=%async_computation.2 | async-start | bytes 6291456 | tf_op jit(solution)/shard_map/all_to_all | solution.py:750
  417.5 10.4 %slice-start = ((s8[8388608]{0:T(1024)(128)(4,1)}), s8[4194304]{0:T(1024)(128)(4,1)S(1)}, s32[]{:S(2)}) async-start(s8[8388608]{0:T(1024)(128)(4,1)} %bitcast.225), calls=%async_computation.7 | async-start | bytes 8388608
  421.8 6.1 %slice-start.1 = ((s8[8388608]{0:T(1024)(128)(4,1)}), s8[4194304]{0:T(1024)(128)(4,1)S(1)}, s32[]{:S(2)}) async-start(s8[8388608]{0:T(1024)(128)(4,1)} %bitcast.225), calls=%async_computation.8 | async-start | bytes 8388608
  422.0 36.0 %collective-permute-start.20 = (bf16[4,192,1024]{2,1,0:T(8,128)(2,1)S(1)}, bf16[4,192,1024]{2,1,0:T(8,128)(2,1)S(1)}, u32[]{:S(2)}, u32[]{:S(2)}) collective-permute-start(bf16[4,192,1024]{2,1,0:T(8,128)(2,1)S(1)} %fusion.3), channel_id=1, source_target_pairs={{0,16},{16,0},{1,17},{17,1},{2,18},{18,2},{3,19},{19,3},{4,20},{20... | collective-permute-start | bytes 4718600 | tf_op jit(solution)/shard_map/ppermute | solution.py:552
  423.5 4.4 copy-start.6
  426.4 26.1 %collective-permute-start.21 = (bf16[4,128,1024]{2,1,0:T(8,128)(2,1)S(1)}, bf16[4,128,1024]{2,1,0:T(8,128)(2,1)S(1)}, u32[]{:S(2)}, u32[]{:S(2)}) collective-permute-start(bf16[4,128,1024]{2,1,0:T(8,128)(2,1)S(1)} %dynamic-slice_bitcast_fusion.4), channel_id=1, source_target_pairs={{0,8},{8,0},{1,9},{9,1},{2,10},{10,2},{3,11},{11,3},{4,12},{12,4},... | collective-permute-start | bytes 3145736 | tf_op jit(solution)/shard_map/ppermute | solution.py:552
  432.4 26.3 %copy-start.19 = (bf16[1024,384]{1,0:T(8,128)(2,1)}, bf16[1024,384]{1,0:T(8,128)(2,1)S(1)}, u32[]{:S(2)}) copy-start(bf16[1024,384]{1,0:T(8,128)(2,1)S(1)} %convolution_convert_fusion.2) | copy-start | bytes 2359300
  432.5 33.1 %collective-permute-start.26 = (bf16[2,256,384]{2,1,0:T(8,128)(2,1)S(1)}, bf16[2,256,384]{2,1,0:T(8,128)(2,1)S(1)}, u32[]{:S(2)}, u32[]{:S(2)}) collective-permute-start(bf16[2,256,384]{2,1,0:T(8,128)(2,1)S(1)} %dynamic-slice_bitcast_fusion.7), channel_id=1, source_target_pairs={{0,8},{8,0},{1,9},{9,1},{2,10},{10,2},{3,11},{11,3},{4,12},{12,4},... | collective-permute-start | bytes 1179656 | tf_op jit(solution)/shard_map/ppermute | solution.py:552
  459.9 19.2 %collective-permute-start.22 = (bf16[320,1024]{1,0:T(8,128)(2,1)}, bf16[320,1024]{1,0:T(8,128)(2,1)}, u32[]{:S(2)}, u32[]{:S(2)}) collective-permute-start(bf16[320,1024]{1,0:T(8,128)(2,1)} %get-tuple-element.154), channel_id=1, source_target_pairs={{0,2},{1,3},{8,10},{9,11},{16,18},{17,19},{24,26},{25,27}} | collective-permute-start | bytes 1966088 | tf_op jit(solution)/shard_map/ppermute | solution.py:541
  464.0 15.1 %collective-permute-start.23 = (bf16[320,1024]{1,0:T(8,128)(2,1)}, bf16[320,1024]{1,0:T(8,128)(2,1)}, u32[]{:S(2)}, u32[]{:S(2)}) collective-permute-start(bf16[320,1024]{1,0:T(8,128)(2,1)} %get-tuple-element.153), channel_id=1, source_target_pairs={{6,4},{7,5},{14,12},{15,13},{22,20},{23,21},{30,28},{31,29}} | collective-permute-start | bytes 1966088 | tf_op jit(solution)/shard_map/ppermute | solution.py:541
  466.8 24.9 %copy-start.32 = (f32[1,2048]{1,0:T(1,128)S(1)}, f32[1,2048]{1,0:T(1,128)}, u32[]{:S(2)}) copy-start(f32[1,2048]{1,0:T(1,128)} %get-tuple-element.101) | copy-start | bytes 24580
  466.8 27.4 %collective-permute-start.27 = (bf16[256,384]{1,0:T(8,128)(2,1)S(1)}, bf16[256,384]{1,0:T(8,128)(2,1)S(1)}, u32[]{:S(2)}, u32[]{:S(2)}) collective-permute-start(bf16[256,384]{1,0:T(8,128)(2,1)S(1)} %dynamic-slice_bitcast_fusion.8), channel_id=1, source_target_pairs={{0,16},{16,0},{1,17},{17,1},{2,18},{18,2},{3,19},{19,3},{4,20},{20... | collective-permute-start | bytes 589832 | tf_op jit(solution)/shard_map/ppermute | solution.py:552
  487.8 20.5 %collective-permute-start.24 = (bf16[320,1024]{1,0:T(8,128)(2,1)}, bf16[320,1024]{1,0:T(8,128)(2,1)}, u32[]{:S(2)}, u32[]{:S(2)}) collective-permute-start(bf16[320,1024]{1,0:T(8,128)(2,1)} %get-tuple-element.152), channel_id=1, source_target_pairs={{0,2},{2,4},{1,3},{3,5},{8,10},{10,12},{9,11},{11,13},{16,18},{18,... | collective-permute-start | bytes 1966088 | tf_op jit(solution)/shard_map/ppermute | solution.py:541
  489.9 18.3 %collective-permute-start.25 = (bf16[320,1024]{1,0:T(8,128)(2,1)}, bf16[320,1024]{1,0:T(8,128)(2,1)}, u32[]{:S(2)}, u32[]{:S(2)}) collective-permute-start(bf16[320,1024]{1,0:T(8,128)(2,1)} %get-tuple-element.151), channel_id=1, source_target_pairs={{4,2},{6,4},{5,3},{7,5},{12,10},{14,12},{13,11},{15,13},{20,18},{2... | collective-permute-start | bytes 1966088 | tf_op jit(solution)/shard_map/ppermute | solution.py:541
  494.9 14.8 %copy-start.28 = (f32[1,32,32]{2,1,0:T(8,128)S(1)}, f32[1,32,32]{2,1,0:T(8,128)}, u32[]{:S(2)}) copy-start(f32[1,32,32]{2,1,0:T(8,128)} %concatenate.61) | copy-start | bytes 12292
  510.8 11.3 %all-to-all-start.4 = ((f32[32,1,448]{2,1,0:T(1,128)}), f32[32,1,448]{2,1,0:T(1,128)S(1)}, u32[]{:S(2)}, u32[]{:S(2)}) async-start(f32[32,1,448]{2,1,0:T(1,128)} %all_to_all.24), calls=%async_computation.4 | async-start | bytes 131072 | tf_op jit(solution)/shard_map/all_to_all | solution.py:803
  522.0 15.1 %all-to-all-start.3 = ((bf16[8,32,384]{2,1,0:T(8,128)(2,1)}), bf16[8,32,384]{2,1,0:T(8,128)(2,1)}, u32[]{:S(2)}, u32[]{:S(2)}) async-start(bf16[8,32,384]{2,1,0:T(8,128)(2,1)} %bitcast.58), calls=%async_computation.3 | async-start | bytes 393216 | tf_op jit(solution)/shard_map/all_to_all | solution.py:774
  526.1 10.4 %copy-start.29 = (f32[14,32]{1,0:T(8,128)S(1)}, f32[14,32]{1,0:T(8,128)}, u32[]{:S(2)}) copy-start(f32[14,32]{1,0:T(8,128)} %param.27) | copy-start | bytes 5380
  526.1 10.4 %copy-start.30 = (f32[14,32]{1,0:T(8,128)S(1)}, f32[14,32]{1,0:T(8,128)}, u32[]{:S(2)}) copy-start(f32[14,32]{1,0:T(8,128)} %param.32) | copy-start | bytes 5380
  526.1 10.4 %copy-start.31 = (f32[14,32]{1,0:T(8,128)S(1)}, f32[14,32]{1,0:T(8,128)}, u32[]{:S(2)}) copy-start(f32[14,32]{1,0:T(8,128)} %param.37) | copy-start | bytes 5380
  526.1 12.3 %copy-start.14 = (f32[32,3072]{1,0:T(8,128)S(1)}, f32[32,3072]{1,0:T(8,128)}, u32[]{:S(2)}) copy-start(f32[32,3072]{1,0:T(8,128)} %param.23) | copy-start | bytes 1179652
  529.1 19.3 %collective-permute-start.29 = (bf16[320,1024]{1,0:T(8,128)(2,1)}, bf16[320,1024]{1,0:T(8,128)(2,1)}, u32[]{:S(2)}, u32[]{:S(2)}) collective-permute-start(bf16[320,1024]{1,0:T(8,128)(2,1)} %get-tuple-element.150), channel_id=1, source_target_pairs={{2,0},{4,2},{6,4},{3,1},{5,3},{7,5},{10,8},{12,10},{14,12},{11,9},... | collective-permute-start | bytes 1966088 | tf_op jit(solution)/shard_map/ppermute | solution.py:541
  530.4 19.1 %collective-permute-start.28 = (bf16[320,1024]{1,0:T(8,128)(2,1)}, bf16[320,1024]{1,0:T(8,128)(2,1)}, u32[]{:S(2)}, u32[]{:S(2)}) collective-permute-start(bf16[320,1024]{1,0:T(8,128)(2,1)} %get-tuple-element.149), channel_id=1, source_target_pairs={{0,2},{2,4},{4,6},{1,3},{3,5},{5,7},{8,10},{10,12},{12,14},{9,11},... | collective-permute-start | bytes 1966088 | tf_op jit(solution)/shard_map/ppermute | solution.py:541
  540.8 10.5 %copy-start.11 = (f32[128,1024]{1,0:T(8,128)S(1)}, f32[128,1024]{1,0:T(8,128)}, u32[]{:S(2)}) copy-start(f32[128,1024]{1,0:T(8,128)} %param.26) | copy-start | bytes 1572868
  540.8 10.5 %copy-start.24 = (f32[128,1024]{1,0:T(8,128)S(1)}, f32[128,1024]{1,0:T(8,128)}, u32[]{:S(2)}) copy-start(f32[128,1024]{1,0:T(8,128)} %param.31) | copy-start | bytes 1572868
  540.8 10.5 %copy-start.25 = (f32[128,1024]{1,0:T(8,128)S(1)}, f32[128,1024]{1,0:T(8,128)}, u32[]{:S(2)}) copy-start(f32[128,1024]{1,0:T(8,128)} %param.36) | copy-start | bytes 1572868
  551.2 1.5 collective-permute-start.30
  (10 other events, 16.3 us)
Sparse Core Ops, SparseCore 0:
  12.1 88.6 all-gather.4
  127.3 142.7 all-gather.6

commit v8 on v7

--- a/solution.py
+++ b/solution.py
@@ -239,14 +239,7 @@
     half = pl.BlockSpec((block, width), lambda i, place: (i // 2, 0))
     fixed = lambda *shape: pl.BlockSpec(shape, lambda i, place: (0, 0))
     part = jax.ShapeDtypeStruct((length, lanes), jnp.bfloat16)
-    if weight.ndim == 3:
-        count = weight.shape[0]
-        columns = lambda k: pl.BlockSpec(
-            (count, width // count, lanes), lambda i, place: (0, k, place[0])
-        )
-        weights, weight_specs = [weight] * 3, [columns(k) for k in range(3)]
-    else:
-        weights, weight_specs = [weight], [fixed(width, 3 * lanes)]
+    weights, weight_specs = [weight], [fixed(width, 3 * lanes)]
     return pl.pallas_call(
         functools.partial(norm_mix_kernel, len(weights)),
         grid_spec=pltpu.PrefetchScalarGridSpec(
@@ -515,6 +508,22 @@
     return line_order(value, line_pieces(value, axis), axis)
 
 
+def exchange_line(value, axis):
+    place = lax.axis_index(axis)
+    size = lax.axis_size(axis)
+    pick = lambda slot: lax.dynamic_index_in_dim(
+        value, jnp.clip(slot, 0, size - 1), 0, keepdims=False
+    )
+    pieces = []
+    for distance in range(1, size):
+        for move in (-distance, distance):
+            pairs = [(i, i + move) for i in range(size) if 0 <= i + move < size]
+            pieces.append((-move, lax.ppermute(pick(place + move), axis, pairs)))
+    if size == 2:
+        pieces = [(None, pieces[0][1] + pieces[1][1])]
+    return line_order(pick(place), pieces, axis)
+
+
 def rounded_sum(*terms):
     return sum(term.astype(jnp.float32) for term in terms).astype(jnp.bfloat16)
 
@@ -527,18 +536,25 @@
     return (pick(place), lax.ppermute(pick(1 - place), axis, [(0, 1), (1, 0)]))
 
 
-def scatter_step(value, axis, moving, step):
+def scatter_payload(value, axis, moving, step):
     place = lax.axis_index(axis)
     size = lax.axis_size(axis)
+    payload = []
+    for n, sign in enumerate((-1, 1)):
+        slot = jnp.clip(place - sign * (size - step), 0, size - 1)
+        own = lax.dynamic_index_in_dim(value, slot, 0, keepdims=False)
+        payload.append(own if moving is None else rounded_sum(own, moving[n]))
+    return tuple(payload)
+
+
+def scatter_send(payload, axis, step):
+    size = lax.axis_size(axis)
     sums = []
-    for n, sign in enumerate((-1, 1)):
+    for value, sign in zip(payload, (-1, 1)):
         start = 0 if sign < 0 else size - 1
         pairs = [(i, i - sign) for i in range(size) if 0 <= i - sign < size]
         pairs = [(i, j) for i, j in pairs if abs(i - start) <= step - 1]
-        slot = jnp.clip(place - sign * (size - step), 0, size - 1)
-        own = lax.dynamic_index_in_dim(value, slot, 0, keepdims=False)
-        payload = own if moving is None else rounded_sum(own, moving[n])
-        sums.append(lax.ppermute(payload, axis, pairs))
+        sums.append(lax.ppermute(value, axis, pairs))
     return tuple(sums)
 
 
@@ -620,13 +636,24 @@
     small = jnp.concatenate([low(gains_biases).reshape(-1), low(first // 32), low(first % 32)])
     fold = lambda value: low(value).reshape(share, -1, width).swapaxes(0, 1).reshape(-1, width)
     if direct:
-        small = jnp.pad(small, (0, 16 * width - small.shape[0])).reshape(16, width)
-        whole_in = lax.all_gather(
-            jnp.concatenate([fold(project_in), small], axis=0), everyone, axis=0, tiled=False
-        )
-        small = whole_in[:, 3 * share]
+        extra = 16
+        small = jnp.pad(small, (0, extra * 3 * lanes - small.shape[0]))
+        small = jnp.broadcast_to(small.reshape(1, extra, 3 * lanes), (group, extra, 3 * lanes))
+        owned = low(project_in).reshape(share, 3, group, lanes).transpose(2, 0, 1, 3)
+        blocks = jnp.concatenate([owned.reshape(group, share, 3 * lanes), small], axis=1)
+        blocks = blocks.reshape(line, 2, share + extra, 3 * lanes)
+        keep = jnp.where(first_core, blocks[:, 0], blocks[:, 1])
+        sent = swap_cores(jnp.where(first_core, blocks[:, 1], blocks[:, 0]))
+        blocks = exchange_line(in_order(keep[:, None], sent[:, None], 1), "line")
+        blocks = gather_line(gather_line(blocks, "inner"), "outer")
+        blocks = blocks.reshape(count, share + extra, 3 * lanes)
+        mine_in = blocks[:, :share].reshape(width, 3 * lanes)
+        small = blocks[:, share:].reshape(count, -1)
     else:
         whole_in = lax.all_gather(low(project_in), everyone, axis=0, tiled=True)
+        mine_in = lax.dynamic_index_in_dim(
+            whole_in.reshape(width, 3, group, lanes), lax.axis_index(seq), axis=2, keepdims=False
+        ).reshape(width, 3 * lanes)
         small = lax.all_gather(small, everyone, axis=0, tiled=False)
     vector_size = gains_biases.size
     vectors = small[:, :vector_size].reshape(count, -1, share).transpose(1, 0, 2)
@@ -645,6 +672,7 @@
         gathered = lax.all_gather(packed, everyone, axis=0, tiled=False)
         whole_out = gathered[:, packed.shape[0] - share :].reshape(width, width)
         mlp_weights = (gathered,)
+        whole_in = lax.all_gather(fold(project_in), everyone, axis=0, tiled=False)
     own_tokens = line_order(tokens, pieces, "line").reshape(-1, width)
     swapped = [(distance, swap_cores(piece)) for distance, piece in pieces]
     other_tokens = line_order(swap_cores(tokens), swapped, "line").reshape(-1, width)
@@ -678,12 +706,6 @@
     grad_branch = (scale_two * grad_rows).astype(jnp.bfloat16)
 
     place = lax.axis_index(seq)
-    if direct:
-        mine_in = whole_in
-    else:
-        mine_in = lax.dynamic_index_in_dim(
-            whole_in.reshape(width, 3, group, lanes), place, axis=2, keepdims=False
-        ).reshape(width, 3 * lanes)
     normed_one, query, keys, values = norm_mix(
         place.reshape(1), own_tokens, other_tokens, rows, gain_one, shift_one, mine_in, bias_in
     )
@@ -744,7 +766,7 @@
         scatter_terms(grad_out, "inner", 1),
         scatter_terms(grad_down, "outer", 0),
     )
-    out_terms, grad_stream = lax.optimization_barrier((begun[1], grad_stream))
+    out_terms, whole_in, grad_stream = lax.optimization_barrier((begun[1], whole_in, grad_stream))
     begun = (begun[0], out_terms, begun[2])
     grad_mixed_stream = attend_back(starts, query, keys, values, wide, logs, grad_stream)
     grad_mixed = lax.all_to_all(
@@ -755,7 +777,7 @@
     grad_down = scatter_line(grad_down, "inner", 0)
     grad_up = scatter_line(jnp.concatenate([grad_up, grad_out], axis=2), "outer", 0)
     plane_sums = jnp.concatenate([grad_up, grad_down], axis=1)
-    moving = scatter_step(plane_sums, "line", None, 1)
+    moving = scatter_send(scatter_payload(plane_sums, "line", None, 1), "line", 1)
     moving, grad_mixed = lax.optimization_barrier((moving, grad_mixed))
     grad_in = inner_rows(normed_one, grad_mixed_stream).astype(jnp.bfloat16)
     parts = grad_in.reshape(outer, inner, group * share, 3 * lanes)
@@ -764,9 +786,10 @@
         grad_mixed, whole_in, tokens, grad_second, gain_one
     )
     for step in range(2, line):
-        moving = scatter_step(plane_sums, "line", moving, step)
-        if step == 2:
-            moving, parts, grad_gain_one = lax.optimization_barrier((moving, parts, grad_gain_one))
+        payload = scatter_payload(plane_sums, "line", moving, step)
+        if step == 3:
+            payload, parts, grad_gain_one = lax.optimization_barrier((payload, parts, grad_gain_one))
+        moving = scatter_send(payload, "line", step)
     summed = rounded_sum(
         lax.dynamic_index_in_dim(plane_sums, lax.axis_index("line"), 0, keepdims=False), *moving
     )

time: 573 us -> 550 us (0.960)
  waiting for transfers between devices: 253 us -> 197 us
  starting transfers between devices: 62.2 us -> 78.2 us
  blocking collectives: 0 us -> 9.47 us
    all_gather x1, waiting for transfers between devices: 68.2 us -> 0.01 us  [on_device(): gathered = lax.all_gather(packed, everyone, axis=0, tiled=False)]
    ppermute x6, waiting for transfers between devices: 102 us -> 67.5 us  [line_pieces(): moving = lax.ppermute(moving, axis, pairs)]
    ppermute x6 -> x14, waiting for transfers between devices: 19.4 us -> 47.8 us  [the longest x2 24.4 us: line_pieces(): other = lax.ppermute(value, axis, [(0, 1), (1, 0)])]
    ppermute x6 -> x14, starting transfers between devices: 16.2 us -> 40 us  [the longest x6 20.2 us: exchange_line(): pieces.append((-move, lax.ppermute(pick(place + move), axis, pairs)))]
    all_to_all x1, waiting for transfers between devices: 0.01 us -> 21.9 us  [on_device(): lax.all_to_all(attended.reshape(group, rows, lanes), seq, split_axis=0, c...]
    all_to_all x0 -> x1, blocking collectives: none -> 9.47 us  [on_device(): lax.all_to_all(parts.reshape(count, small_rows * share), everyone, split_...]
    dynamic_update_slice x14 -> x20, local copies, waits for them, and re-layouts: 14.5 us -> 6.69 us  [line_order(): whole = lax.dynamic_update_index_in_dim(whole, piece, slot, 0)]
    all_to_all x1 -> x0, waiting for transfers between devices: 7.38 us -> none  [on_device(): lax.all_to_all(parts.reshape(count, small_rows * share), everyone, split_...]
  transfers between devices with their start and end apart: 38 -> 46, of which waited for: 16 -> 20; matrix products, arithmetic and copies ran while one was open for 15% -> 18% of each run, Pallas kernels for 15% -> 23%
where the time goes in v8:
time: 550 us; the launch traced here: 540 us
  waiting for transfers between devices  197 us (36%)
  Pallas kernels  124 us (23%)
  starting transfers between devices  78.2 us (14%)
  local copies, waits for them, and re-layouts  51.7 us (9%)
  other arithmetic  50.9 us (9%)
  between operations  15.7 us (3%)
  matrix products  11.9 us (2%)
  blocking collectives  9.47 us (2%)
    ppermute x6, waiting for transfers between devices, line_pieces(): moving = lax.ppermute(moving, axis, pairs)  67.5 us
    pallas_call x1, Pallas kernels, mlp(): pl.pallas_call(functools.partial(mlp_kernel, pieces), grid_spec=pltpu.Pre...  38 us
    pallas_call x1, Pallas kernels, attend_back(): pl.pallas_call(attend_back_kernel, grid_spec=pltpu.PrefetchScalarGridSpec...  34.9 us
    pallas_call x1, Pallas kernels, attend(): pl.pallas_call(attend_kernel, grid_spec=pltpu.PrefetchScalarGridSpec(num_...  26.3 us
    ppermute x4, waiting for transfers between devices, scatter_line(): lax.ppermute(pick(1 - place), axis, [(0, 1), (1, 0)])  24.4 us
    ppermute x2, waiting for transfers between devices, line_pieces(): other = lax.ppermute(value, axis, [(0, 1), (1, 0)])  24.4 us
    all_to_all x1, waiting for transfers between devices, on_device(): lax.all_to_all(attended.reshape(group, rows, lanes), seq, split_axis=0, c...  21.9 us
    ppermute x3, waiting for transfers between devices, scatter_terms(): return (pick(place), lax.ppermute(pick(1 - place), axis, [(0, 1), (1, 0)]))  21.5 us
  transfers between devices with their start and end apart: 46, of which 20 were waited for; matrix products, arithmetic and copies ran while one was open for 18% of the time, Pallas kernels for 23%

profile of v8, /device:TPU:0, one launch (start us, length us, event | category | flops | bytes accessed | tf_op | source)
XLA Modules:
  0.0 539.5 jit_solution(346877073444181712)
XLA Ops:
  7.3 5.1 collective-permute-start.9
  13.7 21.3 %collective-permute-done.9 = bf16[512,1024]{1,0:T(8,128)(2,1)S(1)} collective-permute-done((bf16[512,1024]{1,0:T(8,128)(2,1)}, bf16[512,1024]{1,0:T(8,128)(2,1)S(1)}, u32[]{:S(2)}, u32[]{:S(2)}) %collective-permute-start.9) | collective-permute-done | bytes 1048608 | tf_op jit(solution)/shard_map/ppermute | solution.py:489
  35.8 3.4 collective-permute-done.12
  40.5 1.6 collective-permute-start.11
  42.1 22.9 %collective-permute-done.13 = bf16[512,1024]{1,0:T(8,128)(2,1)} collective-permute-done((bf16[512,1024]{1,0:T(8,128)(2,1)S(1)}, bf16[512,1024]{1,0:T(8,128)(2,1)}, u32[]{:S(2)}, u32[]{:S(2)}) %collective-permute-start.13) | collective-permute-done | bytes 1048608 | tf_op jit(solution)/shard_map/ppermute | solution.py:489
  70.3 19.9 %collective-permute-done.14 = bf16[512,1024]{1,0:T(8,128)(2,1)} collective-permute-done((bf16[512,1024]{1,0:T(8,128)(2,1)}, bf16[512,1024]{1,0:T(8,128)(2,1)}, u32[]{:S(2)}, u32[]{:S(2)}) %collective-permute-start.14) | collective-permute-done | bytes 1048608 | tf_op jit(solution)/shard_map/ppermute | solution.py:489
  93.9 6.3 %collective-permute-start.2 = (bf16[2,48,384]{2,1,0:T(8,128)(2,1)S(1)}, bf16[2,48,384]{2,1,0:T(8,128)(2,1)S(1)}, u32[]{:S(2)}, u32[]{:S(2)}) collective-permute-start(bf16[2,48,384]{2,1,0:T(8,128)(2,1)S(1)} %get-tuple-element.169), channel_id=1, source_target_pairs={{0,6},{1,7},{8,14},{9,15},{16,22},{17,23},{24,30},{25,31}} | collective-permute-start | bytes 221192 | tf_op jit(solution)/shard_map/ppermute | solution.py:521
  101.6 5.4 %collective-permute-start.4 = (bf16[2,48,384]{2,1,0:T(8,128)(2,1)S(1)}, bf16[2,48,384]{2,1,0:T(8,128)(2,1)S(1)}, u32[]{:S(2)}, u32[]{:S(2)}) collective-permute-start(bf16[2,48,384]{2,1,0:T(8,128)(2,1)S(1)} %get-tuple-element.171), channel_id=1, source_target_pairs={{0,4},{2,6},{1,5},{3,7},{8,12},{10,14},{9,13},{11,15},{16,20},{18,... | collective-permute-start | bytes 221192 | tf_op jit(solution)/shard_map/ppermute | solution.py:521
  108.3 4.5 collective-permute-start.6
  113.1 3.6 collective-permute-done.5
  116.8 2.1 collective-permute-start.7
  118.9 5.3 collective-permute-done.7
  125.1 1.8 collective-permute-start.8
  127.5 19.1 %collective-permute-done.8 = bf16[2,4,2,48,384]{4,3,2,1,0:T(8,128)(2,1)} collective-permute-done((bf16[2,4,2,48,384]{4,3,2,1,0:T(8,128)(2,1)}, bf16[2,4,2,48,384]{4,3,2,1,0:T(8,128)(2,1)}, u32[]{:S(2)}, u32[]{:S(2)}) %collective-permute-start.8) | collective-permute-done | bytes 589856 | tf_op jit(solution)/shard_map/ppermute | solution.py:481
  146.6 1.6 maximum_select_fusion
  154.9 1.4 bitcast_dynamic-update-slice_fusion.13
  160.2 1.4 copy-done.6
  162.4 3.5 collective-permute-done.20
  167.4 2.0 copy-done.5
  169.3 14.2 %norm_mix.1 = (bf16[4096,1024]{1,0:T(8,128)(2,1)}, bf16[4096,128]{1,0:T(8,128)(2,1)}, bf16[4096,128]{1,0:T(8,128)(2,1)}, bf16[4096,128]{1,0:T(8,128)(2,1)}) custom-call(s32[1]{0:T(128)} %bitcast.28.place_ref, bf16[2048,1024]{1,0:T(8,128)(2,1)} %bitcast.266, bf16[2048,1024]{1,0:T(8,128)(2,1)} %bitcast.265, f32[1,1024]{1,0:T(1,128)} %slice.133.gain_ref, ...), custom_call_target="tpu_custom_call" | custom-call | flops 3221225472 | bytes 16777216 | tf_op jit(solution)/shard_map/norm_mix/pallas_call | solution.py:243
  183.5 26.3 %attend_forward.1 = (f32[4096,128]{1,0:T(8,128)}, bf16[4096,128]{1,0:T(8,128)(2,1)}, f32[4096,128]{1,0:T(8,128)}) custom-call(s32[2]{0:T(128)} %select_reduce_fusion.starts_ref, bf16[4096,128]{1,0:T(8,128)(2,1)} %get-tuple-element.67.q_ref, bf16[4096,128]{1,0:T(8,128)(2,1)} %get-tuple-element.68.k_ref, bf16[4096,128]{1,0:T(8,128)(2,1)} %get-tuple-element.69.v_ref), custom_call_target="tpu_custom_call" | custom-call | flops 4060086272 | bytes 8388608 | tf_op jit(solution)/shard_map/attend_forward/pallas_call | solution.py:116
  209.8 2.3 copy.126
  212.1 5.1 all-to-all-start
  220.4 2.0 convert_reduce_fusion
  222.8 3.3 slice.174
  226.0 21.9 %all-to-all-done = bf16[8,512,128]{1,2,0:T(8,128)(2,1)S(1)} async-done(((bf16[8,512,128]{1,2,0:T(8,128)(2,1)}), bf16[8,512,128]{1,2,0:T(8,128)(2,1)S(1)}, u32[]{:S(2)}, u32[]{:S(2)}) %all-to-all-start) | async-done | bytes 1048608 | tf_op jit(solution)/shard_map/all_to_all | solution.py:721
  249.0 4.9 fusion.78
  257.7 1.5 reshape.388
  260.6 38.0 %mlp_both_ways.1 = (bf16[16,128,1024]{2,1,0:T(8,128)(2,1)}, bf16[16,128,1024]{2,1,0:T(8,128)(2,1)}, f32[512,1024]{1,0:T(8,128)}, f32[512,1024]{1,0:T(8,128)}, f3...) custom-call(s32[1]{0:T(128)} %bitcast.55.core_ref, bf16[512,1024]{1,0:T(8,128)(2,1)} %add_convert_fusion.4.own_ref, ...), custom_call_target="tpu_custom_call" | custom-call | flops 25769803776 | bytes 29360128 | tf_op jit(solution)/shard_map/mlp_both_ways/pallas_call | solution.py:353
  300.6 2.7 collective-permute-done.26
  303.3 3.8 multiply_reduce_fusion.1
  307.1 4.2 multiply_reduce_fusion
  317.3 4.4 all-to-all-start.1
  324.2 4.3 dynamic-slice_bitcast_fusion.2
  328.5 2.0 collective-permute-start.25
  330.6 2.5 dynamic-slice_bitcast_fusion
  333.2 17.3 %collective-permute-done.27 = bf16[2,4,64,1024]{3,2,1,0:T(8,128)(2,1)} collective-permute-done((bf16[2,4,64,1024]{3,2,1,0:T(8,128)(2,1)}, bf16[2,4,64,1024]{3,2,1,0:T(8,128)(2,1)}, u32[]{:S(2)}, u32[]{:S(2)}) %collective-permute-start.27) | collective-permute-done | bytes 1048608 | tf_op jit(solution)/shard_map/ppermute | solution.py:536
  350.5 34.9 %attend_backward.1 = bf16[4096,384]{1,0:T(8,128)(2,1)} custom-call(s32[2]{0:T(128)} %select_reduce_fusion.starts_ref, bf16[4096,128]{1,0:T(8,128)(2,1)} %get-tuple-element.67.q_ref, bf16[4096,128]{1,0:T(8,128)(2,1)} %get-tuple-element.68.k_ref, bf16[4096,128]{1,0:T(8,128)(2,1)} %get-tuple-element.69.v_ref, f32[4096,128]{1,0:T(8,128)} %get-tuple-element.80.wide_ref, ...), custom_call_target="tpu_custom_call" | custom-call | flops 10150215680 | bytes 11534336 | tf_op jit(solution)/shard_map/attend_backward/pallas_call | solution.py:196
  385.4 5.4 all-to-all-start.2
  390.7 4.2 collective-permute-done.25
  395.0 1.8 add_convert_fusion.2
  396.8 2.6 add_convert_fusion.1
  400.9 2.9 add_convert_fusion
  404.3 4.5 convolution_convert_fusion.2
  408.9 1.8 collective-permute-start.35
  410.7 19.4 %collective-permute-done.30 = bf16[4,128,1024]{2,1,0:T(8,128)(2,1)S(1)} collective-permute-done((bf16[4,128,1024]{2,1,0:T(8,128)(2,1)S(1)}, bf16[4,128,1024]{2,1,0:T(8,128)(2,1)S(1)}, u32[]{:S(2)}, u32[]{:S(2)}) %collective-permute-start.30) | collective-permute-done | bytes 1048608 | tf_op jit(solution)/shard_map/ppermute | solution.py:568
  430.5 5.0 collective-permute-done.29
  437.4 4.1 collective-permute-start.31
  441.5 1.5 collective-permute-start.32
  445.4 11.2 %collective-permute-done.31 = bf16[320,1024]{1,0:T(8,128)(2,1)} collective-permute-done((bf16[320,1024]{1,0:T(8,128)(2,1)}, bf16[320,1024]{1,0:T(8,128)(2,1)}, u32[]{:S(2)}, u32[]{:S(2)}) %collective-permute-start.31) | collective-permute-done | bytes 655392 | tf_op jit(solution)/shard_map/ppermute | solution.py:557
  456.5 5.8 %all-to-all-done.2.grad_ref = bf16[8,512,384]{2,1,0:T(8,128)(2,1)} async-done(((bf16[8,512,384]{2,1,0:T(8,128)(2,1)}), bf16[8,512,384]{2,1,0:T(8,128)(2,1)}, u32[]{:S(2)}, u32[]{:S(2)}) %all-to-all-start.2) | async-done | bytes 3145760 | tf_op jit(solution)/shard_map/all_to_all | solution.py:772
  462.3 2.9 fusion.9
  465.2 1.5 collective-permute-start.34
  466.8 2.1 collective-permute-start.33
  471.4 1.7 fusion.33
  473.1 10.8 %finish_input.1 = (f32[512,1024]{1,0:T(8,128)}, f32[1,1024]{1,0:T(1,128)}, f32[1,1024]{1,0:T(1,128)}, f32[3,1,1024]{2,1,0:T(1,128)}) custom-call(bf16[8,512,384]{2,1,0:T(8,128)(2,1)} %all-to-all-done.2.grad_ref, bf16[32,96,1024]{2,1,0:T(8,128)(2,1)} %all-gather.4.cloned.1.call-done.weight_ref, bf16[512,1024]{1,0:T(8,128)(2,1)} %x_ref.1, ...), custom_call_target="tpu_custom_call" | custom-call | flops 3221225472 | bytes 16777216 | tf_op jit(solution)/shard_map/finish_input/pallas_call | solution.py:443
  486.7 3.0 fusion.10
  490.9 9.5 %all_to_all.30 = f32[32,1,448]{2,1,0:T(1,128)S(1)} all-to-all(f32[32,1,448]{2,1,0:T(1,128)S(1)} %all_to_all.24), channel_id=1, replica_groups=mesh['outer'=2,'inner'=2,'line'=4,'core'=2] {'outer','inner','line','core'}, dimensions={0} | all-to-all | bytes 114688 | tf_op jit(solution)/shard_map/all_to_all | solution.py:826
  500.3 4.0 all-to-all-start.3
  505.7 5.4 %collective-permute-start.37 = (bf16[320,1024]{1,0:T(8,128)(2,1)}, bf16[320,1024]{1,0:T(8,128)(2,1)}, u32[]{:S(2)}, u32[]{:S(2)}) collective-permute-start(bf16[320,1024]{1,0:T(8,128)(2,1)} %get-tuple-element.98), channel_id=1, source_target_pairs={{0,2},{2,4},{4,6},{1,3},{3,5},{5,7},{8,10},{10,12},{12,14},{9,11},... | collective-permute-start | bytes 1966088 | tf_op jit(solution)/shard_map/ppermute | solution.py:557
  514.5 2.4 multiply_subtract_fusion.2
  516.9 8.6 %collective-permute-done.38 = bf16[320,1024]{1,0:T(8,128)(2,1)} collective-permute-done((bf16[320,1024]{1,0:T(8,128)(2,1)}, bf16[320,1024]{1,0:T(8,128)(2,1)}, u32[]{:S(2)}, u32[]{:S(2)}) %collective-permute-start.38) | collective-permute-done | bytes 655392 | tf_op jit(solution)/shard_map/ppermute | solution.py:557
  525.4 1.6 fusion.8
  527.3 1.4 multiply_subtract_fusion
  (315 shorter events, 71.2 us)
Async XLA Ops:
  7.2 83.0 %copy-start.30 = (f32[14,32]{1,0:T(8,128)S(1)}, f32[14,32]{1,0:T(8,128)}, u32[]{:S(2)}) copy-start(f32[14,32]{1,0:T(8,128)} %param.27) | copy-start | bytes 5380
  7.2 83.1 %copy-start.49 = (s32[512]{0:T(512)S(1)}, s32[512]{0:T(512)}, u32[]{:S(2)}) copy-start(s32[512]{0:T(512)} %param.22) | copy-start | bytes 6148
  7.2 83.1 %copy-start.52 = (s32[512]{0:T(512)S(1)}, s32[512]{0:T(512)}, u32[]{:S(2)}) copy-start(s32[512]{0:T(512)} %param.21) | copy-start | bytes 6148
  7.2 83.3 %copy-start.7 = (f32[32,3072]{1,0:T(8,128)S(1)}, f32[32,3072]{1,0:T(8,128)}, u32[]{:S(2)}) copy-start(f32[32,3072]{1,0:T(8,128)} %param.23) | copy-start | bytes 1179652
  7.2 215.6 %all-gather.6.cloned.1.call-start = ((), (), s32[]{:S(2)}) async-start(), calls=%async_computation.6 | async-start | bytes 19464192 | tf_op jit(solution)/shard_map/all_gather | solution.py:672
  7.3 27.8 %collective-permute-start.9 = (bf16[512,1024]{1,0:T(8,128)(2,1)}, bf16[512,1024]{1,0:T(8,128)(2,1)S(1)}, u32[]{:S(2)}, u32[]{:S(2)}) collective-permute-start(bf16[512,1024]{1,0:T(8,128)(2,1)} %x_ref.1), channel_id=1, source_target_pairs={{0,2},{2,4},{4,6},{1,3},{3,5},{5,7},{8,10},{10,12},{12,14},{9,11},... | collective-permute-start | bytes 3145736 | tf_op jit(solution)/shard_map/ppermute | solution.py:489
  12.4 26.7 %collective-permute-start.12 = (bf16[512,1024]{1,0:T(8,128)(2,1)}, bf16[512,1024]{1,0:T(8,128)(2,1)S(1)}, u32[]{:S(2)}, u32[]{:S(2)}) collective-permute-start(bf16[512,1024]{1,0:T(8,128)(2,1)} %x_ref.1), channel_id=1, source_target_pairs={{2,0},{4,2},{6,4},{3,1},{5,3},{7,5},{10,8},{12,10},{14,12},{11,9},... | collective-permute-start | bytes 3145736 | tf_op jit(solution)/shard_map/ppermute | solution.py:489
  35.1 29.9 %copy-start.14 = (bf16[512,1024]{1,0:T(8,128)(2,1)}, bf16[512,1024]{1,0:T(8,128)(2,1)S(1)}, u32[]{:S(2)}) copy-start(bf16[512,1024]{1,0:T(8,128)(2,1)S(1)} %collective-permute-done.9) | copy-start | bytes 3145732
  35.1 5.4 collective-permute-start.10
  39.1 25.9 %collective-permute-start.13 = (bf16[512,1024]{1,0:T(8,128)(2,1)S(1)}, bf16[512,1024]{1,0:T(8,128)(2,1)}, u32[]{:S(2)}, u32[]{:S(2)}) collective-permute-start(bf16[512,1024]{1,0:T(8,128)(2,1)S(1)} %collective-permute-done.12), channel_id=1, source_target_pairs={{2,0},{4,2},{3,1},{5,3},{10,8},{12,10},{11,9},{13,11},{18,16},{20,... | collective-permute-start | bytes 3145736 | tf_op jit(solution)/shard_map/ppermute | solution.py:489
  40.4 50.2 %copy-start.16 = (bf16[512,1024]{1,0:T(8,128)(2,1)}, bf16[512,1024]{1,0:T(8,128)(2,1)S(1)}, u32[]{:S(2)}) copy-start(bf16[512,1024]{1,0:T(8,128)(2,1)S(1)} %collective-permute-done.10) | copy-start | bytes 3145732
  40.5 29.8 %collective-permute-start.11 = (bf16[512,1024]{1,0:T(8,128)(2,1)S(1)}, bf16[512,1024]{1,0:T(8,128)(2,1)}, u32[]{:S(2)}, u32[]{:S(2)}) collective-permute-start(bf16[512,1024]{1,0:T(8,128)(2,1)S(1)} %collective-permute-done.10), channel_id=1, source_target_pairs={{4,6},{5,7},{12,14},{13,15},{20,22},{21,23},{28,30},{29,31}} | collective-permute-start | bytes 3145736 | tf_op jit(solution)/shard_map/ppermute | solution.py:489
  65.0 25.2 %collective-permute-start.14 = (bf16[512,1024]{1,0:T(8,128)(2,1)}, bf16[512,1024]{1,0:T(8,128)(2,1)}, u32[]{:S(2)}, u32[]{:S(2)}) collective-permute-start(bf16[512,1024]{1,0:T(8,128)(2,1)} %collective-permute-done.13), channel_id=1, source_target_pairs={{2,0},{3,1},{10,8},{11,9},{18,16},{19,17},{26,24},{27,25}} | collective-permute-start | bytes 3145736 | tf_op jit(solution)/shard_map/ppermute | solution.py:489
  91.0 1.4 collective-permute-start
  91.1 35.8 %copy-start.3 = (bf16[512,1024]{1,0:T(8,128)(2,1)S(1)}, bf16[512,1024]{1,0:T(8,128)(2,1)}, u32[]{:S(2)}) copy-start(bf16[512,1024]{1,0:T(8,128)(2,1)} %x_ref.1) | copy-start | bytes 3145732
  92.6 15.7 %collective-permute-start.1 = (bf16[2,48,384]{2,1,0:T(8,128)(2,1)S(1)}, bf16[2,48,384]{2,1,0:T(8,128)(2,1)S(1)}, u32[]{:S(2)}, u32[]{:S(2)}) collective-permute-start(bf16[2,48,384]{2,1,0:T(8,128)(2,1)S(1)} %get-tuple-element.168), channel_id=1, source_target_pairs={{6,0},{7,1},{14,8},{15,9},{22,16},{23,17},{30,24},{31,25}} | collective-permute-start | bytes 221192 | tf_op jit(solution)/shard_map/ppermute | solution.py:521
  93.9 19.0 %collective-permute-start.2 = (bf16[2,48,384]{2,1,0:T(8,128)(2,1)S(1)}, bf16[2,48,384]{2,1,0:T(8,128)(2,1)S(1)}, u32[]{:S(2)}, u32[]{:S(2)}) collective-permute-start(bf16[2,48,384]{2,1,0:T(8,128)(2,1)S(1)} %get-tuple-element.169), channel_id=1, source_target_pairs={{0,6},{1,7},{8,14},{9,15},{16,22},{17,23},{24,30},{25,31}} | collective-permute-start | bytes 221192 | tf_op jit(solution)/shard_map/ppermute | solution.py:521
  100.3 12.7 %collective-permute-start.3 = (bf16[2,48,384]{2,1,0:T(8,128)(2,1)S(1)}, bf16[2,48,384]{2,1,0:T(8,128)(2,1)S(1)}, u32[]{:S(2)}, u32[]{:S(2)}) collective-permute-start(bf16[2,48,384]{2,1,0:T(8,128)(2,1)S(1)} %get-tuple-element.170), channel_id=1, source_target_pairs={{4,0},{6,2},{5,1},{7,3},{12,8},{14,10},{13,9},{15,11},{20,16},{22,... | collective-permute-start | bytes 221192 | tf_op jit(solution)/shard_map/ppermute | solution.py:521
  101.6 11.5 %collective-permute-start.4 = (bf16[2,48,384]{2,1,0:T(8,128)(2,1)S(1)}, bf16[2,48,384]{2,1,0:T(8,128)(2,1)S(1)}, u32[]{:S(2)}, u32[]{:S(2)}) collective-permute-start(bf16[2,48,384]{2,1,0:T(8,128)(2,1)S(1)} %get-tuple-element.171), channel_id=1, source_target_pairs={{0,4},{2,6},{1,5},{3,7},{8,12},{10,14},{9,13},{11,15},{16,20},{18,... | collective-permute-start | bytes 221192 | tf_op jit(solution)/shard_map/ppermute | solution.py:521
  107.0 9.7 %collective-permute-start.5 = (bf16[2,48,384]{2,1,0:T(8,128)(2,1)S(1)}, bf16[2,48,384]{2,1,0:T(8,128)(2,1)S(1)}, u32[]{:S(2)}, u32[]{:S(2)}) collective-permute-start(bf16[2,48,384]{2,1,0:T(8,128)(2,1)S(1)} %get-tuple-element.172), channel_id=1, source_target_pairs={{2,0},{4,2},{6,4},{3,1},{5,3},{7,5},{10,8},{12,10},{14,12},{11,9},... | collective-permute-start | bytes 221192 | tf_op jit(solution)/shard_map/ppermute | solution.py:521
  108.3 8.4 %collective-permute-start.6 = (bf16[2,48,384]{2,1,0:T(8,128)(2,1)S(1)}, bf16[2,48,384]{2,1,0:T(8,128)(2,1)S(1)}, u32[]{:S(2)}, u32[]{:S(2)}) collective-permute-start(bf16[2,48,384]{2,1,0:T(8,128)(2,1)S(1)} %get-tuple-element.167), channel_id=1, source_target_pairs={{0,2},{2,4},{4,6},{1,3},{3,5},{5,7},{8,10},{10,12},{12,14},{9,11},... | collective-permute-start | bytes 221192 | tf_op jit(solution)/shard_map/ppermute | solution.py:521
  116.8 7.4 %collective-permute-start.7 = (bf16[4,2,48,384]{3,2,1,0:T(8,128)(2,1)S(1)}, bf16[4,2,48,384]{3,2,1,0:T(8,128)(2,1)S(1)}, u32[]{:S(2)}, u32[]{:S(2)}) collective-permute-start(bf16[4,2,48,384]{3,2,1,0:T(8,128)(2,1)S(1)} %fusion.42), channel_id=1, source_target_pairs={{0,8},{8,0},{1,9},{9,1},{2,10},{10,2},{3,11},{11,3},{4,12},{12,4},... | collective-permute-start | bytes 884744 | tf_op jit(solution)/shard_map/ppermute | solution.py:481
  125.1 21.5 %collective-permute-start.8 = (bf16[2,4,2,48,384]{4,3,2,1,0:T(8,128)(2,1)}, bf16[2,4,2,48,384]{4,3,2,1,0:T(8,128)(2,1)}, u32[]{:S(2)}, u32[]{:S(2)}) collective-permute-start(bf16[2,4,2,48,384]{4,3,2,1,0:T(8,128)(2,1)} %maximum_select_fusion.2), channel_id=1, source_target_pairs={{0,16},{16,0},{1,17},{17,1},{2,18},{18,2},{3,19},{19,3},{4,20},{20... | collective-permute-start | bytes 1769480 | tf_op jit(solution)/shard_map/ppermute | solution.py:481
  126.9 39.1 %collective-permute-start.21 = (bf16[512,1024]{1,0:T(8,128)(2,1)S(1)}, bf16[512,1024]{1,0:T(8,128)(2,1)}, u32[]{:S(2)}, u32[]{:S(2)}) collective-permute-start(bf16[512,1024]{1,0:T(8,128)(2,1)S(1)} %copy-done.3), channel_id=1, source_target_pairs={{0,1},{1,0},{2,3},{3,2},{4,5},{5,4},{6,7},{7,6},{8,9},{9,8},{10,11... | collective-permute-start | bytes 3145736 | tf_op jit(solution)/shard_map/ppermute | solution.py:475
  153.3 6.3 %collective-permute-start.15 = (bf16[512,1024]{1,0:T(8,128)(2,1)}, bf16[512,1024]{1,0:T(8,128)(2,1)S(1)}, u32[]{:S(2)}, u32[]{:S(2)}) collective-permute-start(bf16[512,1024]{1,0:T(8,128)(2,1)} %collective-permute-done.11), channel_id=1, source_target_pairs={{0,1},{1,0},{2,3},{3,2},{4,5},{5,4},{6,7},{7,6},{8,9},{9,8},{10,11... | collective-permute-start | bytes 3145736 | tf_op jit(solution)/shard_map/ppermute | solution.py:475
  153.3 8.4 %collective-permute-start.16 = (bf16[512,1024]{1,0:T(8,128)(2,1)}, bf16[512,1024]{1,0:T(8,128)(2,1)S(1)}, u32[]{:S(2)}, u32[]{:S(2)}) collective-permute-start(bf16[512,1024]{1,0:T(8,128)(2,1)} %collective-permute-done.14), channel_id=1, source_target_pairs={{0,1},{1,0},{2,3},{3,2},{4,5},{5,4},{6,7},{7,6},{8,9},{9,8},{10,11... | collective-permute-start | bytes 3145736 | tf_op jit(solution)/shard_map/ppermute | solution.py:475
  153.8 8.1 %collective-permute-start.17 = (bf16[512,1024]{1,0:T(8,128)(2,1)}, bf16[512,1024]{1,0:T(8,128)(2,1)S(1)}, u32[]{:S(2)}, u32[]{:S(2)}) collective-permute-start(bf16[512,1024]{1,0:T(8,128)(2,1)} %copy-done.16), channel_id=1, source_target_pairs={{0,1},{1,0},{2,3},{3,2},{4,5},{5,4},{6,7},{7,6},{8,9},{9,8},{10,11... | collective-permute-start | bytes 3145736 | tf_op jit(solution)/shard_map/ppermute | solution.py:475
  153.8 8.2 %collective-permute-start.18 = (bf16[512,1024]{1,0:T(8,128)(2,1)}, bf16[512,1024]{1,0:T(8,128)(2,1)S(1)}, u32[]{:S(2)}, u32[]{:S(2)}) collective-permute-start(bf16[512,1024]{1,0:T(8,128)(2,1)} %collective-permute-done.13), channel_id=1, source_target_pairs={{0,1},{1,0},{2,3},{3,2},{4,5},{5,4},{6,7},{7,6},{8,9},{9,8},{10,11... | collective-permute-start | bytes 3145736 | tf_op jit(solution)/shard_map/ppermute | solution.py:475
  159.5 2.7 collective-permute-start.19
  161.7 4.2 collective-permute-start.20
  212.1 35.9 %all-to-all-start = ((bf16[8,512,128]{1,2,0:T(8,128)(2,1)}), bf16[8,512,128]{1,2,0:T(8,128)(2,1)S(1)}, u32[]{:S(2)}, u32[]{:S(2)}) async-start(bf16[8,512,128]{1,2,0:T(8,128)(2,1)} %copy.126), calls=%async_computation | async-start | bytes 2097152 | tf_op jit(solution)/shard_map/all_to_all | solution.py:721
  217.2 116.1 %all-gather.4.cloned.1.call-start = ((), (), s32[]{:S(2)}) async-start(), calls=%async_computation.5 | async-start | bytes 6488064 | tf_op jit(solution)/shard_map/all_gather | solution.py:675
  219.6 29.4 %copy-start.40 = (f32[1024]{0:T(1024)}, f32[1024]{0:T(1024)S(1)}, u32[]{:S(2)}) copy-start(f32[1024]{0:T(1024)S(1)} %mul.322) | copy-start | bytes 12292
  222.3 38.2 %collective-permute-start.23 = (bf16[512,1024]{1,0:T(8,128)(2,1)}, bf16[512,1024]{1,0:T(8,128)(2,1)}, u32[]{:S(2)}, u32[]{:S(2)}) collective-permute-start(bf16[512,1024]{1,0:T(8,128)(2,1)} %get-tuple-element.123.gm_own_ref), channel_id=1, source_target_pairs={{0,1},{1,0},{2,3},{3,2},{4,5},{5,4},{6,7},{7,6},{8,9},{9,8},{10,11... | collective-permute-start | bytes 3145736 | tf_op jit(solution)/shard_map/ppermute | solution.py:475
  222.8 26.2 %copy-start.42 = (f32[1024]{0:T(1024)S(1)}, f32[1024]{0:T(1024)}, u32[]{:S(2)}) copy-start(f32[1024]{0:T(1024)} %add.338) | copy-start | bytes 12292
  256.1 4.4 collective-permute-start.22
  298.6 4.7 collective-permute-start.26
  299.1 7.9 %collective-permute-start.24 = (f32[512,1024]{1,0:T(8,128)}, f32[512,1024]{1,0:T(8,128)}, u32[]{:S(2)}, u32[]{:S(2)}) collective-permute-start(f32[512,1024]{1,0:T(8,128)} %get-tuple-element.73), channel_id=1, source_target_pairs={{0,1},{1,0},{2,3},{3,2},{4,5},{5,4},{6,7},{7,6},{8,9},{9,8},{10,11... | collective-permute-start | bytes 6291464 | tf_op jit(solution)/shard_map/ppermute | solution.py:475
  317.3 33.1 %all-to-all-start.1 = ((bf16[8,512,128]{2,1,0:T(8,128)(2,1)}), bf16[8,512,128]{2,1,0:T(8,128)(2,1)}, u32[]{:S(2)}, u32[]{:S(2)}) async-start(bf16[8,512,128]{2,1,0:T(8,128)(2,1)} %bitcast.258), calls=%async_computation.1 | async-start | bytes 2097152 | tf_op jit(solution)/shard_map/all_to_all | solution.py:751
  324.2 26.3 %collective-permute-start.27 = (bf16[2,4,64,1024]{3,2,1,0:T(8,128)(2,1)}, bf16[2,4,64,1024]{3,2,1,0:T(8,128)(2,1)}, u32[]{:S(2)}, u32[]{:S(2)}) collective-permute-start(bf16[2,4,64,1024]{3,2,1,0:T(8,128)(2,1)} %get-tuple-element.159), channel_id=1, source_target_pairs={{0,8},{8,0},{1,9},{9,1},{2,10},{10,2},{3,11},{11,3},{4,12},{12,4},... | collective-permute-start | bytes 3145736 | tf_op jit(solution)/shard_map/ppermute | solution.py:536
  328.5 66.4 %collective-permute-start.25 = (bf16[2,4,128,1024]{3,2,1,0:T(8,128)(2,1)}, bf16[2,4,128,1024]{3,2,1,0:T(8,128)(2,1)}, u32[]{:S(2)}, u32[]{:S(2)}) collective-permute-start(bf16[2,4,128,1024]{3,2,1,0:T(8,128)(2,1)} %get-tuple-element.149), channel_id=1, source_target_pairs={{0,8},{8,0},{1,9},{9,1},{2,10},{10,2},{3,11},{11,3},{4,12},{12,4},... | collective-permute-start | bytes 6291464 | tf_op jit(solution)/shard_map/ppermute | solution.py:536
  333.0 61.9 %collective-permute-start.28 = (bf16[2,4,128,1024]{3,2,1,0:T(8,128)(2,1)}, bf16[2,4,128,1024]{3,2,1,0:T(8,128)(2,1)}, u32[]{:S(2)}, u32[]{:S(2)}) collective-permute-start(bf16[2,4,128,1024]{3,2,1,0:T(8,128)(2,1)} %get-tuple-element.147), channel_id=1, source_target_pairs={{0,16},{16,0},{1,17},{17,1},{2,18},{18,2},{3,19},{19,3},{4,20},{20... | collective-permute-start | bytes 6291464 | tf_op jit(solution)/shard_map/ppermute | solution.py:536
  385.4 77.0 %all-to-all-start.2 = ((bf16[8,512,384]{2,1,0:T(8,128)(2,1)}), bf16[8,512,384]{2,1,0:T(8,128)(2,1)}, u32[]{:S(2)}, u32[]{:S(2)}) async-start(bf16[8,512,384]{2,1,0:T(8,128)(2,1)} %bitcast.267), calls=%async_computation.2 | async-start | bytes 6291456 | tf_op jit(solution)/shard_map/all_to_all | solution.py:772
  399.5 36.0 %collective-permute-start.29 = (bf16[4,192,1024]{2,1,0:T(8,128)(2,1)S(1)}, bf16[4,192,1024]{2,1,0:T(8,128)(2,1)S(1)}, u32[]{:S(2)}, u32[]{:S(2)}) collective-permute-start(bf16[4,192,1024]{2,1,0:T(8,128)(2,1)S(1)} %fusion.3), channel_id=1, source_target_pairs={{0,16},{16,0},{1,17},{17,1},{2,18},{18,2},{3,19},{19,3},{4,20},{20... | collective-permute-start | bytes 4718600 | tf_op jit(solution)/shard_map/ppermute | solution.py:568
  403.9 26.1 %collective-permute-start.30 = (bf16[4,128,1024]{2,1,0:T(8,128)(2,1)S(1)}, bf16[4,128,1024]{2,1,0:T(8,128)(2,1)S(1)}, u32[]{:S(2)}, u32[]{:S(2)}) collective-permute-start(bf16[4,128,1024]{2,1,0:T(8,128)(2,1)S(1)} %dynamic-slice_bitcast_fusion.4), channel_id=1, source_target_pairs={{0,8},{8,0},{1,9},{9,1},{2,10},{10,2},{3,11},{11,3},{4,12},{12,4},... | collective-permute-start | bytes 3145736 | tf_op jit(solution)/shard_map/ppermute | solution.py:568
  408.8 27.4 %copy-start.21 = (bf16[1024,384]{1,0:T(8,128)(2,1)}, bf16[1024,384]{1,0:T(8,128)(2,1)S(1)}, u32[]{:S(2)}) copy-start(bf16[1024,384]{1,0:T(8,128)(2,1)S(1)} %convolution_convert_fusion.2) | copy-start | bytes 2359300
  408.9 34.2 %collective-permute-start.35 = (bf16[2,256,384]{2,1,0:T(8,128)(2,1)S(1)}, bf16[2,256,384]{2,1,0:T(8,128)(2,1)}, u32[]{:S(2)}, u32[]{:S(2)}) collective-permute-start(bf16[2,256,384]{2,1,0:T(8,128)(2,1)S(1)} %dynamic-slice_bitcast_fusion.7), channel_id=1, source_target_pairs={{0,8},{8,0},{1,9},{9,1},{2,10},{10,2},{3,11},{11,3},{4,12},{12,4},... | collective-permute-start | bytes 1179656 | tf_op jit(solution)/shard_map/ppermute | solution.py:568
  437.4 19.1 %collective-permute-start.31 = (bf16[320,1024]{1,0:T(8,128)(2,1)}, bf16[320,1024]{1,0:T(8,128)(2,1)}, u32[]{:S(2)}, u32[]{:S(2)}) collective-permute-start(bf16[320,1024]{1,0:T(8,128)(2,1)} %get-tuple-element.156), channel_id=1, source_target_pairs={{0,2},{1,3},{8,10},{9,11},{16,18},{17,19},{24,26},{25,27}} | collective-permute-start | bytes 1966088 | tf_op jit(solution)/shard_map/ppermute | solution.py:557
  441.5 15.0 %collective-permute-start.32 = (bf16[320,1024]{1,0:T(8,128)(2,1)}, bf16[320,1024]{1,0:T(8,128)(2,1)}, u32[]{:S(2)}, u32[]{:S(2)}) collective-permute-start(bf16[320,1024]{1,0:T(8,128)(2,1)} %get-tuple-element.155), channel_id=1, source_target_pairs={{6,4},{7,5},{14,12},{15,13},{22,20},{23,21},{30,28},{31,29}} | collective-permute-start | bytes 1966088 | tf_op jit(solution)/shard_map/ppermute | solution.py:557
  445.0 23.9 %copy-start.48 = (f32[1,2048]{1,0:T(1,128)S(1)}, f32[1,2048]{1,0:T(1,128)}, u32[]{:S(2)}) copy-start(f32[1,2048]{1,0:T(1,128)} %get-tuple-element.103) | copy-start | bytes 24580
  445.0 24.1 %copy-start.39 = (f32[1024]{0:T(1024)S(1)}, f32[1024]{0:T(1024)}, u32[]{:S(2)}) copy-start(f32[1024]{0:T(1024)} %get-tuple-element.126) | copy-start | bytes 12292
  445.0 24.2 %copy-start.38 = (f32[1024]{0:T(1024)S(1)}, f32[1024]{0:T(1024)}, u32[]{:S(2)}) copy-start(f32[1024]{0:T(1024)} %get-tuple-element.124) | copy-start | bytes 12292
  445.0 24.8 %copy-start.37 = (f32[1024]{0:T(1024)S(1)}, f32[1024]{0:T(1024)}, u32[]{:S(2)}) copy-start(f32[1024]{0:T(1024)} %get-tuple-element.104) | copy-start | bytes 12292
  445.0 26.4 %collective-permute-start.36 = (bf16[256,384]{1,0:T(8,128)(2,1)}, bf16[256,384]{1,0:T(8,128)(2,1)}, u32[]{:S(2)}, u32[]{:S(2)}) collective-permute-start(bf16[256,384]{1,0:T(8,128)(2,1)} %dynamic-slice_bitcast_fusion.8), channel_id=1, source_target_pairs={{0,16},{16,0},{1,17},{17,1},{2,18},{18,2},{3,19},{19,3},{4,20},{20... | collective-permute-start | bytes 589832 | tf_op jit(solution)/shard_map/ppermute | solution.py:568
  465.2 21.5 %collective-permute-start.34 = (bf16[320,1024]{1,0:T(8,128)(2,1)}, bf16[320,1024]{1,0:T(8,128)(2,1)}, u32[]{:S(2)}, u32[]{:S(2)}) collective-permute-start(bf16[320,1024]{1,0:T(8,128)(2,1)} %get-tuple-element.153), channel_id=1, source_target_pairs={{4,2},{6,4},{5,3},{7,5},{12,10},{14,12},{13,11},{15,13},{20,18},{2... | collective-permute-start | bytes 1966088 | tf_op jit(solution)/shard_map/ppermute | solution.py:557
  466.8 19.9 %collective-permute-start.33 = (bf16[320,1024]{1,0:T(8,128)(2,1)}, bf16[320,1024]{1,0:T(8,128)(2,1)}, u32[]{:S(2)}, u32[]{:S(2)}) collective-permute-start(bf16[320,1024]{1,0:T(8,128)(2,1)} %get-tuple-element.154), channel_id=1, source_target_pairs={{0,2},{2,4},{1,3},{3,5},{8,10},{10,12},{9,11},{11,13},{16,18},{18,... | collective-permute-start | bytes 1966088 | tf_op jit(solution)/shard_map/ppermute | solution.py:557
  486.7 25.1 %copy-start.31 = (f32[14,32]{1,0:T(8,128)S(1)}, f32[14,32]{1,0:T(8,128)}, u32[]{:S(2)}) copy-start(f32[14,32]{1,0:T(8,128)} %param.27) | copy-start | bytes 5380
  486.7 25.1 %copy-start.46 = (f32[14,32]{1,0:T(8,128)S(1)}, f32[14,32]{1,0:T(8,128)}, u32[]{:S(2)}) copy-start(f32[14,32]{1,0:T(8,128)} %param.32) | copy-start | bytes 5380
  486.7 25.1 %copy-start.47 = (f32[14,32]{1,0:T(8,128)S(1)}, f32[14,32]{1,0:T(8,128)}, u32[]{:S(2)}) copy-start(f32[14,32]{1,0:T(8,128)} %param.37) | copy-start | bytes 5380
  500.3 12.8 %all-to-all-start.3 = ((bf16[8,32,384]{2,1,0:T(8,128)(2,1)}), bf16[8,32,384]{2,1,0:T(8,128)(2,1)}, u32[]{:S(2)}, u32[]{:S(2)}) async-start(bf16[8,32,384]{2,1,0:T(8,128)(2,1)} %bitcast.87), calls=%async_computation.3 | async-start | bytes 393216 | tf_op jit(solution)/shard_map/all_to_all | solution.py:797
  504.4 21.1 %collective-permute-start.38 = (bf16[320,1024]{1,0:T(8,128)(2,1)}, bf16[320,1024]{1,0:T(8,128)(2,1)}, u32[]{:S(2)}, u32[]{:S(2)}) collective-permute-start(bf16[320,1024]{1,0:T(8,128)(2,1)} %get-tuple-element.99), channel_id=1, source_target_pairs={{2,0},{4,2},{6,4},{3,1},{5,3},{7,5},{10,8},{12,10},{14,12},{11,9},... | collective-permute-start | bytes 1966088 | tf_op jit(solution)/shard_map/ppermute | solution.py:557
  505.7 19.8 %collective-permute-start.37 = (bf16[320,1024]{1,0:T(8,128)(2,1)}, bf16[320,1024]{1,0:T(8,128)(2,1)}, u32[]{:S(2)}, u32[]{:S(2)}) collective-permute-start(bf16[320,1024]{1,0:T(8,128)(2,1)} %get-tuple-element.98), channel_id=1, source_target_pairs={{0,2},{2,4},{4,6},{1,3},{3,5},{5,7},{8,10},{10,12},{12,14},{9,11},... | collective-permute-start | bytes 1966088 | tf_op jit(solution)/shard_map/ppermute | solution.py:557
  516.9 10.4 %copy-start.26 = (f32[128,1024]{1,0:T(8,128)S(1)}, f32[128,1024]{1,0:T(8,128)}, u32[]{:S(2)}) copy-start(f32[128,1024]{1,0:T(8,128)} %param.36) | copy-start | bytes 1572868
  527.2 1.5 collective-permute-start.39
  (38 other events, 147.8 us)
Sparse Core Ops, SparseCore 0:
  90.3 130.4 all-gather.5
  224.3 71.6 all-gather.3

commit v9 on v8

--- a/solution.py
+++ b/solution.py
@@ -320,27 +320,18 @@
     once = dict(pipeline_mode=pl.Buffered(1))
     fixed = pl.BlockSpec((rows, width), lambda j, core: (0, 0), **once)
     if len(weights) == 1:
-        count = 2 * chips
-        share = width // count
-        pieces = units // unit_block
-        lane_blocks = width // unit_block
-
-        def up_spec(piece):
-            def place(j, core):
-                block = 2 * (j * pieces + piece) + core[0]
-                return (0, block // lane_blocks, lax.rem(block, lane_blocks))
-
-            return pl.BlockSpec((count, share, unit_block), place)
-
-        def down_spec(piece):
-            return pl.BlockSpec(
-                (1, unit_block, width), lambda j, core: (2 * (j * pieces + piece) + core[0], 1, 0)
-            )
-
-        weights = list(weights) * (2 * pieces)
-        weight_specs = [up_spec(n) for n in range(pieces)] + [down_spec(n) for n in range(pieces)]
+        up_rows = width // chips
+        pieces = 1
+        owners = units // unit_block
+        weights = list(weights) * 2
+        weight_specs = [
+            pl.BlockSpec((chips, up_rows, units), lambda j, core: (0, j // folds, lax.rem(j, folds))),
+            pl.BlockSpec(
+                (owners, unit_block, width), lambda j, core: (j, half // width * up_rows // unit_block, 0)
+            ),
+        ]
         up_shape, down_shape = (chips, half // chips, width), (chips, half // chips, width)
-        down_grad_spec = pl.BlockSpec((pieces, unit_block, width), lambda j, core: (j, 0, 0))
+        down_grad_spec = pl.BlockSpec((owners, unit_block, width), lambda j, core: (j, 0, 0))
     else:
         pieces = 1
         weight_specs = [
@@ -383,7 +374,7 @@
         name="mlp_both_ways",
     )(core, own, other, gm_own, gm_other, bias[None], *weights)
     up_grad, down_grad = outs[0], outs[1]
-    if pieces == 1:
+    if up_shape[0] == 1:
         up_grad = up_grad.reshape(half // width, chips, width // chips, width).swapaxes(0, 1)
         up_grad = up_grad.reshape(chips, -1, width)
         down_grad = down_grad.reshape(chips, -1, width)
@@ -475,6 +466,11 @@
     return lax.ppermute(value, "core", [(0, 1), (1, 0)])
 
 
+def line_pairs(size, sign, step):
+    pairs = [(i, i - sign) for i in range(size) if 0 <= i - sign < size]
+    return [(i, j) for i, j in pairs if 0 <= i + sign * (step - 1) < size]
+
+
 def line_pieces(value, axis):
     size = lax.axis_size(axis)
     if size == 2:
@@ -484,9 +480,7 @@
     for sign in (-1, 1):
         moving = value
         for step in range(1, size):
-            pairs = [(i, i - sign) for i in range(size) if 0 <= i - sign < size]
-            pairs = [(i, j) for i, j in pairs if 0 <= i + sign * (step - 1) < size]
-            moving = lax.ppermute(moving, axis, pairs)
+            moving = lax.ppermute(moving, axis, line_pairs(size, sign, step))
             pieces.append((sign * step, moving))
     return pieces
 
@@ -627,7 +621,7 @@
     folds = half // width
     up_end = 2 * share * folds
     low = lambda value: value.astype(jnp.bfloat16)
-    direct = share % 16 == 0 and unit_block == 128
+    direct = share % 16 == 0 and unit_block == 128 and line > 3
     position = lax.broadcasted_iota(jnp.int32, (images, rows), 1)
     found = (segment_ids[None, :] == lax.broadcasted_iota(jnp.int32, (images, rows), 0)) & (
         valid[None, :] == 1
@@ -644,8 +638,50 @@
         blocks = blocks.reshape(line, 2, share + extra, 3 * lanes)
         keep = jnp.where(first_core, blocks[:, 0], blocks[:, 1])
         sent = swap_cores(jnp.where(first_core, blocks[:, 1], blocks[:, 0]))
-        blocks = exchange_line(in_order(keep[:, None], sent[:, None], 1), "line")
-        blocks = gather_line(gather_line(blocks, "inner"), "outer")
+        blocks = in_order(keep[:, None], sent[:, None], 1)
+
+        up_blocks = low(hidden_up).reshape(share, chips, 2, unit_block)
+        up_first = up_blocks[:, :, 0].reshape(share, half)
+        up_second = up_blocks[:, :, 1].reshape(share, half)
+        out_rows = low(project_out)
+        received = swap_cores(
+            jnp.concatenate(
+                [jnp.where(first_core, up_second, up_first).reshape(-1, width), out_rows], axis=0
+            )
+        )
+        up_rows = in_order(
+            jnp.where(first_core, up_first, up_second),
+            received[: share * folds].reshape(share, half),
+            0,
+        )
+        packed = jnp.concatenate(
+            [
+                up_rows.reshape(2 * share, folds, width).transpose(1, 0, 2).reshape(-1, width),
+                low(hidden_down),
+                in_order(out_rows, received[share * folds :], 0),
+            ],
+            axis=0,
+        )
+        gathered = lax.all_gather(packed, ("outer", "inner", "line"), axis=0, tiled=False)
+        whole_out = gathered[:, packed.shape[0] - 2 * share :].reshape(width, width)
+        mlp_weights = (gathered,)
+        whole_in = lax.all_gather(fold(project_in), everyone, axis=0, tiled=False)
+
+        pieces, swapped = [], []
+        moving = [tokens, tokens]
+        for step in range(1, line):
+            moving = [
+                lax.ppermute(value, "line", line_pairs(line, sign, step))
+                for sign, value in zip((-1, 1), moving)
+            ]
+            if step == 1:
+                blocks = exchange_line(blocks, "line")
+            elif step == 2:
+                blocks = gather_line(gather_line(blocks, "inner"), "outer")
+            moving, blocks, swapped = lax.optimization_barrier((moving, blocks, swapped))
+            pieces += [(sign * step, value) for sign, value in zip((-1, 1), moving)]
+            swapped = swapped + [swap_cores(value) for value in moving]
+        swapped = [(distance, value) for (distance, _), value in zip(pieces, swapped)]
         blocks = blocks.reshape(count, share + extra, 3 * lanes)
         mine_in = blocks[:, :share].reshape(width, 3 * lanes)
         small = blocks[:, share:].reshape(count, -1)
@@ -664,17 +700,10 @@
     offsets = lax.broadcasted_iota(jnp.int32, (group, images), 0) * rows
     starts = jnp.min(jnp.where(first < rows, first + offsets, length), axis=0)
 
-    pieces = line_pieces(tokens, "line")
-    if direct:
-        packed = jnp.concatenate([fold(hidden_up), low(hidden_down), low(project_out)], axis=0)
-        packed, pieces_in = lax.optimization_barrier((packed, tuple(piece for _, piece in pieces)))
-        pieces = [(distance, piece) for (distance, _), piece in zip(pieces, pieces_in)]
-        gathered = lax.all_gather(packed, everyone, axis=0, tiled=False)
-        whole_out = gathered[:, packed.shape[0] - share :].reshape(width, width)
-        mlp_weights = (gathered,)
-        whole_in = lax.all_gather(fold(project_in), everyone, axis=0, tiled=False)
+    if not direct:
+        pieces = line_pieces(tokens, "line")
+        swapped = [(distance, swap_cores(piece)) for distance, piece in pieces]
     own_tokens = line_order(tokens, pieces, "line").reshape(-1, width)
-    swapped = [(distance, swap_cores(piece)) for distance, piece in pieces]
     other_tokens = line_order(swap_cores(tokens), swapped, "line").reshape(-1, width)
 
     gain_one, shift_one, bias_query, bias_value, bias_out = (

time: 550 us -> 606 us (1.10)
  waiting for transfers between devices: 197 us -> 239 us
  local copies, waits for them, and re-layouts: 51.7 us -> 67.2 us
    ppermute x6, waiting for transfers between devices: 3.65 us -> 35.9 us  [exchange_line(): pieces.append((-move, lax.ppermute(pick(place + move), axis, pairs)))]
    ppermute x6, waiting for transfers between devices: 67.5 us -> 92.5 us  [on_device(): lax.ppermute(value, 'line', line_pairs(line, sign, step))]
    ppermute x2, waiting for transfers between devices: 24.4 us -> 15.5 us  [line_pieces(): other = lax.ppermute(value, axis, [(0, 1), (1, 0)])]
    dynamic_update_slice x20 -> x19, local copies, waits for them, and re-layouts: 6.69 us -> 15 us  [line_order(): whole = lax.dynamic_update_index_in_dim(whole, piece, slot, 0)]
  transfers between devices with their start and end apart: 46 -> 47, of which waited for: 20 -> 19; matrix products, arithmetic and copies ran while one was open for 18% -> 18% of each run, Pallas kernels for 23% -> 21%
where the time goes in v9:
time: 606 us; the launch traced here: 600 us
  waiting for transfers between devices  239 us (39%)
  Pallas kernels  124 us (20%)
  starting transfers between devices  81.9 us (14%)
  local copies, waits for them, and re-layouts  67.2 us (11%)
  other arithmetic  49.4 us (8%)
  between operations  15.7 us (3%)
  matrix products  11.9 us (2%)
  blocking collectives  10.9 us (2%)
    ppermute x6, waiting for transfers between devices, on_device(): lax.ppermute(value, 'line', line_pairs(line, sign, step))  92.5 us
    pallas_call x1, Pallas kernels, mlp(): pl.pallas_call(functools.partial(mlp_kernel, pieces), grid_spec=pltpu.Pre...  37.8 us
    ppermute x6, waiting for transfers between devices, exchange_line(): pieces.append((-move, lax.ppermute(pick(place + move), axis, pairs)))  35.9 us
    pallas_call x1, Pallas kernels, attend_back(): pl.pallas_call(attend_back_kernel, grid_spec=pltpu.PrefetchScalarGridSpec...  34.8 us
    pallas_call x1, Pallas kernels, attend(): pl.pallas_call(attend_kernel, grid_spec=pltpu.PrefetchScalarGridSpec(num_...  26.3 us
    ppermute x4, waiting for transfers between devices, scatter_line(): lax.ppermute(pick(1 - place), axis, [(0, 1), (1, 0)])  24.2 us
    all_to_all x1, waiting for transfers between devices, on_device(): lax.all_to_all(attended.reshape(group, rows, lanes), seq, split_axis=0, c...  21.7 us
    ppermute x3, waiting for transfers between devices, scatter_terms(): return (pick(place), lax.ppermute(pick(1 - place), axis, [(0, 1), (1, 0)]))  19.9 us
  transfers between devices with their start and end apart: 47, of which 19 were waited for; matrix products, arithmetic and copies ran while one was open for 18% of the time, Pallas kernels for 21%

profile of v9, /device:TPU:0, one launch (start us, length us, event | category | flops | bytes accessed | tf_op | source)
XLA Modules:
  0.0 599.9 jit_solution(10420034446254281261)
XLA Ops:
  16.8 5.2 collective-permute-start
  23.3 7.3 %collective-permute-start.4 = (bf16[2,48,384]{2,1,0:T(8,128)(2,1)S(1)}, bf16[2,48,384]{2,1,0:T(8,128)(2,1)S(1)}, u32[]{:S(2)}, u32[]{:S(2)}) collective-permute-start(bf16[2,48,384]{2,1,0:T(8,128)(2,1)S(1)} %get-tuple-element.187), channel_id=1, source_target_pairs={{0,6},{1,7},{8,14},{9,15},{16,22},{17,23},{24,30},{25,31}} | collective-permute-start | bytes 221192 | tf_op jit(solution)/shard_map/ppermute | solution.py:515
  31.9 5.4 collective-permute-start.6
  37.4 22.8 %collective-permute-done.4 = bf16[2,48,384]{2,1,0:T(8,128)(2,1)S(1)} collective-permute-done((bf16[2,48,384]{2,1,0:T(8,128)(2,1)S(1)}, bf16[2,48,384]{2,1,0:T(8,128)(2,1)S(1)}, u32[]{:S(2)}, u32[]{:S(2)}) %collective-permute-start.4) | collective-permute-done | bytes 73760 | tf_op jit(solution)/shard_map/ppermute | solution.py:515
  61.5 9.8 %collective-permute-done.5 = bf16[2,48,384]{2,1,0:T(8,128)(2,1)S(1)} collective-permute-done((bf16[2,48,384]{2,1,0:T(8,128)(2,1)S(1)}, bf16[2,48,384]{2,1,0:T(8,128)(2,1)S(1)}, u32[]{:S(2)}, u32[]{:S(2)}) %collective-permute-start.5) | collective-permute-done | bytes 73760 | tf_op jit(solution)/shard_map/ppermute | solution.py:515
  72.6 3.3 collective-permute-done.8
  76.0 2.7 collective-permute-start.11
  78.7 1.7 collective-permute-start.9
  82.2 6.5 %collective-permute-done.11 = bf16[4,2,48,384]{3,2,1,0:T(8,128)(2,1)S(1)} collective-permute-done((bf16[4,2,48,384]{3,2,1,0:T(8,128)(2,1)S(1)}, bf16[4,2,48,384]{3,2,1,0:T(8,128)(2,1)S(1)}, u32[]{:S(2)}, u32[]{:S(2)}) %collective-permute-start.11) | collective-permute-done | bytes 294944 | tf_op jit(solution)/shard_map/ppermute | solution.py:477
  88.8 1.5 collective-permute-start.12
  90.4 9.0 %collective-permute-done.12 = bf16[2,4,2,48,384]{4,3,2,1,0:T(8,128)(2,1)S(1)} collective-permute-done((bf16[2,4,2,48,384]{4,3,2,1,0:T(8,128)(2,1)S(1)}, bf16[2,4,2,48,384]{4,3,2,1,0:T(8,128)(2,1)S(1)}, u32[]{:S(2)}, u32[]{:S(2)}) %collective-permute-start.12) | collective-permute-done | bytes 589856 | tf_op jit(solution)/shard_map/ppermute | solution.py:477
  99.7 37.4 %collective-permute-done.10 = bf16[512,1024]{1,0:T(8,128)(2,1)} collective-permute-done((bf16[512,1024]{1,0:T(8,128)(2,1)}, bf16[512,1024]{1,0:T(8,128)(2,1)}, u32[]{:S(2)}, u32[]{:S(2)}) %collective-permute-start.10) | collective-permute-done | bytes 1048608 | tf_op jit(solution)/shard_map/ppermute | solution.py:674
  137.1 1.6 collective-permute-start.15
  138.7 1.5 collective-permute-start.16
  141.4 55.1 %collective-permute-done.16 = bf16[512,1024]{1,0:T(8,128)(2,1)} collective-permute-done((bf16[512,1024]{1,0:T(8,128)(2,1)}, bf16[512,1024]{1,0:T(8,128)(2,1)}, u32[]{:S(2)}, u32[]{:S(2)}) %collective-permute-start.16) | collective-permute-done | bytes 1048608 | tf_op jit(solution)/shard_map/ppermute | solution.py:674
  199.7 3.2 slice_reduce_fusion.2
  218.4 1.8 bitcast_dynamic-update-slice_fusion.3
  223.0 2.1 bitcast_dynamic-update-slice_fusion.2
  227.9 2.1 copy-done.5
  229.9 14.1 %norm_mix.1 = (bf16[4096,1024]{1,0:T(8,128)(2,1)}, bf16[4096,128]{1,0:T(8,128)(2,1)}, bf16[4096,128]{1,0:T(8,128)(2,1)}, bf16[4096,128]{1,0:T(8,128)(2,1)}) custom-call(s32[1]{0:T(128)} %bitcast.28.place_ref, bf16[2048,1024]{1,0:T(8,128)(2,1)} %bitcast.274, bf16[2048,1024]{1,0:T(8,128)(2,1)} %bitcast.273, f32[1,1024]{1,0:T(1,128)} %slice.145.gain_ref, ...), custom_call_target="tpu_custom_call" | custom-call | flops 3221225472 | bytes 16777216 | tf_op jit(solution)/shard_map/norm_mix/pallas_call | solution.py:243
  244.1 26.3 %attend_forward.1 = (f32[4096,128]{1,0:T(8,128)}, bf16[4096,128]{1,0:T(8,128)(2,1)}, f32[4096,128]{1,0:T(8,128)}) custom-call(s32[2]{0:T(128)} %select_reduce_fusion.starts_ref, bf16[4096,128]{1,0:T(8,128)(2,1)} %get-tuple-element.84.q_ref, bf16[4096,128]{1,0:T(8,128)(2,1)} %get-tuple-element.85.k_ref, bf16[4096,128]{1,0:T(8,128)(2,1)} %get-tuple-element.86.v_ref), custom_call_target="tpu_custom_call" | custom-call | flops 4060086272 | bytes 8388608 | tf_op jit(solution)/shard_map/attend_forward/pallas_call | solution.py:116
  270.4 2.3 copy.135
  272.6 3.7 all-to-all-start
  279.7 2.0 convert_reduce_fusion
  282.1 3.2 slice.194
  285.3 21.7 %all-to-all-done = bf16[8,512,128]{1,2,0:T(8,128)(2,1)S(1)} async-done(((bf16[8,512,128]{1,2,0:T(8,128)(2,1)}), bf16[8,512,128]{1,2,0:T(8,128)(2,1)S(1)}, u32[]{:S(2)}, u32[]{:S(2)}) %all-to-all-start) | async-done | bytes 1048608 | tf_op jit(solution)/shard_map/all_to_all | solution.py:750
  308.0 4.8 fusion.78
  316.7 1.5 reshape.407
  319.5 37.8 %mlp_both_ways.1 = (bf16[16,128,1024]{2,1,0:T(8,128)(2,1)}, bf16[16,128,1024]{2,1,0:T(8,128)(2,1)}, f32[512,1024]{1,0:T(8,128)}, f32[512,1024]{1,0:T(8,128)}, f3...) custom-call(s32[1]{0:T(128)} %bitcast.55.core_ref, bf16[512,1024]{1,0:T(8,128)(2,1)} %add_convert_fusion.4.own_ref, ...), custom_call_target="tpu_custom_call" | custom-call | flops 25769803776 | bytes 29360128 | tf_op jit(solution)/shard_map/mlp_both_ways/pallas_call | solution.py:344
  359.4 2.7 collective-permute-done.27
  362.1 3.8 multiply_reduce_fusion.1
  366.0 4.2 multiply_reduce_fusion
  376.2 4.7 all-to-all-start.1
  384.3 4.4 dynamic-slice_bitcast_fusion.2
  389.7 2.4 dynamic-slice_bitcast_fusion
  392.1 1.8 collective-permute-start.29
  394.0 15.6 %collective-permute-done.28 = bf16[2,4,64,1024]{3,2,1,0:T(8,128)(2,1)} collective-permute-done((bf16[2,4,64,1024]{3,2,1,0:T(8,128)(2,1)}, bf16[2,4,64,1024]{3,2,1,0:T(8,128)(2,1)}, u32[]{:S(2)}, u32[]{:S(2)}) %collective-permute-start.28) | collective-permute-done | bytes 1048608 | tf_op jit(solution)/shard_map/ppermute | solution.py:530
  409.6 34.8 %attend_backward.1 = bf16[4096,384]{1,0:T(8,128)(2,1)} custom-call(s32[2]{0:T(128)} %select_reduce_fusion.starts_ref, bf16[4096,128]{1,0:T(8,128)(2,1)} %get-tuple-element.84.q_ref, bf16[4096,128]{1,0:T(8,128)(2,1)} %get-tuple-element.85.k_ref, bf16[4096,128]{1,0:T(8,128)(2,1)} %get-tuple-element.86.v_ref, f32[4096,128]{1,0:T(8,128)} %get-tuple-element.96.wide_ref, ...), custom_call_target="tpu_custom_call" | custom-call | flops 10150215680 | bytes 11534336 | tf_op jit(solution)/shard_map/attend_backward/pallas_call | solution.py:196
  444.4 5.3 all-to-all-start.2
  449.8 4.3 collective-permute-done.26
  454.1 1.8 add_convert_fusion.2
  455.9 2.6 add_convert_fusion.1
  458.6 1.9 collective-permute-start.30
  460.5 2.7 add_convert_fusion
  464.3 4.5 convolution_convert_fusion.2
  470.0 19.4 %collective-permute-done.31 = bf16[4,128,1024]{2,1,0:T(8,128)(2,1)S(1)} collective-permute-done((bf16[4,128,1024]{2,1,0:T(8,128)(2,1)S(1)}, bf16[4,128,1024]{2,1,0:T(8,128)(2,1)S(1)}, u32[]{:S(2)}, u32[]{:S(2)}) %collective-permute-start.31) | collective-permute-done | bytes 1048608 | tf_op jit(solution)/shard_map/ppermute | solution.py:562
  489.9 4.8 collective-permute-done.30
  496.6 4.1 collective-permute-start.32
  500.7 1.5 collective-permute-start.33
  504.2 1.8 collective-permute-start.37
  506.1 9.5 %collective-permute-done.32 = bf16[320,1024]{1,0:T(8,128)(2,1)} collective-permute-done((bf16[320,1024]{1,0:T(8,128)(2,1)}, bf16[320,1024]{1,0:T(8,128)(2,1)}, u32[]{:S(2)}, u32[]{:S(2)}) %collective-permute-start.32) | collective-permute-done | bytes 655392 | tf_op jit(solution)/shard_map/ppermute | solution.py:551
  515.6 5.8 all-to-all-done.2.grad_ref
  521.4 2.9 fusion.9
  524.3 1.5 collective-permute-start.35
  525.8 2.1 collective-permute-start.34
  530.5 1.7 fusion.33
  532.1 10.7 %finish_input.1 = (f32[512,1024]{1,0:T(8,128)}, f32[1,1024]{1,0:T(1,128)}, f32[1,1024]{1,0:T(1,128)}, f32[3,1,1024]{2,1,0:T(1,128)}) custom-call(bf16[8,512,384]{2,1,0:T(8,128)(2,1)} %all-to-all-done.2.grad_ref, bf16[32,96,1024]{2,1,0:T(8,128)(2,1)} %all-gather.4.cloned.1.call-done.weight_ref, bf16[512,1024]{1,0:T(8,128)(2,1)} %x_ref.1, ...), custom_call_target="tpu_custom_call" | custom-call | flops 3221225472 | bytes 16777216 | tf_op jit(solution)/shard_map/finish_input/pallas_call | solution.py:434
  545.7 3.0 fusion.10
  549.9 10.9 %all_to_all.30 = f32[32,1,448]{2,1,0:T(1,128)S(1)} all-to-all(f32[32,1,448]{2,1,0:T(1,128)S(1)} %all_to_all.24), channel_id=1, replica_groups=mesh['outer'=2,'inner'=2,'line'=4,'core'=2] {'outer','inner','line','core'}, dimensions={0} | all-to-all | bytes 114688 | tf_op jit(solution)/shard_map/all_to_all | solution.py:855
  560.7 4.0 all-to-all-start.3
  566.1 5.4 collective-permute-start.38
  574.9 2.4 multiply_subtract_fusion.2
  577.3 8.6 %collective-permute-done.39 = bf16[320,1024]{1,0:T(8,128)(2,1)} collective-permute-done((bf16[320,1024]{1,0:T(8,128)(2,1)}, bf16[320,1024]{1,0:T(8,128)(2,1)}, u32[]{:S(2)}, u32[]{:S(2)}) %collective-permute-start.39) | collective-permute-done | bytes 655392 | tf_op jit(solution)/shard_map/ppermute | solution.py:551
  585.8 1.6 fusion.8
  (329 shorter events, 87.6 us)
Async XLA Ops:
  7.2 274.9 %all-gather.6.cloned.1.call-start = ((), (), s32[]{:S(2)}) async-start(), calls=%async_computation.6 | async-start | bytes 11141120 | tf_op jit(solution)/shard_map/all_gather | solution.py:665
  10.0 1.6 collective-permute-start.22
  13.9 1.4 collective-permute-start.2
  15.5 16.4 %collective-permute-start.3 = (bf16[2,48,384]{2,1,0:T(8,128)(2,1)S(1)}, bf16[2,48,384]{2,1,0:T(8,128)(2,1)S(1)}, u32[]{:S(2)}, u32[]{:S(2)}) collective-permute-start(bf16[2,48,384]{2,1,0:T(8,128)(2,1)S(1)} %get-tuple-element.186), channel_id=1, source_target_pairs={{6,0},{7,1},{14,8},{15,9},{22,16},{23,17},{30,24},{31,25}} | collective-permute-start | bytes 221192 | tf_op jit(solution)/shard_map/ppermute | solution.py:515
  16.8 59.2 %collective-permute-start = (bf16[512,1024]{1,0:T(8,128)(2,1)S(1)}, bf16[512,1024]{1,0:T(8,128)(2,1)}, u32[]{:S(2)}, u32[]{:S(2)}) collective-permute-start(bf16[512,1024]{1,0:T(8,128)(2,1)S(1)} %copy-done.3), channel_id=1, source_target_pairs={{0,2},{2,4},{4,6},{1,3},{3,5},{5,7},{8,10},{10,12},{12,14},{9,11},... | collective-permute-start | bytes 3145736 | tf_op jit(solution)/shard_map/ppermute | solution.py:674
  22.0 54.0 %collective-permute-start.1 = (bf16[512,1024]{1,0:T(8,128)(2,1)S(1)}, bf16[512,1024]{1,0:T(8,128)(2,1)}, u32[]{:S(2)}, u32[]{:S(2)}) collective-permute-start(bf16[512,1024]{1,0:T(8,128)(2,1)S(1)} %copy-done.3), channel_id=1, source_target_pairs={{2,0},{4,2},{6,4},{3,1},{5,3},{7,5},{10,8},{12,10},{14,12},{11,9},... | collective-permute-start | bytes 3145736 | tf_op jit(solution)/shard_map/ppermute | solution.py:674
  23.3 36.9 %collective-permute-start.4 = (bf16[2,48,384]{2,1,0:T(8,128)(2,1)S(1)}, bf16[2,48,384]{2,1,0:T(8,128)(2,1)S(1)}, u32[]{:S(2)}, u32[]{:S(2)}) collective-permute-start(bf16[2,48,384]{2,1,0:T(8,128)(2,1)S(1)} %get-tuple-element.187), channel_id=1, source_target_pairs={{0,6},{1,7},{8,14},{9,15},{16,22},{17,23},{24,30},{25,31}} | collective-permute-start | bytes 221192 | tf_op jit(solution)/shard_map/ppermute | solution.py:515
  30.6 40.7 %collective-permute-start.5 = (bf16[2,48,384]{2,1,0:T(8,128)(2,1)S(1)}, bf16[2,48,384]{2,1,0:T(8,128)(2,1)S(1)}, u32[]{:S(2)}, u32[]{:S(2)}) collective-permute-start(bf16[2,48,384]{2,1,0:T(8,128)(2,1)S(1)} %get-tuple-element.188), channel_id=1, source_target_pairs={{4,0},{6,2},{5,1},{7,3},{12,8},{14,10},{13,9},{15,11},{20,16},{22,... | collective-permute-start | bytes 221192 | tf_op jit(solution)/shard_map/ppermute | solution.py:515
  31.9 40.7 %collective-permute-start.6 = (bf16[2,48,384]{2,1,0:T(8,128)(2,1)S(1)}, bf16[2,48,384]{2,1,0:T(8,128)(2,1)S(1)}, u32[]{:S(2)}, u32[]{:S(2)}) collective-permute-start(bf16[2,48,384]{2,1,0:T(8,128)(2,1)S(1)} %get-tuple-element.189), channel_id=1, source_target_pairs={{0,4},{2,6},{1,5},{3,7},{8,12},{10,14},{9,13},{11,15},{16,20},{18,... | collective-permute-start | bytes 221192 | tf_op jit(solution)/shard_map/ppermute | solution.py:515
  60.2 12.4 %collective-permute-start.7 = (bf16[2,48,384]{2,1,0:T(8,128)(2,1)S(1)}, bf16[2,48,384]{2,1,0:T(8,128)(2,1)S(1)}, u32[]{:S(2)}, u32[]{:S(2)}) collective-permute-start(bf16[2,48,384]{2,1,0:T(8,128)(2,1)S(1)} %get-tuple-element.190), channel_id=1, source_target_pairs={{2,0},{4,2},{6,4},{3,1},{5,3},{7,5},{10,8},{12,10},{14,12},{11,9},... | collective-permute-start | bytes 221192 | tf_op jit(solution)/shard_map/ppermute | solution.py:515
  71.3 4.7 collective-permute-start.8
  76.0 12.7 %collective-permute-start.11 = (bf16[4,2,48,384]{3,2,1,0:T(8,128)(2,1)S(1)}, bf16[4,2,48,384]{3,2,1,0:T(8,128)(2,1)S(1)}, u32[]{:S(2)}, u32[]{:S(2)}) collective-permute-start(bf16[4,2,48,384]{3,2,1,0:T(8,128)(2,1)S(1)} %fusion.42), channel_id=1, source_target_pairs={{0,8},{8,0},{1,9},{9,1},{2,10},{10,2},{3,11},{11,3},{4,12},{12,4},... | collective-permute-start | bytes 884744 | tf_op jit(solution)/shard_map/ppermute | solution.py:477
  78.7 21.0 %collective-permute-start.9 = (bf16[512,1024]{1,0:T(8,128)(2,1)}, bf16[512,1024]{1,0:T(8,128)(2,1)}, u32[]{:S(2)}, u32[]{:S(2)}) collective-permute-start(bf16[512,1024]{1,0:T(8,128)(2,1)} %collective-permute-done), channel_id=1, source_target_pairs={{2,4},{4,6},{3,5},{5,7},{10,12},{12,14},{11,13},{13,15},{18,20},{2... | collective-permute-start | bytes 3145736 | tf_op jit(solution)/shard_map/ppermute | solution.py:674
  80.4 56.7 %collective-permute-start.10 = (bf16[512,1024]{1,0:T(8,128)(2,1)}, bf16[512,1024]{1,0:T(8,128)(2,1)}, u32[]{:S(2)}, u32[]{:S(2)}) collective-permute-start(bf16[512,1024]{1,0:T(8,128)(2,1)} %collective-permute-done.1), channel_id=1, source_target_pairs={{2,0},{4,2},{3,1},{5,3},{10,8},{12,10},{11,9},{13,11},{18,16},{20,... | collective-permute-start | bytes 3145736 | tf_op jit(solution)/shard_map/ppermute | solution.py:674
  81.6 55.5 %collective-permute-start.13 = (bf16[512,1024]{1,0:T(8,128)(2,1)}, bf16[512,1024]{1,0:T(8,128)(2,1)}, u32[]{:S(2)}, u32[]{:S(2)}) collective-permute-start(bf16[512,1024]{1,0:T(8,128)(2,1)} %collective-permute-done), channel_id=1, source_target_pairs={{0,1},{1,0},{2,3},{3,2},{4,5},{5,4},{6,7},{7,6},{8,9},{9,8},{10,11... | collective-permute-start | bytes 3145736 | tf_op jit(solution)/shard_map/ppermute | solution.py:466
  81.7 55.4 %collective-permute-start.14 = (bf16[512,1024]{1,0:T(8,128)(2,1)}, bf16[512,1024]{1,0:T(8,128)(2,1)}, u32[]{:S(2)}, u32[]{:S(2)}) collective-permute-start(bf16[512,1024]{1,0:T(8,128)(2,1)} %collective-permute-done.1), channel_id=1, source_target_pairs={{0,1},{1,0},{2,3},{3,2},{4,5},{5,4},{6,7},{7,6},{8,9},{9,8},{10,11... | collective-permute-start | bytes 3145736 | tf_op jit(solution)/shard_map/ppermute | solution.py:466
  88.8 10.6 %collective-permute-start.12 = (bf16[2,4,2,48,384]{4,3,2,1,0:T(8,128)(2,1)S(1)}, bf16[2,4,2,48,384]{4,3,2,1,0:T(8,128)(2,1)S(1)}, u32[]{:S(2)}, u32[]{:S(2)}) collective-permute-start(bf16[2,4,2,48,384]{4,3,2,1,0:T(8,128)(2,1)S(1)} %maximum_select_fusion.2), channel_id=1, source_target_pairs={{0,16},{16,0},{1,17},{17,1},{2,18},{18,2},{3,19},{19,3},{4,20},{20... | collective-permute-start | bytes 1769480 | tf_op jit(solution)/shard_map/ppermute | solution.py:477
  137.1 4.3 collective-permute-start.15
  138.7 57.7 %collective-permute-start.16 = (bf16[512,1024]{1,0:T(8,128)(2,1)}, bf16[512,1024]{1,0:T(8,128)(2,1)}, u32[]{:S(2)}, u32[]{:S(2)}) collective-permute-start(bf16[512,1024]{1,0:T(8,128)(2,1)} %collective-permute-done.10), channel_id=1, source_target_pairs={{2,0},{3,1},{10,8},{11,9},{18,16},{19,17},{26,24},{27,25}} | collective-permute-start | bytes 3145736 | tf_op jit(solution)/shard_map/ppermute | solution.py:674
  140.2 56.2 %collective-permute-start.17 = (bf16[512,1024]{1,0:T(8,128)(2,1)}, bf16[512,1024]{1,0:T(8,128)(2,1)}, u32[]{:S(2)}, u32[]{:S(2)}) collective-permute-start(bf16[512,1024]{1,0:T(8,128)(2,1)} %collective-permute-done.9), channel_id=1, source_target_pairs={{0,1},{1,0},{2,3},{3,2},{4,5},{5,4},{6,7},{7,6},{8,9},{9,8},{10,11... | collective-permute-start | bytes 3145736 | tf_op jit(solution)/shard_map/ppermute | solution.py:466
  140.3 56.2 %collective-permute-start.18 = (bf16[512,1024]{1,0:T(8,128)(2,1)}, bf16[512,1024]{1,0:T(8,128)(2,1)}, u32[]{:S(2)}, u32[]{:S(2)}) collective-permute-start(bf16[512,1024]{1,0:T(8,128)(2,1)} %collective-permute-done.10), channel_id=1, source_target_pairs={{0,1},{1,0},{2,3},{3,2},{4,5},{5,4},{6,7},{7,6},{8,9},{9,8},{10,11... | collective-permute-start | bytes 3145736 | tf_op jit(solution)/shard_map/ppermute | solution.py:466
  140.8 85.7 %collective-permute-start.21 = (bf16[512,1024]{1,0:T(8,128)(2,1)S(1)}, bf16[512,1024]{1,0:T(8,128)(2,1)}, u32[]{:S(2)}, u32[]{:S(2)}) collective-permute-start(bf16[512,1024]{1,0:T(8,128)(2,1)S(1)} %copy-done.3), channel_id=1, source_target_pairs={{0,1},{1,0},{2,3},{3,2},{4,5},{5,4},{6,7},{7,6},{8,9},{9,8},{10,11... | collective-permute-start | bytes 3145736 | tf_op jit(solution)/shard_map/ppermute | solution.py:466
  199.1 17.1 %collective-permute-start.19 = (bf16[512,1024]{1,0:T(8,128)(2,1)}, bf16[512,1024]{1,0:T(8,128)(2,1)S(1)}, u32[]{:S(2)}, u32[]{:S(2)}) collective-permute-start(bf16[512,1024]{1,0:T(8,128)(2,1)} %collective-permute-done.15), channel_id=1, source_target_pairs={{0,1},{1,0},{2,3},{3,2},{4,5},{5,4},{6,7},{7,6},{8,9},{9,8},{10,11... | collective-permute-start | bytes 3145736 | tf_op jit(solution)/shard_map/ppermute | solution.py:466
  199.1 17.8 %collective-permute-start.20 = (bf16[512,1024]{1,0:T(8,128)(2,1)}, bf16[512,1024]{1,0:T(8,128)(2,1)S(1)}, u32[]{:S(2)}, u32[]{:S(2)}) collective-permute-start(bf16[512,1024]{1,0:T(8,128)(2,1)} %collective-permute-done.16), channel_id=1, source_target_pairs={{0,1},{1,0},{2,3},{3,2},{4,5},{5,4},{6,7},{7,6},{8,9},{9,8},{10,11... | collective-permute-start | bytes 3145736 | tf_op jit(solution)/shard_map/ppermute | solution.py:466
  272.6 7.0 %copy-start.27 = (f32[32,32]{1,0:T(8,128)S(1)}, f32[32,32]{1,0:T(8,128)}, u32[]{:S(2)}) copy-start(f32[32,32]{1,0:T(8,128)} %get-tuple-element.126) | copy-start | bytes 12292
  272.6 7.1 %copy-start.1 = (bf16[512,1024]{1,0:T(8,128)(2,1)S(1)}, bf16[512,1024]{1,0:T(8,128)(2,1)}, u32[]{:S(2)}) copy-start(bf16[512,1024]{1,0:T(8,128)(2,1)} %param.20) | copy-start | bytes 3145732
  272.6 34.3 %all-to-all-start = ((bf16[8,512,128]{1,2,0:T(8,128)(2,1)}), bf16[8,512,128]{1,2,0:T(8,128)(2,1)S(1)}, u32[]{:S(2)}, u32[]{:S(2)}) async-start(bf16[8,512,128]{1,2,0:T(8,128)(2,1)} %copy.135), calls=%async_computation | async-start | bytes 2097152 | tf_op jit(solution)/shard_map/all_to_all | solution.py:750
  276.4 117.6 %all-gather.4.cloned.1.call-start = ((), (), s32[]{:S(2)}) async-start(), calls=%async_computation.5 | async-start | bytes 6488064 | tf_op jit(solution)/shard_map/all_gather | solution.py:668
  277.5 7.7 %copy-start.34 = (f32[512]{0:T(512)}, f32[512]{0:T(512)S(1)}, u32[]{:S(2)}) copy-start(f32[512]{0:T(512)S(1)} %convert_element_type.246) | copy-start | bytes 6148
  281.7 37.8 %collective-permute-start.24 = (bf16[512,1024]{1,0:T(8,128)(2,1)}, bf16[512,1024]{1,0:T(8,128)(2,1)}, u32[]{:S(2)}, u32[]{:S(2)}) collective-permute-start(bf16[512,1024]{1,0:T(8,128)(2,1)} %get-tuple-element.139.gm_own_ref), channel_id=1, source_target_pairs={{0,1},{1,0},{2,3},{3,2},{4,5},{5,4},{6,7},{7,6},{8,9},{9,8},{10,11... | collective-permute-start | bytes 3145736 | tf_op jit(solution)/shard_map/ppermute | solution.py:466
  282.1 25.9 %copy-start.42 = (f32[1024]{0:T(1024)S(1)}, f32[1024]{0:T(1024)}, u32[]{:S(2)}) copy-start(f32[1024]{0:T(1024)} %mul.322) | copy-start | bytes 12292
  282.1 25.9 %copy-start.44 = (f32[1024]{0:T(1024)S(1)}, f32[1024]{0:T(1024)}, u32[]{:S(2)}) copy-start(f32[1024]{0:T(1024)} %add.338) | copy-start | bytes 12292
  315.1 4.4 collective-permute-start.23
  357.4 4.7 collective-permute-start.27
  358.0 7.9 %collective-permute-start.25 = (f32[512,1024]{1,0:T(8,128)}, f32[512,1024]{1,0:T(8,128)}, u32[]{:S(2)}, u32[]{:S(2)}) collective-permute-start(f32[512,1024]{1,0:T(8,128)} %get-tuple-element.89), channel_id=1, source_target_pairs={{0,1},{1,0},{2,3},{3,2},{4,5},{5,4},{6,7},{7,6},{8,9},{9,8},{10,11... | collective-permute-start | bytes 6291464 | tf_op jit(solution)/shard_map/ppermute | solution.py:466
  376.2 33.4 %all-to-all-start.1 = ((bf16[8,512,128]{2,1,0:T(8,128)(2,1)}), bf16[8,512,128]{2,1,0:T(8,128)(2,1)}, u32[]{:S(2)}, u32[]{:S(2)}) async-start(bf16[8,512,128]{2,1,0:T(8,128)(2,1)} %bitcast.263), calls=%async_computation.1 | async-start | bytes 2097152 | tf_op jit(solution)/shard_map/all_to_all | solution.py:780
  383.3 26.3 %collective-permute-start.28 = (bf16[2,4,64,1024]{3,2,1,0:T(8,128)(2,1)}, bf16[2,4,64,1024]{3,2,1,0:T(8,128)(2,1)}, u32[]{:S(2)}, u32[]{:S(2)}) collective-permute-start(bf16[2,4,64,1024]{3,2,1,0:T(8,128)(2,1)} %get-tuple-element.175), channel_id=1, source_target_pairs={{0,8},{8,0},{1,9},{9,1},{2,10},{10,2},{3,11},{11,3},{4,12},{12,4},... | collective-permute-start | bytes 3145736 | tf_op jit(solution)/shard_map/ppermute | solution.py:530
  388.7 65.4 %collective-permute-start.26 = (bf16[2,4,128,1024]{3,2,1,0:T(8,128)(2,1)}, bf16[2,4,128,1024]{3,2,1,0:T(8,128)(2,1)}, u32[]{:S(2)}, u32[]{:S(2)}) collective-permute-start(bf16[2,4,128,1024]{3,2,1,0:T(8,128)(2,1)} %get-tuple-element.165), channel_id=1, source_target_pairs={{0,8},{8,0},{1,9},{9,1},{2,10},{10,2},{3,11},{11,3},{4,12},{12,4},... | collective-permute-start | bytes 6291464 | tf_op jit(solution)/shard_map/ppermute | solution.py:530
  392.1 61.9 %collective-permute-start.29 = (bf16[2,4,128,1024]{3,2,1,0:T(8,128)(2,1)}, bf16[2,4,128,1024]{3,2,1,0:T(8,128)(2,1)}, u32[]{:S(2)}, u32[]{:S(2)}) collective-permute-start(bf16[2,4,128,1024]{3,2,1,0:T(8,128)(2,1)} %get-tuple-element.163), channel_id=1, source_target_pairs={{0,16},{16,0},{1,17},{17,1},{2,18},{18,2},{3,19},{19,3},{4,20},{20... | collective-permute-start | bytes 6291464 | tf_op jit(solution)/shard_map/ppermute | solution.py:530
  444.4 76.9 %all-to-all-start.2 = ((bf16[8,512,384]{2,1,0:T(8,128)(2,1)}), bf16[8,512,384]{2,1,0:T(8,128)(2,1)}, u32[]{:S(2)}, u32[]{:S(2)}) async-start(bf16[8,512,384]{2,1,0:T(8,128)(2,1)} %bitcast.275), calls=%async_computation.2 | async-start | bytes 6291456 | tf_op jit(solution)/shard_map/all_to_all | solution.py:801
  454.1 10.2 %slice-start = ((s8[8388608]{0:T(1024)(128)(4,1)}), s8[4194304]{0:T(1024)(128)(4,1)S(1)}, s32[]{:S(2)}) async-start(s8[8388608]{0:T(1024)(128)(4,1)} %bitcast.313), calls=%async_computation.7 | async-start | bytes 8388608
  458.6 36.1 %collective-permute-start.30 = (bf16[4,192,1024]{2,1,0:T(8,128)(2,1)S(1)}, bf16[4,192,1024]{2,1,0:T(8,128)(2,1)S(1)}, u32[]{:S(2)}, u32[]{:S(2)}) collective-permute-start(bf16[4,192,1024]{2,1,0:T(8,128)(2,1)S(1)} %fusion.3), channel_id=1, source_target_pairs={{0,16},{16,0},{1,17},{17,1},{2,18},{18,2},{3,19},{19,3},{4,20},{20... | collective-permute-start | bytes 4718600 | tf_op jit(solution)/shard_map/ppermute | solution.py:562
  463.3 26.2 %collective-permute-start.31 = (bf16[4,128,1024]{2,1,0:T(8,128)(2,1)S(1)}, bf16[4,128,1024]{2,1,0:T(8,128)(2,1)S(1)}, u32[]{:S(2)}, u32[]{:S(2)}) collective-permute-start(bf16[4,128,1024]{2,1,0:T(8,128)(2,1)S(1)} %dynamic-slice_bitcast_fusion.4), channel_id=1, source_target_pairs={{0,8},{8,0},{1,9},{9,1},{2,10},{10,2},{3,11},{11,3},{4,12},{12,4},... | collective-permute-start | bytes 3145736 | tf_op jit(solution)/shard_map/ppermute | solution.py:562
  468.8 26.6 %copy-start.19 = (bf16[1024,384]{1,0:T(8,128)(2,1)}, bf16[1024,384]{1,0:T(8,128)(2,1)S(1)}, u32[]{:S(2)}) copy-start(bf16[1024,384]{1,0:T(8,128)(2,1)S(1)} %convolution_convert_fusion.2) | copy-start | bytes 2359300
  468.9 33.4 %collective-permute-start.36 = (bf16[2,256,384]{2,1,0:T(8,128)(2,1)S(1)}, bf16[2,256,384]{2,1,0:T(8,128)(2,1)}, u32[]{:S(2)}, u32[]{:S(2)}) collective-permute-start(bf16[2,256,384]{2,1,0:T(8,128)(2,1)S(1)} %dynamic-slice_bitcast_fusion.7), channel_id=1, source_target_pairs={{0,8},{8,0},{1,9},{9,1},{2,10},{10,2},{3,11},{11,3},{4,12},{12,4},... | collective-permute-start | bytes 1179656 | tf_op jit(solution)/shard_map/ppermute | solution.py:562
  496.6 19.0 %collective-permute-start.32 = (bf16[320,1024]{1,0:T(8,128)(2,1)}, bf16[320,1024]{1,0:T(8,128)(2,1)}, u32[]{:S(2)}, u32[]{:S(2)}) collective-permute-start(bf16[320,1024]{1,0:T(8,128)(2,1)} %get-tuple-element.172), channel_id=1, source_target_pairs={{0,2},{1,3},{8,10},{9,11},{16,18},{17,19},{24,26},{25,27}} | collective-permute-start | bytes 1966088 | tf_op jit(solution)/shard_map/ppermute | solution.py:551
  500.7 14.8 %collective-permute-start.33 = (bf16[320,1024]{1,0:T(8,128)(2,1)}, bf16[320,1024]{1,0:T(8,128)(2,1)}, u32[]{:S(2)}, u32[]{:S(2)}) collective-permute-start(bf16[320,1024]{1,0:T(8,128)(2,1)} %get-tuple-element.171), channel_id=1, source_target_pairs={{6,4},{7,5},{14,12},{15,13},{22,20},{23,21},{30,28},{31,29}} | collective-permute-start | bytes 1966088 | tf_op jit(solution)/shard_map/ppermute | solution.py:551
  504.2 23.7 %copy-start.50 = (f32[1,2048]{1,0:T(1,128)S(1)}, f32[1,2048]{1,0:T(1,128)}, u32[]{:S(2)}) copy-start(f32[1,2048]{1,0:T(1,128)} %get-tuple-element.119) | copy-start | bytes 24580
  504.2 23.9 %copy-start.41 = (f32[1024]{0:T(1024)S(1)}, f32[1024]{0:T(1024)}, u32[]{:S(2)}) copy-start(f32[1024]{0:T(1024)} %get-tuple-element.142) | copy-start | bytes 12292
  504.2 23.9 %copy-start.40 = (f32[1024]{0:T(1024)S(1)}, f32[1024]{0:T(1024)}, u32[]{:S(2)}) copy-start(f32[1024]{0:T(1024)} %get-tuple-element.140) | copy-start | bytes 12292
  504.2 24.6 %copy-start.39 = (f32[1024]{0:T(1024)S(1)}, f32[1024]{0:T(1024)}, u32[]{:S(2)}) copy-start(f32[1024]{0:T(1024)} %get-tuple-element.120) | copy-start | bytes 12292
  504.2 26.2 %collective-permute-start.37 = (bf16[256,384]{1,0:T(8,128)(2,1)}, bf16[256,384]{1,0:T(8,128)(2,1)}, u32[]{:S(2)}, u32[]{:S(2)}) collective-permute-start(bf16[256,384]{1,0:T(8,128)(2,1)} %dynamic-slice_bitcast_fusion.8), channel_id=1, source_target_pairs={{0,16},{16,0},{1,17},{17,1},{2,18},{18,2},{3,19},{19,3},{4,20},{20... | collective-permute-start | bytes 589832 | tf_op jit(solution)/shard_map/ppermute | solution.py:562
  524.3 21.4 %collective-permute-start.35 = (bf16[320,1024]{1,0:T(8,128)(2,1)}, bf16[320,1024]{1,0:T(8,128)(2,1)}, u32[]{:S(2)}, u32[]{:S(2)}) collective-permute-start(bf16[320,1024]{1,0:T(8,128)(2,1)} %get-tuple-element.169), channel_id=1, source_target_pairs={{4,2},{6,4},{5,3},{7,5},{12,10},{14,12},{13,11},{15,13},{20,18},{2... | collective-permute-start | bytes 1966088 | tf_op jit(solution)/shard_map/ppermute | solution.py:551
  525.8 19.9 %collective-permute-start.34 = (bf16[320,1024]{1,0:T(8,128)(2,1)}, bf16[320,1024]{1,0:T(8,128)(2,1)}, u32[]{:S(2)}, u32[]{:S(2)}) collective-permute-start(bf16[320,1024]{1,0:T(8,128)(2,1)} %get-tuple-element.170), channel_id=1, source_target_pairs={{0,2},{2,4},{1,3},{3,5},{8,10},{10,12},{9,11},{11,13},{16,18},{18,... | collective-permute-start | bytes 1966088 | tf_op jit(solution)/shard_map/ppermute | solution.py:551
  545.7 26.5 %copy-start.33 = (f32[14,32]{1,0:T(8,128)S(1)}, f32[14,32]{1,0:T(8,128)}, u32[]{:S(2)}) copy-start(f32[14,32]{1,0:T(8,128)} %param.27) | copy-start | bytes 5380
  545.7 26.5 %copy-start.48 = (f32[14,32]{1,0:T(8,128)S(1)}, f32[14,32]{1,0:T(8,128)}, u32[]{:S(2)}) copy-start(f32[14,32]{1,0:T(8,128)} %param.32) | copy-start | bytes 5380
  545.7 26.5 %copy-start.49 = (f32[14,32]{1,0:T(8,128)S(1)}, f32[14,32]{1,0:T(8,128)}, u32[]{:S(2)}) copy-start(f32[14,32]{1,0:T(8,128)} %param.37) | copy-start | bytes 5380
  560.7 12.8 %all-to-all-start.3 = ((bf16[8,32,384]{2,1,0:T(8,128)(2,1)}), bf16[8,32,384]{2,1,0:T(8,128)(2,1)}, u32[]{:S(2)}, u32[]{:S(2)}) async-start(bf16[8,32,384]{2,1,0:T(8,128)(2,1)} %bitcast.87), calls=%async_computation.3 | async-start | bytes 393216 | tf_op jit(solution)/shard_map/all_to_all | solution.py:826
  564.8 21.1 %collective-permute-start.39 = (bf16[320,1024]{1,0:T(8,128)(2,1)}, bf16[320,1024]{1,0:T(8,128)(2,1)}, u32[]{:S(2)}, u32[]{:S(2)}) collective-permute-start(bf16[320,1024]{1,0:T(8,128)(2,1)} %get-tuple-element.115), channel_id=1, source_target_pairs={{2,0},{4,2},{6,4},{3,1},{5,3},{7,5},{10,8},{12,10},{14,12},{11,9},... | collective-permute-start | bytes 1966088 | tf_op jit(solution)/shard_map/ppermute | solution.py:551
  566.1 19.8 %collective-permute-start.38 = (bf16[320,1024]{1,0:T(8,128)(2,1)}, bf16[320,1024]{1,0:T(8,128)(2,1)}, u32[]{:S(2)}, u32[]{:S(2)}) collective-permute-start(bf16[320,1024]{1,0:T(8,128)(2,1)} %get-tuple-element.114), channel_id=1, source_target_pairs={{0,2},{2,4},{4,6},{1,3},{3,5},{5,7},{8,10},{10,12},{12,14},{9,11},... | collective-permute-start | bytes 1966088 | tf_op jit(solution)/shard_map/ppermute | solution.py:551
  577.3 10.4 %copy-start.12 = (f32[128,1024]{1,0:T(8,128)S(1)}, f32[128,1024]{1,0:T(8,128)}, u32[]{:S(2)}) copy-start(f32[128,1024]{1,0:T(8,128)} %param.26) | copy-start | bytes 1572868
  577.3 10.4 %copy-start.22 = (f32[128,1024]{1,0:T(8,128)S(1)}, f32[128,1024]{1,0:T(8,128)}, u32[]{:S(2)}) copy-start(f32[128,1024]{1,0:T(8,128)} %param.31) | copy-start | bytes 1572868
  577.3 10.4 %copy-start.23 = (f32[128,1024]{1,0:T(8,128)S(1)}, f32[128,1024]{1,0:T(8,128)}, u32[]{:S(2)}) copy-start(f32[128,1024]{1,0:T(8,128)} %param.36) | copy-start | bytes 1572868
  587.6 1.5 collective-permute-start.40
  (40 other events, 122.9 us)
Sparse Core Ops, SparseCore 0:
  13.2 177.4 all-gather.5
  280.8 75.4 all-gather.3

commit v10 on v8

--- a/solution.py
+++ b/solution.py
@@ -475,6 +475,11 @@
     return lax.ppermute(value, "core", [(0, 1), (1, 0)])
 
 
+def line_pairs(size, sign, step):
+    pairs = [(i, i - sign) for i in range(size) if 0 <= i - sign < size]
+    return [(i, j) for i, j in pairs if 0 <= i + sign * (step - 1) < size]
+
+
 def line_pieces(value, axis):
     size = lax.axis_size(axis)
     if size == 2:
@@ -484,9 +489,7 @@
     for sign in (-1, 1):
         moving = value
         for step in range(1, size):
-            pairs = [(i, i - sign) for i in range(size) if 0 <= i - sign < size]
-            pairs = [(i, j) for i, j in pairs if 0 <= i + sign * (step - 1) < size]
-            moving = lax.ppermute(moving, axis, pairs)
+            moving = lax.ppermute(moving, axis, line_pairs(size, sign, step))
             pieces.append((sign * step, moving))
     return pieces
 
@@ -627,7 +630,7 @@
     folds = half // width
     up_end = 2 * share * folds
     low = lambda value: value.astype(jnp.bfloat16)
-    direct = share % 16 == 0 and unit_block == 128
+    direct = share % 16 == 0 and unit_block == 128 and line > 3
     position = lax.broadcasted_iota(jnp.int32, (images, rows), 1)
     found = (segment_ids[None, :] == lax.broadcasted_iota(jnp.int32, (images, rows), 0)) & (
         valid[None, :] == 1
@@ -644,8 +647,30 @@
         blocks = blocks.reshape(line, 2, share + extra, 3 * lanes)
         keep = jnp.where(first_core, blocks[:, 0], blocks[:, 1])
         sent = swap_cores(jnp.where(first_core, blocks[:, 1], blocks[:, 0]))
-        blocks = exchange_line(in_order(keep[:, None], sent[:, None], 1), "line")
-        blocks = gather_line(gather_line(blocks, "inner"), "outer")
+        blocks = in_order(keep[:, None], sent[:, None], 1)
+
+        pieces, swapped = [], []
+        moving = [tokens, tokens]
+        for step in range(1, line):
+            moving = [
+                lax.ppermute(value, "line", line_pairs(line, sign, step))
+                for sign, value in zip((-1, 1), moving)
+            ]
+            if step == 1:
+                blocks = exchange_line(blocks, "line")
+            elif step == 2:
+                blocks = gather_line(gather_line(blocks, "inner"), "outer")
+            moving, blocks, swapped = lax.optimization_barrier((moving, blocks, swapped))
+            pieces += [(sign * step, value) for sign, value in zip((-1, 1), moving)]
+            if step == line - 1:
+                packed = jnp.concatenate([fold(hidden_up), low(hidden_down), low(project_out)], axis=0)
+                packed, moving = lax.optimization_barrier((packed, moving))
+                gathered = lax.all_gather(packed, everyone, axis=0, tiled=False)
+            swapped = swapped + [swap_cores(value) for value in moving]
+        swapped = [(distance, value) for (distance, _), value in zip(pieces, swapped)]
+        whole_out = gathered[:, packed.shape[0] - share :].reshape(width, width)
+        mlp_weights = (gathered,)
+        whole_in = lax.all_gather(fold(project_in), everyone, axis=0, tiled=False)
         blocks = blocks.reshape(count, share + extra, 3 * lanes)
         mine_in = blocks[:, :share].reshape(width, 3 * lanes)
         small = blocks[:, share:].reshape(count, -1)
@@ -664,17 +689,10 @@
     offsets = lax.broadcasted_iota(jnp.int32, (group, images), 0) * rows
     starts = jnp.min(jnp.where(first < rows, first + offsets, length), axis=0)
 
-    pieces = line_pieces(tokens, "line")
-    if direct:
-        packed = jnp.concatenate([fold(hidden_up), low(hidden_down), low(project_out)], axis=0)
-        packed, pieces_in = lax.optimization_barrier((packed, tuple(piece for _, piece in pieces)))
-        pieces = [(distance, piece) for (distance, _), piece in zip(pieces, pieces_in)]
-        gathered = lax.all_gather(packed, everyone, axis=0, tiled=False)
-        whole_out = gathered[:, packed.shape[0] - share :].reshape(width, width)
-        mlp_weights = (gathered,)
-        whole_in = lax.all_gather(fold(project_in), everyone, axis=0, tiled=False)
+    if not direct:
+        pieces = line_pieces(tokens, "line")
+        swapped = [(distance, swap_cores(piece)) for distance, piece in pieces]
     own_tokens = line_order(tokens, pieces, "line").reshape(-1, width)
-    swapped = [(distance, swap_cores(piece)) for distance, piece in pieces]
     other_tokens = line_order(swap_cores(tokens), swapped, "line").reshape(-1, width)
 
     gain_one, shift_one, bias_query, bias_value, bias_out = (

time: 550 us -> 557 us (1.013)
  local copies, waits for them, and re-layouts: 51.7 us -> 58.9 us
    all_gather x1, waiting for transfers between devices: 0.01 us -> 63 us  [on_device(): gathered = lax.all_gather(packed, everyone, axis=0, tiled=False)]
    ppermute x6, waiting for transfers between devices: 67.5 us -> 27.5 us  [on_device(): lax.ppermute(value, 'line', line_pairs(line, sign, step))]
    all_to_all x1, waiting for transfers between devices: 21.9 us -> 0.01 us  [on_device(): lax.all_to_all(attended.reshape(group, rows, lanes), seq, split_axis=0, c...]
    ppermute x6, waiting for transfers between devices: 3.65 us -> 16.5 us  [exchange_line(): pieces.append((-move, lax.ppermute(pick(place + move), axis, pairs)))]
    ppermute x2, waiting for transfers between devices: 24.4 us -> 13.2 us  [line_pieces(): other = lax.ppermute(value, axis, [(0, 1), (1, 0)])]
    dynamic_update_slice x20 -> x19, local copies, waits for them, and re-layouts: 6.69 us -> 15.1 us  [line_order(): whole = lax.dynamic_update_index_in_dim(whole, piece, slot, 0)]
  transfers between devices with their start and end apart: 46 -> 46, of which waited for: 20 -> 18; matrix products, arithmetic and copies ran while one was open for 18% -> 19% of each run, Pallas kernels for 23% -> 23%
where the time goes in v10:
time: 557 us; the launch traced here: 547 us
  waiting for transfers between devices  194 us (35%)
  Pallas kernels  124 us (22%)
  starting transfers between devices  81.7 us (15%)
  local copies, waits for them, and re-layouts  58.9 us (11%)
  other arithmetic  50.2 us (9%)
  between operations  15.7 us (3%)
  matrix products  11.9 us (2%)
  blocking collectives  11.1 us (2%)
    all_gather x1, waiting for transfers between devices, on_device(): gathered = lax.all_gather(packed, everyone, axis=0, tiled=False)  63 us
    pallas_call x1, Pallas kernels, mlp(): pl.pallas_call(functools.partial(mlp_kernel, pieces), grid_spec=pltpu.Pre...  38 us
    pallas_call x1, Pallas kernels, attend_back(): pl.pallas_call(attend_back_kernel, grid_spec=pltpu.PrefetchScalarGridSpec...  34.8 us
    ppermute x6, waiting for transfers between devices, on_device(): lax.ppermute(value, 'line', line_pairs(line, sign, step))  27.5 us
    pallas_call x1, Pallas kernels, attend(): pl.pallas_call(attend_kernel, grid_spec=pltpu.PrefetchScalarGridSpec(num_...  26.2 us
    ppermute x4, waiting for transfers between devices, scatter_line(): lax.ppermute(pick(1 - place), axis, [(0, 1), (1, 0)])  24.4 us
    ppermute x3, waiting for transfers between devices, scatter_terms(): return (pick(place), lax.ppermute(pick(1 - place), axis, [(0, 1), (1, 0)]))  20.3 us
    ppermute x6, starting transfers between devices, exchange_line(): pieces.append((-move, lax.ppermute(pick(place + move), axis, pairs)))  18.7 us
  transfers between devices with their start and end apart: 46, of which 18 were waited for; matrix products, arithmetic and copies ran while one was open for 19% of the time, Pallas kernels for 23%

profile of v10, /device:TPU:0, one launch (start us, length us, event | category | flops | bytes accessed | tf_op | source)
XLA Modules:
  0.0 546.9 jit_solution(12333386910924514855)
XLA Ops:
  14.1 5.2 collective-permute-start
  20.6 7.2 %collective-permute-start.4 = (bf16[2,48,384]{2,1,0:T(8,128)(2,1)S(1)}, bf16[2,48,384]{2,1,0:T(8,128)(2,1)S(1)}, u32[]{:S(2)}, u32[]{:S(2)}) collective-permute-start(bf16[2,48,384]{2,1,0:T(8,128)(2,1)S(1)} %get-tuple-element.191), channel_id=1, source_target_pairs={{0,6},{1,7},{8,14},{9,15},{16,22},{17,23},{24,30},{25,31}} | collective-permute-start | bytes 221192 | tf_op jit(solution)/shard_map/ppermute | solution.py:524
  29.2 5.4 collective-permute-start.6
  34.7 8.8 %collective-permute-done.4 = bf16[2,48,384]{2,1,0:T(8,128)(2,1)S(1)} collective-permute-done((bf16[2,48,384]{2,1,0:T(8,128)(2,1)S(1)}, bf16[2,48,384]{2,1,0:T(8,128)(2,1)S(1)}, u32[]{:S(2)}, u32[]{:S(2)}) %collective-permute-start.4) | collective-permute-done | bytes 73760 | tf_op jit(solution)/shard_map/ppermute | solution.py:524
  44.8 5.8 %collective-permute-done.5 = bf16[2,48,384]{2,1,0:T(8,128)(2,1)S(1)} collective-permute-done((bf16[2,48,384]{2,1,0:T(8,128)(2,1)S(1)}, bf16[2,48,384]{2,1,0:T(8,128)(2,1)S(1)}, u32[]{:S(2)}, u32[]{:S(2)}) %collective-permute-start.5) | collective-permute-done | bytes 73760 | tf_op jit(solution)/shard_map/ppermute | solution.py:524
  50.6 2.2 collective-permute-start.8
  52.9 1.9 collective-permute-done.8
  54.8 2.1 collective-permute-start.11
  56.9 1.7 collective-permute-start.9
  61.8 2.1 collective-permute-start.12
  64.0 12.0 %collective-permute-done.12 = bf16[2,4,2,48,384]{4,3,2,1,0:T(8,128)(2,1)S(1)} collective-permute-done((bf16[2,4,2,48,384]{4,3,2,1,0:T(8,128)(2,1)S(1)}, bf16[2,4,2,48,384]{4,3,2,1,0:T(8,128)(2,1)S(1)}, u32[]{:S(2)}, u32[]{:S(2)}) %collective-permute-start.12) | collective-permute-done | bytes 589856 | tf_op jit(solution)/shard_map/ppermute | solution.py:486
  76.3 7.6 %collective-permute-done.10 = bf16[512,1024]{1,0:T(8,128)(2,1)} collective-permute-done((bf16[512,1024]{1,0:T(8,128)(2,1)}, bf16[512,1024]{1,0:T(8,128)(2,1)}, u32[]{:S(2)}, u32[]{:S(2)}) %collective-permute-start.10) | collective-permute-done | bytes 1048608 | tf_op jit(solution)/shard_map/ppermute | solution.py:656
  83.9 1.7 collective-permute-start.15
  88.5 19.8 %collective-permute-done.16 = bf16[512,1024]{1,0:T(8,128)(2,1)} collective-permute-done((bf16[512,1024]{1,0:T(8,128)(2,1)}, bf16[512,1024]{1,0:T(8,128)(2,1)}, u32[]{:S(2)}, u32[]{:S(2)}) %collective-permute-start.16) | collective-permute-done | bytes 1048608 | tf_op jit(solution)/shard_map/ppermute | solution.py:656
  124.5 1.8 bitcast_dynamic-update-slice_fusion.3
  129.1 2.1 bitcast_dynamic-update-slice_fusion.2
  132.7 2.0 copy-done.5
  134.7 14.2 %norm_mix.1 = (bf16[4096,1024]{1,0:T(8,128)(2,1)}, bf16[4096,128]{1,0:T(8,128)(2,1)}, bf16[4096,128]{1,0:T(8,128)(2,1)}, bf16[4096,128]{1,0:T(8,128)(2,1)}) custom-call(s32[1]{0:T(128)} %bitcast.28.place_ref, bf16[2048,1024]{1,0:T(8,128)(2,1)} %bitcast.266, bf16[2048,1024]{1,0:T(8,128)(2,1)} %bitcast.265, f32[1,1024]{1,0:T(1,128)} %slice.133.gain_ref, ...), custom_call_target="tpu_custom_call" | custom-call | flops 3221225472 | bytes 16777216 | tf_op jit(solution)/shard_map/norm_mix/pallas_call | solution.py:243
  148.8 26.2 %attend_forward.1 = (f32[4096,128]{1,0:T(8,128)}, bf16[4096,128]{1,0:T(8,128)(2,1)}, f32[4096,128]{1,0:T(8,128)}) custom-call(s32[2]{0:T(128)} %select_reduce_fusion.starts_ref, bf16[4096,128]{1,0:T(8,128)(2,1)} %get-tuple-element.89.q_ref, bf16[4096,128]{1,0:T(8,128)(2,1)} %get-tuple-element.90.k_ref, bf16[4096,128]{1,0:T(8,128)(2,1)} %get-tuple-element.91.v_ref), custom_call_target="tpu_custom_call" | custom-call | flops 4060086272 | bytes 8388608 | tf_op jit(solution)/shard_map/attend_forward/pallas_call | solution.py:116
  175.0 2.3 copy.126
  177.4 3.7 all-to-all-start
  184.9 1.9 convert_reduce_fusion
  187.4 63.0 %all-gather.6.cloned.1.call-done = bf16[9216,1024]{1,0:T(8,128)(2,1)} async-done(((bf16[288,1024]{1,0:T(8,128)(2,1)}), bf16[9216,1024]{1,0:T(8,128)(2,1)}) %all-gather.6.cloned.1.call-update) | async-done | bytes 18874384 | tf_op jit(solution)/shard_map/all_gather | solution.py:668
  250.3 3.3 slice.174
  254.6 4.9 fusion.78
  263.6 1.5 reshape.387
  266.4 38.0 %mlp_both_ways.1 = (bf16[16,128,1024]{2,1,0:T(8,128)(2,1)}, bf16[16,128,1024]{2,1,0:T(8,128)(2,1)}, f32[512,1024]{1,0:T(8,128)}, f32[512,1024]{1,0:T(8,128)}, f3...) custom-call(s32[1]{0:T(128)} %bitcast.55.core_ref, bf16[512,1024]{1,0:T(8,128)(2,1)} %add_convert_fusion.4.own_ref, ...), custom_call_target="tpu_custom_call" | custom-call | flops 25769803776 | bytes 29360128 | tf_op jit(solution)/shard_map/mlp_both_ways/pallas_call | solution.py:353
  306.4 2.6 collective-permute-done.26
  309.0 3.8 multiply_reduce_fusion.1
  312.9 4.2 multiply_reduce_fusion
  323.2 4.4 all-to-all-start.1
  330.0 1.5 collective-permute-start.27
  331.5 4.3 dynamic-slice_bitcast_fusion.2
  336.4 2.5 dynamic-slice_bitcast_fusion
  338.9 1.5 collective-permute-start.28
  340.3 16.0 %collective-permute-done.27 = bf16[2,4,64,1024]{3,2,1,0:T(8,128)(2,1)} collective-permute-done((bf16[2,4,64,1024]{3,2,1,0:T(8,128)(2,1)}, bf16[2,4,64,1024]{3,2,1,0:T(8,128)(2,1)}, u32[]{:S(2)}, u32[]{:S(2)}) %collective-permute-start.27) | collective-permute-done | bytes 1048608 | tf_op jit(solution)/shard_map/ppermute | solution.py:539
  356.3 34.8 %attend_backward.1 = bf16[4096,384]{1,0:T(8,128)(2,1)} custom-call(s32[2]{0:T(128)} %select_reduce_fusion.starts_ref, bf16[4096,128]{1,0:T(8,128)(2,1)} %get-tuple-element.89.q_ref, bf16[4096,128]{1,0:T(8,128)(2,1)} %get-tuple-element.90.k_ref, bf16[4096,128]{1,0:T(8,128)(2,1)} %get-tuple-element.91.v_ref, f32[4096,128]{1,0:T(8,128)} %get-tuple-element.102.wide_ref, ...), custom_call_target="tpu_custom_call" | custom-call | flops 10150215680 | bytes 11534336 | tf_op jit(solution)/shard_map/attend_backward/pallas_call | solution.py:196
  391.1 5.4 all-to-all-start.2
  396.4 4.3 collective-permute-done.25
  400.8 1.8 add_convert_fusion.2
  402.6 2.6 add_convert_fusion.1
  405.3 1.5 collective-permute-start.29
  406.8 2.8 add_convert_fusion
  409.7 1.5 collective-permute-start.30
  411.3 4.5 convolution_convert_fusion.2
  416.5 19.4 %collective-permute-done.30 = bf16[4,128,1024]{2,1,0:T(8,128)(2,1)S(1)} collective-permute-done((bf16[4,128,1024]{2,1,0:T(8,128)(2,1)S(1)}, bf16[4,128,1024]{2,1,0:T(8,128)(2,1)S(1)}, u32[]{:S(2)}, u32[]{:S(2)}) %collective-permute-start.30) | collective-permute-done | bytes 1048608 | tf_op jit(solution)/shard_map/ppermute | solution.py:571
  436.3 5.0 collective-permute-done.29
  443.2 4.1 collective-permute-start.31
  447.3 1.5 collective-permute-start.32
  450.8 1.5 collective-permute-start.36
  452.3 9.9 %collective-permute-done.31 = bf16[320,1024]{1,0:T(8,128)(2,1)} collective-permute-done((bf16[320,1024]{1,0:T(8,128)(2,1)}, bf16[320,1024]{1,0:T(8,128)(2,1)}, u32[]{:S(2)}, u32[]{:S(2)}) %collective-permute-start.31) | collective-permute-done | bytes 655392 | tf_op jit(solution)/shard_map/ppermute | solution.py:560
  462.2 5.8 %all-to-all-done.2.grad_ref = bf16[8,512,384]{2,1,0:T(8,128)(2,1)} async-done(((bf16[8,512,384]{2,1,0:T(8,128)(2,1)}), bf16[8,512,384]{2,1,0:T(8,128)(2,1)}, u32[]{:S(2)}, u32[]{:S(2)}) %all-to-all-start.2) | async-done | bytes 3145760 | tf_op jit(solution)/shard_map/all_to_all | solution.py:790
  468.0 2.9 fusion.9
  470.9 1.5 collective-permute-start.34
  472.4 2.1 collective-permute-start.33
  477.1 1.7 fusion.33
  478.8 10.8 %finish_input.1 = (f32[512,1024]{1,0:T(8,128)}, f32[1,1024]{1,0:T(1,128)}, f32[1,1024]{1,0:T(1,128)}, f32[3,1,1024]{2,1,0:T(1,128)}) custom-call(bf16[8,512,384]{2,1,0:T(8,128)(2,1)} %all-to-all-done.2.grad_ref, bf16[32,96,1024]{2,1,0:T(8,128)(2,1)} %all-gather.4.cloned.1.call-done.weight_ref, bf16[512,1024]{1,0:T(8,128)(2,1)} %x_ref.1, ...), custom_call_target="tpu_custom_call" | custom-call | flops 3221225472 | bytes 16777216 | tf_op jit(solution)/shard_map/finish_input/pallas_call | solution.py:443
  492.4 3.0 fusion.10
  496.6 11.1 %all_to_all.30 = f32[32,1,448]{2,1,0:T(1,128)S(1)} all-to-all(f32[32,1,448]{2,1,0:T(1,128)S(1)} %all_to_all.24), channel_id=1, replica_groups=mesh['outer'=2,'inner'=2,'line'=4,'core'=2] {'outer','inner','line','core'}, dimensions={0} | all-to-all | bytes 114688 | tf_op jit(solution)/shard_map/all_to_all | solution.py:844
  507.7 4.0 all-to-all-start.3
  513.0 5.4 collective-permute-start.37
  521.8 2.4 multiply_subtract_fusion.2
  524.2 8.6 %collective-permute-done.38 = bf16[320,1024]{1,0:T(8,128)(2,1)} collective-permute-done((bf16[320,1024]{1,0:T(8,128)(2,1)}, bf16[320,1024]{1,0:T(8,128)(2,1)}, u32[]{:S(2)}, u32[]{:S(2)}) %collective-permute-start.38) | collective-permute-done | bytes 655392 | tf_op jit(solution)/shard_map/ppermute | solution.py:560
  532.8 1.6 fusion.8
  (314 shorter events, 80.6 us)
Async XLA Ops:
  7.2 243.1 %all-gather.6.cloned.1.call-start = ((), (), s32[]{:S(2)}) async-start(), calls=%async_computation.6 | async-start | bytes 19464192 | tf_op jit(solution)/shard_map/all_gather | solution.py:668
  11.2 1.5 collective-permute-start.2
  12.8 16.3 %collective-permute-start.3 = (bf16[2,48,384]{2,1,0:T(8,128)(2,1)S(1)}, bf16[2,48,384]{2,1,0:T(8,128)(2,1)S(1)}, u32[]{:S(2)}, u32[]{:S(2)}) collective-permute-start(bf16[2,48,384]{2,1,0:T(8,128)(2,1)S(1)} %get-tuple-element.190), channel_id=1, source_target_pairs={{6,0},{7,1},{14,8},{15,9},{22,16},{23,17},{30,24},{31,25}} | collective-permute-start | bytes 221192 | tf_op jit(solution)/shard_map/ppermute | solution.py:524
  14.1 40.7 %collective-permute-start = (bf16[512,1024]{1,0:T(8,128)(2,1)S(1)}, bf16[512,1024]{1,0:T(8,128)(2,1)}, u32[]{:S(2)}, u32[]{:S(2)}) collective-permute-start(bf16[512,1024]{1,0:T(8,128)(2,1)S(1)} %copy-done.3), channel_id=1, source_target_pairs={{0,2},{2,4},{4,6},{1,3},{3,5},{5,7},{8,10},{10,12},{12,14},{9,11},... | collective-permute-start | bytes 3145736 | tf_op jit(solution)/shard_map/ppermute | solution.py:656
  19.3 35.5 %collective-permute-start.1 = (bf16[512,1024]{1,0:T(8,128)(2,1)S(1)}, bf16[512,1024]{1,0:T(8,128)(2,1)}, u32[]{:S(2)}, u32[]{:S(2)}) collective-permute-start(bf16[512,1024]{1,0:T(8,128)(2,1)S(1)} %copy-done.3), channel_id=1, source_target_pairs={{2,0},{4,2},{6,4},{3,1},{5,3},{7,5},{10,8},{12,10},{14,12},{11,9},... | collective-permute-start | bytes 3145736 | tf_op jit(solution)/shard_map/ppermute | solution.py:656
  20.6 22.9 %collective-permute-start.4 = (bf16[2,48,384]{2,1,0:T(8,128)(2,1)S(1)}, bf16[2,48,384]{2,1,0:T(8,128)(2,1)S(1)}, u32[]{:S(2)}, u32[]{:S(2)}) collective-permute-start(bf16[2,48,384]{2,1,0:T(8,128)(2,1)S(1)} %get-tuple-element.191), channel_id=1, source_target_pairs={{0,6},{1,7},{8,14},{9,15},{16,22},{17,23},{24,30},{25,31}} | collective-permute-start | bytes 221192 | tf_op jit(solution)/shard_map/ppermute | solution.py:524
  27.8 22.8 %collective-permute-start.5 = (bf16[2,48,384]{2,1,0:T(8,128)(2,1)S(1)}, bf16[2,48,384]{2,1,0:T(8,128)(2,1)S(1)}, u32[]{:S(2)}, u32[]{:S(2)}) collective-permute-start(bf16[2,48,384]{2,1,0:T(8,128)(2,1)S(1)} %get-tuple-element.192), channel_id=1, source_target_pairs={{4,0},{6,2},{5,1},{7,3},{12,8},{14,10},{13,9},{15,11},{20,16},{22,... | collective-permute-start | bytes 221192 | tf_op jit(solution)/shard_map/ppermute | solution.py:524
  29.2 23.7 %collective-permute-start.6 = (bf16[2,48,384]{2,1,0:T(8,128)(2,1)S(1)}, bf16[2,48,384]{2,1,0:T(8,128)(2,1)S(1)}, u32[]{:S(2)}, u32[]{:S(2)}) collective-permute-start(bf16[2,48,384]{2,1,0:T(8,128)(2,1)S(1)} %get-tuple-element.193), channel_id=1, source_target_pairs={{0,4},{2,6},{1,5},{3,7},{8,12},{10,14},{9,13},{11,15},{16,20},{18,... | collective-permute-start | bytes 221192 | tf_op jit(solution)/shard_map/ppermute | solution.py:524
  43.5 9.4 %collective-permute-start.7 = (bf16[2,48,384]{2,1,0:T(8,128)(2,1)S(1)}, bf16[2,48,384]{2,1,0:T(8,128)(2,1)S(1)}, u32[]{:S(2)}, u32[]{:S(2)}) collective-permute-start(bf16[2,48,384]{2,1,0:T(8,128)(2,1)S(1)} %get-tuple-element.194), channel_id=1, source_target_pairs={{2,0},{4,2},{6,4},{3,1},{5,3},{7,5},{10,8},{12,10},{14,12},{11,9},... | collective-permute-start | bytes 221192 | tf_op jit(solution)/shard_map/ppermute | solution.py:524
  50.6 4.1 collective-permute-start.8
  54.8 6.8 %collective-permute-start.11 = (bf16[4,2,48,384]{3,2,1,0:T(8,128)(2,1)S(1)}, bf16[4,2,48,384]{3,2,1,0:T(8,128)(2,1)S(1)}, u32[]{:S(2)}, u32[]{:S(2)}) collective-permute-start(bf16[4,2,48,384]{3,2,1,0:T(8,128)(2,1)S(1)} %fusion.42), channel_id=1, source_target_pairs={{0,8},{8,0},{1,9},{9,1},{2,10},{10,2},{3,11},{11,3},{4,12},{12,4},... | collective-permute-start | bytes 884744 | tf_op jit(solution)/shard_map/ppermute | solution.py:486
  56.9 19.3 %collective-permute-start.9 = (bf16[512,1024]{1,0:T(8,128)(2,1)}, bf16[512,1024]{1,0:T(8,128)(2,1)}, u32[]{:S(2)}, u32[]{:S(2)}) collective-permute-start(bf16[512,1024]{1,0:T(8,128)(2,1)} %collective-permute-done), channel_id=1, source_target_pairs={{2,4},{4,6},{3,5},{5,7},{10,12},{12,14},{11,13},{13,15},{18,20},{2... | collective-permute-start | bytes 3145736 | tf_op jit(solution)/shard_map/ppermute | solution.py:656
  58.7 25.2 %collective-permute-start.10 = (bf16[512,1024]{1,0:T(8,128)(2,1)}, bf16[512,1024]{1,0:T(8,128)(2,1)}, u32[]{:S(2)}, u32[]{:S(2)}) collective-permute-start(bf16[512,1024]{1,0:T(8,128)(2,1)} %collective-permute-done.1), channel_id=1, source_target_pairs={{2,0},{4,2},{3,1},{5,3},{10,8},{12,10},{11,9},{13,11},{18,16},{20,... | collective-permute-start | bytes 3145736 | tf_op jit(solution)/shard_map/ppermute | solution.py:656
  59.9 23.9 %collective-permute-start.13 = (bf16[512,1024]{1,0:T(8,128)(2,1)}, bf16[512,1024]{1,0:T(8,128)(2,1)}, u32[]{:S(2)}, u32[]{:S(2)}) collective-permute-start(bf16[512,1024]{1,0:T(8,128)(2,1)} %collective-permute-done), channel_id=1, source_target_pairs={{0,1},{1,0},{2,3},{3,2},{4,5},{5,4},{6,7},{7,6},{8,9},{9,8},{10,11... | collective-permute-start | bytes 3145736 | tf_op jit(solution)/shard_map/ppermute | solution.py:475
  60.0 23.9 %collective-permute-start.14 = (bf16[512,1024]{1,0:T(8,128)(2,1)}, bf16[512,1024]{1,0:T(8,128)(2,1)}, u32[]{:S(2)}, u32[]{:S(2)}) collective-permute-start(bf16[512,1024]{1,0:T(8,128)(2,1)} %collective-permute-done.1), channel_id=1, source_target_pairs={{0,1},{1,0},{2,3},{3,2},{4,5},{5,4},{6,7},{7,6},{8,9},{9,8},{10,11... | collective-permute-start | bytes 3145736 | tf_op jit(solution)/shard_map/ppermute | solution.py:475
  61.6 25.8 %copy-start.22 = (f32[32,1024]{1,0:T(8,128)S(1)}, f32[32,1024]{1,0:T(8,128)}, u32[]{:S(2)}) copy-start(f32[32,1024]{1,0:T(8,128)} %param.24) | copy-start | bytes 393220
  61.7 25.7 %copy-start.12 = (f32[128,1024]{1,0:T(8,128)S(1)}, f32[128,1024]{1,0:T(8,128)}, u32[]{:S(2)}) copy-start(f32[128,1024]{1,0:T(8,128)} %param.26) | copy-start | bytes 1572868
  61.8 14.3 %collective-permute-start.12 = (bf16[2,4,2,48,384]{4,3,2,1,0:T(8,128)(2,1)S(1)}, bf16[2,4,2,48,384]{4,3,2,1,0:T(8,128)(2,1)S(1)}, u32[]{:S(2)}, u32[]{:S(2)}) collective-permute-start(bf16[2,4,2,48,384]{4,3,2,1,0:T(8,128)(2,1)S(1)} %maximum_select_fusion.2), channel_id=1, source_target_pairs={{0,16},{16,0},{1,17},{17,1},{2,18},{18,2},{3,19},{19,3},{4,20},{20... | collective-permute-start | bytes 1769480 | tf_op jit(solution)/shard_map/ppermute | solution.py:486
  63.9 23.7 %copy-start.9 = (f32[32,4096]{1,0:T(8,128)S(1)}, f32[32,4096]{1,0:T(8,128)}, u32[]{:S(2)}) copy-start(f32[32,4096]{1,0:T(8,128)} %param.25) | copy-start | bytes 1572868
  83.9 4.6 collective-permute-start.15
  85.6 22.7 %collective-permute-start.16 = (bf16[512,1024]{1,0:T(8,128)(2,1)}, bf16[512,1024]{1,0:T(8,128)(2,1)}, u32[]{:S(2)}, u32[]{:S(2)}) collective-permute-start(bf16[512,1024]{1,0:T(8,128)(2,1)} %collective-permute-done.10), channel_id=1, source_target_pairs={{2,0},{3,1},{10,8},{11,9},{18,16},{19,17},{26,24},{27,25}} | collective-permute-start | bytes 3145736 | tf_op jit(solution)/shard_map/ppermute | solution.py:656
  86.9 21.4 %collective-permute-start.17 = (bf16[512,1024]{1,0:T(8,128)(2,1)}, bf16[512,1024]{1,0:T(8,128)(2,1)}, u32[]{:S(2)}, u32[]{:S(2)}) collective-permute-start(bf16[512,1024]{1,0:T(8,128)(2,1)} %collective-permute-done.9), channel_id=1, source_target_pairs={{0,1},{1,0},{2,3},{3,2},{4,5},{5,4},{6,7},{7,6},{8,9},{9,8},{10,11... | collective-permute-start | bytes 3145736 | tf_op jit(solution)/shard_map/ppermute | solution.py:475
  87.0 21.3 %collective-permute-start.18 = (bf16[512,1024]{1,0:T(8,128)(2,1)}, bf16[512,1024]{1,0:T(8,128)(2,1)}, u32[]{:S(2)}, u32[]{:S(2)}) collective-permute-start(bf16[512,1024]{1,0:T(8,128)(2,1)} %collective-permute-done.10), channel_id=1, source_target_pairs={{0,1},{1,0},{2,3},{3,2},{4,5},{5,4},{6,7},{7,6},{8,9},{9,8},{10,11... | collective-permute-start | bytes 3145736 | tf_op jit(solution)/shard_map/ppermute | solution.py:475
  108.3 24.3 %collective-permute-start.21 = (bf16[512,1024]{1,0:T(8,128)(2,1)S(1)}, bf16[512,1024]{1,0:T(8,128)(2,1)S(1)}, u32[]{:S(2)}, u32[]{:S(2)}) collective-permute-start(bf16[512,1024]{1,0:T(8,128)(2,1)S(1)} %copy-done.3), channel_id=1, source_target_pairs={{0,1},{1,0},{2,3},{3,2},{4,5},{5,4},{6,7},{7,6},{8,9},{9,8},{10,11... | collective-permute-start | bytes 3145736 | tf_op jit(solution)/shard_map/ppermute | solution.py:475
  110.8 10.3 %collective-permute-start.19 = (bf16[512,1024]{1,0:T(8,128)(2,1)}, bf16[512,1024]{1,0:T(8,128)(2,1)}, u32[]{:S(2)}, u32[]{:S(2)}) collective-permute-start(bf16[512,1024]{1,0:T(8,128)(2,1)} %collective-permute-done.15), channel_id=1, source_target_pairs={{0,1},{1,0},{2,3},{3,2},{4,5},{5,4},{6,7},{7,6},{8,9},{9,8},{10,11... | collective-permute-start | bytes 3145736 | tf_op jit(solution)/shard_map/ppermute | solution.py:475
  111.2 11.7 %collective-permute-start.20 = (bf16[512,1024]{1,0:T(8,128)(2,1)}, bf16[512,1024]{1,0:T(8,128)(2,1)S(1)}, u32[]{:S(2)}, u32[]{:S(2)}) collective-permute-start(bf16[512,1024]{1,0:T(8,128)(2,1)} %collective-permute-done.16), channel_id=1, source_target_pairs={{0,1},{1,0},{2,3},{3,2},{4,5},{5,4},{6,7},{7,6},{8,9},{9,8},{10,11... | collective-permute-start | bytes 3145736 | tf_op jit(solution)/shard_map/ppermute | solution.py:475
  177.3 7.5 %copy-start.29 = (f32[32,32]{1,0:T(8,128)S(1)}, f32[32,32]{1,0:T(8,128)}, u32[]{:S(2)}) copy-start(f32[32,32]{1,0:T(8,128)} %get-tuple-element.132) | copy-start | bytes 12292
  177.4 7.5 %copy-start.1 = (bf16[512,1024]{1,0:T(8,128)(2,1)S(1)}, bf16[512,1024]{1,0:T(8,128)(2,1)}, u32[]{:S(2)}) copy-start(bf16[512,1024]{1,0:T(8,128)(2,1)} %param.20) | copy-start | bytes 3145732
  177.4 76.2 %all-to-all-start = ((bf16[8,512,128]{1,2,0:T(8,128)(2,1)}), bf16[8,512,128]{1,2,0:T(8,128)(2,1)S(1)}, u32[]{:S(2)}, u32[]{:S(2)}) async-start(bf16[8,512,128]{1,2,0:T(8,128)(2,1)} %copy.126), calls=%async_computation | async-start | bytes 2097152 | tf_op jit(solution)/shard_map/all_to_all | solution.py:739
  181.1 159.2 %all-gather.4.cloned.1.call-start = ((), (), s32[]{:S(2)}) async-start(), calls=%async_computation.5 | async-start | bytes 6488064 | tf_op jit(solution)/shard_map/all_gather | solution.py:673
  182.7 70.8 %copy-start.35 = (f32[512]{0:T(512)}, f32[512]{0:T(512)S(1)}, u32[]{:S(2)}) copy-start(f32[512]{0:T(512)S(1)} %convert_element_type.246) | copy-start | bytes 6148
  186.8 79.6 %collective-permute-start.23 = (bf16[512,1024]{1,0:T(8,128)(2,1)}, bf16[512,1024]{1,0:T(8,128)(2,1)}, u32[]{:S(2)}, u32[]{:S(2)}) collective-permute-start(bf16[512,1024]{1,0:T(8,128)(2,1)} %get-tuple-element.145.gm_own_ref), channel_id=1, source_target_pairs={{0,1},{1,0},{2,3},{3,2},{4,5},{5,4},{6,7},{7,6},{8,9},{9,8},{10,11... | collective-permute-start | bytes 3145736 | tf_op jit(solution)/shard_map/ppermute | solution.py:475
  261.8 4.7 collective-permute-start.22
  304.4 4.6 collective-permute-start.26
  304.7 8.1 %collective-permute-start.24 = (f32[512,1024]{1,0:T(8,128)}, f32[512,1024]{1,0:T(8,128)}, u32[]{:S(2)}, u32[]{:S(2)}) collective-permute-start(f32[512,1024]{1,0:T(8,128)} %get-tuple-element.95), channel_id=1, source_target_pairs={{0,1},{1,0},{2,3},{3,2},{4,5},{5,4},{6,7},{7,6},{8,9},{9,8},{10,11... | collective-permute-start | bytes 6291464 | tf_op jit(solution)/shard_map/ppermute | solution.py:475
  323.2 33.1 %all-to-all-start.1 = ((bf16[8,512,128]{2,1,0:T(8,128)(2,1)}), bf16[8,512,128]{2,1,0:T(8,128)(2,1)}, u32[]{:S(2)}, u32[]{:S(2)}) async-start(bf16[8,512,128]{2,1,0:T(8,128)(2,1)} %bitcast.258), calls=%async_computation.1 | async-start | bytes 2097152 | tf_op jit(solution)/shard_map/all_to_all | solution.py:769
  330.0 26.3 %collective-permute-start.27 = (bf16[2,4,64,1024]{3,2,1,0:T(8,128)(2,1)}, bf16[2,4,64,1024]{3,2,1,0:T(8,128)(2,1)}, u32[]{:S(2)}, u32[]{:S(2)}) collective-permute-start(bf16[2,4,64,1024]{3,2,1,0:T(8,128)(2,1)} %get-tuple-element.181), channel_id=1, source_target_pairs={{0,8},{8,0},{1,9},{9,1},{2,10},{10,2},{3,11},{11,3},{4,12},{12,4},... | collective-permute-start | bytes 3145736 | tf_op jit(solution)/shard_map/ppermute | solution.py:539
  335.8 64.9 %collective-permute-start.25 = (bf16[2,4,128,1024]{3,2,1,0:T(8,128)(2,1)}, bf16[2,4,128,1024]{3,2,1,0:T(8,128)(2,1)}, u32[]{:S(2)}, u32[]{:S(2)}) collective-permute-start(bf16[2,4,128,1024]{3,2,1,0:T(8,128)(2,1)} %get-tuple-element.171), channel_id=1, source_target_pairs={{0,8},{8,0},{1,9},{9,1},{2,10},{10,2},{3,11},{11,3},{4,12},{12,4},... | collective-permute-start | bytes 6291464 | tf_op jit(solution)/shard_map/ppermute | solution.py:539
  338.9 61.9 %collective-permute-start.28 = (bf16[2,4,128,1024]{3,2,1,0:T(8,128)(2,1)}, bf16[2,4,128,1024]{3,2,1,0:T(8,128)(2,1)}, u32[]{:S(2)}, u32[]{:S(2)}) collective-permute-start(bf16[2,4,128,1024]{3,2,1,0:T(8,128)(2,1)} %get-tuple-element.169), channel_id=1, source_target_pairs={{0,16},{16,0},{1,17},{17,1},{2,18},{18,2},{3,19},{19,3},{4,20},{20... | collective-permute-start | bytes 6291464 | tf_op jit(solution)/shard_map/ppermute | solution.py:539
  391.1 77.0 %all-to-all-start.2 = ((bf16[8,512,384]{2,1,0:T(8,128)(2,1)}), bf16[8,512,384]{2,1,0:T(8,128)(2,1)}, u32[]{:S(2)}, u32[]{:S(2)}) async-start(bf16[8,512,384]{2,1,0:T(8,128)(2,1)} %bitcast.267), calls=%async_computation.2 | async-start | bytes 6291456 | tf_op jit(solution)/shard_map/all_to_all | solution.py:790
  400.8 10.5 %slice-start = ((s8[8388608]{0:T(1024)(128)(4,1)}), s8[4194304]{0:T(1024)(128)(4,1)S(1)}, s32[]{:S(2)}) async-start(s8[8388608]{0:T(1024)(128)(4,1)} %bitcast.304), calls=%async_computation.7 | async-start | bytes 8388608
  405.3 36.0 %collective-permute-start.29 = (bf16[4,192,1024]{2,1,0:T(8,128)(2,1)S(1)}, bf16[4,192,1024]{2,1,0:T(8,128)(2,1)S(1)}, u32[]{:S(2)}, u32[]{:S(2)}) collective-permute-start(bf16[4,192,1024]{2,1,0:T(8,128)(2,1)S(1)} %fusion.3), channel_id=1, source_target_pairs={{0,16},{16,0},{1,17},{17,1},{2,18},{18,2},{3,19},{19,3},{4,20},{20... | collective-permute-start | bytes 4718600 | tf_op jit(solution)/shard_map/ppermute | solution.py:571
  409.7 26.1 %collective-permute-start.30 = (bf16[4,128,1024]{2,1,0:T(8,128)(2,1)S(1)}, bf16[4,128,1024]{2,1,0:T(8,128)(2,1)S(1)}, u32[]{:S(2)}, u32[]{:S(2)}) collective-permute-start(bf16[4,128,1024]{2,1,0:T(8,128)(2,1)S(1)} %dynamic-slice_bitcast_fusion.4), channel_id=1, source_target_pairs={{0,8},{8,0},{1,9},{9,1},{2,10},{10,2},{3,11},{11,3},{4,12},{12,4},... | collective-permute-start | bytes 3145736 | tf_op jit(solution)/shard_map/ppermute | solution.py:571
  415.8 26.3 %copy-start.19 = (bf16[1024,384]{1,0:T(8,128)(2,1)}, bf16[1024,384]{1,0:T(8,128)(2,1)S(1)}, u32[]{:S(2)}) copy-start(bf16[1024,384]{1,0:T(8,128)(2,1)S(1)} %convolution_convert_fusion.2) | copy-start | bytes 2359300
  415.8 33.0 %collective-permute-start.35 = (bf16[2,256,384]{2,1,0:T(8,128)(2,1)S(1)}, bf16[2,256,384]{2,1,0:T(8,128)(2,1)}, u32[]{:S(2)}, u32[]{:S(2)}) collective-permute-start(bf16[2,256,384]{2,1,0:T(8,128)(2,1)S(1)} %dynamic-slice_bitcast_fusion.7), channel_id=1, source_target_pairs={{0,8},{8,0},{1,9},{9,1},{2,10},{10,2},{3,11},{11,3},{4,12},{12,4},... | collective-permute-start | bytes 1179656 | tf_op jit(solution)/shard_map/ppermute | solution.py:571
  443.2 19.0 %collective-permute-start.31 = (bf16[320,1024]{1,0:T(8,128)(2,1)}, bf16[320,1024]{1,0:T(8,128)(2,1)}, u32[]{:S(2)}, u32[]{:S(2)}) collective-permute-start(bf16[320,1024]{1,0:T(8,128)(2,1)} %get-tuple-element.178), channel_id=1, source_target_pairs={{0,2},{1,3},{8,10},{9,11},{16,18},{17,19},{24,26},{25,27}} | collective-permute-start | bytes 1966088 | tf_op jit(solution)/shard_map/ppermute | solution.py:560
  447.3 14.9 %collective-permute-start.32 = (bf16[320,1024]{1,0:T(8,128)(2,1)}, bf16[320,1024]{1,0:T(8,128)(2,1)}, u32[]{:S(2)}, u32[]{:S(2)}) collective-permute-start(bf16[320,1024]{1,0:T(8,128)(2,1)} %get-tuple-element.177), channel_id=1, source_target_pairs={{6,4},{7,5},{14,12},{15,13},{22,20},{23,21},{30,28},{31,29}} | collective-permute-start | bytes 1966088 | tf_op jit(solution)/shard_map/ppermute | solution.py:560
  450.8 23.8 %copy-start.51 = (f32[1,2048]{1,0:T(1,128)S(1)}, f32[1,2048]{1,0:T(1,128)}, u32[]{:S(2)}) copy-start(f32[1,2048]{1,0:T(1,128)} %get-tuple-element.125) | copy-start | bytes 24580
  450.8 24.0 %copy-start.42 = (f32[1024]{0:T(1024)S(1)}, f32[1024]{0:T(1024)}, u32[]{:S(2)}) copy-start(f32[1024]{0:T(1024)} %get-tuple-element.148) | copy-start | bytes 12292
  450.8 24.0 %copy-start.41 = (f32[1024]{0:T(1024)S(1)}, f32[1024]{0:T(1024)}, u32[]{:S(2)}) copy-start(f32[1024]{0:T(1024)} %get-tuple-element.146) | copy-start | bytes 12292
  450.8 24.7 %copy-start.40 = (f32[1024]{0:T(1024)S(1)}, f32[1024]{0:T(1024)}, u32[]{:S(2)}) copy-start(f32[1024]{0:T(1024)} %get-tuple-element.126) | copy-start | bytes 12292
  450.8 26.3 %collective-permute-start.36 = (bf16[256,384]{1,0:T(8,128)(2,1)}, bf16[256,384]{1,0:T(8,128)(2,1)}, u32[]{:S(2)}, u32[]{:S(2)}) collective-permute-start(bf16[256,384]{1,0:T(8,128)(2,1)} %dynamic-slice_bitcast_fusion.8), channel_id=1, source_target_pairs={{0,16},{16,0},{1,17},{17,1},{2,18},{18,2},{3,19},{19,3},{4,20},{20... | collective-permute-start | bytes 589832 | tf_op jit(solution)/shard_map/ppermute | solution.py:571
  470.9 21.5 %collective-permute-start.34 = (bf16[320,1024]{1,0:T(8,128)(2,1)}, bf16[320,1024]{1,0:T(8,128)(2,1)}, u32[]{:S(2)}, u32[]{:S(2)}) collective-permute-start(bf16[320,1024]{1,0:T(8,128)(2,1)} %get-tuple-element.175), channel_id=1, source_target_pairs={{4,2},{6,4},{5,3},{7,5},{12,10},{14,12},{13,11},{15,13},{20,18},{2... | collective-permute-start | bytes 1966088 | tf_op jit(solution)/shard_map/ppermute | solution.py:560
  472.4 20.0 %collective-permute-start.33 = (bf16[320,1024]{1,0:T(8,128)(2,1)}, bf16[320,1024]{1,0:T(8,128)(2,1)}, u32[]{:S(2)}, u32[]{:S(2)}) collective-permute-start(bf16[320,1024]{1,0:T(8,128)(2,1)} %get-tuple-element.176), channel_id=1, source_target_pairs={{0,2},{2,4},{1,3},{3,5},{8,10},{10,12},{9,11},{11,13},{16,18},{18,... | collective-permute-start | bytes 1966088 | tf_op jit(solution)/shard_map/ppermute | solution.py:560
  492.4 26.7 %copy-start.34 = (f32[14,32]{1,0:T(8,128)S(1)}, f32[14,32]{1,0:T(8,128)}, u32[]{:S(2)}) copy-start(f32[14,32]{1,0:T(8,128)} %param.27) | copy-start | bytes 5380
  492.4 26.7 %copy-start.49 = (f32[14,32]{1,0:T(8,128)S(1)}, f32[14,32]{1,0:T(8,128)}, u32[]{:S(2)}) copy-start(f32[14,32]{1,0:T(8,128)} %param.32) | copy-start | bytes 5380
  492.4 26.7 %copy-start.50 = (f32[14,32]{1,0:T(8,128)S(1)}, f32[14,32]{1,0:T(8,128)}, u32[]{:S(2)}) copy-start(f32[14,32]{1,0:T(8,128)} %param.37) | copy-start | bytes 5380
  507.7 12.8 %all-to-all-start.3 = ((bf16[8,32,384]{2,1,0:T(8,128)(2,1)}), bf16[8,32,384]{2,1,0:T(8,128)(2,1)}, u32[]{:S(2)}, u32[]{:S(2)}) async-start(bf16[8,32,384]{2,1,0:T(8,128)(2,1)} %bitcast.87), calls=%async_computation.3 | async-start | bytes 393216 | tf_op jit(solution)/shard_map/all_to_all | solution.py:815
  511.7 21.1 %collective-permute-start.38 = (bf16[320,1024]{1,0:T(8,128)(2,1)}, bf16[320,1024]{1,0:T(8,128)(2,1)}, u32[]{:S(2)}, u32[]{:S(2)}) collective-permute-start(bf16[320,1024]{1,0:T(8,128)(2,1)} %get-tuple-element.121), channel_id=1, source_target_pairs={{2,0},{4,2},{6,4},{3,1},{5,3},{7,5},{10,8},{12,10},{14,12},{11,9},... | collective-permute-start | bytes 1966088 | tf_op jit(solution)/shard_map/ppermute | solution.py:560
  513.0 19.8 %collective-permute-start.37 = (bf16[320,1024]{1,0:T(8,128)(2,1)}, bf16[320,1024]{1,0:T(8,128)(2,1)}, u32[]{:S(2)}, u32[]{:S(2)}) collective-permute-start(bf16[320,1024]{1,0:T(8,128)(2,1)} %get-tuple-element.120), channel_id=1, source_target_pairs={{0,2},{2,4},{4,6},{1,3},{3,5},{5,7},{8,10},{10,12},{12,14},{9,11},... | collective-permute-start | bytes 1966088 | tf_op jit(solution)/shard_map/ppermute | solution.py:560
  524.2 10.4 %copy-start.13 = (f32[128,1024]{1,0:T(8,128)S(1)}, f32[128,1024]{1,0:T(8,128)}, u32[]{:S(2)}) copy-start(f32[128,1024]{1,0:T(8,128)} %param.26) | copy-start | bytes 1572868
  524.2 10.4 %copy-start.24 = (f32[128,1024]{1,0:T(8,128)S(1)}, f32[128,1024]{1,0:T(8,128)}, u32[]{:S(2)}) copy-start(f32[128,1024]{1,0:T(8,128)} %param.31) | copy-start | bytes 1572868
  524.2 10.4 %copy-start.25 = (f32[128,1024]{1,0:T(8,128)S(1)}, f32[128,1024]{1,0:T(8,128)}, u32[]{:S(2)}) copy-start(f32[128,1024]{1,0:T(8,128)} %param.36) | copy-start | bytes 1572868
  534.5 1.5 collective-permute-start.39
  (38 other events, 137.3 us)
Sparse Core Ops, SparseCore 0:
  108.4 141.8 all-gather.5
  253.9 68.4 all-gather.3

commit v11 on v10

--- a/solution.py
+++ b/solution.py
@@ -511,22 +511,6 @@
     return line_order(value, line_pieces(value, axis), axis)
 
 
-def exchange_line(value, axis):
-    place = lax.axis_index(axis)
-    size = lax.axis_size(axis)
-    pick = lambda slot: lax.dynamic_index_in_dim(
-        value, jnp.clip(slot, 0, size - 1), 0, keepdims=False
-    )
-    pieces = []
-    for distance in range(1, size):
-        for move in (-distance, distance):
-            pairs = [(i, i + move) for i in range(size) if 0 <= i + move < size]
-            pieces.append((-move, lax.ppermute(pick(place + move), axis, pairs)))
-    if size == 2:
-        pieces = [(None, pieces[0][1] + pieces[1][1])]
-    return line_order(pick(place), pieces, axis)
-
-
 def rounded_sum(*terms):
     return sum(term.astype(jnp.float32) for term in terms).astype(jnp.bfloat16)
 
@@ -644,11 +628,6 @@
         small = jnp.broadcast_to(small.reshape(1, extra, 3 * lanes), (group, extra, 3 * lanes))
         owned = low(project_in).reshape(share, 3, group, lanes).transpose(2, 0, 1, 3)
         blocks = jnp.concatenate([owned.reshape(group, share, 3 * lanes), small], axis=1)
-        blocks = blocks.reshape(line, 2, share + extra, 3 * lanes)
-        keep = jnp.where(first_core, blocks[:, 0], blocks[:, 1])
-        sent = swap_cores(jnp.where(first_core, blocks[:, 1], blocks[:, 0]))
-        blocks = in_order(keep[:, None], sent[:, None], 1)
-
         pieces, swapped = [], []
         moving = [tokens, tokens]
         for step in range(1, line):
@@ -657,12 +636,12 @@
                 for sign, value in zip((-1, 1), moving)
             ]
             if step == 1:
-                blocks = exchange_line(blocks, "line")
+                blocks = lax.all_to_all(blocks, seq, split_axis=0, concat_axis=0, tiled=True)
             elif step == 2:
                 blocks = gather_line(gather_line(blocks, "inner"), "outer")
             moving, blocks, swapped = lax.optimization_barrier((moving, blocks, swapped))
             pieces += [(sign * step, value) for sign, value in zip((-1, 1), moving)]
-            if step == line - 1:
+            if step == line - 2:
                 packed = jnp.concatenate([fold(hidden_up), low(hidden_down), low(project_out)], axis=0)
                 packed, moving = lax.optimization_barrier((packed, moving))
                 gathered = lax.all_gather(packed, everyone, axis=0, tiled=False)

time: 557 us -> 537 us (0.964)
  waiting for transfers between devices: 194 us -> 162 us
  blocking collectives: 11.1 us -> 39.2 us
  starting transfers between devices: 81.7 us -> 61.1 us
    all_gather x1, waiting for transfers between devices: 63 us -> 0.01 us  [on_device(): gathered = lax.all_gather(packed, everyone, axis=0, tiled=False)]
    all_to_all x0 -> x1, blocking collectives: none -> 28.8 us  [on_device(): lax.all_to_all(blocks, seq, split_axis=0, concat_axis=0, tiled=True)]
    ppermute x6, waiting for transfers between devices: 27.5 us -> 53.1 us  [on_device(): lax.ppermute(value, 'line', line_pairs(line, sign, step))]
    all_to_all x1, waiting for transfers between devices: 0.01 us -> 21.3 us  [on_device(): lax.all_to_all(attended.reshape(group, rows, lanes), seq, split_axis=0, c...]
    ppermute x6 -> x0, starting transfers between devices: 18.7 us -> none  [exchange_line(): pieces.append((-move, lax.ppermute(pick(place + move), axis, pairs)))]
    ppermute x6 -> x0, waiting for transfers between devices: 16.5 us -> none  [exchange_line(): pieces.append((-move, lax.ppermute(pick(place + move), axis, pairs)))]
    dynamic_update_slice x19 -> x14, local copies, waits for them, and re-layouts: 15.1 us -> 15.7 us  [line_order(): whole = lax.dynamic_update_index_in_dim(whole, piece, slot, 0)]
  transfers between devices with their start and end apart: 46 -> 39, of which waited for: 18 -> 14; matrix products, arithmetic and copies ran while one was open for 19% -> 21% of each run, Pallas kernels for 23% -> 24%
where the time goes in v11:
time: 537 us; the launch traced here: 527 us
  waiting for transfers between devices  162 us (30%)
  Pallas kernels  124 us (23%)
  starting transfers between devices  61.1 us (11%)
  local copies, waits for them, and re-layouts  60.9 us (11%)
  other arithmetic  52 us (10%)
  blocking collectives  39.2 us (7%)
  between operations  15.5 us (3%)
  matrix products  11.9 us (2%)
    ppermute x6, waiting for transfers between devices, on_device(): lax.ppermute(value, 'line', line_pairs(line, sign, step))  53.1 us
    pallas_call x1, Pallas kernels, mlp(): pl.pallas_call(functools.partial(mlp_kernel, pieces), grid_spec=pltpu.Pre...  38 us
    pallas_call x1, Pallas kernels, attend_back(): pl.pallas_call(attend_back_kernel, grid_spec=pltpu.PrefetchScalarGridSpec...  34.8 us
    all_to_all x1, blocking collectives, on_device(): lax.all_to_all(blocks, seq, split_axis=0, concat_axis=0, tiled=True)  28.8 us
    pallas_call x1, Pallas kernels, attend(): pl.pallas_call(attend_kernel, grid_spec=pltpu.PrefetchScalarGridSpec(num_...  26.2 us
    ppermute x4, waiting for transfers between devices, scatter_line(): lax.ppermute(pick(1 - place), axis, [(0, 1), (1, 0)])  24.4 us
    all_to_all x1, waiting for transfers between devices, on_device(): lax.all_to_all(attended.reshape(group, rows, lanes), seq, split_axis=0, c...  21.3 us
    ppermute x3, waiting for transfers between devices, scatter_terms(): return (pick(place), lax.ppermute(pick(1 - place), axis, [(0, 1), (1, 0)]))  20.1 us
  transfers between devices with their start and end apart: 39, of which 14 were waited for; matrix products, arithmetic and copies ran while one was open for 21% of the time, Pallas kernels for 24%

profile of v11, /device:TPU:0, one launch (start us, length us, event | category | flops | bytes accessed | tf_op | source)
XLA Modules:
  0.0 527.1 jit_solution(4829286860346393616)
XLA Ops:
  7.2 5.0 collective-permute-start
  17.4 28.8 %all_to_all.35 = bf16[8,48,384]{2,1,0:T(8,128)(2,1)S(1)} all-to-all(bf16[8,48,384]{2,1,0:T(8,128)(2,1)S(1)} %pad_maximum_fusion.1), channel_id=1, replica_groups=mesh['outer'=2,'inner'=2,'line'=4,'core'=2] {'line','core'}, dimensions={0} | all-to-all | bytes 589824 | tf_op jit(solution)/shard_map/all_to_all | solution.py:639
  46.2 1.5 collective-permute-start.4
  47.7 1.6 collective-permute-start.2
  51.2 3.9 collective-permute-done.4
  56.0 1.5 collective-permute-start.5
  58.7 12.0 %collective-permute-done.5 = bf16[2,8,48,384]{3,2,1,0:T(8,128)(2,1)} collective-permute-done((bf16[2,8,48,384]{3,2,1,0:T(8,128)(2,1)}, bf16[2,8,48,384]{3,2,1,0:T(8,128)(2,1)}, u32[]{:S(2)}, u32[]{:S(2)}) %collective-permute-start.5) | collective-permute-done | bytes 589856 | tf_op jit(solution)/shard_map/ppermute | solution.py:486
  70.7 1.5 maximum_select_fusion
  72.2 4.1 collective-permute-done.3
  76.3 1.7 collective-permute-start.8
  80.5 49.0 %collective-permute-done.9 = bf16[512,1024]{1,0:T(8,128)(2,1)} collective-permute-done((bf16[512,1024]{1,0:T(8,128)(2,1)}, bf16[512,1024]{1,0:T(8,128)(2,1)}, u32[]{:S(2)}, u32[]{:S(2)}) %collective-permute-start.9) | collective-permute-done | bytes 1048608 | tf_op jit(solution)/shard_map/ppermute | solution.py:635
  145.1 1.5 copy-done.6
  146.6 1.6 bitcast_dynamic-update-slice_fusion.6
  148.4 1.6 bitcast_dynamic-update-slice_fusion.4
  155.5 2.0 copy-done.5
  157.5 14.2 %norm_mix.1 = (bf16[4096,1024]{1,0:T(8,128)(2,1)}, bf16[4096,128]{1,0:T(8,128)(2,1)}, bf16[4096,128]{1,0:T(8,128)(2,1)}, bf16[4096,128]{1,0:T(8,128)(2,1)}) custom-call(s32[1]{0:T(128)} %bitcast.10.place_ref, bf16[2048,1024]{1,0:T(8,128)(2,1)} %bitcast.206, bf16[2048,1024]{1,0:T(8,128)(2,1)} %bitcast.205, f32[1,1024]{1,0:T(1,128)} %slice.123.gain_ref, ...), custom_call_target="tpu_custom_call" | custom-call | flops 3221225472 | bytes 16777216 | tf_op jit(solution)/shard_map/norm_mix/pallas_call | solution.py:243
  171.7 26.2 %attend_forward.1 = (f32[4096,128]{1,0:T(8,128)}, bf16[4096,128]{1,0:T(8,128)(2,1)}, f32[4096,128]{1,0:T(8,128)}) custom-call(s32[2]{0:T(128)} %select_reduce_fusion.starts_ref, bf16[4096,128]{1,0:T(8,128)(2,1)} %get-tuple-element.89.q_ref, bf16[4096,128]{1,0:T(8,128)(2,1)} %get-tuple-element.90.k_ref, bf16[4096,128]{1,0:T(8,128)(2,1)} %get-tuple-element.91.v_ref), custom_call_target="tpu_custom_call" | custom-call | flops 4060086272 | bytes 8388608 | tf_op jit(solution)/shard_map/attend_forward/pallas_call | solution.py:116
  197.8 2.3 copy.98
  200.2 3.7 all-to-all-start.1
  207.7 2.0 convert_reduce_fusion
  210.0 3.3 slice.162
  213.3 21.3 %all-to-all-done.1 = bf16[8,512,128]{1,2,0:T(8,128)(2,1)S(1)} async-done(((bf16[8,512,128]{1,2,0:T(8,128)(2,1)}), bf16[8,512,128]{1,2,0:T(8,128)(2,1)S(1)}, u32[]{:S(2)}, u32[]{:S(2)}) %all-to-all-start.1) | async-done | bytes 1048608 | tf_op jit(solution)/shard_map/all_to_all | solution.py:718
  235.6 4.9 fusion.60
  244.4 1.5 reshape.380
  247.2 38.0 %mlp_both_ways.1 = (bf16[16,128,1024]{2,1,0:T(8,128)(2,1)}, bf16[16,128,1024]{2,1,0:T(8,128)(2,1)}, f32[512,1024]{1,0:T(8,128)}, f32[512,1024]{1,0:T(8,128)}, f3...) custom-call(s32[1]{0:T(128)} %bitcast.35.core_ref, bf16[512,1024]{1,0:T(8,128)(2,1)} %add_convert_fusion.4.own_ref, ...), custom_call_target="tpu_custom_call" | custom-call | flops 25769803776 | bytes 29360128 | tf_op jit(solution)/shard_map/mlp_both_ways/pallas_call | solution.py:353
  287.3 2.7 collective-permute-done.19
  289.9 3.8 multiply_reduce_fusion.1
  293.8 4.2 multiply_reduce_fusion
  300.1 1.4 copy-done.11
  304.0 4.4 all-to-all-start.2
  310.9 4.3 dynamic-slice_bitcast_fusion.2
  315.2 2.0 collective-permute-start.18
  317.2 2.5 dynamic-slice_bitcast_fusion
  319.7 1.6 collective-permute-start.21
  321.3 15.8 %collective-permute-done.20 = bf16[2,4,64,1024]{3,2,1,0:T(8,128)(2,1)} collective-permute-done((bf16[2,4,64,1024]{3,2,1,0:T(8,128)(2,1)}, bf16[2,4,64,1024]{3,2,1,0:T(8,128)(2,1)}, u32[]{:S(2)}, u32[]{:S(2)}) %collective-permute-start.20) | collective-permute-done | bytes 1048608 | tf_op jit(solution)/shard_map/ppermute | solution.py:523
  337.1 34.8 %attend_backward.1 = bf16[4096,384]{1,0:T(8,128)(2,1)} custom-call(s32[2]{0:T(128)} %select_reduce_fusion.starts_ref, bf16[4096,128]{1,0:T(8,128)(2,1)} %get-tuple-element.89.q_ref, bf16[4096,128]{1,0:T(8,128)(2,1)} %get-tuple-element.90.k_ref, bf16[4096,128]{1,0:T(8,128)(2,1)} %get-tuple-element.91.v_ref, f32[4096,128]{1,0:T(8,128)} %get-tuple-element.102.wide_ref, ...), custom_call_target="tpu_custom_call" | custom-call | flops 10150215680 | bytes 11534336 | tf_op jit(solution)/shard_map/attend_backward/pallas_call | solution.py:196
  371.9 5.4 %all-to-all-start.3 = ((bf16[8,512,384]{2,1,0:T(8,128)(2,1)}), bf16[8,512,384]{2,1,0:T(8,128)(2,1)}, u32[]{:S(2)}, u32[]{:S(2)}) async-start(bf16[8,512,384]{2,1,0:T(8,128)(2,1)} %bitcast.207), calls=%async_computation.3 | async-start | bytes 6291456 | tf_op jit(solution)/shard_map/all_to_all | solution.py:769
  377.3 4.3 collective-permute-done.18
  381.6 1.8 add_convert_fusion.2
  383.4 2.6 add_convert_fusion.1
  386.1 1.7 collective-permute-start.22
  387.8 2.7 add_convert_fusion
  391.0 4.5 convolution_convert_fusion.2
  395.6 1.8 collective-permute-start.28
  397.4 19.4 %collective-permute-done.23 = bf16[4,128,1024]{2,1,0:T(8,128)(2,1)S(1)} collective-permute-done((bf16[4,128,1024]{2,1,0:T(8,128)(2,1)S(1)}, bf16[4,128,1024]{2,1,0:T(8,128)(2,1)S(1)}, u32[]{:S(2)}, u32[]{:S(2)}) %collective-permute-start.23) | collective-permute-done | bytes 1048608 | tf_op jit(solution)/shard_map/ppermute | solution.py:555
  417.2 5.0 collective-permute-done.22
  424.1 4.1 collective-permute-start.24
  428.1 1.5 collective-permute-start.25
  431.7 1.7 collective-permute-start.29
  433.3 9.7 %collective-permute-done.24 = bf16[320,1024]{1,0:T(8,128)(2,1)} collective-permute-done((bf16[320,1024]{1,0:T(8,128)(2,1)}, bf16[320,1024]{1,0:T(8,128)(2,1)}, u32[]{:S(2)}, u32[]{:S(2)}) %collective-permute-start.24) | collective-permute-done | bytes 655392 | tf_op jit(solution)/shard_map/ppermute | solution.py:544
  443.1 5.8 %all-to-all-done.3.grad_ref = bf16[8,512,384]{2,1,0:T(8,128)(2,1)} async-done(((bf16[8,512,384]{2,1,0:T(8,128)(2,1)}), bf16[8,512,384]{2,1,0:T(8,128)(2,1)}, u32[]{:S(2)}, u32[]{:S(2)}) %all-to-all-start.3) | async-done | bytes 3145760 | tf_op jit(solution)/shard_map/all_to_all | solution.py:769
  448.9 2.9 fusion.9
  451.8 1.5 collective-permute-start.27
  453.3 2.1 collective-permute-start.26
  458.0 1.7 fusion.33
  459.6 10.9 %finish_input.1 = (f32[512,1024]{1,0:T(8,128)}, f32[1,1024]{1,0:T(1,128)}, f32[1,1024]{1,0:T(1,128)}, f32[3,1,1024]{2,1,0:T(1,128)}) custom-call(bf16[8,512,384]{2,1,0:T(8,128)(2,1)} %all-to-all-done.3.grad_ref, bf16[32,96,1024]{2,1,0:T(8,128)(2,1)} %all-gather.4.cloned.1.call-done.weight_ref, bf16[512,1024]{1,0:T(8,128)(2,1)} %x_ref.1, ...), custom_call_target="tpu_custom_call" | custom-call | flops 3221225472 | bytes 16777216 | tf_op jit(solution)/shard_map/finish_input/pallas_call | solution.py:443
  473.4 3.0 fusion.10
  477.5 10.4 %all_to_all.36 = f32[32,1,448]{2,1,0:T(1,128)S(1)} all-to-all(f32[32,1,448]{2,1,0:T(1,128)S(1)} %all_to_all.28), channel_id=1, replica_groups=mesh['outer'=2,'inner'=2,'line'=4,'core'=2] {'outer','inner','line','core'}, dimensions={0} | all-to-all | bytes 114688 | tf_op jit(solution)/shard_map/all_to_all | solution.py:823
  487.9 4.0 all-to-all-start.4
  493.3 5.4 %collective-permute-start.30 = (bf16[320,1024]{1,0:T(8,128)(2,1)}, bf16[320,1024]{1,0:T(8,128)(2,1)}, u32[]{:S(2)}, u32[]{:S(2)}) collective-permute-start(bf16[320,1024]{1,0:T(8,128)(2,1)} %get-tuple-element.120), channel_id=1, source_target_pairs={{0,2},{2,4},{4,6},{1,3},{3,5},{5,7},{8,10},{10,12},{12,14},{9,11},... | collective-permute-start | bytes 1966088 | tf_op jit(solution)/shard_map/ppermute | solution.py:544
  502.1 2.4 multiply_subtract_fusion.2
  504.5 8.6 %collective-permute-done.31 = bf16[320,1024]{1,0:T(8,128)(2,1)} collective-permute-done((bf16[320,1024]{1,0:T(8,128)(2,1)}, bf16[320,1024]{1,0:T(8,128)(2,1)}, u32[]{:S(2)}, u32[]{:S(2)}) %collective-permute-start.31) | collective-permute-done | bytes 655392 | tf_op jit(solution)/shard_map/ppermute | solution.py:544
  513.0 1.6 fusion.8
  514.9 1.4 multiply_subtract_fusion
  (292 shorter events, 71.7 us)
Async XLA Ops:
  7.2 202.9 %all-gather.6.cloned.1.call-start = ((), (), s32[]{:S(2)}) async-start(), calls=%async_computation.7 | async-start | bytes 19464192 | tf_op jit(solution)/shard_map/all_gather | solution.py:647
  7.2 39.0 %collective-permute-start = (bf16[512,1024]{1,0:T(8,128)(2,1)}, bf16[512,1024]{1,0:T(8,128)(2,1)S(1)}, u32[]{:S(2)}, u32[]{:S(2)}) collective-permute-start(bf16[512,1024]{1,0:T(8,128)(2,1)} %x_ref.1), channel_id=1, source_target_pairs={{0,2},{2,4},{4,6},{1,3},{3,5},{5,7},{8,10},{10,12},{12,14},{9,11},... | collective-permute-start | bytes 3145736 | tf_op jit(solution)/shard_map/ppermute | solution.py:635
  12.2 34.0 %collective-permute-start.1 = (bf16[512,1024]{1,0:T(8,128)(2,1)}, bf16[512,1024]{1,0:T(8,128)(2,1)}, u32[]{:S(2)}, u32[]{:S(2)}) collective-permute-start(bf16[512,1024]{1,0:T(8,128)(2,1)} %x_ref.1), channel_id=1, source_target_pairs={{2,0},{4,2},{6,4},{3,1},{5,3},{7,5},{10,8},{12,10},{14,12},{11,9},... | collective-permute-start | bytes 3145736 | tf_op jit(solution)/shard_map/ppermute | solution.py:635
  15.9 41.6 %copy-start.22 = (f32[32,1024]{1,0:T(8,128)S(1)}, f32[32,1024]{1,0:T(8,128)}, u32[]{:S(2)}) copy-start(f32[32,1024]{1,0:T(8,128)} %param.24) | copy-start | bytes 393220
  17.0 40.5 %copy-start.12 = (f32[128,1024]{1,0:T(8,128)S(1)}, f32[128,1024]{1,0:T(8,128)}, u32[]{:S(2)}) copy-start(f32[128,1024]{1,0:T(8,128)} %param.26) | copy-start | bytes 1572868
  17.1 40.5 %copy-start.9 = (f32[32,4096]{1,0:T(8,128)S(1)}, f32[32,4096]{1,0:T(8,128)}, u32[]{:S(2)}) copy-start(f32[32,4096]{1,0:T(8,128)} %param.25) | copy-start | bytes 1572868
  46.2 8.9 %collective-permute-start.4 = (bf16[8,48,384]{2,1,0:T(8,128)(2,1)S(1)}, bf16[8,48,384]{2,1,0:T(8,128)(2,1)S(1)}, u32[]{:S(2)}, u32[]{:S(2)}) collective-permute-start(bf16[8,48,384]{2,1,0:T(8,128)(2,1)S(1)} %all_to_all.35), channel_id=1, source_target_pairs={{0,8},{8,0},{1,9},{9,1},{2,10},{10,2},{3,11},{11,3},{4,12},{12,4},... | collective-permute-start | bytes 884744 | tf_op jit(solution)/shard_map/ppermute | solution.py:486
  47.7 24.4 %collective-permute-start.2 = (bf16[512,1024]{1,0:T(8,128)(2,1)S(1)}, bf16[512,1024]{1,0:T(8,128)(2,1)}, u32[]{:S(2)}, u32[]{:S(2)}) collective-permute-start(bf16[512,1024]{1,0:T(8,128)(2,1)S(1)} %collective-permute-done), channel_id=1, source_target_pairs={{2,4},{4,6},{3,5},{5,7},{10,12},{12,14},{11,13},{13,15},{18,20},{2... | collective-permute-start | bytes 3145736 | tf_op jit(solution)/shard_map/ppermute | solution.py:635
  49.4 26.9 %collective-permute-start.3 = (bf16[512,1024]{1,0:T(8,128)(2,1)}, bf16[512,1024]{1,0:T(8,128)(2,1)}, u32[]{:S(2)}, u32[]{:S(2)}) collective-permute-start(bf16[512,1024]{1,0:T(8,128)(2,1)} %collective-permute-done.1), channel_id=1, source_target_pairs={{2,0},{4,2},{3,1},{5,3},{10,8},{12,10},{11,9},{13,11},{18,16},{20,... | collective-permute-start | bytes 3145736 | tf_op jit(solution)/shard_map/ppermute | solution.py:635
  50.7 25.6 %collective-permute-start.6 = (bf16[512,1024]{1,0:T(8,128)(2,1)S(1)}, bf16[512,1024]{1,0:T(8,128)(2,1)}, u32[]{:S(2)}, u32[]{:S(2)}) collective-permute-start(bf16[512,1024]{1,0:T(8,128)(2,1)S(1)} %collective-permute-done), channel_id=1, source_target_pairs={{0,1},{1,0},{2,3},{3,2},{4,5},{5,4},{6,7},{7,6},{8,9},{9,8},{10,11... | collective-permute-start | bytes 3145736 | tf_op jit(solution)/shard_map/ppermute | solution.py:475
  50.7 25.6 %collective-permute-start.7 = (bf16[512,1024]{1,0:T(8,128)(2,1)}, bf16[512,1024]{1,0:T(8,128)(2,1)}, u32[]{:S(2)}, u32[]{:S(2)}) collective-permute-start(bf16[512,1024]{1,0:T(8,128)(2,1)} %collective-permute-done.1), channel_id=1, source_target_pairs={{0,1},{1,0},{2,3},{3,2},{4,5},{5,4},{6,7},{7,6},{8,9},{9,8},{10,11... | collective-permute-start | bytes 3145736 | tf_op jit(solution)/shard_map/ppermute | solution.py:475
  56.0 14.6 %collective-permute-start.5 = (bf16[2,8,48,384]{3,2,1,0:T(8,128)(2,1)}, bf16[2,8,48,384]{3,2,1,0:T(8,128)(2,1)}, u32[]{:S(2)}, u32[]{:S(2)}) collective-permute-start(bf16[2,8,48,384]{3,2,1,0:T(8,128)(2,1)} %maximum_select_fusion.2), channel_id=1, source_target_pairs={{0,16},{16,0},{1,17},{17,1},{2,18},{18,2},{3,19},{19,3},{4,20},{20... | collective-permute-start | bytes 1769480 | tf_op jit(solution)/shard_map/ppermute | solution.py:486
  58.5 21.3 %copy-start.3 = (bf16[512,1024]{1,0:T(8,128)(2,1)S(1)}, bf16[512,1024]{1,0:T(8,128)(2,1)}, u32[]{:S(2)}) copy-start(bf16[512,1024]{1,0:T(8,128)(2,1)} %x_ref.1) | copy-start | bytes 3145732
  76.3 4.1 collective-permute-start.8
  78.0 51.5 %collective-permute-start.9 = (bf16[512,1024]{1,0:T(8,128)(2,1)}, bf16[512,1024]{1,0:T(8,128)(2,1)}, u32[]{:S(2)}, u32[]{:S(2)}) collective-permute-start(bf16[512,1024]{1,0:T(8,128)(2,1)} %collective-permute-done.3), channel_id=1, source_target_pairs={{2,0},{3,1},{10,8},{11,9},{18,16},{19,17},{26,24},{27,25}} | collective-permute-start | bytes 3145736 | tf_op jit(solution)/shard_map/ppermute | solution.py:635
  79.3 50.2 %collective-permute-start.10 = (bf16[512,1024]{1,0:T(8,128)(2,1)}, bf16[512,1024]{1,0:T(8,128)(2,1)}, u32[]{:S(2)}, u32[]{:S(2)}) collective-permute-start(bf16[512,1024]{1,0:T(8,128)(2,1)} %collective-permute-done.2), channel_id=1, source_target_pairs={{0,1},{1,0},{2,3},{3,2},{4,5},{5,4},{6,7},{7,6},{8,9},{9,8},{10,11... | collective-permute-start | bytes 3145736 | tf_op jit(solution)/shard_map/ppermute | solution.py:475
  79.4 50.1 %collective-permute-start.11 = (bf16[512,1024]{1,0:T(8,128)(2,1)}, bf16[512,1024]{1,0:T(8,128)(2,1)}, u32[]{:S(2)}, u32[]{:S(2)}) collective-permute-start(bf16[512,1024]{1,0:T(8,128)(2,1)} %collective-permute-done.3), channel_id=1, source_target_pairs={{0,1},{1,0},{2,3},{3,2},{4,5},{5,4},{6,7},{7,6},{8,9},{9,8},{10,11... | collective-permute-start | bytes 3145736 | tf_op jit(solution)/shard_map/ppermute | solution.py:475
  79.9 74.2 %collective-permute-start.14 = (bf16[512,1024]{1,0:T(8,128)(2,1)S(1)}, bf16[512,1024]{1,0:T(8,128)(2,1)}, u32[]{:S(2)}, u32[]{:S(2)}) collective-permute-start(bf16[512,1024]{1,0:T(8,128)(2,1)S(1)} %copy-done.3), channel_id=1, source_target_pairs={{0,1},{1,0},{2,3},{3,2},{4,5},{5,4},{6,7},{7,6},{8,9},{9,8},{10,11... | collective-permute-start | bytes 3145736 | tf_op jit(solution)/shard_map/ppermute | solution.py:475
  131.3 13.2 %collective-permute-start.12 = (bf16[512,1024]{1,0:T(8,128)(2,1)}, bf16[512,1024]{1,0:T(8,128)(2,1)}, u32[]{:S(2)}, u32[]{:S(2)}) collective-permute-start(bf16[512,1024]{1,0:T(8,128)(2,1)} %collective-permute-done.8), channel_id=1, source_target_pairs={{0,1},{1,0},{2,3},{3,2},{4,5},{5,4},{6,7},{7,6},{8,9},{9,8},{10,11... | collective-permute-start | bytes 3145736 | tf_op jit(solution)/shard_map/ppermute | solution.py:475
  131.3 17.0 %collective-permute-start.13 = (bf16[512,1024]{1,0:T(8,128)(2,1)}, bf16[512,1024]{1,0:T(8,128)(2,1)S(1)}, u32[]{:S(2)}, u32[]{:S(2)}) collective-permute-start(bf16[512,1024]{1,0:T(8,128)(2,1)} %collective-permute-done.9), channel_id=1, source_target_pairs={{0,1},{1,0},{2,3},{3,2},{4,5},{5,4},{6,7},{7,6},{8,9},{9,8},{10,11... | collective-permute-start | bytes 3145736 | tf_op jit(solution)/shard_map/ppermute | solution.py:475
  197.8 6.6 %copy-start.7 = (f32[32,3072]{1,0:T(8,128)S(1)}, f32[32,3072]{1,0:T(8,128)}, u32[]{:S(2)}) copy-start(f32[32,3072]{1,0:T(8,128)} %param.23) | copy-start | bytes 1179652
  200.2 7.4 %copy-start.30 = (f32[32,32]{1,0:T(8,128)S(1)}, f32[32,32]{1,0:T(8,128)}, u32[]{:S(2)}) copy-start(f32[32,32]{1,0:T(8,128)} %get-tuple-element.129) | copy-start | bytes 12292
  200.2 7.5 %copy-start.29 = (f32[32,32]{1,0:T(8,128)S(1)}, f32[32,32]{1,0:T(8,128)}, u32[]{:S(2)}) copy-start(f32[32,32]{1,0:T(8,128)} %get-tuple-element.132) | copy-start | bytes 12292
  200.2 7.5 %copy-start.1 = (bf16[512,1024]{1,0:T(8,128)(2,1)S(1)}, bf16[512,1024]{1,0:T(8,128)(2,1)}, u32[]{:S(2)}) copy-start(bf16[512,1024]{1,0:T(8,128)(2,1)} %param.20) | copy-start | bytes 3145732
  200.2 34.4 %all-to-all-start.1 = ((bf16[8,512,128]{1,2,0:T(8,128)(2,1)}), bf16[8,512,128]{1,2,0:T(8,128)(2,1)S(1)}, u32[]{:S(2)}, u32[]{:S(2)}) async-start(bf16[8,512,128]{1,2,0:T(8,128)(2,1)} %copy.98), calls=%async_computation.1 | async-start | bytes 2097152 | tf_op jit(solution)/shard_map/all_to_all | solution.py:718
  203.9 117.4 %all-gather.4.cloned.1.call-start = ((), (), s32[]{:S(2)}) async-start(), calls=%async_computation.6 | async-start | bytes 6488064 | tf_op jit(solution)/shard_map/all_gather | solution.py:652
  205.6 7.7 %copy-start.35 = (f32[512]{0:T(512)}, f32[512]{0:T(512)S(1)}, u32[]{:S(2)}) copy-start(f32[512]{0:T(512)S(1)} %convert_element_type.246) | copy-start | bytes 6148
  209.7 37.5 %collective-permute-start.16 = (bf16[512,1024]{1,0:T(8,128)(2,1)}, bf16[512,1024]{1,0:T(8,128)(2,1)}, u32[]{:S(2)}, u32[]{:S(2)}) collective-permute-start(bf16[512,1024]{1,0:T(8,128)(2,1)} %get-tuple-element.145.gm_own_ref), channel_id=1, source_target_pairs={{0,1},{1,0},{2,3},{3,2},{4,5},{5,4},{6,7},{7,6},{8,9},{9,8},{10,11... | collective-permute-start | bytes 3145736 | tf_op jit(solution)/shard_map/ppermute | solution.py:475
  210.0 25.5 %copy-start.43 = (f32[1024]{0:T(1024)S(1)}, f32[1024]{0:T(1024)}, u32[]{:S(2)}) copy-start(f32[1024]{0:T(1024)} %mul.322) | copy-start | bytes 12292
  210.0 25.5 %copy-start.45 = (f32[1024]{0:T(1024)S(1)}, f32[1024]{0:T(1024)}, u32[]{:S(2)}) copy-start(f32[1024]{0:T(1024)} %add.310) | copy-start | bytes 12292
  242.8 4.4 collective-permute-start.15
  285.2 4.7 collective-permute-start.19
  285.8 7.9 %collective-permute-start.17 = (f32[512,1024]{1,0:T(8,128)}, f32[512,1024]{1,0:T(8,128)}, u32[]{:S(2)}, u32[]{:S(2)}) collective-permute-start(f32[512,1024]{1,0:T(8,128)} %get-tuple-element.95), channel_id=1, source_target_pairs={{0,1},{1,0},{2,3},{3,2},{4,5},{5,4},{6,7},{7,6},{8,9},{9,8},{10,11... | collective-permute-start | bytes 6291464 | tf_op jit(solution)/shard_map/ppermute | solution.py:475
  304.0 33.1 %all-to-all-start.2 = ((bf16[8,512,128]{2,1,0:T(8,128)(2,1)}), bf16[8,512,128]{2,1,0:T(8,128)(2,1)}, u32[]{:S(2)}, u32[]{:S(2)}) async-start(bf16[8,512,128]{2,1,0:T(8,128)(2,1)} %bitcast.198), calls=%async_computation.2 | async-start | bytes 2097152 | tf_op jit(solution)/shard_map/all_to_all | solution.py:748
  310.8 26.3 %collective-permute-start.20 = (bf16[2,4,64,1024]{3,2,1,0:T(8,128)(2,1)}, bf16[2,4,64,1024]{3,2,1,0:T(8,128)(2,1)}, u32[]{:S(2)}, u32[]{:S(2)}) collective-permute-start(bf16[2,4,64,1024]{3,2,1,0:T(8,128)(2,1)} %get-tuple-element.181), channel_id=1, source_target_pairs={{0,8},{8,0},{1,9},{9,1},{2,10},{10,2},{3,11},{11,3},{4,12},{12,4},... | collective-permute-start | bytes 3145736 | tf_op jit(solution)/shard_map/ppermute | solution.py:523
  310.8 6.4 %copy-start.4 = (bf16[16,128,1024]{2,1,0:T(8,128)(2,1)S(1)}, bf16[16,128,1024]{2,1,0:T(8,128)(2,1)}, u32[]{:S(2)}) copy-start(bf16[16,128,1024]{2,1,0:T(8,128)(2,1)} %get-tuple-element.101) | copy-start | bytes 12582916
  315.2 66.4 %collective-permute-start.18 = (bf16[2,4,128,1024]{3,2,1,0:T(8,128)(2,1)}, bf16[2,4,128,1024]{3,2,1,0:T(8,128)(2,1)}, u32[]{:S(2)}, u32[]{:S(2)}) collective-permute-start(bf16[2,4,128,1024]{3,2,1,0:T(8,128)(2,1)} %get-tuple-element.171), channel_id=1, source_target_pairs={{0,8},{8,0},{1,9},{9,1},{2,10},{10,2},{3,11},{11,3},{4,12},{12,4},... | collective-permute-start | bytes 6291464 | tf_op jit(solution)/shard_map/ppermute | solution.py:523
  319.7 61.9 %collective-permute-start.21 = (bf16[2,4,128,1024]{3,2,1,0:T(8,128)(2,1)}, bf16[2,4,128,1024]{3,2,1,0:T(8,128)(2,1)}, u32[]{:S(2)}, u32[]{:S(2)}) collective-permute-start(bf16[2,4,128,1024]{3,2,1,0:T(8,128)(2,1)} %get-tuple-element.169), channel_id=1, source_target_pairs={{0,16},{16,0},{1,17},{17,1},{2,18},{18,2},{3,19},{19,3},{4,20},{20... | collective-permute-start | bytes 6291464 | tf_op jit(solution)/shard_map/ppermute | solution.py:523
  371.9 77.0 %all-to-all-start.3 = ((bf16[8,512,384]{2,1,0:T(8,128)(2,1)}), bf16[8,512,384]{2,1,0:T(8,128)(2,1)}, u32[]{:S(2)}, u32[]{:S(2)}) async-start(bf16[8,512,384]{2,1,0:T(8,128)(2,1)} %bitcast.207), calls=%async_computation.3 | async-start | bytes 6291456 | tf_op jit(solution)/shard_map/all_to_all | solution.py:769
  381.6 9.3 %slice-start = ((s8[8388608]{0:T(1024)(128)(4,1)}), s8[4194304]{0:T(1024)(128)(4,1)S(1)}, s32[]{:S(2)}) async-start(s8[8388608]{0:T(1024)(128)(4,1)} %bitcast.243), calls=%async_computation.8 | async-start | bytes 8388608
  386.1 36.0 %collective-permute-start.22 = (bf16[4,192,1024]{2,1,0:T(8,128)(2,1)S(1)}, bf16[4,192,1024]{2,1,0:T(8,128)(2,1)S(1)}, u32[]{:S(2)}, u32[]{:S(2)}) collective-permute-start(bf16[4,192,1024]{2,1,0:T(8,128)(2,1)S(1)} %fusion.3), channel_id=1, source_target_pairs={{0,16},{16,0},{1,17},{17,1},{2,18},{18,2},{3,19},{19,3},{4,20},{20... | collective-permute-start | bytes 4718600 | tf_op jit(solution)/shard_map/ppermute | solution.py:555
  390.6 26.1 %collective-permute-start.23 = (bf16[4,128,1024]{2,1,0:T(8,128)(2,1)S(1)}, bf16[4,128,1024]{2,1,0:T(8,128)(2,1)S(1)}, u32[]{:S(2)}, u32[]{:S(2)}) collective-permute-start(bf16[4,128,1024]{2,1,0:T(8,128)(2,1)S(1)} %dynamic-slice_bitcast_fusion.4), channel_id=1, source_target_pairs={{0,8},{8,0},{1,9},{9,1},{2,10},{10,2},{3,11},{11,3},{4,12},{12,4},... | collective-permute-start | bytes 3145736 | tf_op jit(solution)/shard_map/ppermute | solution.py:555
  395.5 27.4 %copy-start.19 = (bf16[1024,384]{1,0:T(8,128)(2,1)}, bf16[1024,384]{1,0:T(8,128)(2,1)S(1)}, u32[]{:S(2)}) copy-start(bf16[1024,384]{1,0:T(8,128)(2,1)S(1)} %convolution_convert_fusion.2) | copy-start | bytes 2359300
  395.6 34.2 %collective-permute-start.28 = (bf16[2,256,384]{2,1,0:T(8,128)(2,1)S(1)}, bf16[2,256,384]{2,1,0:T(8,128)(2,1)}, u32[]{:S(2)}, u32[]{:S(2)}) collective-permute-start(bf16[2,256,384]{2,1,0:T(8,128)(2,1)S(1)} %dynamic-slice_bitcast_fusion.7), channel_id=1, source_target_pairs={{0,8},{8,0},{1,9},{9,1},{2,10},{10,2},{3,11},{11,3},{4,12},{12,4},... | collective-permute-start | bytes 1179656 | tf_op jit(solution)/shard_map/ppermute | solution.py:555
  422.9 6.8 %copy-start.39 = (f32[1024]{0:T(1024)S(1)}, f32[1024]{0:T(1024)}, u32[]{:S(2)}) copy-start(f32[1024]{0:T(1024)} %get-tuple-element.144) | copy-start | bytes 12292
  424.1 19.0 %collective-permute-start.24 = (bf16[320,1024]{1,0:T(8,128)(2,1)}, bf16[320,1024]{1,0:T(8,128)(2,1)}, u32[]{:S(2)}, u32[]{:S(2)}) collective-permute-start(bf16[320,1024]{1,0:T(8,128)(2,1)} %get-tuple-element.178), channel_id=1, source_target_pairs={{0,2},{1,3},{8,10},{9,11},{16,18},{17,19},{24,26},{25,27}} | collective-permute-start | bytes 1966088 | tf_op jit(solution)/shard_map/ppermute | solution.py:544
  428.1 14.9 %collective-permute-start.25 = (bf16[320,1024]{1,0:T(8,128)(2,1)}, bf16[320,1024]{1,0:T(8,128)(2,1)}, u32[]{:S(2)}, u32[]{:S(2)}) collective-permute-start(bf16[320,1024]{1,0:T(8,128)(2,1)} %get-tuple-element.177), channel_id=1, source_target_pairs={{6,4},{7,5},{14,12},{15,13},{22,20},{23,21},{30,28},{31,29}} | collective-permute-start | bytes 1966088 | tf_op jit(solution)/shard_map/ppermute | solution.py:544
  431.6 23.8 %copy-start.51 = (f32[1,2048]{1,0:T(1,128)S(1)}, f32[1,2048]{1,0:T(1,128)}, u32[]{:S(2)}) copy-start(f32[1,2048]{1,0:T(1,128)} %get-tuple-element.125) | copy-start | bytes 24580
  431.7 24.0 %copy-start.42 = (f32[1024]{0:T(1024)S(1)}, f32[1024]{0:T(1024)}, u32[]{:S(2)}) copy-start(f32[1024]{0:T(1024)} %get-tuple-element.148) | copy-start | bytes 12292
  431.7 24.1 %copy-start.41 = (f32[1024]{0:T(1024)S(1)}, f32[1024]{0:T(1024)}, u32[]{:S(2)}) copy-start(f32[1024]{0:T(1024)} %get-tuple-element.146) | copy-start | bytes 12292
  431.7 24.7 %copy-start.40 = (f32[1024]{0:T(1024)S(1)}, f32[1024]{0:T(1024)}, u32[]{:S(2)}) copy-start(f32[1024]{0:T(1024)} %get-tuple-element.126) | copy-start | bytes 12292
  431.7 26.3 %collective-permute-start.29 = (bf16[256,384]{1,0:T(8,128)(2,1)}, bf16[256,384]{1,0:T(8,128)(2,1)}, u32[]{:S(2)}, u32[]{:S(2)}) collective-permute-start(bf16[256,384]{1,0:T(8,128)(2,1)} %dynamic-slice_bitcast_fusion.8), channel_id=1, source_target_pairs={{0,16},{16,0},{1,17},{17,1},{2,18},{18,2},{3,19},{19,3},{4,20},{20... | collective-permute-start | bytes 589832 | tf_op jit(solution)/shard_map/ppermute | solution.py:555
  451.8 21.6 %collective-permute-start.27 = (bf16[320,1024]{1,0:T(8,128)(2,1)}, bf16[320,1024]{1,0:T(8,128)(2,1)}, u32[]{:S(2)}, u32[]{:S(2)}) collective-permute-start(bf16[320,1024]{1,0:T(8,128)(2,1)} %get-tuple-element.175), channel_id=1, source_target_pairs={{4,2},{6,4},{5,3},{7,5},{12,10},{14,12},{13,11},{15,13},{20,18},{2... | collective-permute-start | bytes 1966088 | tf_op jit(solution)/shard_map/ppermute | solution.py:544
  453.3 20.0 %collective-permute-start.26 = (bf16[320,1024]{1,0:T(8,128)(2,1)}, bf16[320,1024]{1,0:T(8,128)(2,1)}, u32[]{:S(2)}, u32[]{:S(2)}) collective-permute-start(bf16[320,1024]{1,0:T(8,128)(2,1)} %get-tuple-element.176), channel_id=1, source_target_pairs={{0,2},{2,4},{1,3},{3,5},{8,10},{10,12},{9,11},{11,13},{16,18},{18,... | collective-permute-start | bytes 1966088 | tf_op jit(solution)/shard_map/ppermute | solution.py:544
  473.3 26.0 %copy-start.34 = (f32[14,32]{1,0:T(8,128)S(1)}, f32[14,32]{1,0:T(8,128)}, u32[]{:S(2)}) copy-start(f32[14,32]{1,0:T(8,128)} %param.27) | copy-start | bytes 5380
  473.3 26.0 %copy-start.49 = (f32[14,32]{1,0:T(8,128)S(1)}, f32[14,32]{1,0:T(8,128)}, u32[]{:S(2)}) copy-start(f32[14,32]{1,0:T(8,128)} %param.32) | copy-start | bytes 5380
  473.3 26.0 %copy-start.50 = (f32[14,32]{1,0:T(8,128)S(1)}, f32[14,32]{1,0:T(8,128)}, u32[]{:S(2)}) copy-start(f32[14,32]{1,0:T(8,128)} %param.37) | copy-start | bytes 5380
  487.9 12.8 %all-to-all-start.4 = ((bf16[8,32,384]{2,1,0:T(8,128)(2,1)}), bf16[8,32,384]{2,1,0:T(8,128)(2,1)}, u32[]{:S(2)}, u32[]{:S(2)}) async-start(bf16[8,32,384]{2,1,0:T(8,128)(2,1)} %bitcast.67), calls=%async_computation.4 | async-start | bytes 393216 | tf_op jit(solution)/shard_map/all_to_all | solution.py:794
  492.0 21.1 %collective-permute-start.31 = (bf16[320,1024]{1,0:T(8,128)(2,1)}, bf16[320,1024]{1,0:T(8,128)(2,1)}, u32[]{:S(2)}, u32[]{:S(2)}) collective-permute-start(bf16[320,1024]{1,0:T(8,128)(2,1)} %get-tuple-element.121), channel_id=1, source_target_pairs={{2,0},{4,2},{6,4},{3,1},{5,3},{7,5},{10,8},{12,10},{14,12},{11,9},... | collective-permute-start | bytes 1966088 | tf_op jit(solution)/shard_map/ppermute | solution.py:544
  493.3 19.8 %collective-permute-start.30 = (bf16[320,1024]{1,0:T(8,128)(2,1)}, bf16[320,1024]{1,0:T(8,128)(2,1)}, u32[]{:S(2)}, u32[]{:S(2)}) collective-permute-start(bf16[320,1024]{1,0:T(8,128)(2,1)} %get-tuple-element.120), channel_id=1, source_target_pairs={{0,2},{2,4},{4,6},{1,3},{3,5},{5,7},{8,10},{10,12},{12,14},{9,11},... | collective-permute-start | bytes 1966088 | tf_op jit(solution)/shard_map/ppermute | solution.py:544
  504.5 10.4 %copy-start.13 = (f32[128,1024]{1,0:T(8,128)S(1)}, f32[128,1024]{1,0:T(8,128)}, u32[]{:S(2)}) copy-start(f32[128,1024]{1,0:T(8,128)} %param.26) | copy-start | bytes 1572868
  504.5 10.4 %copy-start.24 = (f32[128,1024]{1,0:T(8,128)S(1)}, f32[128,1024]{1,0:T(8,128)}, u32[]{:S(2)}) copy-start(f32[128,1024]{1,0:T(8,128)} %param.31) | copy-start | bytes 1572868
  504.5 10.4 %copy-start.25 = (f32[128,1024]{1,0:T(8,128)S(1)}, f32[128,1024]{1,0:T(8,128)}, u32[]{:S(2)}) copy-start(f32[128,1024]{1,0:T(8,128)} %param.36) | copy-start | bytes 1572868
  514.8 1.5 collective-permute-start.32
  (31 other events, 92.2 us)
Sparse Core Ops, SparseCore 0:
  76.5 128.9 all-gather.5
  209.1 74.3 all-gather.3

commit v12 on v11

--- a/solution.py
+++ b/solution.py
@@ -232,8 +232,8 @@
     v_ref[...] = mixed[:, 2 * lanes :]
 
 
-def norm_mix(place, own, other, block, gain, shift, weight, bias):
-    length, width = own.shape[0] * 2, own.shape[1]
+def norm_mix(place, own, other, length, block, gain, shift, weight, bias):
+    width = own.shape[1]
     lanes = bias.shape[0] // 3
     row = lambda size: pl.BlockSpec((block, size), lambda i, place: (i, 0))
     half = pl.BlockSpec((block, width), lambda i, place: (i // 2, 0))
@@ -494,17 +494,18 @@
     return pieces
 
 
-def line_order(value, pieces, axis):
+def line_order(value, pieces, axis, spare=False):
     place = lax.axis_index(axis)
     size = lax.axis_size(axis)
     if size == 2:
         other = pieces[0][1]
         return jnp.where(place == 0, jnp.stack([value, other]), jnp.stack([other, value]))
-    whole = jnp.zeros((size, *value.shape), value.dtype)
-    for distance, piece in sorted(pieces, key=lambda item: -abs(item[0])) + [(0, value)]:
-        slot = jnp.clip(place + distance, 0, size - 1)
+    whole = jnp.zeros((size + 1, *value.shape), value.dtype)
+    for distance, piece in [(0, value)] + sorted(pieces, key=lambda item: abs(item[0])):
+        slot = place + distance
+        slot = jnp.where((slot >= 0) & (slot < size), slot, size)
         whole = lax.dynamic_update_index_in_dim(whole, piece, slot, 0)
-    return whole
+    return whole if spare else whole[:size]
 
 
 def gather_line(value, axis):
@@ -671,8 +672,8 @@
     if not direct:
         pieces = line_pieces(tokens, "line")
         swapped = [(distance, swap_cores(piece)) for distance, piece in pieces]
-    own_tokens = line_order(tokens, pieces, "line").reshape(-1, width)
-    other_tokens = line_order(swap_cores(tokens), swapped, "line").reshape(-1, width)
+    own_tokens = line_order(tokens, pieces, "line", True).reshape(-1, width)
+    other_tokens = line_order(swap_cores(tokens), swapped, "line", True).reshape(-1, width)
 
     gain_one, shift_one, bias_query, bias_value, bias_out = (
         vectors[0],
@@ -704,7 +705,7 @@
 
     place = lax.axis_index(seq)
     normed_one, query, keys, values = norm_mix(
-        place.reshape(1), own_tokens, other_tokens, rows, gain_one, shift_one, mine_in, bias_in
+        place.reshape(1), own_tokens, other_tokens, length, rows, gain_one, shift_one, mine_in, bias_in
     )
     wide, attended, logs = attend(starts, query, keys, values)
     if not direct:

time: 537 us -> 544 us (1.013)
  local copies, waits for them, and re-layouts: 60.9 us -> 73.3 us
    dynamic_update_slice x14 -> x13, local copies, waits for them, and re-layouts: 15.7 us -> 25.2 us  [line_order(): whole = lax.dynamic_update_index_in_dim(whole, piece, slot, 0)]
  transfers between devices with their start and end apart: 39 -> 39, of which waited for: 14 -> 14; matrix products, arithmetic and copies ran while one was open for 21% -> 22% of each run, Pallas kernels for 24% -> 23%
where the time goes in v12:
time: 544 us; the launch traced here: 534 us
  waiting for transfers between devices  161 us (30%)
  Pallas kernels  124 us (23%)
  local copies, waits for them, and re-layouts  73.3 us (13%)
  starting transfers between devices  59.9 us (11%)
  other arithmetic  48.9 us (9%)
  blocking collectives  39.1 us (7%)
  between operations  15.4 us (3%)
  matrix products  12 us (2%)
    ppermute x6, waiting for transfers between devices, on_device(): lax.ppermute(value, 'line', line_pairs(line, sign, step))  50.7 us
    pallas_call x1, Pallas kernels, mlp(): pl.pallas_call(functools.partial(mlp_kernel, pieces), grid_spec=pltpu.Pre...  38 us
    pallas_call x1, Pallas kernels, attend_back(): pl.pallas_call(attend_back_kernel, grid_spec=pltpu.PrefetchScalarGridSpec...  34.9 us
    all_to_all x1, blocking collectives, on_device(): lax.all_to_all(blocks, seq, split_axis=0, concat_axis=0, tiled=True)  28.8 us
    pallas_call x1, Pallas kernels, attend(): pl.pallas_call(attend_kernel, grid_spec=pltpu.PrefetchScalarGridSpec(num_...  26.3 us
    dynamic_update_slice x13, local copies, waits for them, and re-layouts, line_order(): whole = lax.dynamic_update_index_in_dim(whole, piece, slot, 0)  25.2 us
    ppermute x4, waiting for transfers between devices, scatter_line(): lax.ppermute(pick(1 - place), axis, [(0, 1), (1, 0)])  24.4 us
    all_to_all x1, waiting for transfers between devices, on_device(): lax.all_to_all(attended.reshape(group, rows, lanes), seq, split_axis=0, c...  21.9 us
  transfers between devices with their start and end apart: 39, of which 14 were waited for; matrix products, arithmetic and copies ran while one was open for 22% of the time, Pallas kernels for 23%

profile of v12, /device:TPU:0, one launch (start us, length us, event | category | flops | bytes accessed | tf_op | source)
XLA Modules:
  0.0 533.7 jit_solution(18149310776704593844)
XLA Ops:
  7.2 5.0 collective-permute-start
  17.4 28.8 %all_to_all.35 = bf16[8,48,384]{2,1,0:T(8,128)(2,1)S(1)} all-to-all(bf16[8,48,384]{2,1,0:T(8,128)(2,1)S(1)} %pad_maximum_fusion.1), channel_id=1, replica_groups=mesh['outer'=2,'inner'=2,'line'=4,'core'=2] {'line','core'}, dimensions={0} | all-to-all | bytes 589824 | tf_op jit(solution)/shard_map/all_to_all | solution.py:640
  47.2 1.5 collective-permute-start.4
  48.7 1.7 collective-permute-start.2
  52.2 3.8 collective-permute-done.4
  57.0 1.5 collective-permute-start.5
  59.7 11.9 %collective-permute-done.5 = bf16[2,8,48,384]{3,2,1,0:T(8,128)(2,1)S(1)} collective-permute-done((bf16[2,8,48,384]{3,2,1,0:T(8,128)(2,1)}, bf16[2,8,48,384]{3,2,1,0:T(8,128)(2,1)S(1)}, u32[]{:S(2)}, u32[]{:S(2)}) %collective-permute-start.5) | collective-permute-done | bytes 589856 | tf_op jit(solution)/shard_map/ppermute | solution.py:486
  71.7 5.5 %collective-permute-done.3 = bf16[512,1024]{1,0:T(8,128)(2,1)} collective-permute-done((bf16[512,1024]{1,0:T(8,128)(2,1)}, bf16[512,1024]{1,0:T(8,128)(2,1)}, u32[]{:S(2)}, u32[]{:S(2)}) %collective-permute-start.3) | collective-permute-done | bytes 1048608 | tf_op jit(solution)/shard_map/ppermute | solution.py:636
  77.5 3.1 broadcast.126.clone.1
  85.9 2.3 bitcast_dynamic-update-slice_fusion.11
  88.1 3.0 broadcast.126.clone
  91.1 2.2 bitcast_dynamic-update-slice_fusion.6
  93.3 2.3 bitcast_dynamic-update-slice_fusion.10
  95.6 2.3 bitcast_dynamic-update-slice_fusion.9
  97.9 45.1 %collective-permute-done.9 = bf16[512,1024]{1,0:T(8,128)(2,1)S(1)} collective-permute-done((bf16[512,1024]{1,0:T(8,128)(2,1)}, bf16[512,1024]{1,0:T(8,128)(2,1)S(1)}, u32[]{:S(2)}, u32[]{:S(2)}) %collective-permute-start.9) | collective-permute-done | bytes 1048608 | tf_op jit(solution)/shard_map/ppermute | solution.py:636
  146.3 2.4 bitcast_dynamic-update-slice_fusion.5
  148.6 2.3 bitcast_dynamic-update-slice_fusion.4
  155.6 2.3 bitcast_dynamic-update-slice_fusion.8
  159.3 2.3 bitcast_dynamic-update-slice_fusion.1
  161.6 2.3 bitcast_dynamic-update-slice_fusion
  163.9 14.3 %norm_mix.1 = (bf16[4096,1024]{1,0:T(8,128)(2,1)}, bf16[4096,128]{1,0:T(8,128)(2,1)}, bf16[4096,128]{1,0:T(8,128)(2,1)}, bf16[4096,128]{1,0:T(8,128)(2,1)}) custom-call(s32[1]{0:T(128)} %bitcast.10.place_ref, bf16[2560,1024]{1,0:T(8,128)(2,1)} %bitcast.18.own_ref, bf16[2560,1024]{1,0:T(8,128)(2,1)} %bitcast.26.other_ref, f32[1,1024]{1,0:T(1,128)} %slice.123.gain_ref, ...), custom_call_target="tpu_custom_call" | custom-call | flops 3221225472 | bytes 16777216 | tf_op jit(solution)/shard_map/norm_mix/pallas_call | solution.py:243
  178.1 26.3 %attend_forward.1 = (f32[4096,128]{1,0:T(8,128)}, bf16[4096,128]{1,0:T(8,128)(2,1)}, f32[4096,128]{1,0:T(8,128)}) custom-call(s32[2]{0:T(128)} %select_reduce_fusion.starts_ref, bf16[4096,128]{1,0:T(8,128)(2,1)} %get-tuple-element.89.q_ref, bf16[4096,128]{1,0:T(8,128)(2,1)} %get-tuple-element.90.k_ref, bf16[4096,128]{1,0:T(8,128)(2,1)} %get-tuple-element.91.v_ref), custom_call_target="tpu_custom_call" | custom-call | flops 4060086272 | bytes 8388608 | tf_op jit(solution)/shard_map/attend_forward/pallas_call | solution.py:116
  204.4 2.3 copy.98
  206.8 3.7 all-to-all-start.1
  213.7 2.0 convert_reduce_fusion
  216.0 3.2 slice.162
  219.2 21.9 %all-to-all-done.1 = bf16[8,512,128]{1,2,0:T(8,128)(2,1)S(1)} async-done(((bf16[8,512,128]{1,2,0:T(8,128)(2,1)}), bf16[8,512,128]{1,2,0:T(8,128)(2,1)S(1)}, u32[]{:S(2)}, u32[]{:S(2)}) %all-to-all-start.1) | async-done | bytes 1048608 | tf_op jit(solution)/shard_map/all_to_all | solution.py:719
  242.1 4.9 fusion.60
  250.9 1.5 reshape.380
  253.8 38.0 %mlp_both_ways.1 = (bf16[16,128,1024]{2,1,0:T(8,128)(2,1)}, bf16[16,128,1024]{2,1,0:T(8,128)(2,1)}, f32[512,1024]{1,0:T(8,128)}, f32[512,1024]{1,0:T(8,128)}, f3...) custom-call(s32[1]{0:T(128)} %bitcast.35.core_ref, bf16[512,1024]{1,0:T(8,128)(2,1)} %add_convert_fusion.4.own_ref, ...), custom_call_target="tpu_custom_call" | custom-call | flops 25769803776 | bytes 29360128 | tf_op jit(solution)/shard_map/mlp_both_ways/pallas_call | solution.py:353
  293.8 2.7 collective-permute-done.19
  296.5 3.8 multiply_reduce_fusion.1
  300.3 4.2 multiply_reduce_fusion
  310.5 4.4 all-to-all-start.2
  318.6 4.3 dynamic-slice_bitcast_fusion.2
  323.8 2.5 dynamic-slice_bitcast_fusion
  327.7 16.0 %collective-permute-done.20 = bf16[2,4,64,1024]{3,2,1,0:T(8,128)(2,1)} collective-permute-done((bf16[2,4,64,1024]{3,2,1,0:T(8,128)(2,1)}, bf16[2,4,64,1024]{3,2,1,0:T(8,128)(2,1)}, u32[]{:S(2)}, u32[]{:S(2)}) %collective-permute-start.20) | collective-permute-done | bytes 1048608 | tf_op jit(solution)/shard_map/ppermute | solution.py:524
  343.7 34.9 %attend_backward.1 = bf16[4096,384]{1,0:T(8,128)(2,1)} custom-call(s32[2]{0:T(128)} %select_reduce_fusion.starts_ref, bf16[4096,128]{1,0:T(8,128)(2,1)} %get-tuple-element.89.q_ref, bf16[4096,128]{1,0:T(8,128)(2,1)} %get-tuple-element.90.k_ref, bf16[4096,128]{1,0:T(8,128)(2,1)} %get-tuple-element.91.v_ref, f32[4096,128]{1,0:T(8,128)} %get-tuple-element.102.wide_ref, ...), custom_call_target="tpu_custom_call" | custom-call | flops 10150215680 | bytes 11534336 | tf_op jit(solution)/shard_map/attend_backward/pallas_call | solution.py:196
  378.6 5.4 %all-to-all-start.3 = ((bf16[8,512,384]{2,1,0:T(8,128)(2,1)}), bf16[8,512,384]{2,1,0:T(8,128)(2,1)}, u32[]{:S(2)}, u32[]{:S(2)}) async-start(bf16[8,512,384]{2,1,0:T(8,128)(2,1)} %bitcast.205), calls=%async_computation.3 | async-start | bytes 6291456 | tf_op jit(solution)/shard_map/all_to_all | solution.py:770
  384.0 4.1 collective-permute-done.18
  388.2 1.8 add_convert_fusion.2
  389.9 2.6 add_convert_fusion.1
  392.7 1.5 collective-permute-start.22
  394.2 2.8 add_convert_fusion
  398.3 4.5 convolution_convert_fusion.2
  403.8 19.4 %collective-permute-done.23 = bf16[4,128,1024]{2,1,0:T(8,128)(2,1)S(1)} collective-permute-done((bf16[4,128,1024]{2,1,0:T(8,128)(2,1)S(1)}, bf16[4,128,1024]{2,1,0:T(8,128)(2,1)S(1)}, u32[]{:S(2)}, u32[]{:S(2)}) %collective-permute-start.23) | collective-permute-done | bytes 1048608 | tf_op jit(solution)/shard_map/ppermute | solution.py:556
  423.6 5.0 collective-permute-done.22
  430.6 4.1 collective-permute-start.24
  434.7 1.5 collective-permute-start.25
  438.2 1.5 collective-permute-start.29
  439.7 10.0 %collective-permute-done.24 = bf16[320,1024]{1,0:T(8,128)(2,1)} collective-permute-done((bf16[320,1024]{1,0:T(8,128)(2,1)}, bf16[320,1024]{1,0:T(8,128)(2,1)}, u32[]{:S(2)}, u32[]{:S(2)}) %collective-permute-start.24) | collective-permute-done | bytes 655392 | tf_op jit(solution)/shard_map/ppermute | solution.py:545
  449.8 5.8 %all-to-all-done.3.grad_ref = bf16[8,512,384]{2,1,0:T(8,128)(2,1)} async-done(((bf16[8,512,384]{2,1,0:T(8,128)(2,1)}), bf16[8,512,384]{2,1,0:T(8,128)(2,1)}, u32[]{:S(2)}, u32[]{:S(2)}) %all-to-all-start.3) | async-done | bytes 3145760 | tf_op jit(solution)/shard_map/all_to_all | solution.py:770
  455.6 2.9 fusion.9
  458.5 1.5 collective-permute-start.27
  460.0 2.1 collective-permute-start.26
  464.7 1.7 fusion.33
  466.4 10.9 %finish_input.1 = (f32[512,1024]{1,0:T(8,128)}, f32[1,1024]{1,0:T(1,128)}, f32[1,1024]{1,0:T(1,128)}, f32[3,1,1024]{2,1,0:T(1,128)}) custom-call(bf16[8,512,384]{2,1,0:T(8,128)(2,1)} %all-to-all-done.3.grad_ref, bf16[32,96,1024]{2,1,0:T(8,128)(2,1)} %all-gather.4.cloned.1.call-done.weight_ref, bf16[512,1024]{1,0:T(8,128)(2,1)} %x_ref.1, ...), custom_call_target="tpu_custom_call" | custom-call | flops 3221225472 | bytes 16777216 | tf_op jit(solution)/shard_map/finish_input/pallas_call | solution.py:443
  480.1 3.0 fusion.10
  484.2 10.3 %all_to_all.36 = f32[32,1,448]{2,1,0:T(1,128)S(1)} all-to-all(f32[32,1,448]{2,1,0:T(1,128)S(1)} %all_to_all.28), channel_id=1, replica_groups=mesh['outer'=2,'inner'=2,'line'=4,'core'=2] {'outer','inner','line','core'}, dimensions={0} | all-to-all | bytes 114688 | tf_op jit(solution)/shard_map/all_to_all | solution.py:824
  494.6 4.0 all-to-all-start.4
  499.9 5.4 %collective-permute-start.30 = (bf16[320,1024]{1,0:T(8,128)(2,1)}, bf16[320,1024]{1,0:T(8,128)(2,1)}, u32[]{:S(2)}, u32[]{:S(2)}) collective-permute-start(bf16[320,1024]{1,0:T(8,128)(2,1)} %get-tuple-element.120), channel_id=1, source_target_pairs={{0,2},{2,4},{4,6},{1,3},{3,5},{5,7},{8,10},{10,12},{12,14},{9,11},... | collective-permute-start | bytes 1966088 | tf_op jit(solution)/shard_map/ppermute | solution.py:545
  508.7 2.4 multiply_subtract_fusion.2
  511.1 8.6 %collective-permute-done.31 = bf16[320,1024]{1,0:T(8,128)(2,1)} collective-permute-done((bf16[320,1024]{1,0:T(8,128)(2,1)}, bf16[320,1024]{1,0:T(8,128)(2,1)}, u32[]{:S(2)}, u32[]{:S(2)}) %collective-permute-start.31) | collective-permute-done | bytes 655392 | tf_op jit(solution)/shard_map/ppermute | solution.py:545
  519.6 1.6 fusion.8
  (289 shorter events, 71.6 us)
Async XLA Ops:
  7.2 208.8 %all-gather.6.cloned.1.call-start = ((), (), s32[]{:S(2)}) async-start(), calls=%async_computation.7 | async-start | bytes 19464192 | tf_op jit(solution)/shard_map/all_gather | solution.py:648
  7.2 39.0 %collective-permute-start = (bf16[512,1024]{1,0:T(8,128)(2,1)}, bf16[512,1024]{1,0:T(8,128)(2,1)S(1)}, u32[]{:S(2)}, u32[]{:S(2)}) collective-permute-start(bf16[512,1024]{1,0:T(8,128)(2,1)} %x_ref.1), channel_id=1, source_target_pairs={{0,2},{2,4},{4,6},{1,3},{3,5},{5,7},{8,10},{10,12},{12,14},{9,11},... | collective-permute-start | bytes 3145736 | tf_op jit(solution)/shard_map/ppermute | solution.py:636
  12.2 35.0 %collective-permute-start.1 = (bf16[512,1024]{1,0:T(8,128)(2,1)}, bf16[512,1024]{1,0:T(8,128)(2,1)}, u32[]{:S(2)}, u32[]{:S(2)}) collective-permute-start(bf16[512,1024]{1,0:T(8,128)(2,1)} %x_ref.1), channel_id=1, source_target_pairs={{2,0},{4,2},{6,4},{3,1},{5,3},{7,5},{10,8},{12,10},{14,12},{11,9},... | collective-permute-start | bytes 3145736 | tf_op jit(solution)/shard_map/ppermute | solution.py:636
  15.9 42.6 %copy-start.27 = (f32[32,1024]{1,0:T(8,128)S(1)}, f32[32,1024]{1,0:T(8,128)}, u32[]{:S(2)}) copy-start(f32[32,1024]{1,0:T(8,128)} %param.24) | copy-start | bytes 393220
  17.0 41.5 %copy-start.10 = (f32[128,1024]{1,0:T(8,128)S(1)}, f32[128,1024]{1,0:T(8,128)}, u32[]{:S(2)}) copy-start(f32[128,1024]{1,0:T(8,128)} %param.26) | copy-start | bytes 1572868
  17.1 41.5 %copy-start.7 = (f32[32,4096]{1,0:T(8,128)S(1)}, f32[32,4096]{1,0:T(8,128)}, u32[]{:S(2)}) copy-start(f32[32,4096]{1,0:T(8,128)} %param.25) | copy-start | bytes 1572868
  47.2 8.9 %collective-permute-start.4 = (bf16[8,48,384]{2,1,0:T(8,128)(2,1)S(1)}, bf16[8,48,384]{2,1,0:T(8,128)(2,1)S(1)}, u32[]{:S(2)}, u32[]{:S(2)}) collective-permute-start(bf16[8,48,384]{2,1,0:T(8,128)(2,1)S(1)} %all_to_all.35), channel_id=1, source_target_pairs={{0,8},{8,0},{1,9},{9,1},{2,10},{10,2},{3,11},{11,3},{4,12},{12,4},... | collective-permute-start | bytes 884744 | tf_op jit(solution)/shard_map/ppermute | solution.py:486
  48.7 23.0 %collective-permute-start.2 = (bf16[512,1024]{1,0:T(8,128)(2,1)}, bf16[512,1024]{1,0:T(8,128)(2,1)}, u32[]{:S(2)}, u32[]{:S(2)}) collective-permute-start(bf16[512,1024]{1,0:T(8,128)(2,1)} %copy-done.16), channel_id=1, source_target_pairs={{2,4},{4,6},{3,5},{5,7},{10,12},{12,14},{11,13},{13,15},{18,20},{2... | collective-permute-start | bytes 3145736 | tf_op jit(solution)/shard_map/ppermute | solution.py:636
  50.4 26.9 %collective-permute-start.3 = (bf16[512,1024]{1,0:T(8,128)(2,1)}, bf16[512,1024]{1,0:T(8,128)(2,1)}, u32[]{:S(2)}, u32[]{:S(2)}) collective-permute-start(bf16[512,1024]{1,0:T(8,128)(2,1)} %collective-permute-done.1), channel_id=1, source_target_pairs={{2,0},{4,2},{3,1},{5,3},{10,8},{12,10},{11,9},{13,11},{18,16},{20,... | collective-permute-start | bytes 3145736 | tf_op jit(solution)/shard_map/ppermute | solution.py:636
  51.6 25.6 %collective-permute-start.6 = (bf16[512,1024]{1,0:T(8,128)(2,1)}, bf16[512,1024]{1,0:T(8,128)(2,1)}, u32[]{:S(2)}, u32[]{:S(2)}) collective-permute-start(bf16[512,1024]{1,0:T(8,128)(2,1)} %copy-done.16), channel_id=1, source_target_pairs={{0,1},{1,0},{2,3},{3,2},{4,5},{5,4},{6,7},{7,6},{8,9},{9,8},{10,11... | collective-permute-start | bytes 3145736 | tf_op jit(solution)/shard_map/ppermute | solution.py:475
  51.7 25.6 %collective-permute-start.7 = (bf16[512,1024]{1,0:T(8,128)(2,1)}, bf16[512,1024]{1,0:T(8,128)(2,1)}, u32[]{:S(2)}, u32[]{:S(2)}) collective-permute-start(bf16[512,1024]{1,0:T(8,128)(2,1)} %collective-permute-done.1), channel_id=1, source_target_pairs={{0,1},{1,0},{2,3},{3,2},{4,5},{5,4},{6,7},{7,6},{8,9},{9,8},{10,11... | collective-permute-start | bytes 3145736 | tf_op jit(solution)/shard_map/ppermute | solution.py:475
  57.0 14.5 %collective-permute-start.5 = (bf16[2,8,48,384]{3,2,1,0:T(8,128)(2,1)}, bf16[2,8,48,384]{3,2,1,0:T(8,128)(2,1)S(1)}, u32[]{:S(2)}, u32[]{:S(2)}) collective-permute-start(bf16[2,8,48,384]{3,2,1,0:T(8,128)(2,1)} %maximum_select_fusion.2), channel_id=1, source_target_pairs={{0,16},{16,0},{1,17},{17,1},{2,18},{18,2},{3,19},{19,3},{4,20},{20... | collective-permute-start | bytes 1769480 | tf_op jit(solution)/shard_map/ppermute | solution.py:486
  59.6 17.8 %copy-start.3 = (bf16[512,1024]{1,0:T(8,128)(2,1)S(1)}, bf16[512,1024]{1,0:T(8,128)(2,1)}, u32[]{:S(2)}) copy-start(bf16[512,1024]{1,0:T(8,128)(2,1)} %x_ref.1) | copy-start | bytes 3145732
  77.3 10.8 %collective-permute-start.12 = (bf16[512,1024]{1,0:T(8,128)(2,1)S(1)}, bf16[512,1024]{1,0:T(8,128)(2,1)}, u32[]{:S(2)}, u32[]{:S(2)}) collective-permute-start(bf16[512,1024]{1,0:T(8,128)(2,1)S(1)} %copy-done.3), channel_id=1, source_target_pairs={{0,1},{1,0},{2,3},{3,2},{4,5},{5,4},{6,7},{7,6},{8,9},{9,8},{10,11... | collective-permute-start | bytes 3145736 | tf_op jit(solution)/shard_map/ppermute | solution.py:475
  83.2 14.6 %collective-permute-start.8 = (bf16[512,1024]{1,0:T(8,128)(2,1)}, bf16[512,1024]{1,0:T(8,128)(2,1)S(1)}, u32[]{:S(2)}, u32[]{:S(2)}) collective-permute-start(bf16[512,1024]{1,0:T(8,128)(2,1)} %collective-permute-done.2), channel_id=1, source_target_pairs={{4,6},{5,7},{12,14},{13,15},{20,22},{21,23},{28,30},{29,31}} | collective-permute-start | bytes 3145736 | tf_op jit(solution)/shard_map/ppermute | solution.py:636
  83.9 59.1 %collective-permute-start.10 = (bf16[512,1024]{1,0:T(8,128)(2,1)}, bf16[512,1024]{1,0:T(8,128)(2,1)S(1)}, u32[]{:S(2)}, u32[]{:S(2)}) collective-permute-start(bf16[512,1024]{1,0:T(8,128)(2,1)} %collective-permute-done.2), channel_id=1, source_target_pairs={{0,1},{1,0},{2,3},{3,2},{4,5},{5,4},{6,7},{7,6},{8,9},{9,8},{10,11... | collective-permute-start | bytes 3145736 | tf_op jit(solution)/shard_map/ppermute | solution.py:475
  84.4 58.6 %collective-permute-start.9 = (bf16[512,1024]{1,0:T(8,128)(2,1)}, bf16[512,1024]{1,0:T(8,128)(2,1)S(1)}, u32[]{:S(2)}, u32[]{:S(2)}) collective-permute-start(bf16[512,1024]{1,0:T(8,128)(2,1)} %collective-permute-done.3), channel_id=1, source_target_pairs={{2,0},{3,1},{10,8},{11,9},{18,16},{19,17},{26,24},{27,25}} | collective-permute-start | bytes 3145736 | tf_op jit(solution)/shard_map/ppermute | solution.py:636
  85.7 57.3 %collective-permute-start.11 = (bf16[512,1024]{1,0:T(8,128)(2,1)}, bf16[512,1024]{1,0:T(8,128)(2,1)S(1)}, u32[]{:S(2)}, u32[]{:S(2)}) collective-permute-start(bf16[512,1024]{1,0:T(8,128)(2,1)} %collective-permute-done.3), channel_id=1, source_target_pairs={{0,1},{1,0},{2,3},{3,2},{4,5},{5,4},{6,7},{7,6},{8,9},{9,8},{10,11... | collective-permute-start | bytes 3145736 | tf_op jit(solution)/shard_map/ppermute | solution.py:475
  97.9 46.2 %copy-start.18 = (bf16[512,1024]{1,0:T(8,128)(2,1)}, bf16[512,1024]{1,0:T(8,128)(2,1)S(1)}, u32[]{:S(2)}) copy-start(bf16[512,1024]{1,0:T(8,128)(2,1)S(1)} %collective-permute-done.8) | copy-start | bytes 3145732
  144.5 14.8 %collective-permute-start.13 = (bf16[512,1024]{1,0:T(8,128)(2,1)}, bf16[512,1024]{1,0:T(8,128)(2,1)}, u32[]{:S(2)}, u32[]{:S(2)}) collective-permute-start(bf16[512,1024]{1,0:T(8,128)(2,1)} %copy-done.18), channel_id=1, source_target_pairs={{0,1},{1,0},{2,3},{3,2},{4,5},{5,4},{6,7},{7,6},{8,9},{9,8},{10,11... | collective-permute-start | bytes 3145736 | tf_op jit(solution)/shard_map/ppermute | solution.py:475
  144.5 17.1 %collective-permute-start.14 = (bf16[512,1024]{1,0:T(8,128)(2,1)S(1)}, bf16[512,1024]{1,0:T(8,128)(2,1)}, u32[]{:S(2)}, u32[]{:S(2)}) collective-permute-start(bf16[512,1024]{1,0:T(8,128)(2,1)S(1)} %collective-permute-done.9), channel_id=1, source_target_pairs={{0,1},{1,0},{2,3},{3,2},{4,5},{5,4},{6,7},{7,6},{8,9},{9,8},{10,11... | collective-permute-start | bytes 3145736 | tf_op jit(solution)/shard_map/ppermute | solution.py:475
  152.0 5.8 %copy-start.15 = (bf16[512,1024]{1,0:T(8,128)(2,1)S(1)}, bf16[512,1024]{1,0:T(8,128)(2,1)}, u32[]{:S(2)}) copy-start(bf16[512,1024]{1,0:T(8,128)(2,1)} %copy-done.14) | copy-start | bytes 3145732
  204.4 6.6 %copy-start.5 = (f32[32,3072]{1,0:T(8,128)S(1)}, f32[32,3072]{1,0:T(8,128)}, u32[]{:S(2)}) copy-start(f32[32,3072]{1,0:T(8,128)} %param.23) | copy-start | bytes 1179652
  206.8 6.9 %copy-start.1 = (bf16[512,1024]{1,0:T(8,128)(2,1)S(1)}, bf16[512,1024]{1,0:T(8,128)(2,1)}, u32[]{:S(2)}) copy-start(bf16[512,1024]{1,0:T(8,128)(2,1)} %param.20) | copy-start | bytes 3145732
  206.8 34.4 %all-to-all-start.1 = ((bf16[8,512,128]{1,2,0:T(8,128)(2,1)}), bf16[8,512,128]{1,2,0:T(8,128)(2,1)S(1)}, u32[]{:S(2)}, u32[]{:S(2)}) async-start(bf16[8,512,128]{1,2,0:T(8,128)(2,1)} %copy.98), calls=%async_computation.1 | async-start | bytes 2097152 | tf_op jit(solution)/shard_map/all_to_all | solution.py:719
  210.5 117.3 %all-gather.4.cloned.1.call-start = ((), (), s32[]{:S(2)}) async-start(), calls=%async_computation.6 | async-start | bytes 6488064 | tf_op jit(solution)/shard_map/all_gather | solution.py:653
  212.1 7.1 %copy-start.35 = (f32[512]{0:T(512)}, f32[512]{0:T(512)S(1)}, u32[]{:S(2)}) copy-start(f32[512]{0:T(512)S(1)} %convert_element_type.246) | copy-start | bytes 6148
  212.8 29.3 %copy-start.43 = (f32[1024]{0:T(1024)}, f32[1024]{0:T(1024)S(1)}, u32[]{:S(2)}) copy-start(f32[1024]{0:T(1024)S(1)} %mul.322) | copy-start | bytes 12292
  215.6 38.2 %collective-permute-start.16 = (bf16[512,1024]{1,0:T(8,128)(2,1)}, bf16[512,1024]{1,0:T(8,128)(2,1)}, u32[]{:S(2)}, u32[]{:S(2)}) collective-permute-start(bf16[512,1024]{1,0:T(8,128)(2,1)} %get-tuple-element.145.gm_own_ref), channel_id=1, source_target_pairs={{0,1},{1,0},{2,3},{3,2},{4,5},{5,4},{6,7},{7,6},{8,9},{9,8},{10,11... | collective-permute-start | bytes 3145736 | tf_op jit(solution)/shard_map/ppermute | solution.py:475
  249.4 4.4 collective-permute-start.15
  291.8 4.7 collective-permute-start.19
  292.3 7.9 %collective-permute-start.17 = (f32[512,1024]{1,0:T(8,128)}, f32[512,1024]{1,0:T(8,128)}, u32[]{:S(2)}, u32[]{:S(2)}) collective-permute-start(f32[512,1024]{1,0:T(8,128)} %get-tuple-element.95), channel_id=1, source_target_pairs={{0,1},{1,0},{2,3},{3,2},{4,5},{5,4},{6,7},{7,6},{8,9},{9,8},{10,11... | collective-permute-start | bytes 6291464 | tf_op jit(solution)/shard_map/ppermute | solution.py:475
  309.4 5.6 %copy-start.22 = (bf16[8,512,128]{1,2,0:T(8,128)(2,1)S(1)}, bf16[8,512,128]{1,2,0:T(8,128)(2,1)}, u32[]{:S(2)}) copy-start(bf16[8,512,128]{1,2,0:T(8,128)(2,1)} %copy-done.21) | copy-start | bytes 3145732
  310.5 33.1 %all-to-all-start.2 = ((bf16[8,512,128]{2,1,0:T(8,128)(2,1)}), bf16[8,512,128]{2,1,0:T(8,128)(2,1)}, u32[]{:S(2)}, u32[]{:S(2)}) async-start(bf16[8,512,128]{2,1,0:T(8,128)(2,1)} %bitcast.198), calls=%async_computation.2 | async-start | bytes 2097152 | tf_op jit(solution)/shard_map/all_to_all | solution.py:749
  317.4 26.3 %collective-permute-start.20 = (bf16[2,4,64,1024]{3,2,1,0:T(8,128)(2,1)}, bf16[2,4,64,1024]{3,2,1,0:T(8,128)(2,1)}, u32[]{:S(2)}, u32[]{:S(2)}) collective-permute-start(bf16[2,4,64,1024]{3,2,1,0:T(8,128)(2,1)} %get-tuple-element.181), channel_id=1, source_target_pairs={{0,8},{8,0},{1,9},{9,1},{2,10},{10,2},{3,11},{11,3},{4,12},{12,4},... | collective-permute-start | bytes 3145736 | tf_op jit(solution)/shard_map/ppermute | solution.py:524
  322.9 65.3 %collective-permute-start.18 = (bf16[2,4,128,1024]{3,2,1,0:T(8,128)(2,1)}, bf16[2,4,128,1024]{3,2,1,0:T(8,128)(2,1)}, u32[]{:S(2)}, u32[]{:S(2)}) collective-permute-start(bf16[2,4,128,1024]{3,2,1,0:T(8,128)(2,1)} %get-tuple-element.171), channel_id=1, source_target_pairs={{0,8},{8,0},{1,9},{9,1},{2,10},{10,2},{3,11},{11,3},{4,12},{12,4},... | collective-permute-start | bytes 6291464 | tf_op jit(solution)/shard_map/ppermute | solution.py:524
  326.2 61.9 %collective-permute-start.21 = (bf16[2,4,128,1024]{3,2,1,0:T(8,128)(2,1)}, bf16[2,4,128,1024]{3,2,1,0:T(8,128)(2,1)}, u32[]{:S(2)}, u32[]{:S(2)}) collective-permute-start(bf16[2,4,128,1024]{3,2,1,0:T(8,128)(2,1)} %get-tuple-element.169), channel_id=1, source_target_pairs={{0,16},{16,0},{1,17},{17,1},{2,18},{18,2},{3,19},{19,3},{4,20},{20... | collective-permute-start | bytes 6291464 | tf_op jit(solution)/shard_map/ppermute | solution.py:524
  378.6 77.0 %all-to-all-start.3 = ((bf16[8,512,384]{2,1,0:T(8,128)(2,1)}), bf16[8,512,384]{2,1,0:T(8,128)(2,1)}, u32[]{:S(2)}, u32[]{:S(2)}) async-start(bf16[8,512,384]{2,1,0:T(8,128)(2,1)} %bitcast.205), calls=%async_computation.3 | async-start | bytes 6291456 | tf_op jit(solution)/shard_map/all_to_all | solution.py:770
  388.2 10.2 %slice-start = ((s8[8388608]{0:T(1024)(128)(4,1)}), s8[4194304]{0:T(1024)(128)(4,1)S(1)}, s32[]{:S(2)}) async-start(s8[8388608]{0:T(1024)(128)(4,1)} %bitcast.242), calls=%async_computation.8 | async-start | bytes 8388608
  392.5 5.8 %slice-start.1 = ((s8[8388608]{0:T(1024)(128)(4,1)}), s8[4194304]{0:T(1024)(128)(4,1)S(1)}, s32[]{:S(2)}) async-start(s8[8388608]{0:T(1024)(128)(4,1)} %bitcast.242), calls=%async_computation.9 | async-start | bytes 8388608
  392.7 36.0 %collective-permute-start.22 = (bf16[4,192,1024]{2,1,0:T(8,128)(2,1)S(1)}, bf16[4,192,1024]{2,1,0:T(8,128)(2,1)S(1)}, u32[]{:S(2)}, u32[]{:S(2)}) collective-permute-start(bf16[4,192,1024]{2,1,0:T(8,128)(2,1)S(1)} %fusion.3), channel_id=1, source_target_pairs={{0,16},{16,0},{1,17},{17,1},{2,18},{18,2},{3,19},{19,3},{4,20},{20... | collective-permute-start | bytes 4718600 | tf_op jit(solution)/shard_map/ppermute | solution.py:556
  397.1 26.1 %collective-permute-start.23 = (bf16[4,128,1024]{2,1,0:T(8,128)(2,1)S(1)}, bf16[4,128,1024]{2,1,0:T(8,128)(2,1)S(1)}, u32[]{:S(2)}, u32[]{:S(2)}) collective-permute-start(bf16[4,128,1024]{2,1,0:T(8,128)(2,1)S(1)} %dynamic-slice_bitcast_fusion.4), channel_id=1, source_target_pairs={{0,8},{8,0},{1,9},{9,1},{2,10},{10,2},{3,11},{11,3},{4,12},{12,4},... | collective-permute-start | bytes 3145736 | tf_op jit(solution)/shard_map/ppermute | solution.py:556
  402.9 26.6 %copy-start.24 = (bf16[1024,384]{1,0:T(8,128)(2,1)}, bf16[1024,384]{1,0:T(8,128)(2,1)S(1)}, u32[]{:S(2)}) copy-start(bf16[1024,384]{1,0:T(8,128)(2,1)S(1)} %convolution_convert_fusion.2) | copy-start | bytes 2359300
  402.9 33.3 %collective-permute-start.28 = (bf16[2,256,384]{2,1,0:T(8,128)(2,1)S(1)}, bf16[2,256,384]{2,1,0:T(8,128)(2,1)}, u32[]{:S(2)}, u32[]{:S(2)}) collective-permute-start(bf16[2,256,384]{2,1,0:T(8,128)(2,1)S(1)} %dynamic-slice_bitcast_fusion.7), channel_id=1, source_target_pairs={{0,8},{8,0},{1,9},{9,1},{2,10},{10,2},{3,11},{11,3},{4,12},{12,4},... | collective-permute-start | bytes 1179656 | tf_op jit(solution)/shard_map/ppermute | solution.py:556
  429.4 6.8 %copy-start.39 = (f32[1024]{0:T(1024)S(1)}, f32[1024]{0:T(1024)}, u32[]{:S(2)}) copy-start(f32[1024]{0:T(1024)} %get-tuple-element.144) | copy-start | bytes 12292
  430.6 19.2 %collective-permute-start.24 = (bf16[320,1024]{1,0:T(8,128)(2,1)}, bf16[320,1024]{1,0:T(8,128)(2,1)}, u32[]{:S(2)}, u32[]{:S(2)}) collective-permute-start(bf16[320,1024]{1,0:T(8,128)(2,1)} %get-tuple-element.178), channel_id=1, source_target_pairs={{0,2},{1,3},{8,10},{9,11},{16,18},{17,19},{24,26},{25,27}} | collective-permute-start | bytes 1966088 | tf_op jit(solution)/shard_map/ppermute | solution.py:545
  434.7 15.1 %collective-permute-start.25 = (bf16[320,1024]{1,0:T(8,128)(2,1)}, bf16[320,1024]{1,0:T(8,128)(2,1)}, u32[]{:S(2)}, u32[]{:S(2)}) collective-permute-start(bf16[320,1024]{1,0:T(8,128)(2,1)} %get-tuple-element.177), channel_id=1, source_target_pairs={{6,4},{7,5},{14,12},{15,13},{22,20},{23,21},{30,28},{31,29}} | collective-permute-start | bytes 1966088 | tf_op jit(solution)/shard_map/ppermute | solution.py:545
  438.2 24.0 %copy-start.50 = (f32[1,2048]{1,0:T(1,128)S(1)}, f32[1,2048]{1,0:T(1,128)}, u32[]{:S(2)}) copy-start(f32[1,2048]{1,0:T(1,128)} %get-tuple-element.125) | copy-start | bytes 24580
  438.2 24.2 %copy-start.42 = (f32[1024]{0:T(1024)S(1)}, f32[1024]{0:T(1024)}, u32[]{:S(2)}) copy-start(f32[1024]{0:T(1024)} %get-tuple-element.148) | copy-start | bytes 12292
  438.2 24.2 %copy-start.41 = (f32[1024]{0:T(1024)S(1)}, f32[1024]{0:T(1024)}, u32[]{:S(2)}) copy-start(f32[1024]{0:T(1024)} %get-tuple-element.146) | copy-start | bytes 12292
  438.2 24.9 %copy-start.40 = (f32[1024]{0:T(1024)S(1)}, f32[1024]{0:T(1024)}, u32[]{:S(2)}) copy-start(f32[1024]{0:T(1024)} %get-tuple-element.126) | copy-start | bytes 12292
  438.2 26.5 %collective-permute-start.29 = (bf16[256,384]{1,0:T(8,128)(2,1)}, bf16[256,384]{1,0:T(8,128)(2,1)}, u32[]{:S(2)}, u32[]{:S(2)}) collective-permute-start(bf16[256,384]{1,0:T(8,128)(2,1)} %dynamic-slice_bitcast_fusion.8), channel_id=1, source_target_pairs={{0,16},{16,0},{1,17},{17,1},{2,18},{18,2},{3,19},{19,3},{4,20},{20... | collective-permute-start | bytes 589832 | tf_op jit(solution)/shard_map/ppermute | solution.py:556
  458.5 21.6 %collective-permute-start.27 = (bf16[320,1024]{1,0:T(8,128)(2,1)}, bf16[320,1024]{1,0:T(8,128)(2,1)}, u32[]{:S(2)}, u32[]{:S(2)}) collective-permute-start(bf16[320,1024]{1,0:T(8,128)(2,1)} %get-tuple-element.175), channel_id=1, source_target_pairs={{4,2},{6,4},{5,3},{7,5},{12,10},{14,12},{13,11},{15,13},{20,18},{2... | collective-permute-start | bytes 1966088 | tf_op jit(solution)/shard_map/ppermute | solution.py:545
  460.0 20.0 %collective-permute-start.26 = (bf16[320,1024]{1,0:T(8,128)(2,1)}, bf16[320,1024]{1,0:T(8,128)(2,1)}, u32[]{:S(2)}, u32[]{:S(2)}) collective-permute-start(bf16[320,1024]{1,0:T(8,128)(2,1)} %get-tuple-element.176), channel_id=1, source_target_pairs={{0,2},{2,4},{1,3},{3,5},{8,10},{10,12},{9,11},{11,13},{16,18},{18,... | collective-permute-start | bytes 1966088 | tf_op jit(solution)/shard_map/ppermute | solution.py:545
  480.0 25.9 %copy-start.34 = (f32[14,32]{1,0:T(8,128)S(1)}, f32[14,32]{1,0:T(8,128)}, u32[]{:S(2)}) copy-start(f32[14,32]{1,0:T(8,128)} %param.27) | copy-start | bytes 5380
  480.0 25.9 %copy-start.48 = (f32[14,32]{1,0:T(8,128)S(1)}, f32[14,32]{1,0:T(8,128)}, u32[]{:S(2)}) copy-start(f32[14,32]{1,0:T(8,128)} %param.32) | copy-start | bytes 5380
  480.0 25.9 %copy-start.49 = (f32[14,32]{1,0:T(8,128)S(1)}, f32[14,32]{1,0:T(8,128)}, u32[]{:S(2)}) copy-start(f32[14,32]{1,0:T(8,128)} %param.37) | copy-start | bytes 5380
  494.6 12.8 %all-to-all-start.4 = ((bf16[8,32,384]{2,1,0:T(8,128)(2,1)}), bf16[8,32,384]{2,1,0:T(8,128)(2,1)}, u32[]{:S(2)}, u32[]{:S(2)}) async-start(bf16[8,32,384]{2,1,0:T(8,128)(2,1)} %bitcast.67), calls=%async_computation.4 | async-start | bytes 393216 | tf_op jit(solution)/shard_map/all_to_all | solution.py:795
  498.6 21.1 %collective-permute-start.31 = (bf16[320,1024]{1,0:T(8,128)(2,1)}, bf16[320,1024]{1,0:T(8,128)(2,1)}, u32[]{:S(2)}, u32[]{:S(2)}) collective-permute-start(bf16[320,1024]{1,0:T(8,128)(2,1)} %get-tuple-element.121), channel_id=1, source_target_pairs={{2,0},{4,2},{6,4},{3,1},{5,3},{7,5},{10,8},{12,10},{14,12},{11,9},... | collective-permute-start | bytes 1966088 | tf_op jit(solution)/shard_map/ppermute | solution.py:545
  499.9 19.8 %collective-permute-start.30 = (bf16[320,1024]{1,0:T(8,128)(2,1)}, bf16[320,1024]{1,0:T(8,128)(2,1)}, u32[]{:S(2)}, u32[]{:S(2)}) collective-permute-start(bf16[320,1024]{1,0:T(8,128)(2,1)} %get-tuple-element.120), channel_id=1, source_target_pairs={{0,2},{2,4},{4,6},{1,3},{3,5},{5,7},{8,10},{10,12},{12,14},{9,11},... | collective-permute-start | bytes 1966088 | tf_op jit(solution)/shard_map/ppermute | solution.py:545
  511.1 10.4 %copy-start.11 = (f32[128,1024]{1,0:T(8,128)S(1)}, f32[128,1024]{1,0:T(8,128)}, u32[]{:S(2)}) copy-start(f32[128,1024]{1,0:T(8,128)} %param.26) | copy-start | bytes 1572868
  511.1 10.4 %copy-start.29 = (f32[128,1024]{1,0:T(8,128)S(1)}, f32[128,1024]{1,0:T(8,128)}, u32[]{:S(2)}) copy-start(f32[128,1024]{1,0:T(8,128)} %param.31) | copy-start | bytes 1572868
  511.1 10.4 %copy-start.30 = (f32[128,1024]{1,0:T(8,128)S(1)}, f32[128,1024]{1,0:T(8,128)}, u32[]{:S(2)}) copy-start(f32[128,1024]{1,0:T(8,128)} %param.36) | copy-start | bytes 1572868
  521.4 1.5 collective-permute-start.32
  (30 other events, 76.3 us)
Sparse Core Ops, SparseCore 0:
  77.4 134.8 all-gather.5
  215.9 74.1 all-gather.3
